TPU v7x, 32 devices: a whole 2x2x4 slice. The times are simulated.
32 devices in a mesh: blk: 16 (over z, x, core), group: 2 (over y).
Axes of the slice: x: 2, y: 2, z: 4, core: 2. Of those that a mesh axis runs over, the one named last changes fastest.
Arguments:
- sketch: bfloat16 [8192, 768], P('blk'), may hold values from -6 to 6
- far_tiles: bfloat16 [16, 2, 3, 1, 512, 512], P('blk', 'group'), may hold values from -0.1875 to 0.1875
- row_blocks: int32 [16, 2, 3, 1], P('blk', 'group'), may hold values from 0 to 1, as said below
- owner_route: int32 [16, 2, 2], P('blk', 'group'), may hold values from 0 to 1, each once within a row
- cluster_basis: bfloat16 [16, 2, 1024, 256], P('blk', 'group'), may hold values from -0.1875 to 0.1875
Outputs:
- coefficients: float32 [16, 2, 256, 768], P('blk', 'group')
Inputs may be any that keep to these rules, and one draw needn't show every extreme that they name: `row_blocks`: for one device and one offset, the 1 entries are distinct. `owner_route`: for each device the entries are a permutation of 0 .. 2 - 1.
All inputs are finite; a program needn't handle non-finite values.
Results may differ from a plain program's by a relative error of at most 0.0029.
Values may be sent and summed in bfloat16 or wider, within the bound.
No kernel may reach another device: no remote copies, remote signals or barrier semaphores. Data moves between devices by JAX's collectives and lax.ppermute only.
A program may use at most 64 MiB of HBM per device.

v0:
```python
import jax
import jax.numpy as jnp
from jax import lax
from jax.sharding import PartitionSpec as P


def from_behind(array, axis, by):
    devices = lax.axis_size(axis)
    return lax.ppermute(array, axis, [(i, (i + by) % devices) for i in range(devices)])


def contribute(summed, far_tiles, row_blocks, offset, current):
    product = jnp.einsum(
        "trk,kc->trc", far_tiles[0, 0, offset], current, preferred_element_type=jnp.float32
    )
    return summed.at[row_blocks[0, 0, offset]].add(product)


def body(sketch, far_tiles, row_blocks, owner_route, cluster_basis):
    offsets = far_tiles.shape[2]
    radius = (offsets - 1) // 2
    groups = lax.axis_size("group")
    tile_rows = far_tiles.shape[4]
    columns = sketch.shape[1]
    summed = jnp.zeros((groups, tile_rows, columns), jnp.float32)
    current = from_behind(sketch, "blk", -radius)
    summed = contribute(summed, far_tiles, row_blocks, 2 * radius, current)
    for hop_count in range(1, 2 * radius + 1):
        current = from_behind(current, "blk", 1)
        summed = contribute(summed, far_tiles, row_blocks, 2 * radius - hop_count, current)
    sampled = summed.astype(jnp.bfloat16)
    ordered = jnp.zeros_like(sampled).at[owner_route[0, 0]].set(sampled)
    basis_local = cluster_basis[0, 0]
    received = lax.all_to_all(ordered, "group", split_axis=0, concat_axis=0, tiled=True)
    stacked = received.reshape(received.shape[0] * received.shape[1], received.shape[2])
    coefficients = lax.dot_general(
        basis_local, stacked, (((0,), (0,)), ((), ())), preferred_element_type=jnp.float32
    )
    return coefficients[None, None]


def solution(mesh):
    placed = (
        P("blk", None),
        P("blk", "group", None, None, None, None),
        P("blk", "group", None, None),
        P("blk", "group", None),
        P("blk", "group", None, None),
    )
    return jax.shard_map(
        body, mesh=mesh, in_specs=placed, out_specs=P("blk", "group", None, None), check_vma=False
    )
```

profile of v0, /device:TPU:0, one launch (start us, length us, event | category | flops | bytes accessed | tf_op | source)
XLA Modules:
  0.0 66.0 jit_solution(172004403094819492)
XLA Ops:
  0.0 0.0 copy-start
  0.0 5.4 %collective-permute-start = (bf16[512,768]{1,0:T(8,128)(2,1)}, bf16[512,768]{1,0:T(8,128)(2,1)S(1)}, u32[]{:S(2)}, u32[]{:S(2)}) collective-permute-start(bf16[512,768]{1,0:T(8,128)(2,1)} %param.11), channel_id=1, source_target_pairs={{0,30},{2,0},{4,2},{6,4},{8,6},{10,8},{12,10},{14,12},{16,14},{18,... | collective-permute-start | bytes 2359304 | tf_op jit(solution)/shard_map/ppermute | solution.py:9
  5.4 9.8 %collective-permute-done = bf16[512,768]{1,0:T(8,128)(2,1)S(1)} collective-permute-done((bf16[512,768]{1,0:T(8,128)(2,1)}, bf16[512,768]{1,0:T(8,128)(2,1)S(1)}, u32[]{:S(2)}, u32[]{:S(2)}) %collective-permute-start) | collective-permute-done | bytes 786464 | tf_op jit(solution)/shard_map/ppermute | solution.py:9
  15.2 0.0 collective-permute-start.1
  15.2 1.4 %fusion.10 = (s32[1,1,1,1]{2,3,1,0:T(1,128)}, s32[1,1,1,1]{2,3,1,0:T(1,128)}, s32[1,1,1,1]{2,3,1,0:T(1,128)}) fusion(s32[1,1,3,1]{2,3,1,0:T(1,128)} %param.13), kind=kLoop, calls=%fused_computation.25 | loop fusion | bytes 24 | tf_op jit(solution)/shard_map/slice | solution.py:16
  22.2 1.4 %and_reduce_fusion = (pred[]{:T(512)}, pred[]{:T(512)}, pred[]{:T(512)}) fusion(s32[3]{0:T(128)} %constant.71.clone.1, s32[1]{0:T(128)} %constant.69.clone.1, s32[1]{0:T(128)} %select_n.22, s32[1]{0:T(128)} %select_n.21, s32[1]{0:T(128)} %select_n.20), kind=kLoop, calls=%fused_computation.15 | loop fusion | flops 51 | bytes 31 | tf_op jit(solution)/shard_map/reduce.5
  23.6 5.9 %collective-permute-done.1 = bf16[512,768]{1,0:T(8,128)(2,1)S(1)} collective-permute-done((bf16[512,768]{1,0:T(8,128)(2,1)S(1)}, bf16[512,768]{1,0:T(8,128)(2,1)S(1)}, u32[]{:S(2)}, u32[]{:S(2)}) %collective-permute-start.1) | collective-permute-done | bytes 786464 | tf_op jit(solution)/shard_map/ppermute | solution.py:9
  29.5 0.0 collective-permute-start.2
  29.5 0.7 fusion.9
  30.2 0.0 copy-start.1
  30.2 0.2 broadcast_in_dim.14
  30.4 1.2 %copy-done.1 = bf16[1,1,3,1,512,512]{5,4,3,2,1,0:T(8,128)(2,1)S(1)} copy-done((bf16[1,1,3,1,512,512]{5,4,3,2,1,0:T(8,128)(2,1)S(1)}, bf16[1,1,3,1,512,512]{5,4,3,2,1,0:T(8,128)(2,1)}, u32[]{:S(2)}) %copy-start.1) | copy-done | bytes 1572888
  31.6 1.2 %bitcast_dynamic-update-slice_fusion = f32[2,512,768]{2,1,0:T(8,128)S(1)} fusion(f32[2,512,768]{2,1,0:T(8,128)S(1)} %broadcast_in_dim.14, s32[]{:T(128)} %bitcast.5, bf16[512,768]{1,0:T(8,128)(2,1)S(1)} %collective-permute-done, pred[]{:T(512)} %get-tuple-element.43, bf16[1,1,3,1,512,512]{5,4,3,2,1,0:T(8,128)(2,1)S(1)} %copy-done.1), kind=kOutput, calls=%fused_computation.5 | convolution fusion | flops 403046400 | bytes 2883589 | tf_op jit(solution)/shard_map/trk,kc->trc/dot_general | solution.py:13
  32.8 1.3 %fusion = f32[2,512,768]{2,1,0:T(8,128)S(1)} fusion(f32[2,512,768]{2,1,0:T(8,128)S(1)} %bitcast_dynamic-update-slice_fusion, s32[]{:T(128)} %bitcast.7, bf16[512,768]{1,0:T(8,128)(2,1)S(1)} %collective-permute-done.1, pred[]{:T(512)} %get-tuple-element.42, bf16[1,1,3,1,512,512]{5,4,3,2,1,0:T(8,128)(2,1)S(1)} %copy-done.1), kind=kOutput, calls=%fused_computation.3 | convolution fusion | flops 403439616 | bytes 4456453 | tf_op jit(solution)/shard_map/trk,kc->trc/dot_general | solution.py:13
  34.1 9.5 %collective-permute-done.2 = bf16[512,768]{1,0:T(8,128)(2,1)S(1)} collective-permute-done((bf16[512,768]{1,0:T(8,128)(2,1)S(1)}, bf16[512,768]{1,0:T(8,128)(2,1)S(1)}, u32[]{:S(2)}, u32[]{:S(2)}) %collective-permute-start.2) | collective-permute-done | bytes 786464 | tf_op jit(solution)/shard_map/ppermute | solution.py:9
  43.6 1.3 %fusion.1 = f32[2,512,768]{2,1,0:T(8,128)S(1)} fusion(f32[2,512,768]{2,1,0:T(8,128)S(1)} %fusion, s32[]{:T(128)} %bitcast.11, bf16[512,768]{1,0:T(8,128)(2,1)S(1)} %collective-permute-done.2, pred[]{:T(512)} %get-tuple-element.41, bf16[1,1,3,1,512,512]{5,4,3,2,1,0:T(8,128)(2,1)S(1)} %copy-done.1), kind=kOutput, calls=%fused_computation.4 | convolution fusion | flops 403439616 | bytes 4456453 | tf_op jit(solution)/shard_map/trk,kc->trc/dot_general | solution.py:13
  45.0 1.3 %convert_element_type.3 = bf16[2,512,768]{2,1,0:T(8,128)(2,1)} convert(f32[2,512,768]{2,1,0:T(8,128)S(1)} %fusion.1) | non-fusion elementwise | flops 786432 | bytes 4718592 | tf_op jit(solution)/shard_map/convert_element_type | solution.py:31
  46.3 0.1 broadcast_in_dim.6
  46.4 3.0 %scatter_fusion = bf16[2,512,768]{2,1,0:T(8,128)(2,1)S(1)} fusion(bf16[2,512,768]{2,1,0:T(8,128)(2,1)S(1)} %broadcast_in_dim.6, s32[2]{0:T(128)S(1)} %fusion.9, bf16[2,512,768]{2,1,0:T(8,128)(2,1)} %convert_element_type.3), kind=kCustom, calls=%fused_computation | custom fusion | bytes 4718600 | tf_op jit(solution)/shard_map/scatter | solution.py:32
  49.4 14.8 %all_to_all.5 = bf16[2,512,768]{2,1,0:T(8,128)(2,1)S(1)} all-to-all(bf16[2,512,768]{2,1,0:T(8,128)(2,1)S(1)} %scatter_fusion), channel_id=1, replica_groups=mesh['blk'=16,'group'=2] {'group'}, dimensions={0} | all-to-all | bytes 3145728 | tf_op jit(solution)/shard_map/all_to_all | solution.py:34
  64.2 0.0 copy-done
  64.2 0.6 convolution_bitcast_fusion
  64.8 1.1 %copy.6 = f32[1,1,256,768]{3,2,1,0:T(8,128)} copy(f32[1,1,256,768]{2,3,1,0:T(8,128)S(1)} %convolution_bitcast_fusion) | data formatting | bytes 1572864 | tf_op jit(solution)/shard_map/broadcast_in_dim | solution.py:39
Async XLA Ops:
  0.0 64.2 %copy-start = (bf16[1,1,1024,256]{3,2,1,0:T(8,128)(2,1)S(1)}, bf16[1,1,1024,256]{3,2,1,0:T(8,128)(2,1)}, u32[]{:S(2)}) copy-start(bf16[1,1,1024,256]{3,2,1,0:T(8,128)(2,1)} %param.15) | copy-start | bytes 1572868
  0.0 15.2 %collective-permute-start = (bf16[512,768]{1,0:T(8,128)(2,1)}, bf16[512,768]{1,0:T(8,128)(2,1)S(1)}, u32[]{:S(2)}, u32[]{:S(2)}) collective-permute-start(bf16[512,768]{1,0:T(8,128)(2,1)} %param.11), channel_id=1, source_target_pairs={{0,30},{2,0},{4,2},{6,4},{8,6},{10,8},{12,10},{14,12},{16,14},{18,... | collective-permute-start | bytes 2359304 | tf_op jit(solution)/shard_map/ppermute | solution.py:9
  15.2 14.3 %collective-permute-start.1 = (bf16[512,768]{1,0:T(8,128)(2,1)S(1)}, bf16[512,768]{1,0:T(8,128)(2,1)S(1)}, u32[]{:S(2)}, u32[]{:S(2)}) collective-permute-start(bf16[512,768]{1,0:T(8,128)(2,1)S(1)} %collective-permute-done), channel_id=1, source_target_pairs={{0,2},{2,4},{4,6},{6,8},{8,10},{10,12},{12,14},{14,16},{16,18},{18... | collective-permute-start | bytes 2359304 | tf_op jit(solution)/shard_map/ppermute | solution.py:9
  29.5 14.1 %collective-permute-start.2 = (bf16[512,768]{1,0:T(8,128)(2,1)S(1)}, bf16[512,768]{1,0:T(8,128)(2,1)S(1)}, u32[]{:S(2)}, u32[]{:S(2)}) collective-permute-start(bf16[512,768]{1,0:T(8,128)(2,1)S(1)} %collective-permute-done.1), channel_id=1, source_target_pairs={{0,2},{2,4},{4,6},{6,8},{8,10},{10,12},{12,14},{14,16},{16,18},{18... | collective-permute-start | bytes 2359304 | tf_op jit(solution)/shard_map/ppermute | solution.py:9
  30.2 1.4 %copy-start.1 = (bf16[1,1,3,1,512,512]{5,4,3,2,1,0:T(8,128)(2,1)S(1)}, bf16[1,1,3,1,512,512]{5,4,3,2,1,0:T(8,128)(2,1)}, u32[]{:S(2)}) copy-start(bf16[1,1,3,1,512,512]{5,4,3,2,1,0:T(8,128)(2,1)} %param.12) | copy-start | bytes 4718596
where the time goes:
time: 66.4 us; the launch traced here: 66 us
  waiting for transfers between devices  25.3 us (38%)
  blocking collectives  14.8 us (22%)
  local copies, waits for them, and re-layouts  7.06 us (11%)
  between operations  5.58 us (8%)
  starting transfers between devices  5.42 us (8%)
  matrix products  4.43 us (7%)
  other arithmetic  3.41 us (5%)
    ppermute x3, waiting for transfers between devices, from_behind(): lax.ppermute(array, axis, [(i, (i + by) % devices) for i in range(devices)])  25.3 us
    all_to_all x1, blocking collectives, body(): lax.all_to_all(ordered, 'group', split_axis=0, concat_axis=0, tiled=True)  14.8 us
    ppermute x3, starting transfers between devices, from_behind(): lax.ppermute(array, axis, [(i, (i + by) % devices) for i in range(devices)])  5.42 us
    dot_general x3, matrix products, contribute(): jnp.einsum('trk,kc->trc', far_tiles[0, 0, offset], current, preferred_ele...  3.83 us
    scatter x1, local copies, waits for them, and re-layouts, body(): ordered = jnp.zeros_like(sampled).at[owner_route[0, 0]].set(sampled)  3.02 us
    another operation x1, other arithmetic  1.44 us
    slice x1, local copies, waits for them, and re-layouts, contribute(): return summed.at[row_blocks[0, 0, offset]].add(product)  1.38 us
  transfers between devices with their start and end apart: 3, of which 3 were waited for; matrix products, arithmetic and copies ran while one was open for 9% of the time, Pallas kernels for 0%

commit v1 on v0

v1 whole, which is shorter than its diff:
```python
import functools

import jax
import jax.numpy as jnp
from jax import lax
from jax.experimental import pallas as pl
from jax.experimental.pallas import tpu as pltpu
from jax.sharding import PartitionSpec as P

CUTS = (8, 4)
TRANSPOSED = (((0,), (0,)), ((), ()))


def from_behind(array, axis, by):
    devices = lax.axis_size(axis)
    return lax.ppermute(array, axis, [(i, (i + by) % devices) for i in range(devices)])


def swap_near(array):
    devices = lax.axis_size("blk")
    return lax.ppermute(array, "blk", [(i, i ^ 1) for i in range(devices)])


def swap_far(array):
    devices = lax.axis_size("blk")
    return lax.ppermute(
        array, "blk", [(i, (i + 1 if i % 2 else i - 1) % devices) for i in range(devices)]
    )


def in_vmem(array):
    return pltpu.with_memory_space_constraint(array, pltpu.VMEM)


def partial_kernel(
    start, row_blocks, owner_route, tiles, own, near, far, kept_basis, lent_basis, kept, sent, summed
):
    parity = lax.rem(lax.axis_index("blk"), 2)
    group = lax.axis_index("group")
    slots = tiles.shape[3]
    width = far.shape[1]
    columns = pl.ds(start, width)
    summed[...] = jnp.zeros_like(summed)
    for offset, panel in (
        (1, own[:, columns]),
        (2 - 2 * parity, near[:, columns]),
        (2 * parity, far[...]),
    ):
        for slot in range(slots):
            owner = owner_route[0, 0, row_blocks[0, 0, offset, slot]]
            place = jnp.where(owner == group, 0, 1)
            summed[place] += jnp.dot(
                tiles[0, 0, offset, slot], panel, preferred_element_type=jnp.float32
            )
    sent[...] = lax.dot_general(
        lent_basis[...], summed[1].astype(jnp.bfloat16), TRANSPOSED, preferred_element_type=jnp.float32
    ).astype(jnp.bfloat16)
    kept[...] = lax.dot_general(
        kept_basis[...], summed[0].astype(jnp.bfloat16), TRANSPOSED, preferred_element_type=jnp.float32
    )


def partials(start, row_blocks, owner_route, tiles, own, near, far, kept_basis, lent_basis):
    rank = kept_basis.shape[1]
    rows, width = tiles.shape[4], far.shape[1]
    vmem = pl.BlockSpec(memory_space=pltpu.VMEM)
    smem = pl.BlockSpec(memory_space=pltpu.SMEM)
    return pl.pallas_call(
        functools.partial(partial_kernel, start),
        out_shape=(
            pltpu.VMEM((rank, width), jnp.float32),
            pltpu.VMEM((rank, width), jnp.bfloat16),
        ),
        in_specs=[smem] * 2 + [vmem] * 6,
        out_specs=[vmem] * 2,
        scratch_shapes=[pltpu.VMEM((2, rows, width), jnp.float32)],
        compiler_params=pltpu.CompilerParams(vmem_limit_bytes=16 << 20),
        cost_estimate=pl.CostEstimate(
            flops=2 * rows * width * (3 * own.shape[0] + 2 * rank),
            bytes_accessed=4 << 20,
            transcendentals=0,
        ),
    )(
        row_blocks,
        owner_route,
        *(in_vmem(x) for x in (tiles, own, near, far, kept_basis, lent_basis)),
    )


def join_kernel(starts, *refs):
    parts, out = refs[:-1], refs[-1]
    for start, kept, received in zip(starts, parts[0::2], parts[1::2]):
        out[:, pl.ds(start, kept.shape[1])] = kept[...] + received[...].astype(jnp.float32)


def join(starts, parts, columns):
    vmem = pl.BlockSpec(memory_space=pltpu.VMEM)
    flat = [in_vmem(x) for part in parts for x in part]
    return pl.pallas_call(
        functools.partial(join_kernel, starts),
        out_shape=jax.ShapeDtypeStruct((flat[0].shape[0], columns), jnp.float32),
        in_specs=[vmem] * len(flat),
        out_specs=vmem,
        compiler_params=pltpu.CompilerParams(vmem_limit_bytes=16 << 20),
        cost_estimate=pl.CostEstimate(flops=0, bytes_accessed=2 << 20, transcendentals=0),
    )(*flat)


def paired_body(sketch, far_tiles, row_blocks, owner_route, cluster_basis):
    columns = sketch.shape[1]
    half = cluster_basis.shape[2] // 2
    group = lax.axis_index("group")
    starts, widths = [], []
    for cut in CUTS:
        starts.append(sum(widths))
        widths.append(columns * cut // sum(CUTS))
    far = [swap_far(sketch[:, s : s + w]) for s, w in zip(starts, widths)]
    near = swap_near(sketch)
    basis = cluster_basis[0, 0]
    lent_basis = from_behind(
        lax.dynamic_slice_in_dim(basis, (1 - group) * half, half, 0), "group", 1
    )
    kept_basis = lax.dynamic_slice_in_dim(basis, group * half, half, 0)
    parts = []
    for start, panel in zip(starts, far):
        kept, sent = partials(
            start, row_blocks, owner_route, far_tiles, sketch, near, panel, kept_basis, lent_basis
        )
        parts.append((kept, from_behind(sent, "group", 1)))
    return join(tuple(starts), parts, columns)[None, None]


def contribute(summed, far_tiles, row_blocks, offset, current):
    product = jnp.einsum(
        "trk,kc->trc", far_tiles[0, 0, offset], current, preferred_element_type=jnp.float32
    )
    return summed.at[row_blocks[0, 0, offset]].add(product)


def ring_body(sketch, far_tiles, row_blocks, owner_route, cluster_basis):
    offsets = far_tiles.shape[2]
    radius = (offsets - 1) // 2
    groups = lax.axis_size("group")
    tile_rows = far_tiles.shape[4]
    columns = sketch.shape[1]
    summed = jnp.zeros((groups, tile_rows, columns), jnp.float32)
    for offset in range(offsets):
        current = from_behind(sketch, "blk", radius - offset) if offset != radius else sketch
        summed = contribute(summed, far_tiles, row_blocks, offset, current)
    sampled = summed.astype(jnp.bfloat16)
    ordered = jnp.zeros_like(sampled).at[owner_route[0, 0]].set(sampled)
    received = lax.all_to_all(ordered, "group", split_axis=0, concat_axis=0, tiled=True)
    stacked = received.reshape(received.shape[0] * received.shape[1], received.shape[2])
    coefficients = lax.dot_general(
        cluster_basis[0, 0], stacked, TRANSPOSED, preferred_element_type=jnp.float32
    )
    return coefficients[None, None]


def body(sketch, far_tiles, row_blocks, owner_route, cluster_basis):
    small = cluster_basis.shape[3] < far_tiles.shape[4]
    paired = lax.axis_size("group") == 2 and lax.axis_size("blk") % 2 == 0
    if small and paired and far_tiles.shape[2] == 3:
        return paired_body(sketch, far_tiles, row_blocks, owner_route, cluster_basis)
    return ring_body(sketch, far_tiles, row_blocks, owner_route, cluster_basis)


def solution(mesh):
    placed = (
        P("blk", None),
        P("blk", "group", None, None, None, None),
        P("blk", "group", None, None),
        P("blk", "group", None),
        P("blk", "group", None, None),
    )
    return jax.shard_map(
        body, mesh=mesh, in_specs=placed, out_specs=P("blk", "group", None, None), check_vma=False
    )
```

time: 66.4 us -> 32.5 us (0.49)
  the two profiles are of different devices: /device:TPU:0 before, /device:TPU:1 now
where the time goes in v1:
time: 32.5 us; the launch traced here: 32.3 us
  waiting for transfers between devices  14.1 us (43%)
  starting transfers between devices  7.53 us (23%)
  Pallas kernels  6 us (18%)
  local copies, waits for them, and re-layouts  4.62 us (14%)
    ppermute x2, waiting for transfers between devices, swap_far(): lax.ppermute(array, 'blk', [(i, (i + 1 if i % 2 else i - 1) % devices) fo...  7.26 us
    ppermute x3, waiting for transfers between devices, from_behind(): lax.ppermute(array, axis, [(i, (i + by) % devices) for i in range(devices)])  6.89 us
    pallas_call x2, Pallas kernels, partials(): pl.pallas_call(functools.partial(partial_kernel, start), out_shape=(pltpu...  5.04 us
    ppermute x3, starting transfers between devices, from_behind(): lax.ppermute(array, axis, [(i, (i + by) % devices) for i in range(devices)])  4.07 us
    ppermute x2, starting transfers between devices, swap_far(): lax.ppermute(array, 'blk', [(i, (i + 1 if i % 2 else i - 1) % devices) fo...  3.35 us
    slice x2, local copies, waits for them, and re-layouts, paired_body(): far = [swap_far(sketch[:, s:s + w]) for s, w in zip(starts, widths)]  2.73 us
    dynamic_slice x1, local copies, waits for them, and re-layouts, paired_body(): lax.dynamic_slice_in_dim(basis, (1 - group) * half, half, 0)  1.78 us
    pallas_call x1, Pallas kernels, join(): pl.pallas_call(functools.partial(join_kernel, starts), out_shape=jax.Shap...  0.95 us
  transfers between devices with their start and end apart: 6, of which 3 were waited for; matrix products, arithmetic and copies ran while one was open for 14% of the time, Pallas kernels for 16%

profile of v1, /device:TPU:1, one launch (start us, length us, event | category | flops | bytes accessed | tf_op | source)
XLA Modules:
  0.0 32.3 jit_solution(17483151782112259438)
XLA Ops:
  0.0 0.0 copy-start
  0.0 0.0 copy-start.3
  0.0 0.0 copy-start.1
  0.0 0.0 copy-start.2
  0.0 0.1 collective-permute-start
  0.1 2.0 %slice.6 = bf16[512,512]{1,0:T(8,128)(2,1)} slice(bf16[512,768]{1,0:T(8,128)(2,1)} %own.3), slice={[0:512], [0:512]} | slice | bytes 1048576 | tf_op jit(solution)/shard_map/slice | solution.py:117
  2.1 2.6 %collective-permute-start.1 = (bf16[512,512]{1,0:T(8,128)(2,1)}, bf16[512,512]{1,0:T(8,128)(2,1)}, u32[]{:S(2)}, u32[]{:S(2)}) collective-permute-start(bf16[512,512]{1,0:T(8,128)(2,1)} %slice.6), channel_id=1, source_target_pairs={{0,30},{2,4},{4,2},{6,8},{8,6},{10,12},{12,10},{14,16},{16,14},{18... | collective-permute-start | bytes 1572872 | tf_op jit(solution)/shard_map/ppermute | solution.py:26
  4.7 1.8 %dynamic-slice_bitcast_fusion = (bf16[512,256]{1,0:T(8,128)(2,1)}, bf16[512,256]{1,0:T(8,128)(2,1)S(1)}) fusion(bf16[1,1,1024,256]{3,2,1,0:T(8,128)(2,1)} %param.9, s32[]{:T(128)S(6)} %select_n.7, s32[]{:T(128)S(6)} %select_n.6), kind=kLoop, calls=%fused_computation | loop fusion | bytes 1048584 | tf_op jit(solution)/shard_map/dynamic_slice | solution.py:121
  6.5 1.2 %collective-permute-start.2 = (bf16[512,256]{1,0:T(8,128)(2,1)}, bf16[512,256]{1,0:T(8,128)(2,1)}, u32[]{:S(2)}, u32[]{:S(2)}) collective-permute-start(bf16[512,256]{1,0:T(8,128)(2,1)} %get-tuple-element.13), channel_id=1, source_target_pairs={{0,1},{1,0},{2,3},{3,2},{4,5},{5,4},{6,7},{7,6},{8,9},{9,8},{10,11... | collective-permute-start | bytes 786440 | tf_op jit(solution)/shard_map/ppermute | solution.py:16
  7.7 0.0 copy-done
  7.7 0.7 %slice.7 = bf16[512,256]{1,0:T(8,128)(2,1)} slice(bf16[512,768]{1,0:T(8,128)(2,1)S(1)} %copy-done), slice={[0:512], [512:768]} | slice | bytes 524288 | tf_op jit(solution)/shard_map/slice | solution.py:117
  8.5 0.8 %collective-permute-start.4 = (bf16[512,256]{1,0:T(8,128)(2,1)}, bf16[512,256]{1,0:T(8,128)(2,1)}, u32[]{:S(2)}, u32[]{:S(2)}) collective-permute-start(bf16[512,256]{1,0:T(8,128)(2,1)} %slice.7), channel_id=1, source_target_pairs={{0,30},{2,4},{4,2},{6,8},{8,6},{10,12},{12,10},{14,16},{16,14},{18... | collective-permute-start | bytes 786440 | tf_op jit(solution)/shard_map/ppermute | solution.py:26
  9.2 0.0 copy-done.3
  9.2 0.1 copy.6.row_blocks
  9.3 3.0 %collective-permute-done.2.lent_basis = bf16[512,256]{1,0:T(8,128)(2,1)} collective-permute-done((bf16[512,256]{1,0:T(8,128)(2,1)}, bf16[512,256]{1,0:T(8,128)(2,1)}, u32[]{:S(2)}, u32[]{:S(2)}) %collective-permute-start.2) | collective-permute-done | bytes 262176 | tf_op jit(solution)/shard_map/ppermute | solution.py:16
  12.3 7.3 %collective-permute-done.1.far = bf16[512,512]{1,0:T(8,128)(2,1)} collective-permute-done((bf16[512,512]{1,0:T(8,128)(2,1)}, bf16[512,512]{1,0:T(8,128)(2,1)}, u32[]{:S(2)}, u32[]{:S(2)}) %collective-permute-start.1) | collective-permute-done | bytes 524320 | tf_op jit(solution)/shard_map/ppermute | solution.py:26
  19.6 0.0 collective-permute-done.near
  19.6 0.0 copy-done.1
  19.6 0.0 copy-done.2
  19.6 2.7 %shard_map.55 = (f32[256,512]{1,0:T(8,128)S(1)}, bf16[256,512]{1,0:T(8,128)(2,1)S(1)}) custom-call(s32[1,1,3,1]{3,2,1,0:T(4,128)S(1)} %copy.6.row_blocks, s32[1,1,2]{2,1,0:T(1,128)S(1)} %copy-done.2, bf16[1,1,3,1,512,512]{5,4,3,2,1,0:T(8,128)(2,1)S(1)} %copy-done.1, bf16[512,768]{1,0:T(8,128)(2,1)S(1)} %copy-done, ...), custom_call_target="tpu_custom_call" | custom-call | flops 1073741824 | bytes 4194304 | tf_op jit(solution)/shard_map/pallas_call | solution.py:68
  22.3 2.5 %collective-permute-start.3 = (bf16[256,512]{1,0:T(8,128)(2,1)S(1)}, bf16[256,512]{1,0:T(8,128)(2,1)S(1)}, u32[]{:S(2)}, u32[]{:S(2)}) collective-permute-start(bf16[256,512]{1,0:T(8,128)(2,1)S(1)} %get-tuple-element.10), channel_id=1, source_target_pairs={{0,1},{1,0},{2,3},{3,2},{4,5},{5,4},{6,7},{7,6},{8,9},{9,8},{10,11... | collective-permute-start | bytes 786440 | tf_op jit(solution)/shard_map/ppermute | solution.py:16
  24.8 0.0 collective-permute-done.4.far
  24.8 2.4 %shard_map.56 = (f32[256,256]{1,0:T(8,128)S(1)}, bf16[256,256]{1,0:T(8,128)(2,1)S(1)}) custom-call(s32[1,1,3,1]{3,2,1,0:T(4,128)S(1)} %copy.6.row_blocks, s32[1,1,2]{2,1,0:T(1,128)S(1)} %copy-done.2, bf16[1,1,3,1,512,512]{5,4,3,2,1,0:T(8,128)(2,1)S(1)} %copy-done.1, bf16[512,768]{1,0:T(8,128)(2,1)S(1)} %copy-done, ...), custom_call_target="tpu_custom_call" | custom-call | flops 536870912 | bytes 4194304 | tf_op jit(solution)/shard_map/pallas_call | solution.py:68
  27.2 0.3 collective-permute-start.5
  27.5 3.9 %collective-permute-done.5.refs_3_ = bf16[256,256]{1,0:T(8,128)(2,1)S(1)} collective-permute-done((bf16[256,256]{1,0:T(8,128)(2,1)S(1)}, bf16[256,256]{1,0:T(8,128)(2,1)S(1)}, u32[]{:S(2)}, u32[]{:S(2)}) %collective-permute-start.5) | collective-permute-done | bytes 131104 | tf_op jit(solution)/shard_map/ppermute | solution.py:16
  31.4 0.0 collective-permute-done.3.refs_1_
  31.4 1.0 %shard_map.57 = f32[256,768]{1,0:T(8,128)} custom-call(f32[256,512]{1,0:T(8,128)S(1)} %get-tuple-element.9.refs_0_, bf16[256,512]{1,0:T(8,128)(2,1)S(1)} %collective-permute-done.3.refs_1_, f32[256,256]{1,0:T(8,128)S(1)} %get-tuple-element.11.refs_2_, bf16[256,256]{1,0:T(8,128)(2,1)S(1)} %collective-permute-done.5.refs_3_), custom_call_target="tpu_custom_call" | custom-call | bytes 2097152 | tf_op jit(solution)/shard_map/pallas_call | solution.py:99
Async XLA Ops:
  0.0 7.7 %copy-start = (bf16[512,768]{1,0:T(8,128)(2,1)S(1)}, bf16[512,768]{1,0:T(8,128)(2,1)}, u32[]{:S(2)}) copy-start(bf16[512,768]{1,0:T(8,128)(2,1)} %own.3) | copy-start | bytes 2359300
  0.0 9.2 %copy-start.3 = (s32[1,1,3,1]{2,3,1,0:T(1,128)S(1)}, s32[1,1,3,1]{2,3,1,0:T(1,128)}, u32[]{:S(2)}) copy-start(s32[1,1,3,1]{2,3,1,0:T(1,128)} %param.7) | copy-start | bytes 40
  0.0 19.6 %copy-start.1 = (bf16[1,1,3,1,512,512]{5,4,3,2,1,0:T(8,128)(2,1)S(1)}, bf16[1,1,3,1,512,512]{5,4,3,2,1,0:T(8,128)(2,1)}, u32[]{:S(2)}) copy-start(bf16[1,1,3,1,512,512]{5,4,3,2,1,0:T(8,128)(2,1)} %tiles.3) | copy-start | bytes 4718596
  0.0 19.6 %copy-start.2 = (s32[1,1,2]{2,1,0:T(1,128)S(1)}, s32[1,1,2]{2,1,0:T(1,128)}, u32[]{:S(2)}) copy-start(s32[1,1,2]{2,1,0:T(1,128)} %owner_route.3) | copy-start | bytes 28
  0.0 19.6 %collective-permute-start = (bf16[512,768]{1,0:T(8,128)(2,1)}, bf16[512,768]{1,0:T(8,128)(2,1)S(1)}, u32[]{:S(2)}, u32[]{:S(2)}) collective-permute-start(bf16[512,768]{1,0:T(8,128)(2,1)} %own.3), channel_id=1, source_target_pairs={{0,2},{2,0},{4,6},{6,4},{8,10},{10,8},{12,14},{14,12},{16,18},{18,... | collective-permute-start | bytes 2359304 | tf_op jit(solution)/shard_map/ppermute | solution.py:21
  2.1 17.4 %collective-permute-start.1 = (bf16[512,512]{1,0:T(8,128)(2,1)}, bf16[512,512]{1,0:T(8,128)(2,1)}, u32[]{:S(2)}, u32[]{:S(2)}) collective-permute-start(bf16[512,512]{1,0:T(8,128)(2,1)} %slice.6), channel_id=1, source_target_pairs={{0,30},{2,4},{4,2},{6,8},{8,6},{10,12},{12,10},{14,16},{16,14},{18... | collective-permute-start | bytes 1572872 | tf_op jit(solution)/shard_map/ppermute | solution.py:26
  6.5 5.8 %collective-permute-start.2 = (bf16[512,256]{1,0:T(8,128)(2,1)}, bf16[512,256]{1,0:T(8,128)(2,1)}, u32[]{:S(2)}, u32[]{:S(2)}) collective-permute-start(bf16[512,256]{1,0:T(8,128)(2,1)} %get-tuple-element.13), channel_id=1, source_target_pairs={{0,1},{1,0},{2,3},{3,2},{4,5},{5,4},{6,7},{7,6},{8,9},{9,8},{10,11... | collective-permute-start | bytes 786440 | tf_op jit(solution)/shard_map/ppermute | solution.py:16
  8.5 16.3 %collective-permute-start.4 = (bf16[512,256]{1,0:T(8,128)(2,1)}, bf16[512,256]{1,0:T(8,128)(2,1)}, u32[]{:S(2)}, u32[]{:S(2)}) collective-permute-start(bf16[512,256]{1,0:T(8,128)(2,1)} %slice.7), channel_id=1, source_target_pairs={{0,30},{2,4},{4,2},{6,8},{8,6},{10,12},{12,10},{14,16},{16,14},{18... | collective-permute-start | bytes 786440 | tf_op jit(solution)/shard_map/ppermute | solution.py:26
  22.3 9.1 %collective-permute-start.3 = (bf16[256,512]{1,0:T(8,128)(2,1)S(1)}, bf16[256,512]{1,0:T(8,128)(2,1)S(1)}, u32[]{:S(2)}, u32[]{:S(2)}) collective-permute-start(bf16[256,512]{1,0:T(8,128)(2,1)S(1)} %get-tuple-element.10), channel_id=1, source_target_pairs={{0,1},{1,0},{2,3},{3,2},{4,5},{5,4},{6,7},{7,6},{8,9},{9,8},{10,11... | collective-permute-start | bytes 786440 | tf_op jit(solution)/shard_map/ppermute | solution.py:16
  27.2 4.2 %collective-permute-start.5 = (bf16[256,256]{1,0:T(8,128)(2,1)S(1)}, bf16[256,256]{1,0:T(8,128)(2,1)S(1)}, u32[]{:S(2)}, u32[]{:S(2)}) collective-permute-start(bf16[256,256]{1,0:T(8,128)(2,1)S(1)} %get-tuple-element.12), channel_id=1, source_target_pairs={{0,1},{1,0},{2,3},{3,2},{4,5},{5,4},{6,7},{7,6},{8,9},{9,8},{10,11... | collective-permute-start | bytes 393224 | tf_op jit(solution)/shard_map/ppermute | solution.py:16

commit v2 on v0

v2 whole, which is shorter than its diff:
```python
import functools

import jax
import jax.numpy as jnp
from jax import lax
from jax.experimental import pallas as pl
from jax.experimental.pallas import tpu as pltpu
from jax.sharding import PartitionSpec as P

TRANSPOSED = (((0,), (0,)), ((), ()))


def from_behind(array, axis, by):
    devices = lax.axis_size(axis)
    return lax.ppermute(array, axis, [(i, (i + by) % devices) for i in range(devices)])


def swap_near(array):
    devices = lax.axis_size("blk")
    return lax.ppermute(array, "blk", [(i, i ^ 1) for i in range(devices)])


def swap_far(array):
    devices = lax.axis_size("blk")
    return lax.ppermute(
        array, "blk", [(i, (i + 1 if i % 2 else i - 1) % devices) for i in range(devices)]
    )


def on_chip(shape, dtype):
    return pltpu.VMEM(shape, dtype)


def call(kernel, out_shape, scalars, arrays, flops, scratch=()):
    scalar, vector = (pl.BlockSpec(memory_space=m) for m in (pltpu.SMEM, pltpu.VMEM))
    placed = [pltpu.with_memory_space_constraint(x, pltpu.SMEM) for x in scalars]
    placed += [pltpu.with_memory_space_constraint(x, pltpu.VMEM) for x in arrays]
    return pl.pallas_call(
        kernel,
        out_shape=out_shape,
        in_specs=[scalar] * len(scalars) + [vector] * len(arrays),
        out_specs=tuple(vector for _ in out_shape) if isinstance(out_shape, tuple) else vector,
        scratch_shapes=list(scratch),
        compiler_params=pltpu.CompilerParams(vmem_limit_bytes=16 << 20),
        cost_estimate=pl.CostEstimate(flops=flops, bytes_accessed=1 << 20, transcendentals=0),
    )(*placed)


def add_tiles(row_blocks, owner_route, tiles, offset, panel, summed):
    group = lax.axis_index("group")
    for slot in range(tiles.shape[3]):
        owner = owner_route[0, 0, row_blocks[0, 0, offset, slot]]
        place = jnp.where(owner == group, 0, 1)
        summed[place] += jnp.dot(
            tiles[0, 0, offset, slot], panel[...], preferred_element_type=jnp.float32
        )


def local_kernel(row_blocks, owner_route, tiles, own, near, summed):
    parity = lax.rem(lax.axis_index("blk"), 2)
    summed[...] = jnp.zeros_like(summed)
    add_tiles(row_blocks, owner_route, tiles, 1, own, summed)
    add_tiles(row_blocks, owner_route, tiles, 2 - 2 * parity, near, summed)


def turn_kernel(basis, lent, kept_turned, lent_turned):
    half = lent.shape[0]
    start = pl.multiple_of(lax.axis_index("group") * half, half)
    kept_turned[...] = basis[0, 0, pl.ds(start, half), :].T
    lent_turned[...] = lent[...].T


def far_kernel(row_blocks, owner_route, tiles, far, local, lent_turned, sampled, sent, summed):
    parity = lax.rem(lax.axis_index("blk"), 2)
    summed[...] = local[...]
    add_tiles(row_blocks, owner_route, tiles, 2 * parity, far, summed)
    sampled[...] = summed[0].astype(jnp.bfloat16)
    sent[...] = jnp.dot(
        lent_turned[...], summed[1].astype(jnp.bfloat16), preferred_element_type=jnp.float32
    ).astype(jnp.bfloat16)


def kept_kernel(kept_turned, sampled, kept):
    kept[...] = jnp.dot(kept_turned[...], sampled[...], preferred_element_type=jnp.float32)


def join_kernel(kept, received, out):
    out[...] = kept[...] + received[...].astype(jnp.float32)


def paired_body(sketch, far_tiles, row_blocks, owner_route, cluster_basis):
    panels, columns = sketch.shape
    rows = far_tiles.shape[4]
    half, rank = cluster_basis.shape[2] // 2, cluster_basis.shape[3]
    scalars = (row_blocks, owner_route)
    far = swap_far(sketch)
    near = swap_near(sketch)
    lent_rows = (1 - lax.axis_index("group")) * half
    lent = from_behind(
        lax.dynamic_slice_in_dim(cluster_basis[0, 0], lent_rows, half, 0), "group", 1
    )
    product = 2 * rows * panels * columns
    local = call(
        local_kernel,
        on_chip((2, rows, columns), jnp.float32),
        scalars,
        (far_tiles, sketch, near),
        2 * product,
    )
    kept_turned, lent_turned = call(
        turn_kernel, (on_chip((rank, half), jnp.bfloat16),) * 2, (), (cluster_basis, lent), 1 << 20
    )
    sampled, sent = call(
        far_kernel,
        (on_chip((rows, columns), jnp.bfloat16), on_chip((rank, columns), jnp.bfloat16)),
        scalars,
        (far_tiles, far, local, lent_turned),
        2 * product,
        (pltpu.VMEM((2, rows, columns), jnp.float32),),
    )
    received = from_behind(sent, "group", 1)
    kept = call(
        kept_kernel, on_chip((rank, columns), jnp.float32), (), (kept_turned, sampled), product // 2
    )
    out = call(
        join_kernel,
        jax.ShapeDtypeStruct((rank, columns), jnp.float32),
        (),
        (kept, received),
        1 << 20,
    )
    return out[None, None]


def contribute(summed, far_tiles, row_blocks, offset, current):
    product = jnp.einsum(
        "trk,kc->trc", far_tiles[0, 0, offset], current, preferred_element_type=jnp.float32
    )
    return summed.at[row_blocks[0, 0, offset]].add(product)


def ring_body(sketch, far_tiles, row_blocks, owner_route, cluster_basis):
    offsets = far_tiles.shape[2]
    radius = (offsets - 1) // 2
    groups = lax.axis_size("group")
    tile_rows = far_tiles.shape[4]
    columns = sketch.shape[1]
    summed = jnp.zeros((groups, tile_rows, columns), jnp.float32)
    for offset in range(offsets):
        current = from_behind(sketch, "blk", radius - offset) if offset != radius else sketch
        summed = contribute(summed, far_tiles, row_blocks, offset, current)
    sampled = summed.astype(jnp.bfloat16)
    ordered = jnp.zeros_like(sampled).at[owner_route[0, 0]].set(sampled)
    received = lax.all_to_all(ordered, "group", split_axis=0, concat_axis=0, tiled=True)
    stacked = received.reshape(received.shape[0] * received.shape[1], received.shape[2])
    coefficients = lax.dot_general(
        cluster_basis[0, 0], stacked, TRANSPOSED, preferred_element_type=jnp.float32
    )
    return coefficients[None, None]


def body(sketch, far_tiles, row_blocks, owner_route, cluster_basis):
    small = cluster_basis.shape[3] < far_tiles.shape[4]
    paired = lax.axis_size("group") == 2 and lax.axis_size("blk") % 2 == 0
    if small and paired and far_tiles.shape[2] == 3:
        return paired_body(sketch, far_tiles, row_blocks, owner_route, cluster_basis)
    return ring_body(sketch, far_tiles, row_blocks, owner_route, cluster_basis)


def solution(mesh):
    placed = (
        P("blk", None),
        P("blk", "group", None, None, None, None),
        P("blk", "group", None, None),
        P("blk", "group", None),
        P("blk", "group", None, None),
    )
    return jax.shard_map(
        body, mesh=mesh, in_specs=placed, out_specs=P("blk", "group", None, None), check_vma=False
    )
```

time: 66.4 us -> 34.6 us (0.52)
  the two profiles are of different devices: /device:TPU:0 before, /device:TPU:1 now
where the time goes in v2:
time: 34.6 us; the launch traced here: 34.3 us
  waiting for transfers between devices  17 us (49%)
  local copies, waits for them, and re-layouts  5.94 us (17%)
  starting transfers between devices  5.81 us (17%)
  Pallas kernels  5.47 us (16%)
    ppermute x2, waiting for transfers between devices, from_behind(): lax.ppermute(array, axis, [(i, (i + by) % devices) for i in range(devices)])  11.5 us
    ppermute x1, waiting for transfers between devices, swap_far(): lax.ppermute(array, 'blk', [(i, (i + 1 if i % 2 else i - 1) % devices) fo...  5.5 us
    pallas_call x5, Pallas kernels, call(): pl.pallas_call(kernel, out_shape=out_shape, in_specs=[scalar] * len(scala...  5.47 us
    unnamed x11, local copies, waits for them, and re-layouts  4.98 us
    ppermute x2, starting transfers between devices, from_behind(): lax.ppermute(array, axis, [(i, (i + by) % devices) for i in range(devices)])  3.2 us
    ppermute x1, starting transfers between devices, swap_far(): lax.ppermute(array, 'blk', [(i, (i + 1 if i % 2 else i - 1) % devices) fo...  2.55 us
    dynamic_slice x1, local copies, waits for them, and re-layouts, paired_body(): lax.dynamic_slice_in_dim(cluster_basis[0, 0], lent_rows, half, 0)  0.97 us
  transfers between devices with their start and end apart: 4, of which 3 were waited for; matrix products, arithmetic and copies ran while one was open for 5% of the time, Pallas kernels for 7%

profile of v2, /device:TPU:1, one launch (start us, length us, event | category | flops | bytes accessed | tf_op | source)
XLA Modules:
  0.0 34.3 jit_solution(17916354500761243281)
XLA Ops:
  0.0 0.1 collective-permute-start.2
  0.1 2.5 %collective-permute-start.1 = (bf16[512,768]{1,0:T(8,128)(2,1)}, bf16[512,768]{1,0:T(8,128)(2,1)S(1)}, u32[]{:S(2)}, u32[]{:S(2)}) collective-permute-start(bf16[512,768]{1,0:T(8,128)(2,1)} %own.1), channel_id=1, source_target_pairs={{0,30},{2,4},{4,2},{6,8},{8,6},{10,12},{12,10},{14,16},{16,14},{18... | collective-permute-start | bytes 2359304 | tf_op jit(solution)/shard_map/ppermute | solution.py:25
  2.6 1.0 %dynamic-slice_bitcast_fusion = bf16[512,256]{1,0:T(8,128)(2,1)S(1)} fusion(bf16[1,1,1024,256]{3,2,1,0:T(8,128)(2,1)} %basis.1, s32[]{:T(128)S(6)} %select_n.3), kind=kLoop, calls=%fused_computation | loop fusion | bytes 524292 | tf_op jit(solution)/shard_map/dynamic_slice | solution.py:100
  3.6 1.3 %collective-permute-start = (bf16[512,256]{1,0:T(8,128)(2,1)S(1)}, bf16[512,256]{1,0:T(8,128)(2,1)S(1)}, u32[]{:S(2)}, u32[]{:S(2)}) collective-permute-start(bf16[512,256]{1,0:T(8,128)(2,1)S(1)} %dynamic-slice_bitcast_fusion), channel_id=1, source_target_pairs={{0,1},{1,0},{2,3},{3,2},{4,5},{5,4},{6,7},{7,6},{8,9},{9,8},{10,11... | collective-permute-start | bytes 786440 | tf_op jit(solution)/shard_map/ppermute | solution.py:15
  4.9 0.7 %copy.7.row_blocks = s32[1,1,3,1]{3,2,1,0:T(4,128)S(1)} copy(s32[1,1,3,1]{2,3,1,0:T(1,128)} %param.7) | data formatting | bytes 24 | tf_op args[2]
  5.6 3.5 %collective-permute-done.lent = bf16[512,256]{1,0:T(8,128)(2,1)S(1)} collective-permute-done((bf16[512,256]{1,0:T(8,128)(2,1)S(1)}, bf16[512,256]{1,0:T(8,128)(2,1)S(1)}, u32[]{:S(2)}, u32[]{:S(2)}) %collective-permute-start) | collective-permute-done | bytes 262176 | tf_op jit(solution)/shard_map/ppermute | solution.py:15
  9.2 0.0 copy-start.2
  9.2 1.0 %copy-done.2 = bf16[1,1,1024,256]{3,2,1,0:T(8,128)(2,1)S(1)} copy-done((bf16[1,1,1024,256]{3,2,1,0:T(8,128)(2,1)S(1)}, bf16[1,1,1024,256]{3,2,1,0:T(8,128)(2,1)}, u32[]{:S(2)}) %copy-start.2) | copy-done | bytes 524312
  10.2 0.2 shard_map.55
  10.4 0.0 collective-permute-done.2.near
  10.4 0.0 copy-start
  10.4 1.4 %copy-done = bf16[1,1,3,1,512,512]{5,4,3,2,1,0:T(8,128)(2,1)S(1)} copy-done((bf16[1,1,3,1,512,512]{5,4,3,2,1,0:T(8,128)(2,1)S(1)}, bf16[1,1,3,1,512,512]{5,4,3,2,1,0:T(8,128)(2,1)}, u32[]{:S(2)}) %copy-start) | copy-done | bytes 1572888
  11.8 0.0 copy-start.3
  11.8 1.1 %copy-done.3 = bf16[512,768]{1,0:T(8,128)(2,1)S(1)} copy-done((bf16[512,768]{1,0:T(8,128)(2,1)S(1)}, bf16[512,768]{1,0:T(8,128)(2,1)}, u32[]{:S(2)}) %copy-start.3) | copy-done | bytes 786456
  12.9 0.0 copy-start.4
  12.9 0.7 %copy-done.4 = s32[1,1,2]{2,1,0:T(1,128)S(1)} copy-done((s32[1,1,2]{2,1,0:T(1,128)S(1)}, s32[1,1,2]{2,1,0:T(1,128)}, u32[]{:S(2)}) %copy-start.4) | copy-done | bytes 32
  13.6 0.0 copy-start.1
  13.6 1.8 %shard_map.56.local = f32[2,512,768]{2,1,0:T(8,128)S(1)} custom-call(s32[1,1,3,1]{3,2,1,0:T(4,128)S(1)} %copy.7.row_blocks, s32[1,1,2]{2,1,0:T(1,128)S(1)} %copy-done.4, bf16[1,1,3,1,512,512]{5,4,3,2,1,0:T(8,128)(2,1)S(1)} %copy-done, bf16[512,768]{1,0:T(8,128)(2,1)S(1)} %copy-done.3, bf16[512,768]{1,0:T(8,128)(2,1)S(1)} %collective-permute-done.2.near), custom_call_target="tpu_custom_call" | custom-call | flops 805306368 | bytes 1048576 | tf_op jit(solution)/shard_map/pallas_call | solution.py:38
  15.4 5.5 %collective-permute-done.1.far = bf16[512,768]{1,0:T(8,128)(2,1)S(1)} collective-permute-done((bf16[512,768]{1,0:T(8,128)(2,1)}, bf16[512,768]{1,0:T(8,128)(2,1)S(1)}, u32[]{:S(2)}, u32[]{:S(2)}) %collective-permute-start.1) | collective-permute-done | bytes 786464 | tf_op jit(solution)/shard_map/ppermute | solution.py:25
  20.9 0.0 copy-done.1
  20.9 2.2 %shard_map.57 = (bf16[512,768]{1,0:T(8,128)(2,1)S(1)}, bf16[256,768]{1,0:T(8,128)(2,1)S(1)}) custom-call(s32[1,1,3,1]{3,2,1,0:T(4,128)S(1)} %copy.7.row_blocks, s32[1,1,2]{2,1,0:T(1,128)S(1)} %copy-done.4, bf16[1,1,3,1,512,512]{5,4,3,2,1,0:T(8,128)(2,1)S(1)} %copy-done.1, bf16[512,768]{1,0:T(8,128)(2,1)S(1)} %collective-permute-done.1.far, ...), custom_call_target="tpu_custom_call" | custom-call | flops 805306368 | bytes 1048576 | tf_op jit(solution)/shard_map/pallas_call | solution.py:38
  23.1 1.9 %collective-permute-start.3 = (bf16[256,768]{1,0:T(8,128)(2,1)S(1)}, bf16[256,768]{1,0:T(8,128)(2,1)S(1)}, u32[]{:S(2)}, u32[]{:S(2)}) collective-permute-start(bf16[256,768]{1,0:T(8,128)(2,1)S(1)} %get-tuple-element.12), channel_id=1, source_target_pairs={{0,1},{1,0},{2,3},{3,2},{4,5},{5,4},{6,7},{7,6},{8,9},{9,8},{10,11... | collective-permute-start | bytes 1179656 | tf_op jit(solution)/shard_map/ppermute | solution.py:15
  25.0 0.4 %shard_map.58.kept = f32[256,768]{1,0:T(8,128)S(1)} custom-call(bf16[256,512]{1,0:T(8,128)(2,1)S(1)} %get-tuple-element.9.kept_turned, bf16[512,768]{1,0:T(8,128)(2,1)S(1)} %get-tuple-element.11.sampled), custom_call_target="tpu_custom_call" | custom-call | flops 201326592 | bytes 1048576 | tf_op jit(solution)/shard_map/pallas_call | solution.py:38
  25.4 8.0 %collective-permute-done.3.received = bf16[256,768]{1,0:T(8,128)(2,1)S(1)} collective-permute-done((bf16[256,768]{1,0:T(8,128)(2,1)S(1)}, bf16[256,768]{1,0:T(8,128)(2,1)S(1)}, u32[]{:S(2)}, u32[]{:S(2)}) %collective-permute-start.3) | collective-permute-done | bytes 393248 | tf_op jit(solution)/shard_map/ppermute | solution.py:15
  33.4 0.9 %shard_map.59 = f32[256,768]{1,0:T(8,128)} custom-call(f32[256,768]{1,0:T(8,128)S(1)} %shard_map.58.kept, bf16[256,768]{1,0:T(8,128)(2,1)S(1)} %collective-permute-done.3.received), custom_call_target="tpu_custom_call" | custom-call | flops 1048576 | bytes 1048576 | tf_op jit(solution)/shard_map/pallas_call | solution.py:38
Async XLA Ops:
  0.0 10.4 %collective-permute-start.2 = (bf16[512,768]{1,0:T(8,128)(2,1)}, bf16[512,768]{1,0:T(8,128)(2,1)S(1)}, u32[]{:S(2)}, u32[]{:S(2)}) collective-permute-start(bf16[512,768]{1,0:T(8,128)(2,1)} %own.1), channel_id=1, source_target_pairs={{0,2},{2,0},{4,6},{6,4},{8,10},{10,8},{12,14},{14,12},{16,18},{18,... | collective-permute-start | bytes 2359304 | tf_op jit(solution)/shard_map/ppermute | solution.py:20
  0.1 20.9 %collective-permute-start.1 = (bf16[512,768]{1,0:T(8,128)(2,1)}, bf16[512,768]{1,0:T(8,128)(2,1)S(1)}, u32[]{:S(2)}, u32[]{:S(2)}) collective-permute-start(bf16[512,768]{1,0:T(8,128)(2,1)} %own.1), channel_id=1, source_target_pairs={{0,30},{2,4},{4,2},{6,8},{8,6},{10,12},{12,10},{14,16},{16,14},{18... | collective-permute-start | bytes 2359304 | tf_op jit(solution)/shard_map/ppermute | solution.py:25
  3.6 5.6 %collective-permute-start = (bf16[512,256]{1,0:T(8,128)(2,1)S(1)}, bf16[512,256]{1,0:T(8,128)(2,1)S(1)}, u32[]{:S(2)}, u32[]{:S(2)}) collective-permute-start(bf16[512,256]{1,0:T(8,128)(2,1)S(1)} %dynamic-slice_bitcast_fusion), channel_id=1, source_target_pairs={{0,1},{1,0},{2,3},{3,2},{4,5},{5,4},{6,7},{7,6},{8,9},{9,8},{10,11... | collective-permute-start | bytes 786440 | tf_op jit(solution)/shard_map/ppermute | solution.py:15
  9.2 1.0 %copy-start.2 = (bf16[1,1,1024,256]{3,2,1,0:T(8,128)(2,1)S(1)}, bf16[1,1,1024,256]{3,2,1,0:T(8,128)(2,1)}, u32[]{:S(2)}) copy-start(bf16[1,1,1024,256]{3,2,1,0:T(8,128)(2,1)} %basis.1) | copy-start | bytes 1572868
  10.4 1.4 %copy-start = (bf16[1,1,3,1,512,512]{5,4,3,2,1,0:T(8,128)(2,1)S(1)}, bf16[1,1,3,1,512,512]{5,4,3,2,1,0:T(8,128)(2,1)}, u32[]{:S(2)}) copy-start(bf16[1,1,3,1,512,512]{5,4,3,2,1,0:T(8,128)(2,1)} %tiles.3) | copy-start | bytes 4718596
  11.8 1.1 %copy-start.3 = (bf16[512,768]{1,0:T(8,128)(2,1)S(1)}, bf16[512,768]{1,0:T(8,128)(2,1)}, u32[]{:S(2)}) copy-start(bf16[512,768]{1,0:T(8,128)(2,1)} %own.1) | copy-start | bytes 2359300
  12.9 0.7 %copy-start.4 = (s32[1,1,2]{2,1,0:T(1,128)S(1)}, s32[1,1,2]{2,1,0:T(1,128)}, u32[]{:S(2)}) copy-start(s32[1,1,2]{2,1,0:T(1,128)} %owner_route.3) | copy-start | bytes 28
  13.6 7.3 %copy-start.1 = (bf16[1,1,3,1,512,512]{5,4,3,2,1,0:T(8,128)(2,1)S(1)}, bf16[1,1,3,1,512,512]{5,4,3,2,1,0:T(8,128)(2,1)}, u32[]{:S(2)}) copy-start(bf16[1,1,3,1,512,512]{5,4,3,2,1,0:T(8,128)(2,1)} %tiles.3) | copy-start | bytes 4718596
  23.1 10.3 %collective-permute-start.3 = (bf16[256,768]{1,0:T(8,128)(2,1)S(1)}, bf16[256,768]{1,0:T(8,128)(2,1)S(1)}, u32[]{:S(2)}, u32[]{:S(2)}) collective-permute-start(bf16[256,768]{1,0:T(8,128)(2,1)S(1)} %get-tuple-element.12), channel_id=1, source_target_pairs={{0,1},{1,0},{2,3},{3,2},{4,5},{5,4},{6,7},{7,6},{8,9},{9,8},{10,11... | collective-permute-start | bytes 1179656 | tf_op jit(solution)/shard_map/ppermute | solution.py:15

commit v3 on v2

v3 whole, which is shorter than its diff:
```python
import functools

import jax
import jax.numpy as jnp
from jax import lax
from jax.experimental import pallas as pl
from jax.experimental.pallas import tpu as pltpu
from jax.sharding import PartitionSpec as P

TRANSPOSED = (((0,), (0,)), ((), ()))


def from_behind(array, axis, by):
    devices = lax.axis_size(axis)
    return lax.ppermute(array, axis, [(i, (i + by) % devices) for i in range(devices)])


def swap_near(array):
    devices = lax.axis_size("blk")
    return lax.ppermute(array, "blk", [(i, i ^ 1) for i in range(devices)])


def swap_far(array):
    devices = lax.axis_size("blk")
    return lax.ppermute(
        array, "blk", [(i, (i + 1 if i % 2 else i - 1) % devices) for i in range(devices)]
    )


def on_chip(shape, dtype):
    return pltpu.VMEM(shape, dtype)


def call(kernel, out_shape, scalars, arrays, flops, scratch=(), hbm=()):
    scalar, vector, main = (
        pl.BlockSpec(memory_space=m) for m in (pltpu.SMEM, pltpu.VMEM, pltpu.HBM)
    )
    placed = [pltpu.with_memory_space_constraint(x, pltpu.SMEM) for x in scalars]
    placed += [pltpu.with_memory_space_constraint(x, pltpu.VMEM) for x in arrays]
    placed += [pltpu.with_memory_space_constraint(x, pltpu.HBM) for x in hbm]
    return pl.pallas_call(
        kernel,
        out_shape=out_shape,
        in_specs=[scalar] * len(scalars) + [vector] * len(arrays) + [main] * len(hbm),
        out_specs=tuple(vector for _ in out_shape) if isinstance(out_shape, tuple) else vector,
        scratch_shapes=list(scratch),
        compiler_params=pltpu.CompilerParams(vmem_limit_bytes=16 << 20),
        cost_estimate=pl.CostEstimate(flops=flops, bytes_accessed=1 << 20, transcendentals=0),
    )(*placed)


def far_offset():
    return 2 * lax.rem(lax.axis_index("blk"), 2)


def owner_of(row_blocks, owner_route, offset):
    return owner_route[0, 0, row_blocks[0, 0, offset, 0]]


def cut_kernel(sketch, basis, first, lent, sems):
    half = lent.shape[0]
    start = pl.multiple_of((1 - lax.axis_index("group")) * half, half)
    copies = (
        pltpu.make_async_copy(sketch.at[:, pl.ds(0, first.shape[1])], first, sems.at[0]),
        pltpu.make_async_copy(basis.at[0, 0, pl.ds(start, half)], lent, sems.at[1]),
    )
    for copy in copies:
        copy.start()
    for copy in copies:
        copy.wait()


def local_kernel(row_blocks, owner_route, tiles, own, near, hit, miss):
    far = far_offset()
    owner = owner_of(row_blocks, owner_route, far)
    own_hits = owner_of(row_blocks, owner_route, 1) == owner
    near_hits = owner_of(row_blocks, owner_route, 2 - far) == owner
    step = 256
    for start in range(0, own.shape[1], step):
        columns = pl.ds(start, step)
        first = jnp.dot(tiles[0, 0, 1, 0], own[:, columns], preferred_element_type=jnp.float32)
        second = jnp.dot(
            tiles[0, 0, 2 - far, 0], near[:, columns], preferred_element_type=jnp.float32
        )
        hit[:, columns] = jnp.where(own_hits, first, 0.0) + jnp.where(near_hits, second, 0.0)
        miss[:, columns] = (
            jnp.where(own_hits, 0.0, first) + jnp.where(near_hits, 0.0, second)
        ).astype(jnp.bfloat16)


def turn_kernel(row_blocks, owner_route, basis, lent, miss, own, hit_turned, missed, second):
    half = lent.shape[0]
    group = lax.axis_index("group")
    kept = basis[0, 0, pl.ds(pl.multiple_of(group * half, half), half), :].T
    other = lent[...].T
    stays = owner_of(row_blocks, owner_route, far_offset()) == group
    hit_turned[...] = jnp.where(stays, kept, other)
    missed[...] = jnp.dot(
        jnp.where(stays, other, kept), miss[...], preferred_element_type=jnp.float32
    )
    second[...] = own[:, pl.ds(own.shape[1] - second.shape[1], second.shape[1])]


def far_kernel(start, row_blocks, owner_route, tiles, far, hit, hit_turned, missed, made, sent):
    offset = far_offset()
    stays = owner_of(row_blocks, owner_route, offset) == lax.axis_index("group")
    columns = pl.ds(start, far.shape[1])
    product = jnp.dot(tiles[0, 0, offset, 0], far[...], preferred_element_type=jnp.float32)
    sampled = (hit[:, columns] + product).astype(jnp.bfloat16)
    result = jnp.dot(hit_turned[...], sampled, preferred_element_type=jnp.float32)
    sent[...] = jnp.where(stays, missed[:, columns], result).astype(jnp.bfloat16)
    made[...] = result


def join_kernel(row_blocks, owner_route, missed, *refs):
    parts, out = refs[:-1], refs[-1]
    stays = owner_of(row_blocks, owner_route, far_offset()) == lax.axis_index("group")
    start = 0
    for made, received in zip(parts[0::2], parts[1::2]):
        columns = pl.ds(start, made.shape[1])
        kept = jnp.where(stays, made[...], missed[:, columns])
        out[:, columns] = kept + received[...].astype(jnp.float32)
        start += made.shape[1]


def paired_body(sketch, far_tiles, row_blocks, owner_route, cluster_basis):
    panels, columns = sketch.shape
    rows = far_tiles.shape[4]
    half, rank = cluster_basis.shape[2] // 2, cluster_basis.shape[3]
    early = 2 * columns // 3
    scalars = (row_blocks, owner_route)
    product = 2 * rows * panels * columns
    first, lent = call(
        cut_kernel,
        (on_chip((panels, early), sketch.dtype), on_chip((half, rank), cluster_basis.dtype)),
        (),
        (),
        0,
        (pltpu.SemaphoreType.DMA((2,)),),
        (sketch, cluster_basis),
    )
    far_first = swap_far(first)
    near = swap_near(sketch)
    lent = from_behind(lent, "group", 1)
    hit, miss = call(
        local_kernel,
        (on_chip((rows, columns), jnp.float32), on_chip((rows, columns), jnp.bfloat16)),
        scalars,
        (far_tiles, sketch, near),
        2 * product,
    )
    hit_turned, missed, second = call(
        turn_kernel,
        (
            on_chip((rank, half), jnp.bfloat16),
            on_chip((rank, columns), jnp.float32),
            on_chip((panels, columns - early), sketch.dtype),
        ),
        scalars,
        (cluster_basis, lent, miss, sketch),
        product // 2,
    )
    far_second = swap_far(second)
    parts = []
    for start, far in ((0, far_first), (early, far_second)):
        width = far.shape[1]
        made, sent = call(
            functools.partial(far_kernel, start),
            (on_chip((rank, width), jnp.float32), on_chip((rank, width), jnp.bfloat16)),
            scalars,
            (far_tiles, far, hit, hit_turned, missed),
            2 * product * width // columns,
        )
        parts += [made, from_behind(sent, "group", 1)]
    out = call(
        join_kernel,
        jax.ShapeDtypeStruct((rank, columns), jnp.float32),
        scalars,
        (missed, *parts),
        1 << 20,
    )
    return out[None, None]


def contribute(summed, far_tiles, row_blocks, offset, current):
    product = jnp.einsum(
        "trk,kc->trc", far_tiles[0, 0, offset], current, preferred_element_type=jnp.float32
    )
    return summed.at[row_blocks[0, 0, offset]].add(product)


def ring_body(sketch, far_tiles, row_blocks, owner_route, cluster_basis):
    offsets = far_tiles.shape[2]
    radius = (offsets - 1) // 2
    groups = lax.axis_size("group")
    tile_rows = far_tiles.shape[4]
    columns = sketch.shape[1]
    summed = jnp.zeros((groups, tile_rows, columns), jnp.float32)
    for offset in range(offsets):
        current = from_behind(sketch, "blk", radius - offset) if offset != radius else sketch
        summed = contribute(summed, far_tiles, row_blocks, offset, current)
    sampled = summed.astype(jnp.bfloat16)
    ordered = jnp.zeros_like(sampled).at[owner_route[0, 0]].set(sampled)
    received = lax.all_to_all(ordered, "group", split_axis=0, concat_axis=0, tiled=True)
    stacked = received.reshape(received.shape[0] * received.shape[1], received.shape[2])
    coefficients = lax.dot_general(
        cluster_basis[0, 0], stacked, TRANSPOSED, preferred_element_type=jnp.float32
    )
    return coefficients[None, None]


def body(sketch, far_tiles, row_blocks, owner_route, cluster_basis):
    small = cluster_basis.shape[3] < far_tiles.shape[4]
    paired = lax.axis_size("group") == 2 and lax.axis_size("blk") % 2 == 0
    if small and paired and far_tiles.shape[2:4] == (3, 1):
        return paired_body(sketch, far_tiles, row_blocks, owner_route, cluster_basis)
    return ring_body(sketch, far_tiles, row_blocks, owner_route, cluster_basis)


def solution(mesh):
    placed = (
        P("blk", None),
        P("blk", "group", None, None, None, None),
        P("blk", "group", None, None),
        P("blk", "group", None),
        P("blk", "group", None, None),
    )
    return jax.shard_map(
        body, mesh=mesh, in_specs=placed, out_specs=P("blk", "group", None, None), check_vma=False
    )
```

time: 34.6 us -> 31.9 us (0.922)
  the two profiles are of different devices: /device:TPU:1 before, /device:TPU:0 now
where the time goes in v3:
time: 31.9 us; the launch traced here: 31.7 us
  starting transfers between devices  10.5 us (33%)
  waiting for transfers between devices  9.52 us (30%)
  Pallas kernels  7.64 us (24%)
  local copies, waits for them, and re-layouts  3.95 us (12%)
    pallas_call x6, Pallas kernels, call(): pl.pallas_call(kernel, out_shape=out_shape, in_specs=[scalar] * len(scala...  7.64 us
    ppermute x2, starting transfers between devices, swap_far(): lax.ppermute(array, 'blk', [(i, (i + 1 if i % 2 else i - 1) % devices) fo...  6.08 us
    ppermute x2, waiting for transfers between devices, swap_far(): lax.ppermute(array, 'blk', [(i, (i + 1 if i % 2 else i - 1) % devices) fo...  5.38 us
    ppermute x3, waiting for transfers between devices, from_behind(): lax.ppermute(array, axis, [(i, (i + by) % devices) for i in range(devices)])  4.14 us
    ppermute x3, starting transfers between devices, from_behind(): lax.ppermute(array, axis, [(i, (i + by) % devices) for i in range(devices)])  4 us
    unnamed x13, local copies, waits for them, and re-layouts  3.95 us
  transfers between devices with their start and end apart: 6, of which 2 were waited for; matrix products, arithmetic and copies ran while one was open for 2% of the time, Pallas kernels for 19%

profile of v3, /device:TPU:0, one launch (start us, length us, event | category | flops | bytes accessed | tf_op | source)
XLA Modules:
  0.0 31.7 jit_solution(14956139385444262294)
XLA Ops:
  0.0 0.5 %collective-permute-start.1 = (bf16[512,768]{1,0:T(8,128)(2,1)}, bf16[512,768]{1,0:T(8,128)(2,1)S(1)}, u32[]{:S(2)}, u32[]{:S(2)}) collective-permute-start(bf16[512,768]{1,0:T(8,128)(2,1)} %own.3), channel_id=1, source_target_pairs={{0,2},{2,0},{4,6},{6,4},{8,10},{10,8},{12,14},{14,12},{16,18},{18,... | collective-permute-start | bytes 2359304 | tf_op jit(solution)/shard_map/ppermute | solution.py:20
  0.5 1.1 %shard_map.55 = (bf16[512,512]{1,0:T(8,128)(2,1)S(1)}, bf16[512,256]{1,0:T(8,128)(2,1)S(1)}) custom-call(bf16[512,768]{1,0:T(8,128)(2,1)} %own.3, bf16[1,1,1024,256]{3,2,1,0:T(8,128)(2,1)} %basis.3), custom_call_target="tpu_custom_call" | custom-call | bytes 1048576 | tf_op jit(solution)/shard_map/pallas_call | solution.py:41
  1.6 5.7 %collective-permute-start.2 = (bf16[512,512]{1,0:T(8,128)(2,1)S(1)}, bf16[512,512]{1,0:T(8,128)(2,1)S(1)}, u32[]{:S(2)}, u32[]{:S(2)}) collective-permute-start(bf16[512,512]{1,0:T(8,128)(2,1)S(1)} %get-tuple-element.19), channel_id=1, source_target_pairs={{0,30},{2,4},{4,2},{6,8},{8,6},{10,12},{12,10},{14,16},{16,14},{18... | collective-permute-start | bytes 1572872 | tf_op jit(solution)/shard_map/ppermute | solution.py:25
  7.3 1.5 %collective-permute-start = (bf16[512,256]{1,0:T(8,128)(2,1)S(1)}, bf16[512,256]{1,0:T(8,128)(2,1)S(1)}, u32[]{:S(2)}, u32[]{:S(2)}) collective-permute-start(bf16[512,256]{1,0:T(8,128)(2,1)S(1)} %get-tuple-element.16), channel_id=1, source_target_pairs={{0,1},{1,0},{2,3},{3,2},{4,5},{5,4},{6,7},{7,6},{8,9},{9,8},{10,11... | collective-permute-start | bytes 786440 | tf_op jit(solution)/shard_map/ppermute | solution.py:15
  8.8 0.7 %copy.10.row_blocks = s32[1,1,3,1]{3,2,1,0:T(4,128)S(1)} copy(s32[1,1,3,1]{2,3,1,0:T(1,128)} %param.7) | data formatting | bytes 24 | tf_op args[2]
  9.6 0.0 collective-permute-done.1.near
  9.6 0.0 copy-start
  9.6 1.4 %copy-done = bf16[1,1,3,1,512,512]{5,4,3,2,1,0:T(8,128)(2,1)S(1)} copy-done((bf16[1,1,3,1,512,512]{5,4,3,2,1,0:T(8,128)(2,1)S(1)}, bf16[1,1,3,1,512,512]{5,4,3,2,1,0:T(8,128)(2,1)}, u32[]{:S(2)}) %copy-start) | copy-done | bytes 1572888
  11.0 0.0 copy-start.2
  11.0 1.1 %copy-done.2 = bf16[512,768]{1,0:T(8,128)(2,1)S(1)} copy-done((bf16[512,768]{1,0:T(8,128)(2,1)S(1)}, bf16[512,768]{1,0:T(8,128)(2,1)}, u32[]{:S(2)}) %copy-start.2) | copy-done | bytes 786456
  12.1 0.0 copy-start.4
  12.1 0.7 %copy-done.4 = s32[1,1,2]{2,1,0:T(1,128)S(1)} copy-done((s32[1,1,2]{2,1,0:T(1,128)S(1)}, s32[1,1,2]{2,1,0:T(1,128)}, u32[]{:S(2)}) %copy-start.4) | copy-done | bytes 32
  12.8 0.0 copy-start.3
  12.8 0.0 copy-start.5
  12.8 1.6 %shard_map.56 = (f32[512,768]{1,0:T(8,128)S(1)}, bf16[512,768]{1,0:T(8,128)(2,1)S(1)}) custom-call(s32[1,1,3,1]{3,2,1,0:T(4,128)S(1)} %copy.10.row_blocks, s32[1,1,2]{2,1,0:T(1,128)S(1)} %copy-done.4, bf16[1,1,3,1,512,512]{5,4,3,2,1,0:T(8,128)(2,1)S(1)} %copy-done, bf16[512,768]{1,0:T(8,128)(2,1)S(1)} %copy-done.2, ...), custom_call_target="tpu_custom_call" | custom-call | flops 805306368 | bytes 1048576 | tf_op jit(solution)/shard_map/pallas_call | solution.py:41
  14.3 0.0 copy-start.1
  14.3 0.0 collective-permute-done.lent
  14.3 0.0 copy-done.3
  14.3 0.0 copy-done.5
  14.4 1.1 %shard_map.57 = (bf16[256,512]{1,0:T(8,128)(2,1)S(1)}, f32[256,768]{1,0:T(8,128)S(1)}, bf16[512,256]{1,0:T(8,128)(2,1)S(1)}) custom-call(s32[1,1,3,1]{3,2,1,0:T(4,128)S(1)} %copy.10.row_blocks, s32[1,1,2]{2,1,0:T(1,128)S(1)} %copy-done.5, bf16[1,1,1024,256]{3,2,1,0:T(8,128)(2,1)S(1)} %copy-done.3, bf16[512,256]{1,0:T(8,128)(2,1)S(1)} %collective-permute-done.lent, ...), custom_call_target="tpu_custom_call" | custom-call | flops 201326592 | bytes 1048576 | tf_op jit(solution)/shard_map/pallas_call | solution.py:41
  15.4 0.4 %collective-permute-start.4 = (bf16[512,256]{1,0:T(8,128)(2,1)S(1)}, bf16[512,256]{1,0:T(8,128)(2,1)S(1)}, u32[]{:S(2)}, u32[]{:S(2)}) collective-permute-start(bf16[512,256]{1,0:T(8,128)(2,1)S(1)} %get-tuple-element.24), channel_id=1, source_target_pairs={{0,30},{2,4},{4,2},{6,8},{8,6},{10,12},{12,10},{14,16},{16,14},{18... | collective-permute-start | bytes 786440 | tf_op jit(solution)/shard_map/ppermute | solution.py:25
  15.8 0.0 collective-permute-done.2.far
  15.8 0.0 copy-done.1
  15.8 1.2 %shard_map.58 = (f32[256,512]{1,0:T(8,128)S(1)}, bf16[256,512]{1,0:T(8,128)(2,1)S(1)}) custom-call(s32[1,1,3,1]{3,2,1,0:T(4,128)S(1)} %copy.10.row_blocks, s32[1,1,2]{2,1,0:T(1,128)S(1)} %copy-done.5, bf16[1,1,3,1,512,512]{5,4,3,2,1,0:T(8,128)(2,1)S(1)} %copy-done.1, bf16[512,512]{1,0:T(8,128)(2,1)S(1)} %collective-permute-done.2.far, ...), custom_call_target="tpu_custom_call" | custom-call | flops 536870912 | bytes 1048576 | tf_op jit(solution)/shard_map/pallas_call | solution.py:41
  17.0 1.6 %collective-permute-start.3 = (bf16[256,512]{1,0:T(8,128)(2,1)S(1)}, bf16[256,512]{1,0:T(8,128)(2,1)S(1)}, u32[]{:S(2)}, u32[]{:S(2)}) collective-permute-start(bf16[256,512]{1,0:T(8,128)(2,1)S(1)} %get-tuple-element.23), channel_id=1, source_target_pairs={{0,1},{1,0},{2,3},{3,2},{4,5},{5,4},{6,7},{7,6},{8,9},{9,8},{10,11... | collective-permute-start | bytes 786440 | tf_op jit(solution)/shard_map/ppermute | solution.py:15
  18.6 5.4 %collective-permute-done.4.far = bf16[512,256]{1,0:T(8,128)(2,1)S(1)} collective-permute-done((bf16[512,256]{1,0:T(8,128)(2,1)S(1)}, bf16[512,256]{1,0:T(8,128)(2,1)S(1)}, u32[]{:S(2)}, u32[]{:S(2)}) %collective-permute-start.4) | collective-permute-done | bytes 262176 | tf_op jit(solution)/shard_map/ppermute | solution.py:25
  24.0 1.1 %shard_map.59 = (f32[256,256]{1,0:T(8,128)S(1)}, bf16[256,256]{1,0:T(8,128)(2,1)S(1)}) custom-call(s32[1,1,3,1]{3,2,1,0:T(4,128)S(1)} %copy.10.row_blocks, s32[1,1,2]{2,1,0:T(1,128)S(1)} %copy-done.5, bf16[1,1,3,1,512,512]{5,4,3,2,1,0:T(8,128)(2,1)S(1)} %copy-done.1, bf16[512,256]{1,0:T(8,128)(2,1)S(1)} %collective-permute-done.4.far, ...), custom_call_target="tpu_custom_call" | custom-call | flops 268435456 | bytes 1048576 | tf_op jit(solution)/shard_map/pallas_call | solution.py:41
  25.1 0.9 %collective-permute-start.5 = (bf16[256,256]{1,0:T(8,128)(2,1)S(1)}, bf16[256,256]{1,0:T(8,128)(2,1)S(1)}, u32[]{:S(2)}, u32[]{:S(2)}) collective-permute-start(bf16[256,256]{1,0:T(8,128)(2,1)S(1)} %get-tuple-element.26), channel_id=1, source_target_pairs={{0,1},{1,0},{2,3},{3,2},{4,5},{5,4},{6,7},{7,6},{8,9},{9,8},{10,11... | collective-permute-start | bytes 393224 | tf_op jit(solution)/shard_map/ppermute | solution.py:15
  26.0 0.0 collective-permute-done.3.refs_1_
  26.0 4.1 %collective-permute-done.5.refs_3_ = bf16[256,256]{1,0:T(8,128)(2,1)S(1)} collective-permute-done((bf16[256,256]{1,0:T(8,128)(2,1)S(1)}, bf16[256,256]{1,0:T(8,128)(2,1)S(1)}, u32[]{:S(2)}, u32[]{:S(2)}) %collective-permute-start.5) | collective-permute-done | bytes 131104 | tf_op jit(solution)/shard_map/ppermute | solution.py:15
  30.2 1.6 %shard_map.60 = f32[256,768]{1,0:T(8,128)} custom-call(s32[1,1,3,1]{3,2,1,0:T(4,128)S(1)} %copy.10.row_blocks, s32[1,1,2]{2,1,0:T(1,128)S(1)} %copy-done.5, f32[256,768]{1,0:T(8,128)S(1)} %get-tuple-element.18.missed, f32[256,512]{1,0:T(8,128)S(1)} %get-tuple-element.22.refs_0_, bf16[256,512]{1,0:T(8,128)(2,1)S(1)} %collective-permute-done.3.refs_1_, ...), custom_call_target="tpu_custom_call" | custom-call | flops 1048576 | bytes 1048576 | tf_op jit(solution)/shard_map/pallas_call | solution.py:41
Async XLA Ops:
  0.0 9.6 %collective-permute-start.1 = (bf16[512,768]{1,0:T(8,128)(2,1)}, bf16[512,768]{1,0:T(8,128)(2,1)S(1)}, u32[]{:S(2)}, u32[]{:S(2)}) collective-permute-start(bf16[512,768]{1,0:T(8,128)(2,1)} %own.3), channel_id=1, source_target_pairs={{0,2},{2,0},{4,6},{6,4},{8,10},{10,8},{12,14},{14,12},{16,18},{18,... | collective-permute-start | bytes 2359304 | tf_op jit(solution)/shard_map/ppermute | solution.py:20
  1.6 14.2 %collective-permute-start.2 = (bf16[512,512]{1,0:T(8,128)(2,1)S(1)}, bf16[512,512]{1,0:T(8,128)(2,1)S(1)}, u32[]{:S(2)}, u32[]{:S(2)}) collective-permute-start(bf16[512,512]{1,0:T(8,128)(2,1)S(1)} %get-tuple-element.19), channel_id=1, source_target_pairs={{0,30},{2,4},{4,2},{6,8},{8,6},{10,12},{12,10},{14,16},{16,14},{18... | collective-permute-start | bytes 1572872 | tf_op jit(solution)/shard_map/ppermute | solution.py:25
  7.3 7.0 %collective-permute-start = (bf16[512,256]{1,0:T(8,128)(2,1)S(1)}, bf16[512,256]{1,0:T(8,128)(2,1)S(1)}, u32[]{:S(2)}, u32[]{:S(2)}) collective-permute-start(bf16[512,256]{1,0:T(8,128)(2,1)S(1)} %get-tuple-element.16), channel_id=1, source_target_pairs={{0,1},{1,0},{2,3},{3,2},{4,5},{5,4},{6,7},{7,6},{8,9},{9,8},{10,11... | collective-permute-start | bytes 786440 | tf_op jit(solution)/shard_map/ppermute | solution.py:15
  9.6 1.4 %copy-start = (bf16[1,1,3,1,512,512]{5,4,3,2,1,0:T(8,128)(2,1)S(1)}, bf16[1,1,3,1,512,512]{5,4,3,2,1,0:T(8,128)(2,1)}, u32[]{:S(2)}) copy-start(bf16[1,1,3,1,512,512]{5,4,3,2,1,0:T(8,128)(2,1)} %tiles.5) | copy-start | bytes 4718596
  11.0 1.1 %copy-start.2 = (bf16[512,768]{1,0:T(8,128)(2,1)S(1)}, bf16[512,768]{1,0:T(8,128)(2,1)}, u32[]{:S(2)}) copy-start(bf16[512,768]{1,0:T(8,128)(2,1)} %own.3) | copy-start | bytes 2359300
  12.1 0.7 %copy-start.4 = (s32[1,1,2]{2,1,0:T(1,128)S(1)}, s32[1,1,2]{2,1,0:T(1,128)}, u32[]{:S(2)}) copy-start(s32[1,1,2]{2,1,0:T(1,128)} %owner_route.9) | copy-start | bytes 28
  12.8 1.6 %copy-start.3 = (bf16[1,1,1024,256]{3,2,1,0:T(8,128)(2,1)S(1)}, bf16[1,1,1024,256]{3,2,1,0:T(8,128)(2,1)}, u32[]{:S(2)}) copy-start(bf16[1,1,1024,256]{3,2,1,0:T(8,128)(2,1)} %basis.3) | copy-start | bytes 1572868
  12.8 1.6 %copy-start.5 = (s32[1,1,2]{2,1,0:T(1,128)S(1)}, s32[1,1,2]{2,1,0:T(1,128)}, u32[]{:S(2)}) copy-start(s32[1,1,2]{2,1,0:T(1,128)} %owner_route.9) | copy-start | bytes 28
  14.3 1.5 %copy-start.1 = (bf16[1,1,3,1,512,512]{5,4,3,2,1,0:T(8,128)(2,1)S(1)}, bf16[1,1,3,1,512,512]{5,4,3,2,1,0:T(8,128)(2,1)}, u32[]{:S(2)}) copy-start(bf16[1,1,3,1,512,512]{5,4,3,2,1,0:T(8,128)(2,1)} %tiles.5) | copy-start | bytes 4718596
  15.4 8.6 %collective-permute-start.4 = (bf16[512,256]{1,0:T(8,128)(2,1)S(1)}, bf16[512,256]{1,0:T(8,128)(2,1)S(1)}, u32[]{:S(2)}, u32[]{:S(2)}) collective-permute-start(bf16[512,256]{1,0:T(8,128)(2,1)S(1)} %get-tuple-element.24), channel_id=1, source_target_pairs={{0,30},{2,4},{4,2},{6,8},{8,6},{10,12},{12,10},{14,16},{16,14},{18... | collective-permute-start | bytes 786440 | tf_op jit(solution)/shard_map/ppermute | solution.py:25
  17.0 9.0 %collective-permute-start.3 = (bf16[256,512]{1,0:T(8,128)(2,1)S(1)}, bf16[256,512]{1,0:T(8,128)(2,1)S(1)}, u32[]{:S(2)}, u32[]{:S(2)}) collective-permute-start(bf16[256,512]{1,0:T(8,128)(2,1)S(1)} %get-tuple-element.23), channel_id=1, source_target_pairs={{0,1},{1,0},{2,3},{3,2},{4,5},{5,4},{6,7},{7,6},{8,9},{9,8},{10,11... | collective-permute-start | bytes 786440 | tf_op jit(solution)/shard_map/ppermute | solution.py:15
  25.1 5.0 %collective-permute-start.5 = (bf16[256,256]{1,0:T(8,128)(2,1)S(1)}, bf16[256,256]{1,0:T(8,128)(2,1)S(1)}, u32[]{:S(2)}, u32[]{:S(2)}) collective-permute-start(bf16[256,256]{1,0:T(8,128)(2,1)S(1)} %get-tuple-element.26), channel_id=1, source_target_pairs={{0,1},{1,0},{2,3},{3,2},{4,5},{5,4},{6,7},{7,6},{8,9},{9,8},{10,11... | collective-permute-start | bytes 393224 | tf_op jit(solution)/shard_map/ppermute | solution.py:15

commit v4 on v3

v4 whole, which is shorter than its diff:
```python
import functools

import jax
import jax.numpy as jnp
from jax import lax
from jax.experimental import pallas as pl
from jax.experimental.pallas import tpu as pltpu
from jax.sharding import PartitionSpec as P

TRANSPOSED = (((0,), (0,)), ((), ()))


def from_behind(array, axis, by):
    devices = lax.axis_size(axis)
    return lax.ppermute(array, axis, [(i, (i + by) % devices) for i in range(devices)])


def swap_near(array):
    devices = lax.axis_size("blk")
    return lax.ppermute(array, "blk", [(i, i ^ 1) for i in range(devices)])


def swap_far(array):
    devices = lax.axis_size("blk")
    return lax.ppermute(
        array, "blk", [(i, (i + 1 if i % 2 else i - 1) % devices) for i in range(devices)]
    )


def on_chip(shape, dtype):
    return pltpu.VMEM(shape, dtype)


def call(kernel, out_shape, arrays, flops, scalars=(), hbm=(), scratch=(), to_hbm=False, alias=False):
    scalar, vector, main = (
        pl.BlockSpec(memory_space=m) for m in (pltpu.SMEM, pltpu.VMEM, pltpu.HBM)
    )
    placed = list(scalars)
    placed += [pltpu.with_memory_space_constraint(x, pltpu.VMEM) for x in arrays]
    placed += [pltpu.with_memory_space_constraint(x, pltpu.HBM) for x in hbm]
    target = main if to_hbm else vector
    return pl.pallas_call(
        kernel,
        out_shape=out_shape,
        in_specs=[scalar] * len(scalars) + [vector] * len(arrays) + [main] * len(hbm),
        out_specs=tuple(target for _ in out_shape) if isinstance(out_shape, tuple) else target,
        scratch_shapes=list(scratch),
        input_output_aliases={len(placed) - 1: 0} if alias else {},
        compiler_params=pltpu.CompilerParams(vmem_limit_bytes=16 << 20),
        cost_estimate=pl.CostEstimate(flops=flops, bytes_accessed=1 << 20, transcendentals=0),
    )(*placed)


def far_offset():
    return 2 * lax.rem(lax.axis_index("blk"), 2)


def copy_all(pairs, sems):
    copies = [pltpu.make_async_copy(*pair, sems.at[i]) for i, pair in enumerate(pairs)]
    for copy in copies:
        copy.start()
    for copy in copies:
        copy.wait()


def cut_kernel(sketch, first, sems):
    copy_all([(sketch.at[:, pl.ds(0, first.shape[1])], first)], sems)


def stage_kernel(sketch, tiles, basis, lent, own, staged, kept, sems):
    half = lent.shape[0]
    group = lax.axis_index("group")
    ours, theirs = (
        basis.at[0, 0, pl.ds(pl.multiple_of(g * half, half), half)] for g in (group, 1 - group)
    )
    copy_all([(theirs, lent), (sketch, own), (tiles.at[0, 0, :, 0], staged), (ours, kept)], sems)


def local_kernel(row_blocks, owner_route, tiles, own, near, hit, miss, stays):
    far = far_offset()
    owner = owner_route[row_blocks[far]]
    own_hits = owner_route[row_blocks[1]] == owner
    near_hits = owner_route[row_blocks[2 - far]] == owner
    step = 256
    for start in range(0, own.shape[1], step):
        columns = pl.ds(start, step)
        first = jnp.dot(tiles[1], own[:, columns], preferred_element_type=jnp.float32)
        second = jnp.dot(tiles[2 - far], near[:, columns], preferred_element_type=jnp.float32)
        hit[:, columns] = jnp.where(own_hits, first, 0.0) + jnp.where(near_hits, second, 0.0)
        miss[:, columns] = (
            jnp.where(own_hits, 0.0, first) + jnp.where(near_hits, 0.0, second)
        ).astype(jnp.bfloat16)
    stays[...] = jnp.full(stays.shape, jnp.where(owner == lax.axis_index("group"), 1.0, 0.0))


def turn_kernel(kept, lent, miss, own, stays, hit_turned, missed, second):
    stay = stays[:, pl.ds(0, kept.shape[0])] > 0.0
    ours, theirs = kept[...].T, lent[...].T
    hit_turned[...] = jnp.where(stay, ours, theirs)
    missed[...] = jnp.dot(
        jnp.where(stay, theirs, ours), miss[...], preferred_element_type=jnp.float32
    )
    second[...] = own[:, pl.ds(own.shape[1] - second.shape[1], second.shape[1])]


def far_kernel(start, tiles, far, hit, hit_turned, missed, stays, kept, sent):
    columns = pl.ds(start, far.shape[1])
    product = jnp.dot(tiles[far_offset()], far[...], preferred_element_type=jnp.float32)
    sampled = (hit[:, columns] + product).astype(jnp.bfloat16)
    made = jnp.dot(hit_turned[...], sampled, preferred_element_type=jnp.float32)
    stay = stays[:, columns] > 0.0
    other = missed[:, columns]
    sent[...] = jnp.where(stay, other, made).astype(jnp.bfloat16)
    kept[...] = jnp.where(stay, made, other)


def join_kernel(start, kept, received, *rest):
    out, total, sems = rest[-3:]
    total[...] = kept[...] + received[...].astype(jnp.float32)
    copy_all([(total, out.at[:, pl.ds(start, total.shape[1])])], sems)


def paired_body(sketch, far_tiles, row_blocks, owner_route, cluster_basis):
    panels, columns = sketch.shape
    offsets, rows = far_tiles.shape[2], far_tiles.shape[4]
    half, rank = cluster_basis.shape[2] // 2, cluster_basis.shape[3]
    early = 2 * columns // 3
    product = 2 * rows * panels * columns
    short, wide = sketch.dtype, jnp.float32
    copies = pltpu.SemaphoreType.DMA
    first = call(
        cut_kernel, on_chip((panels, early), short), (), 0, hbm=(sketch,), scratch=(copies((1,)),)
    )
    far_first = swap_far(first)
    near = swap_near(sketch)
    lent, own, tiles, kept = call(
        stage_kernel,
        (
            on_chip((half, rank), short),
            on_chip((panels, columns), short),
            on_chip((offsets, rows, panels), short),
            on_chip((half, rank), short),
        ),
        (),
        0,
        hbm=(sketch, far_tiles, cluster_basis),
        scratch=(copies((4,)),),
    )
    lent = from_behind(lent, "group", 1)
    hit, miss, stays = call(
        local_kernel,
        (
            on_chip((rows, columns), wide),
            on_chip((rows, columns), short),
            on_chip((1, columns), wide),
        ),
        (tiles, own, near),
        2 * product,
        scalars=(row_blocks.reshape(-1), owner_route.reshape(-1)),
    )
    hit_turned, missed, second = call(
        turn_kernel,
        (
            on_chip((rank, half), short),
            on_chip((rank, columns), wide),
            on_chip((panels, columns - early), short),
        ),
        (kept, lent, miss, own, stays),
        product // 2,
    )
    far_second = swap_far(second)
    out = None
    for start, far in ((0, far_first), (early, far_second)):
        width = far.shape[1]
        kept, sent = call(
            functools.partial(far_kernel, start),
            (on_chip((rank, width), wide), on_chip((rank, width), short)),
            (tiles, far, hit, hit_turned, missed, stays),
            2 * product * width // columns,
        )
        out = call(
            functools.partial(join_kernel, start),
            pltpu.HBM((rank, columns), wide),
            (kept, from_behind(sent, "group", 1)),
            1 << 16,
            hbm=() if out is None else (out,),
            scratch=(on_chip((rank, width), wide), copies((1,))),
            to_hbm=True,
            alias=out is not None,
        )
    return out[None, None]


def contribute(summed, far_tiles, row_blocks, offset, current):
    product = jnp.einsum(
        "trk,kc->trc", far_tiles[0, 0, offset], current, preferred_element_type=jnp.float32
    )
    return summed.at[row_blocks[0, 0, offset]].add(product)


def ring_body(sketch, far_tiles, row_blocks, owner_route, cluster_basis):
    offsets = far_tiles.shape[2]
    radius = (offsets - 1) // 2
    groups = lax.axis_size("group")
    tile_rows = far_tiles.shape[4]
    columns = sketch.shape[1]
    summed = jnp.zeros((groups, tile_rows, columns), jnp.float32)
    for offset in range(offsets):
        current = from_behind(sketch, "blk", radius - offset) if offset != radius else sketch
        summed = contribute(summed, far_tiles, row_blocks, offset, current)
    sampled = summed.astype(jnp.bfloat16)
    ordered = jnp.zeros_like(sampled).at[owner_route[0, 0]].set(sampled)
    received = lax.all_to_all(ordered, "group", split_axis=0, concat_axis=0, tiled=True)
    stacked = received.reshape(received.shape[0] * received.shape[1], received.shape[2])
    coefficients = lax.dot_general(
        cluster_basis[0, 0], stacked, TRANSPOSED, preferred_element_type=jnp.float32
    )
    return coefficients[None, None]


def body(sketch, far_tiles, row_blocks, owner_route, cluster_basis):
    small = cluster_basis.shape[3] < far_tiles.shape[4]
    paired = lax.axis_size("group") == 2 and lax.axis_size("blk") % 2 == 0
    if small and paired and far_tiles.shape[2:4] == (3, 1):
        return paired_body(sketch, far_tiles, row_blocks, owner_route, cluster_basis)
    return ring_body(sketch, far_tiles, row_blocks, owner_route, cluster_basis)


def solution(mesh):
    placed = (
        P("blk", None),
        P("blk", "group", None, None, None, None),
        P("blk", "group", None, None),
        P("blk", "group", None),
        P("blk", "group", None, None),
    )
    return jax.shard_map(
        body, mesh=mesh, in_specs=placed, out_specs=P("blk", "group", None, None), check_vma=False
    )
```

time: 31.9 us -> 31 us (0.972)
  local copies, waits for them, and re-layouts: 3.95 us -> 0.01 us
  waiting for transfers between devices: 9.52 us -> 11.2 us
  starting transfers between devices: 10.5 us -> 11.9 us
    unnamed x13 -> x4, local copies, waits for them, and re-layouts: 3.95 us -> 0.01 us
    ppermute x3, waiting for transfers between devices: 4.14 us -> 5.88 us  [from_behind(): lax.ppermute(array, axis, [(i, (i + by) % devices) for i in range(devices)])]
    ppermute x3, starting transfers between devices: 4 us -> 4.76 us  [from_behind(): lax.ppermute(array, axis, [(i, (i + by) % devices) for i in range(devices)])]
    ppermute x2, starting transfers between devices: 6.08 us -> 6.65 us  [swap_far(): lax.ppermute(array, 'blk', [(i, (i + 1 if i % 2 else i - 1) % devices) fo...]
    pallas_call x6 -> x8, Pallas kernels: 7.64 us -> 7.66 us  [call(): pl.pallas_call(kernel, out_shape=out_shape, in_specs=[scalar] * len(scala...]
  transfers between devices with their start and end apart: 6 -> 6, of which waited for: 2 -> 3; matrix products, arithmetic and copies ran while one was open for 2% -> 0% of each run, Pallas kernels for 19% -> 22%
where the time goes in v4:
time: 31 us; the launch traced here: 30.9 us
  starting transfers between devices  11.9 us (38%)
  waiting for transfers between devices  11.2 us (36%)
  Pallas kernels  7.66 us (25%)
    pallas_call x8, Pallas kernels, call(): pl.pallas_call(kernel, out_shape=out_shape, in_specs=[scalar] * len(scala...  7.66 us
    ppermute x2, starting transfers between devices, swap_far(): lax.ppermute(array, 'blk', [(i, (i + 1 if i % 2 else i - 1) % devices) fo...  6.65 us
    ppermute x3, waiting for transfers between devices, from_behind(): lax.ppermute(array, axis, [(i, (i + by) % devices) for i in range(devices)])  5.88 us
    ppermute x2, waiting for transfers between devices, swap_far(): lax.ppermute(array, 'blk', [(i, (i + 1 if i % 2 else i - 1) % devices) fo...  5.36 us
    ppermute x3, starting transfers between devices, from_behind(): lax.ppermute(array, axis, [(i, (i + by) % devices) for i in range(devices)])  4.76 us
  transfers between devices with their start and end apart: 6, of which 3 were waited for; matrix products, arithmetic and copies ran while one was open for 0% of the time, Pallas kernels for 22%

profile of v4, /device:TPU:0, one launch (start us, length us, event | category | flops | bytes accessed | tf_op | source)
XLA Modules:
  0.0 30.9 jit_solution(15053572641503857991)
XLA Ops:
  0.0 0.5 %collective-permute-start.1 = (bf16[512,768]{1,0:T(8,128)(2,1)}, bf16[512,768]{1,0:T(8,128)(2,1)S(1)}, u32[]{:S(2)}, u32[]{:S(2)}) collective-permute-start(bf16[512,768]{1,0:T(8,128)(2,1)} %sketch.3), channel_id=1, source_target_pairs={{0,2},{2,0},{4,6},{6,4},{8,10},{10,8},{12,14},{14,12},{16,18},{18,... | collective-permute-start | bytes 2359304 | tf_op jit(solution)/shard_map/ppermute | solution.py:20
  0.5 1.0 %shard_map.59 = bf16[512,512]{1,0:T(8,128)(2,1)S(1)} custom-call(bf16[512,768]{1,0:T(8,128)(2,1)} %sketch.3), custom_call_target="tpu_custom_call" | custom-call | bytes 1048576 | tf_op jit(solution)/shard_map/pallas_call | solution.py:42
  1.5 0.0 copy-start
  1.5 0.0 copy-start.1
  1.5 5.7 %collective-permute-start.4 = (bf16[512,512]{1,0:T(8,128)(2,1)S(1)}, bf16[512,512]{1,0:T(8,128)(2,1)S(1)}, u32[]{:S(2)}, u32[]{:S(2)}) collective-permute-start(bf16[512,512]{1,0:T(8,128)(2,1)S(1)} %shard_map.59), channel_id=1, source_target_pairs={{0,30},{2,4},{4,2},{6,8},{8,6},{10,12},{12,10},{14,16},{16,14},{18... | collective-permute-start | bytes 1572872 | tf_op jit(solution)/shard_map/ppermute | solution.py:25
  7.2 1.8 %shard_map.55 = (bf16[512,256]{1,0:T(8,128)(2,1)S(1)}, bf16[512,768]{1,0:T(8,128)(2,1)S(1)}, bf16[3,512,512]{2,1,0:T(8,128)(2,1)S(1)}, bf16[512,256]{1,0:T(8,128)(2,1)S(1)}) custom-call(bf16[512,768]{1,0:T(8,128)(2,1)} %sketch.3, bf16[1,1,3,1,512,512]{5,4,3,2,1,0:T(8,128)(2,1)} %tiles.1, bf16[1,1,1024,256]{3,2,1,0:T(8,128)(2,1)} %basis.1), custom_call_target="tpu_custom_call" | custom-call | bytes 1048576 | tf_op jit(solution)/shard_map/pallas_call | solution.py:42
  9.0 1.6 %collective-permute-start = (bf16[512,256]{1,0:T(8,128)(2,1)S(1)}, bf16[512,256]{1,0:T(8,128)(2,1)S(1)}, u32[]{:S(2)}, u32[]{:S(2)}) collective-permute-start(bf16[512,256]{1,0:T(8,128)(2,1)S(1)} %get-tuple-element.21), channel_id=1, source_target_pairs={{0,1},{1,0},{2,3},{3,2},{4,5},{5,4},{6,7},{7,6},{8,9},{9,8},{10,11... | collective-permute-start | bytes 786440 | tf_op jit(solution)/shard_map/ppermute | solution.py:15
  10.6 0.0 collective-permute-done.1.near
  10.6 0.0 copy-done
  10.6 0.0 copy-done.1
  10.6 1.5 %shard_map.56 = (f32[512,768]{1,0:T(8,128)S(1)}, bf16[512,768]{1,0:T(8,128)(2,1)S(1)}, f32[1,768]{1,0:T(1,128)S(1)}) custom-call(s32[3]{0:T(128)S(1)} %bitcast.3, s32[2]{0:T(128)S(1)} %bitcast.4, bf16[3,512,512]{2,1,0:T(8,128)(2,1)S(1)} %get-tuple-element.19.tiles, bf16[512,768]{1,0:T(8,128)(2,1)S(1)} %get-tuple-element.22.own, ...), custom_call_target="tpu_custom_call" | custom-call | flops 805306368 | bytes 1048576 | tf_op jit(solution)/shard_map/pallas_call | solution.py:42
  12.2 3.3 %collective-permute-done.lent = bf16[512,256]{1,0:T(8,128)(2,1)S(1)} collective-permute-done((bf16[512,256]{1,0:T(8,128)(2,1)S(1)}, bf16[512,256]{1,0:T(8,128)(2,1)S(1)}, u32[]{:S(2)}, u32[]{:S(2)}) %collective-permute-start) | collective-permute-done | bytes 262176 | tf_op jit(solution)/shard_map/ppermute | solution.py:15
  15.5 0.5 %shard_map.57 = (bf16[256,512]{1,0:T(8,128)(2,1)S(1)}, f32[256,768]{1,0:T(8,128)S(1)}, bf16[512,256]{1,0:T(8,128)(2,1)S(1)}) custom-call(bf16[512,256]{1,0:T(8,128)(2,1)S(1)} %get-tuple-element.20.kept, bf16[512,256]{1,0:T(8,128)(2,1)S(1)} %collective-permute-done.lent, bf16[512,768]{1,0:T(8,128)(2,1)S(1)} %get-tuple-element.23.miss, ...), custom_call_target="tpu_custom_call" | custom-call | flops 201326592 | bytes 1048576 | tf_op jit(solution)/shard_map/pallas_call | solution.py:42
  16.0 0.9 %collective-permute-start.2 = (bf16[512,256]{1,0:T(8,128)(2,1)S(1)}, bf16[512,256]{1,0:T(8,128)(2,1)S(1)}, u32[]{:S(2)}, u32[]{:S(2)}) collective-permute-start(bf16[512,256]{1,0:T(8,128)(2,1)S(1)} %get-tuple-element.25), channel_id=1, source_target_pairs={{0,30},{2,4},{4,2},{6,8},{8,6},{10,12},{12,10},{14,16},{16,14},{18... | collective-permute-start | bytes 786440 | tf_op jit(solution)/shard_map/ppermute | solution.py:25
  16.9 0.0 collective-permute-done.4.far
  16.9 0.7 %shard_map.60 = (f32[256,512]{1,0:T(8,128)S(1)}, bf16[256,512]{1,0:T(8,128)(2,1)S(1)}) custom-call(bf16[3,512,512]{2,1,0:T(8,128)(2,1)S(1)} %get-tuple-element.19.tiles, bf16[512,512]{1,0:T(8,128)(2,1)S(1)} %collective-permute-done.4.far, f32[512,768]{1,0:T(8,128)S(1)} %get-tuple-element.26.hit, bf16[256,512]{1,0:T(8,128)(2,1)S(1)} %get-tuple-element.27.hit_turned, ...), custom_call_target="tpu_custom_call" | custom-call | flops 536870912 | bytes 1048576 | tf_op jit(solution)/shard_map/pallas_call | solution.py:42
  17.6 1.6 %collective-permute-start.5 = (bf16[256,512]{1,0:T(8,128)(2,1)S(1)}, bf16[256,512]{1,0:T(8,128)(2,1)S(1)}, u32[]{:S(2)}, u32[]{:S(2)}) collective-permute-start(bf16[256,512]{1,0:T(8,128)(2,1)S(1)} %get-tuple-element.32), channel_id=1, source_target_pairs={{0,1},{1,0},{2,3},{3,2},{4,5},{5,4},{6,7},{7,6},{8,9},{9,8},{10,11... | collective-permute-start | bytes 786440 | tf_op jit(solution)/shard_map/ppermute | solution.py:15
  19.2 5.4 %collective-permute-done.2.far = bf16[512,256]{1,0:T(8,128)(2,1)S(1)} collective-permute-done((bf16[512,256]{1,0:T(8,128)(2,1)S(1)}, bf16[512,256]{1,0:T(8,128)(2,1)S(1)}, u32[]{:S(2)}, u32[]{:S(2)}) %collective-permute-start.2) | collective-permute-done | bytes 262176 | tf_op jit(solution)/shard_map/ppermute | solution.py:25
  24.5 0.6 %shard_map.58 = (f32[256,256]{1,0:T(8,128)S(1)}, bf16[256,256]{1,0:T(8,128)(2,1)S(1)}) custom-call(bf16[3,512,512]{2,1,0:T(8,128)(2,1)S(1)} %get-tuple-element.19.tiles, bf16[512,256]{1,0:T(8,128)(2,1)S(1)} %collective-permute-done.2.far, f32[512,768]{1,0:T(8,128)S(1)} %get-tuple-element.26.hit, bf16[256,512]{1,0:T(8,128)(2,1)S(1)} %get-tuple-element.27.hit_turned, ...), custom_call_target="tpu_custom_call" | custom-call | flops 268435456 | bytes 1048576 | tf_op jit(solution)/shard_map/pallas_call | solution.py:42
  25.1 1.6 %collective-permute-start.3 = (bf16[256,256]{1,0:T(8,128)(2,1)S(1)}, bf16[256,256]{1,0:T(8,128)(2,1)S(1)}, u32[]{:S(2)}, u32[]{:S(2)}) collective-permute-start(bf16[256,256]{1,0:T(8,128)(2,1)S(1)} %get-tuple-element.30), channel_id=1, source_target_pairs={{0,1},{1,0},{2,3},{3,2},{4,5},{5,4},{6,7},{7,6},{8,9},{9,8},{10,11... | collective-permute-start | bytes 393224 | tf_op jit(solution)/shard_map/ppermute | solution.py:15
  26.7 0.0 collective-permute-done.5.received
  26.7 0.9 %shard_map.61.rest_0_ = f32[256,768]{1,0:T(8,128)} custom-call(f32[256,512]{1,0:T(8,128)S(1)} %get-tuple-element.31.kept, bf16[256,512]{1,0:T(8,128)(2,1)S(1)} %collective-permute-done.5.received), custom_call_target="tpu_custom_call" | custom-call | flops 65536 | bytes 1048576 | tf_op jit(solution)/shard_map/pallas_call | solution.py:42
  27.5 2.6 %collective-permute-done.3.received = bf16[256,256]{1,0:T(8,128)(2,1)S(1)} collective-permute-done((bf16[256,256]{1,0:T(8,128)(2,1)S(1)}, bf16[256,256]{1,0:T(8,128)(2,1)S(1)}, u32[]{:S(2)}, u32[]{:S(2)}) %collective-permute-start.3) | collective-permute-done | bytes 131104 | tf_op jit(solution)/shard_map/ppermute | solution.py:15
  30.1 0.7 %shard_map.62 = f32[256,768]{1,0:T(8,128)} custom-call(f32[256,256]{1,0:T(8,128)S(1)} %get-tuple-element.29.kept, bf16[256,256]{1,0:T(8,128)(2,1)S(1)} %collective-permute-done.3.received, f32[256,768]{1,0:T(8,128)} %shard_map.61.rest_0_), custom_call_target="tpu_custom_call", output_to_operand_aliasing={{}: (2, {})} | custom-call | flops 65536 | bytes 1048576 | tf_op jit(solution)/shard_map/pallas_call | solution.py:42
Async XLA Ops:
  0.0 10.6 %collective-permute-start.1 = (bf16[512,768]{1,0:T(8,128)(2,1)}, bf16[512,768]{1,0:T(8,128)(2,1)S(1)}, u32[]{:S(2)}, u32[]{:S(2)}) collective-permute-start(bf16[512,768]{1,0:T(8,128)(2,1)} %sketch.3), channel_id=1, source_target_pairs={{0,2},{2,0},{4,6},{6,4},{8,10},{10,8},{12,14},{14,12},{16,18},{18,... | collective-permute-start | bytes 2359304 | tf_op jit(solution)/shard_map/ppermute | solution.py:20
  1.5 9.1 %copy-start = (s32[1,1,3,1]{2,3,1,0:T(1,128)S(1)}, s32[1,1,3,1]{2,3,1,0:T(1,128)}, u32[]{:S(2)}) copy-start(s32[1,1,3,1]{2,3,1,0:T(1,128)} %param.7) | copy-start | bytes 40
  1.5 9.1 %copy-start.1 = (s32[1,1,2]{2,1,0:T(1,128)S(1)}, s32[1,1,2]{2,1,0:T(1,128)}, u32[]{:S(2)}) copy-start(s32[1,1,2]{2,1,0:T(1,128)} %param.8) | copy-start | bytes 28
  1.5 15.4 %collective-permute-start.4 = (bf16[512,512]{1,0:T(8,128)(2,1)S(1)}, bf16[512,512]{1,0:T(8,128)(2,1)S(1)}, u32[]{:S(2)}, u32[]{:S(2)}) collective-permute-start(bf16[512,512]{1,0:T(8,128)(2,1)S(1)} %shard_map.59), channel_id=1, source_target_pairs={{0,30},{2,4},{4,2},{6,8},{8,6},{10,12},{12,10},{14,16},{16,14},{18... | collective-permute-start | bytes 1572872 | tf_op jit(solution)/shard_map/ppermute | solution.py:25
  9.0 6.4 %collective-permute-start = (bf16[512,256]{1,0:T(8,128)(2,1)S(1)}, bf16[512,256]{1,0:T(8,128)(2,1)S(1)}, u32[]{:S(2)}, u32[]{:S(2)}) collective-permute-start(bf16[512,256]{1,0:T(8,128)(2,1)S(1)} %get-tuple-element.21), channel_id=1, source_target_pairs={{0,1},{1,0},{2,3},{3,2},{4,5},{5,4},{6,7},{7,6},{8,9},{9,8},{10,11... | collective-permute-start | bytes 786440 | tf_op jit(solution)/shard_map/ppermute | solution.py:15
  16.0 8.6 %collective-permute-start.2 = (bf16[512,256]{1,0:T(8,128)(2,1)S(1)}, bf16[512,256]{1,0:T(8,128)(2,1)S(1)}, u32[]{:S(2)}, u32[]{:S(2)}) collective-permute-start(bf16[512,256]{1,0:T(8,128)(2,1)S(1)} %get-tuple-element.25), channel_id=1, source_target_pairs={{0,30},{2,4},{4,2},{6,8},{8,6},{10,12},{12,10},{14,16},{16,14},{18... | collective-permute-start | bytes 786440 | tf_op jit(solution)/shard_map/ppermute | solution.py:25
  17.6 9.1 %collective-permute-start.5 = (bf16[256,512]{1,0:T(8,128)(2,1)S(1)}, bf16[256,512]{1,0:T(8,128)(2,1)S(1)}, u32[]{:S(2)}, u32[]{:S(2)}) collective-permute-start(bf16[256,512]{1,0:T(8,128)(2,1)S(1)} %get-tuple-element.32), channel_id=1, source_target_pairs={{0,1},{1,0},{2,3},{3,2},{4,5},{5,4},{6,7},{7,6},{8,9},{9,8},{10,11... | collective-permute-start | bytes 786440 | tf_op jit(solution)/shard_map/ppermute | solution.py:15
  25.1 5.0 %collective-permute-start.3 = (bf16[256,256]{1,0:T(8,128)(2,1)S(1)}, bf16[256,256]{1,0:T(8,128)(2,1)S(1)}, u32[]{:S(2)}, u32[]{:S(2)}) collective-permute-start(bf16[256,256]{1,0:T(8,128)(2,1)S(1)} %get-tuple-element.30), channel_id=1, source_target_pairs={{0,1},{1,0},{2,3},{3,2},{4,5},{5,4},{6,7},{7,6},{8,9},{9,8},{10,11... | collective-permute-start | bytes 393224 | tf_op jit(solution)/shard_map/ppermute | solution.py:15

commit v5 on v4

--- a/solution.py
+++ b/solution.py
@@ -15,16 +15,36 @@
     return lax.ppermute(array, axis, [(i, (i + by) % devices) for i in range(devices)])
 
 
-def swap_near(array):
-    devices = lax.axis_size("blk")
-    return lax.ppermute(array, "blk", [(i, i ^ 1) for i in range(devices)])
-
-
-def swap_far(array):
-    devices = lax.axis_size("blk")
-    return lax.ppermute(
-        array, "blk", [(i, (i + 1 if i % 2 else i - 1) % devices) for i in range(devices)]
-    )
+def swap(array, wanted, partner):
+    sizes = lax.axis_size("blk"), lax.axis_size("group")
+    places = [(b, g) for b in range(sizes[0]) for g in range(sizes[1]) if wanted(b)]
+    flat = [(b * sizes[1] + g, partner(b, g)) for b, g in places]
+    pairs = [(source, b % sizes[0] * sizes[1] + g) for source, (b, g) in flat]
+    return lax.ppermute(array, ("blk", "group"), pairs)
+
+
+def is_late(b):
+    return (b + 1) // 2 % 2 == 1
+
+
+def is_early(b):
+    return not is_late(b)
+
+
+def every(b):
+    return True
+
+
+def near_of(b, g):
+    return b ^ 1, g
+
+
+def far_of(b, g):
+    return (b + 1 if b % 2 else b - 1), g
+
+
+def across(b, g):
+    return b, 1 - g
 
 
 def on_chip(shape, dtype):
@@ -63,17 +83,26 @@
         copy.wait()
 
 
-def cut_kernel(sketch, first, sems):
-    copy_all([(sketch.at[:, pl.ds(0, first.shape[1])], first)], sems)
-
-
-def stage_kernel(sketch, tiles, basis, lent, own, staged, kept, sems):
+def comes_late():
+    return lax.rem((lax.axis_index("blk") + 1) // 2, 2) == 1
+
+
+def stage_kernel(sketch, tiles, basis, lent, first, second, own, staged, kept, sems):
     half = lent.shape[0]
     group = lax.axis_index("group")
     ours, theirs = (
         basis.at[0, 0, pl.ds(pl.multiple_of(g * half, half), half)] for g in (group, 1 - group)
     )
-    copy_all([(theirs, lent), (sketch, own), (tiles.at[0, 0, :, 0], staged), (ours, kept)], sems)
+    width = first.shape[1]
+    pairs = [
+        (theirs, lent),
+        (sketch.at[:, pl.ds(0, width)], first),
+        (sketch.at[:, pl.ds(width, second.shape[1])], second),
+        (sketch, own),
+        (tiles.at[0, 0, :, 0], staged),
+        (ours, kept),
+    ]
+    copy_all(pairs, sems)
 
 
 def local_kernel(row_blocks, owner_route, tiles, own, near, hit, miss, stays):
@@ -93,50 +122,69 @@
     stays[...] = jnp.full(stays.shape, jnp.where(owner == lax.axis_index("group"), 1.0, 0.0))
 
 
-def turn_kernel(kept, lent, miss, own, stays, hit_turned, missed, second):
+def turn_kernel(kept, lent, miss, stays, hit_turned, missed):
     stay = stays[:, pl.ds(0, kept.shape[0])] > 0.0
     ours, theirs = kept[...].T, lent[...].T
     hit_turned[...] = jnp.where(stay, ours, theirs)
     missed[...] = jnp.dot(
         jnp.where(stay, theirs, ours), miss[...], preferred_element_type=jnp.float32
     )
-    second[...] = own[:, pl.ds(own.shape[1] - second.shape[1], second.shape[1])]
-
-
-def far_kernel(start, tiles, far, hit, hit_turned, missed, stays, kept, sent):
-    columns = pl.ds(start, far.shape[1])
-    product = jnp.dot(tiles[far_offset()], far[...], preferred_element_type=jnp.float32)
-    sampled = (hit[:, columns] + product).astype(jnp.bfloat16)
-    made = jnp.dot(hit_turned[...], sampled, preferred_element_type=jnp.float32)
-    stay = stays[:, columns] > 0.0
-    other = missed[:, columns]
-    sent[...] = jnp.where(stay, other, made).astype(jnp.bfloat16)
-    kept[...] = jnp.where(stay, made, other)
-
-
-def join_kernel(start, kept, received, *rest):
-    out, total, sems = rest[-3:]
-    total[...] = kept[...] + received[...].astype(jnp.float32)
-    copy_all([(total, out.at[:, pl.ds(start, total.shape[1])])], sems)
+
+
+def far_kernel(late, start, tiles, far, hit, hit_turned, missed, stays, kept, sent):
+    @pl.when(comes_late() == late)
+    def _():
+        columns = pl.ds(start, far.shape[1])
+        product = jnp.dot(tiles[far_offset()], far[...], preferred_element_type=jnp.float32)
+        sampled = (hit[:, columns] + product).astype(jnp.bfloat16)
+        made = jnp.dot(hit_turned[...], sampled, preferred_element_type=jnp.float32)
+        stay = stays[:, columns] > 0.0
+        other = missed[:, columns]
+        sent[...] = jnp.where(stay, other, made).astype(jnp.bfloat16)
+        kept[...] = jnp.where(stay, made, other)
+
+
+def join_part(kept, received, start, out, total, sems):
+    width = kept.shape[1]
+    part = total.at[:, pl.ds(0, width)]
+    part[...] = kept[...] + received[...].astype(jnp.float32)
+    copy_all([(part, out.at[:, pl.ds(start, width)])], sems)
+
+
+def join_first_kernel(kept, received, out, total, sems):
+    @pl.when(comes_late())
+    def _():
+        join_part(kept, received, 0, out, total, sems)
+
+
+def join_rest_kernel(kept, received, all_kept, all_received, begun, out, total, sems):
+    late = comes_late()
+
+    @pl.when(late)
+    def _():
+        join_part(kept, received, out.shape[1] - kept.shape[1], out, total, sems)
+
+    @pl.when(jnp.logical_not(late))
+    def _():
+        join_part(all_kept, all_received, 0, out, total, sems)
 
 
 def paired_body(sketch, far_tiles, row_blocks, owner_route, cluster_basis):
     panels, columns = sketch.shape
     offsets, rows = far_tiles.shape[2], far_tiles.shape[4]
     half, rank = cluster_basis.shape[2] // 2, cluster_basis.shape[3]
-    early = 2 * columns // 3
+    width = 2 * columns // 3
     product = 2 * rows * panels * columns
     short, wide = sketch.dtype, jnp.float32
     copies = pltpu.SemaphoreType.DMA
-    first = call(
-        cut_kernel, on_chip((panels, early), short), (), 0, hbm=(sketch,), scratch=(copies((1,)),)
-    )
-    far_first = swap_far(first)
-    near = swap_near(sketch)
-    lent, own, tiles, kept = call(
+    far_whole = swap(sketch, is_early, far_of)
+    near = swap(sketch, every, near_of)
+    lent, first, second, own, tiles, kept = call(
         stage_kernel,
         (
             on_chip((half, rank), short),
+            on_chip((panels, width), short),
+            on_chip((panels, columns - width), short),
             on_chip((panels, columns), short),
             on_chip((offsets, rows, panels), short),
             on_chip((half, rank), short),
@@ -144,9 +192,9 @@
         (),
         0,
         hbm=(sketch, far_tiles, cluster_basis),
-        scratch=(copies((4,)),),
-    )
-    lent = from_behind(lent, "group", 1)
+        scratch=(copies((6,)),),
+    )
+    lent = swap(lent, every, across)
     hit, miss, stays = call(
         local_kernel,
         (
@@ -158,36 +206,42 @@
         2 * product,
         scalars=(row_blocks.reshape(-1), owner_route.reshape(-1)),
     )
-    hit_turned, missed, second = call(
+    hit_turned, missed = call(
         turn_kernel,
-        (
-            on_chip((rank, half), short),
-            on_chip((rank, columns), wide),
-            on_chip((panels, columns - early), short),
-        ),
-        (kept, lent, miss, own, stays),
+        (on_chip((rank, half), short), on_chip((rank, columns), wide)),
+        (kept, lent, miss, stays),
         product // 2,
     )
-    far_second = swap_far(second)
-    out = None
-    for start, far in ((0, far_first), (early, far_second)):
-        width = far.shape[1]
+    first, second, hit_turned = lax.optimization_barrier((first, second, hit_turned))
+    far_first = swap(first, is_late, far_of)
+    far_second = swap(second, is_late, far_of)
+
+    def finish(far, late, start):
+        part = far.shape[1]
         kept, sent = call(
-            functools.partial(far_kernel, start),
-            (on_chip((rank, width), wide), on_chip((rank, width), short)),
+            functools.partial(far_kernel, late, start),
+            (on_chip((rank, part), wide), on_chip((rank, part), short)),
             (tiles, far, hit, hit_turned, missed, stays),
-            2 * product * width // columns,
+            2 * product * part // columns,
         )
-        out = call(
-            functools.partial(join_kernel, start),
-            pltpu.HBM((rank, columns), wide),
-            (kept, from_behind(sent, "group", 1)),
-            1 << 16,
-            hbm=() if out is None else (out,),
-            scratch=(on_chip((rank, width), wide), copies((1,))),
-            to_hbm=True,
-            alias=out is not None,
-        )
+        return kept, swap(sent, is_late if late else is_early, across)
+
+    whole = finish(far_whole, False, 0)
+    part = finish(far_first, True, 0)
+    rest = finish(far_second, True, width)
+    scratch = on_chip((rank, columns), wide), copies((1,))
+    target = pltpu.HBM((rank, columns), wide)
+    out = call(join_first_kernel, target, part, 1 << 16, scratch=scratch, to_hbm=True)
+    out = call(
+        join_rest_kernel,
+        target,
+        (*rest, *whole),
+        1 << 16,
+        hbm=(out,),
+        scratch=scratch,
+        to_hbm=True,
+        alias=True,
+    )
     return out[None, None]
 
 
@@ -220,7 +274,7 @@
 
 def body(sketch, far_tiles, row_blocks, owner_route, cluster_basis):
     small = cluster_basis.shape[3] < far_tiles.shape[4]
-    paired = lax.axis_size("group") == 2 and lax.axis_size("blk") % 2 == 0
+    paired = lax.axis_size("group") == 2 and lax.axis_size("blk") % 4 == 0
     if small and paired and far_tiles.shape[2:4] == (3, 1):
         return paired_body(sketch, far_tiles, row_blocks, owner_route, cluster_basis)
     return ring_body(sketch, far_tiles, row_blocks, owner_route, cluster_basis)

time: 31 us -> 35.1 us (1.13)
  the two profiles are of different devices: /device:TPU:0 before, /device:TPU:26 now
where the time goes in v5:
time: 35.1 us; the launch traced here: 34.9 us
  starting transfers between devices  14.5 us (41%)
  waiting for transfers between devices  13.4 us (38%)
  Pallas kernels  6.89 us (20%)
    ppermute x8, starting transfers between devices, swap(): return lax.ppermute(array, ('blk', 'group'), pairs)  14.5 us
    ppermute x8, waiting for transfers between devices, swap(): return lax.ppermute(array, ('blk', 'group'), pairs)  13.4 us
    pallas_call x8, Pallas kernels, call(): pl.pallas_call(kernel, out_shape=out_shape, in_specs=[scalar] * len(scala...  6.89 us
  transfers between devices with their start and end apart: 8, of which 4 were waited for; matrix products, arithmetic and copies ran while one was open for 0% of the time, Pallas kernels for 18%

profile of v5, /device:TPU:26, one launch (start us, length us, event | category | flops | bytes accessed | tf_op | source)
XLA Modules:
  0.0 34.9 jit_solution(8020089254445542491)
XLA Ops:
  0.0 0.0 copy-start
  0.0 0.0 copy-start.1
  0.0 0.0 collective-permute-start.1
  0.0 0.8 %collective-permute-start.4 = (bf16[512,768]{1,0:T(8,128)(2,1)}, bf16[512,768]{1,0:T(8,128)(2,1)S(1)}, u32[]{:S(2)}, u32[]{:S(2)}) collective-permute-start(bf16[512,768]{1,0:T(8,128)(2,1)} %sketch.1), channel_id=1, source_target_pairs={{0,30},{1,31},{6,8},{7,9},{8,6},{9,7},{14,16},{15,17},{16,14},{17,... | collective-permute-start | bytes 2359304 | tf_op jit(solution)/shard_map/ppermute | solution.py:23
  0.9 2.0 %shard_map.55 = (bf16[512,256]{1,0:T(8,128)(2,1)S(1)}, bf16[512,512]{1,0:T(8,128)(2,1)S(1)}, bf16[512,256]{1,0:T(8,128)(2,1)S(1)}, bf16[512,768]{1,0:T(8,128)(2,...) custom-call(bf16[512,768]{1,0:T(8,128)(2,1)} %sketch.1, bf16[1,1,3,1,512,512]{5,4,3,2,1,0:T(8,128)(2,1)} %tiles.1, ...), custom_call_target="tpu_custom_call" | custom-call | bytes 1048576 | tf_op jit(solution)/shard_map/pallas_call | solution.py:62
  2.9 1.6 %collective-permute-start = (bf16[512,256]{1,0:T(8,128)(2,1)S(1)}, bf16[512,256]{1,0:T(8,128)(2,1)S(1)}, u32[]{:S(2)}, u32[]{:S(2)}) collective-permute-start(bf16[512,256]{1,0:T(8,128)(2,1)S(1)} %get-tuple-element.29), channel_id=1, source_target_pairs={{0,1},{1,0},{2,3},{3,2},{4,5},{5,4},{6,7},{7,6},{8,9},{9,8},{10,11... | collective-permute-start | bytes 786440 | tf_op jit(solution)/shard_map/ppermute | solution.py:23
  4.5 0.0 collective-permute-done.1.near
  4.5 0.0 copy-done
  4.5 0.0 copy-done.1
  4.5 1.5 %shard_map.56 = (f32[512,768]{1,0:T(8,128)S(1)}, bf16[512,768]{1,0:T(8,128)(2,1)S(1)}, f32[1,768]{1,0:T(1,128)S(1)}) custom-call(s32[3]{0:T(128)S(1)} %bitcast.3, s32[2]{0:T(128)S(1)} %bitcast.4, bf16[3,512,512]{2,1,0:T(8,128)(2,1)S(1)} %get-tuple-element.25.tiles, bf16[512,768]{1,0:T(8,128)(2,1)S(1)} %get-tuple-element.30.own, ...), custom_call_target="tpu_custom_call" | custom-call | flops 805306368 | bytes 1048576 | tf_op jit(solution)/shard_map/pallas_call | solution.py:62
  6.0 5.6 %collective-permute-done.lent = bf16[512,256]{1,0:T(8,128)(2,1)S(1)} collective-permute-done((bf16[512,256]{1,0:T(8,128)(2,1)S(1)}, bf16[512,256]{1,0:T(8,128)(2,1)S(1)}, u32[]{:S(2)}, u32[]{:S(2)}) %collective-permute-start) | collective-permute-done | bytes 262176 | tf_op jit(solution)/shard_map/ppermute | solution.py:23
  11.6 0.5 %shard_map.57 = (bf16[256,512]{1,0:T(8,128)(2,1)S(1)}, f32[256,768]{1,0:T(8,128)S(1)}) custom-call(bf16[512,256]{1,0:T(8,128)(2,1)S(1)} %get-tuple-element.28.kept, bf16[512,256]{1,0:T(8,128)(2,1)S(1)} %collective-permute-done.lent, bf16[512,768]{1,0:T(8,128)(2,1)S(1)} %get-tuple-element.31.miss, f32[1,768]{1,0:T(1,128)S(1)} %get-tuple-element.32.stays), custom_call_target="tpu_custom_call" | custom-call | flops 201326592 | bytes 1048576 | tf_op jit(solution)/shard_map/pallas_call | solution.py:62
  12.1 1.9 %collective-permute-start.6 = (bf16[512,512]{1,0:T(8,128)(2,1)S(1)}, bf16[512,512]{1,0:T(8,128)(2,1)S(1)}, u32[]{:S(2)}, u32[]{:S(2)}) collective-permute-start(bf16[512,512]{1,0:T(8,128)(2,1)S(1)} %get-tuple-element.42), channel_id=1, source_target_pairs={{2,4},{3,5},{4,2},{5,3},{10,12},{11,13},{12,10},{13,11},{18,20},{1... | collective-permute-start | bytes 1572872 | tf_op jit(solution)/shard_map/ppermute | solution.py:23
  14.1 3.6 %collective-permute-start.2 = (bf16[512,256]{1,0:T(8,128)(2,1)S(1)}, bf16[512,256]{1,0:T(8,128)(2,1)S(1)}, u32[]{:S(2)}, u32[]{:S(2)}) collective-permute-start(bf16[512,256]{1,0:T(8,128)(2,1)S(1)} %get-tuple-element.34), channel_id=1, source_target_pairs={{2,4},{3,5},{4,2},{5,3},{10,12},{11,13},{12,10},{13,11},{18,20},{1... | collective-permute-start | bytes 786440 | tf_op jit(solution)/shard_map/ppermute | solution.py:23
  17.7 0.0 collective-permute-done.4.far
  17.8 0.7 %collective-permute-start.5 = (bf16[256,768]{1,0:T(8,128)(2,1)S(1)}, bf16[256,768]{1,0:T(8,128)(2,1)S(1)}, u32[]{:S(2)}, u32[]{:S(2)}) collective-permute-start(bf16[256,768]{1,0:T(8,128)(2,1)S(1)} %get-tuple-element.41), channel_id=1, source_target_pairs={{0,1},{1,0},{6,7},{7,6},{8,9},{9,8},{14,15},{15,14},{16,17},{17,16... | collective-permute-start | bytes 1179656 | tf_op jit(solution)/shard_map/ppermute | solution.py:23
  18.4 4.2 %collective-permute-done.6.far = bf16[512,512]{1,0:T(8,128)(2,1)S(1)} collective-permute-done((bf16[512,512]{1,0:T(8,128)(2,1)S(1)}, bf16[512,512]{1,0:T(8,128)(2,1)S(1)}, u32[]{:S(2)}, u32[]{:S(2)}) %collective-permute-start.6) | collective-permute-done | bytes 524320 | tf_op jit(solution)/shard_map/ppermute | solution.py:23
  22.6 0.6 %shard_map.60 = (f32[256,512]{1,0:T(8,128)S(1)}, bf16[256,512]{1,0:T(8,128)(2,1)S(1)}) custom-call(bf16[3,512,512]{2,1,0:T(8,128)(2,1)S(1)} %get-tuple-element.25.tiles, bf16[512,512]{1,0:T(8,128)(2,1)S(1)} %collective-permute-done.6.far, f32[512,768]{1,0:T(8,128)S(1)} %get-tuple-element.35.hit, bf16[256,512]{1,0:T(8,128)(2,1)S(1)} %get-tuple-element.36.hit_turned, ...), custom_call_target="tpu_custom_call" | custom-call | flops 536870912 | bytes 1048576 | tf_op jit(solution)/shard_map/pallas_call | solution.py:62
  23.3 3.4 %collective-permute-start.7 = (bf16[256,512]{1,0:T(8,128)(2,1)S(1)}, bf16[256,512]{1,0:T(8,128)(2,1)S(1)}, u32[]{:S(2)}, u32[]{:S(2)}) collective-permute-start(bf16[256,512]{1,0:T(8,128)(2,1)S(1)} %get-tuple-element.44), channel_id=1, source_target_pairs={{2,3},{3,2},{4,5},{5,4},{10,11},{11,10},{12,13},{13,12},{18,19},{1... | collective-permute-start | bytes 786440 | tf_op jit(solution)/shard_map/ppermute | solution.py:23
  26.7 0.0 collective-permute-done.2.far
  26.7 0.6 %shard_map.58 = (f32[256,256]{1,0:T(8,128)S(1)}, bf16[256,256]{1,0:T(8,128)(2,1)S(1)}) custom-call(bf16[3,512,512]{2,1,0:T(8,128)(2,1)S(1)} %get-tuple-element.25.tiles, bf16[512,256]{1,0:T(8,128)(2,1)S(1)} %collective-permute-done.2.far, f32[512,768]{1,0:T(8,128)S(1)} %get-tuple-element.35.hit, bf16[256,512]{1,0:T(8,128)(2,1)S(1)} %get-tuple-element.36.hit_turned, ...), custom_call_target="tpu_custom_call" | custom-call | flops 268435456 | bytes 1048576 | tf_op jit(solution)/shard_map/pallas_call | solution.py:62
  27.3 2.4 %collective-permute-start.3 = (bf16[256,256]{1,0:T(8,128)(2,1)S(1)}, bf16[256,256]{1,0:T(8,128)(2,1)S(1)}, u32[]{:S(2)}, u32[]{:S(2)}) collective-permute-start(bf16[256,256]{1,0:T(8,128)(2,1)S(1)} %get-tuple-element.39), channel_id=1, source_target_pairs={{2,3},{3,2},{4,5},{5,4},{10,11},{11,10},{12,13},{13,12},{18,19},{1... | collective-permute-start | bytes 393224 | tf_op jit(solution)/shard_map/ppermute | solution.py:23
  29.7 1.8 %collective-permute-done.7.received = bf16[256,512]{1,0:T(8,128)(2,1)S(1)} collective-permute-done((bf16[256,512]{1,0:T(8,128)(2,1)S(1)}, bf16[256,512]{1,0:T(8,128)(2,1)S(1)}, u32[]{:S(2)}, u32[]{:S(2)}) %collective-permute-start.7) | collective-permute-done | bytes 262176 | tf_op jit(solution)/shard_map/ppermute | solution.py:23
  31.5 0.8 %shard_map.61.begun = f32[256,768]{1,0:T(8,128)} custom-call(f32[256,512]{1,0:T(8,128)S(1)} %get-tuple-element.43.kept, bf16[256,512]{1,0:T(8,128)(2,1)S(1)} %collective-permute-done.7.received), custom_call_target="tpu_custom_call" | custom-call | flops 65536 | bytes 1048576 | tf_op jit(solution)/shard_map/pallas_call | solution.py:62
  32.4 1.8 %collective-permute-done.3.received = bf16[256,256]{1,0:T(8,128)(2,1)S(1)} collective-permute-done((bf16[256,256]{1,0:T(8,128)(2,1)S(1)}, bf16[256,256]{1,0:T(8,128)(2,1)S(1)}, u32[]{:S(2)}, u32[]{:S(2)}) %collective-permute-start.3) | collective-permute-done | bytes 131104 | tf_op jit(solution)/shard_map/ppermute | solution.py:23
  34.2 0.0 collective-permute-done.5.all_received
  34.2 0.7 %shard_map.62 = f32[256,768]{1,0:T(8,128)} custom-call(f32[256,256]{1,0:T(8,128)S(1)} %get-tuple-element.38.kept, bf16[256,256]{1,0:T(8,128)(2,1)S(1)} %collective-permute-done.3.received, f32[256,768]{1,0:T(8,128)S(1)} %get-tuple-element.40.all_kept, bf16[256,768]{1,0:T(8,128)(2,1)S(1)} %collective-permute-done.5.all_received, ...), custom_call_target="tpu_custom_call", output_to_operand_aliasing={{}: (4, {})} | custom-call | flops 65536 | bytes 1048576 | tf_op jit(solution)/shard_map/pallas_call | solution.py:62
  (1 shorter events, 0.0 us)
Async XLA Ops:
  0.0 4.5 %copy-start = (s32[1,1,3,1]{2,3,1,0:T(1,128)S(1)}, s32[1,1,3,1]{2,3,1,0:T(1,128)}, u32[]{:S(2)}) copy-start(s32[1,1,3,1]{2,3,1,0:T(1,128)} %param.7) | copy-start | bytes 40
  0.0 4.5 %copy-start.1 = (s32[1,1,2]{2,1,0:T(1,128)S(1)}, s32[1,1,2]{2,1,0:T(1,128)}, u32[]{:S(2)}) copy-start(s32[1,1,2]{2,1,0:T(1,128)} %param.8) | copy-start | bytes 28
  0.0 4.5 %collective-permute-start.1 = (bf16[512,768]{1,0:T(8,128)(2,1)}, bf16[512,768]{1,0:T(8,128)(2,1)S(1)}, u32[]{:S(2)}, u32[]{:S(2)}) collective-permute-start(bf16[512,768]{1,0:T(8,128)(2,1)} %sketch.1), channel_id=1, source_target_pairs={{0,2},{1,3},{2,0},{3,1},{4,6},{5,7},{6,4},{7,5},{8,10},{9,11},{10,... | collective-permute-start | bytes 2359304 | tf_op jit(solution)/shard_map/ppermute | solution.py:23
  0.0 17.7 %collective-permute-start.4 = (bf16[512,768]{1,0:T(8,128)(2,1)}, bf16[512,768]{1,0:T(8,128)(2,1)S(1)}, u32[]{:S(2)}, u32[]{:S(2)}) collective-permute-start(bf16[512,768]{1,0:T(8,128)(2,1)} %sketch.1), channel_id=1, source_target_pairs={{0,30},{1,31},{6,8},{7,9},{8,6},{9,7},{14,16},{15,17},{16,14},{17,... | collective-permute-start | bytes 2359304 | tf_op jit(solution)/shard_map/ppermute | solution.py:23
  2.9 8.7 %collective-permute-start = (bf16[512,256]{1,0:T(8,128)(2,1)S(1)}, bf16[512,256]{1,0:T(8,128)(2,1)S(1)}, u32[]{:S(2)}, u32[]{:S(2)}) collective-permute-start(bf16[512,256]{1,0:T(8,128)(2,1)S(1)} %get-tuple-element.29), channel_id=1, source_target_pairs={{0,1},{1,0},{2,3},{3,2},{4,5},{5,4},{6,7},{7,6},{8,9},{9,8},{10,11... | collective-permute-start | bytes 786440 | tf_op jit(solution)/shard_map/ppermute | solution.py:23
  12.1 10.5 %collective-permute-start.6 = (bf16[512,512]{1,0:T(8,128)(2,1)S(1)}, bf16[512,512]{1,0:T(8,128)(2,1)S(1)}, u32[]{:S(2)}, u32[]{:S(2)}) collective-permute-start(bf16[512,512]{1,0:T(8,128)(2,1)S(1)} %get-tuple-element.42), channel_id=1, source_target_pairs={{2,4},{3,5},{4,2},{5,3},{10,12},{11,13},{12,10},{13,11},{18,20},{1... | collective-permute-start | bytes 1572872 | tf_op jit(solution)/shard_map/ppermute | solution.py:23
  14.1 12.7 %collective-permute-start.2 = (bf16[512,256]{1,0:T(8,128)(2,1)S(1)}, bf16[512,256]{1,0:T(8,128)(2,1)S(1)}, u32[]{:S(2)}, u32[]{:S(2)}) collective-permute-start(bf16[512,256]{1,0:T(8,128)(2,1)S(1)} %get-tuple-element.34), channel_id=1, source_target_pairs={{2,4},{3,5},{4,2},{5,3},{10,12},{11,13},{12,10},{13,11},{18,20},{1... | collective-permute-start | bytes 786440 | tf_op jit(solution)/shard_map/ppermute | solution.py:23
  17.8 16.4 %collective-permute-start.5 = (bf16[256,768]{1,0:T(8,128)(2,1)S(1)}, bf16[256,768]{1,0:T(8,128)(2,1)S(1)}, u32[]{:S(2)}, u32[]{:S(2)}) collective-permute-start(bf16[256,768]{1,0:T(8,128)(2,1)S(1)} %get-tuple-element.41), channel_id=1, source_target_pairs={{0,1},{1,0},{6,7},{7,6},{8,9},{9,8},{14,15},{15,14},{16,17},{17,16... | collective-permute-start | bytes 1179656 | tf_op jit(solution)/shard_map/ppermute | solution.py:23
  23.3 8.3 %collective-permute-start.7 = (bf16[256,512]{1,0:T(8,128)(2,1)S(1)}, bf16[256,512]{1,0:T(8,128)(2,1)S(1)}, u32[]{:S(2)}, u32[]{:S(2)}) collective-permute-start(bf16[256,512]{1,0:T(8,128)(2,1)S(1)} %get-tuple-element.44), channel_id=1, source_target_pairs={{2,3},{3,2},{4,5},{5,4},{10,11},{11,10},{12,13},{13,12},{18,19},{1... | collective-permute-start | bytes 786440 | tf_op jit(solution)/shard_map/ppermute | solution.py:23
  27.3 6.9 %collective-permute-start.3 = (bf16[256,256]{1,0:T(8,128)(2,1)S(1)}, bf16[256,256]{1,0:T(8,128)(2,1)S(1)}, u32[]{:S(2)}, u32[]{:S(2)}) collective-permute-start(bf16[256,256]{1,0:T(8,128)(2,1)S(1)} %get-tuple-element.39), channel_id=1, source_target_pairs={{2,3},{3,2},{4,5},{5,4},{10,11},{11,10},{12,13},{13,12},{18,19},{1... | collective-permute-start | bytes 393224 | tf_op jit(solution)/shard_map/ppermute | solution.py:23

commit v6 on v4

--- a/solution.py
+++ b/solution.py
@@ -67,13 +67,21 @@
     copy_all([(sketch.at[:, pl.ds(0, first.shape[1])], first)], sems)
 
 
-def stage_kernel(sketch, tiles, basis, lent, own, staged, kept, sems):
+def stage_kernel(sketch, tiles, basis, second, lent, own, staged, kept, sems):
     half = lent.shape[0]
     group = lax.axis_index("group")
     ours, theirs = (
         basis.at[0, 0, pl.ds(pl.multiple_of(g * half, half), half)] for g in (group, 1 - group)
     )
-    copy_all([(theirs, lent), (sketch, own), (tiles.at[0, 0, :, 0], staged), (ours, kept)], sems)
+    width = second.shape[1]
+    pairs = [
+        (sketch.at[:, pl.ds(sketch.shape[1] - width, width)], second),
+        (theirs, lent),
+        (sketch, own),
+        (tiles.at[0, 0, :, 0], staged),
+        (ours, kept),
+    ]
+    copy_all(pairs, sems)
 
 
 def local_kernel(row_blocks, owner_route, tiles, own, near, hit, miss, stays):
@@ -93,14 +101,13 @@
     stays[...] = jnp.full(stays.shape, jnp.where(owner == lax.axis_index("group"), 1.0, 0.0))
 
 
-def turn_kernel(kept, lent, miss, own, stays, hit_turned, missed, second):
+def turn_kernel(kept, lent, miss, stays, hit_turned, missed):
     stay = stays[:, pl.ds(0, kept.shape[0])] > 0.0
     ours, theirs = kept[...].T, lent[...].T
     hit_turned[...] = jnp.where(stay, ours, theirs)
     missed[...] = jnp.dot(
         jnp.where(stay, theirs, ours), miss[...], preferred_element_type=jnp.float32
     )
-    second[...] = own[:, pl.ds(own.shape[1] - second.shape[1], second.shape[1])]
 
 
 def far_kernel(start, tiles, far, hit, hit_turned, missed, stays, kept, sent):
@@ -132,10 +139,10 @@
         cut_kernel, on_chip((panels, early), short), (), 0, hbm=(sketch,), scratch=(copies((1,)),)
     )
     far_first = swap_far(first)
-    near = swap_near(sketch)
-    lent, own, tiles, kept = call(
+    second, lent, own, tiles, kept = call(
         stage_kernel,
         (
+            on_chip((panels, columns - early), short),
             on_chip((half, rank), short),
             on_chip((panels, columns), short),
             on_chip((offsets, rows, panels), short),
@@ -144,9 +151,11 @@
         (),
         0,
         hbm=(sketch, far_tiles, cluster_basis),
-        scratch=(copies((4,)),),
-    )
+        scratch=(copies((5,)),),
+    )
+    far_second = swap_far(second)
     lent = from_behind(lent, "group", 1)
+    near = swap_near(own)
     hit, miss, stays = call(
         local_kernel,
         (
@@ -158,17 +167,12 @@
         2 * product,
         scalars=(row_blocks.reshape(-1), owner_route.reshape(-1)),
     )
-    hit_turned, missed, second = call(
+    hit_turned, missed = call(
         turn_kernel,
-        (
-            on_chip((rank, half), short),
-            on_chip((rank, columns), wide),
-            on_chip((panels, columns - early), short),
-        ),
-        (kept, lent, miss, own, stays),
+        (on_chip((rank, half), short), on_chip((rank, columns), wide)),
+        (kept, lent, miss, stays),
         product // 2,
     )
-    far_second = swap_far(second)
     out = None
     for start, far in ((0, far_first), (early, far_second)):
         width = far.shape[1]

time: 31 us -> 30 us (0.968)
  the two profiles are of different devices: /device:TPU:0 before, /device:TPU:1 now
where the time goes in v6:
time: 30 us; the launch traced here: 29.8 us
  waiting for transfers between devices  13.5 us (45%)
  starting transfers between devices  8.47 us (28%)
  Pallas kernels  7.74 us (26%)
    ppermute x2, waiting for transfers between devices, swap_far(): lax.ppermute(array, 'blk', [(i, (i + 1 if i % 2 else i - 1) % devices) fo...  9.78 us
    pallas_call x8, Pallas kernels, call(): pl.pallas_call(kernel, out_shape=out_shape, in_specs=[scalar] * len(scala...  7.74 us
    ppermute x3, starting transfers between devices, from_behind(): lax.ppermute(array, axis, [(i, (i + by) % devices) for i in range(devices)])  4.81 us
    ppermute x3, waiting for transfers between devices, from_behind(): lax.ppermute(array, axis, [(i, (i + by) % devices) for i in range(devices)])  3.72 us
    ppermute x2, starting transfers between devices, swap_far(): lax.ppermute(array, 'blk', [(i, (i + 1 if i % 2 else i - 1) % devices) fo...  3.54 us
  transfers between devices with their start and end apart: 6, of which 5 were waited for; matrix products, arithmetic and copies ran while one was open for 0% of the time, Pallas kernels for 17%

profile of v6, /device:TPU:1, one launch (start us, length us, event | category | flops | bytes accessed | tf_op | source)
XLA Modules:
  0.0 29.8 jit_solution(4268379356564463188)
XLA Ops:
  0.0 0.0 copy-start
  0.0 0.0 copy-start.1
  0.0 1.9 %shard_map.55 = (bf16[512,256]{1,0:T(8,128)(2,1)S(1)}, bf16[512,256]{1,0:T(8,128)(2,1)S(1)}, bf16[512,768]{1,0:T(8,128)(2,1)S(1)}, bf16[3,512,512]{2,1,0:T(8,128)(2,1)S(1)}, bf16[512,256]{1,0:T(8,128)(2,1)S(1)}) custom-call(bf16[512,768]{1,0:T(8,128)(2,1)} %sketch.3, bf16[1,1,3,1,512,512]{5,4,3,2,1,0:T(8,128)(2,1)} %tiles.1, bf16[1,1,1024,256]{3,2,1,0:T(8,128)(2,1)} %basis.1), custom_call_target="tpu_custom_call" | custom-call | bytes 1048576 | tf_op jit(solution)/shard_map/pallas_call | solution.py:42
  1.9 0.1 collective-permute-start.1
  2.0 1.0 %shard_map.59 = bf16[512,512]{1,0:T(8,128)(2,1)S(1)} custom-call(bf16[512,768]{1,0:T(8,128)(2,1)} %sketch.3), custom_call_target="tpu_custom_call" | custom-call | bytes 1048576 | tf_op jit(solution)/shard_map/pallas_call | solution.py:42
  3.1 2.6 %collective-permute-start.4 = (bf16[512,512]{1,0:T(8,128)(2,1)S(1)}, bf16[512,512]{1,0:T(8,128)(2,1)S(1)}, u32[]{:S(2)}, u32[]{:S(2)}) collective-permute-start(bf16[512,512]{1,0:T(8,128)(2,1)S(1)} %shard_map.59), channel_id=1, source_target_pairs={{0,30},{2,4},{4,2},{6,8},{8,6},{10,12},{12,10},{14,16},{16,14},{18... | collective-permute-start | bytes 1572872 | tf_op jit(solution)/shard_map/ppermute | solution.py:25
  5.7 1.2 %collective-permute-start.2 = (bf16[512,256]{1,0:T(8,128)(2,1)S(1)}, bf16[512,256]{1,0:T(8,128)(2,1)S(1)}, u32[]{:S(2)}, u32[]{:S(2)}) collective-permute-start(bf16[512,256]{1,0:T(8,128)(2,1)S(1)} %get-tuple-element.24), channel_id=1, source_target_pairs={{0,1},{1,0},{2,3},{3,2},{4,5},{5,4},{6,7},{7,6},{8,9},{9,8},{10,11... | collective-permute-start | bytes 786440 | tf_op jit(solution)/shard_map/ppermute | solution.py:15
  7.0 0.9 %collective-permute-start = (bf16[512,256]{1,0:T(8,128)(2,1)S(1)}, bf16[512,256]{1,0:T(8,128)(2,1)S(1)}, u32[]{:S(2)}, u32[]{:S(2)}) collective-permute-start(bf16[512,256]{1,0:T(8,128)(2,1)S(1)} %get-tuple-element.20), channel_id=1, source_target_pairs={{0,30},{2,4},{4,2},{6,8},{8,6},{10,12},{12,10},{14,16},{16,14},{18... | collective-permute-start | bytes 786440 | tf_op jit(solution)/shard_map/ppermute | solution.py:25
  7.9 0.0 collective-permute-done.1.near
  7.9 0.0 copy-done
  7.9 0.0 copy-done.1
  7.9 1.5 %shard_map.56 = (f32[512,768]{1,0:T(8,128)S(1)}, bf16[512,768]{1,0:T(8,128)(2,1)S(1)}, f32[1,768]{1,0:T(1,128)S(1)}) custom-call(s32[3]{0:T(128)S(1)} %bitcast.3, s32[2]{0:T(128)S(1)} %bitcast.4, bf16[3,512,512]{2,1,0:T(8,128)(2,1)S(1)} %get-tuple-element.19.tiles, bf16[512,768]{1,0:T(8,128)(2,1)S(1)} %get-tuple-element.21.own, ...), custom_call_target="tpu_custom_call" | custom-call | flops 805306368 | bytes 1048576 | tf_op jit(solution)/shard_map/pallas_call | solution.py:42
  9.4 1.8 %collective-permute-done.2.lent = bf16[512,256]{1,0:T(8,128)(2,1)S(1)} collective-permute-done((bf16[512,256]{1,0:T(8,128)(2,1)S(1)}, bf16[512,256]{1,0:T(8,128)(2,1)S(1)}, u32[]{:S(2)}, u32[]{:S(2)}) %collective-permute-start.2) | collective-permute-done | bytes 262176 | tf_op jit(solution)/shard_map/ppermute | solution.py:15
  11.2 0.5 %shard_map.57 = (bf16[256,512]{1,0:T(8,128)(2,1)S(1)}, f32[256,768]{1,0:T(8,128)S(1)}) custom-call(bf16[512,256]{1,0:T(8,128)(2,1)S(1)} %get-tuple-element.23.kept, bf16[512,256]{1,0:T(8,128)(2,1)S(1)} %collective-permute-done.2.lent, bf16[512,768]{1,0:T(8,128)(2,1)S(1)} %get-tuple-element.25.miss, f32[1,768]{1,0:T(1,128)S(1)} %get-tuple-element.26.stays), custom_call_target="tpu_custom_call" | custom-call | flops 201326592 | bytes 1048576 | tf_op jit(solution)/shard_map/pallas_call | solution.py:42
  11.7 9.6 %collective-permute-done.4.far = bf16[512,512]{1,0:T(8,128)(2,1)S(1)} collective-permute-done((bf16[512,512]{1,0:T(8,128)(2,1)S(1)}, bf16[512,512]{1,0:T(8,128)(2,1)S(1)}, u32[]{:S(2)}, u32[]{:S(2)}) %collective-permute-start.4) | collective-permute-done | bytes 524320 | tf_op jit(solution)/shard_map/ppermute | solution.py:25
  21.3 0.6 %shard_map.60 = (f32[256,512]{1,0:T(8,128)S(1)}, bf16[256,512]{1,0:T(8,128)(2,1)S(1)}) custom-call(bf16[3,512,512]{2,1,0:T(8,128)(2,1)S(1)} %get-tuple-element.19.tiles, bf16[512,512]{1,0:T(8,128)(2,1)S(1)} %collective-permute-done.4.far, f32[512,768]{1,0:T(8,128)S(1)} %get-tuple-element.22.hit, bf16[256,512]{1,0:T(8,128)(2,1)S(1)} %get-tuple-element.27.hit_turned, ...), custom_call_target="tpu_custom_call" | custom-call | flops 536870912 | bytes 1048576 | tf_op jit(solution)/shard_map/pallas_call | solution.py:42
  22.0 1.9 %collective-permute-start.5 = (bf16[256,512]{1,0:T(8,128)(2,1)S(1)}, bf16[256,512]{1,0:T(8,128)(2,1)S(1)}, u32[]{:S(2)}, u32[]{:S(2)}) collective-permute-start(bf16[256,512]{1,0:T(8,128)(2,1)S(1)} %get-tuple-element.32), channel_id=1, source_target_pairs={{0,1},{1,0},{2,3},{3,2},{4,5},{5,4},{6,7},{7,6},{8,9},{9,8},{10,11... | collective-permute-start | bytes 786440 | tf_op jit(solution)/shard_map/ppermute | solution.py:15
  23.9 0.2 collective-permute-done.far
  24.1 0.6 %shard_map.58 = (f32[256,256]{1,0:T(8,128)S(1)}, bf16[256,256]{1,0:T(8,128)(2,1)S(1)}) custom-call(bf16[3,512,512]{2,1,0:T(8,128)(2,1)S(1)} %get-tuple-element.19.tiles, bf16[512,256]{1,0:T(8,128)(2,1)S(1)} %collective-permute-done.far, f32[512,768]{1,0:T(8,128)S(1)} %get-tuple-element.22.hit, bf16[256,512]{1,0:T(8,128)(2,1)S(1)} %get-tuple-element.27.hit_turned, ...), custom_call_target="tpu_custom_call" | custom-call | flops 268435456 | bytes 1048576 | tf_op jit(solution)/shard_map/pallas_call | solution.py:42
  24.7 1.6 %collective-permute-start.3 = (bf16[256,256]{1,0:T(8,128)(2,1)S(1)}, bf16[256,256]{1,0:T(8,128)(2,1)S(1)}, u32[]{:S(2)}, u32[]{:S(2)}) collective-permute-start(bf16[256,256]{1,0:T(8,128)(2,1)S(1)} %get-tuple-element.30), channel_id=1, source_target_pairs={{0,1},{1,0},{2,3},{3,2},{4,5},{5,4},{6,7},{7,6},{8,9},{9,8},{10,11... | collective-permute-start | bytes 393224 | tf_op jit(solution)/shard_map/ppermute | solution.py:15
  26.3 1.3 %collective-permute-done.5.received = bf16[256,512]{1,0:T(8,128)(2,1)S(1)} collective-permute-done((bf16[256,512]{1,0:T(8,128)(2,1)S(1)}, bf16[256,512]{1,0:T(8,128)(2,1)S(1)}, u32[]{:S(2)}, u32[]{:S(2)}) %collective-permute-start.5) | collective-permute-done | bytes 262176 | tf_op jit(solution)/shard_map/ppermute | solution.py:15
  27.7 0.8 %shard_map.61.rest_0_ = f32[256,768]{1,0:T(8,128)} custom-call(f32[256,512]{1,0:T(8,128)S(1)} %get-tuple-element.31.kept, bf16[256,512]{1,0:T(8,128)(2,1)S(1)} %collective-permute-done.5.received), custom_call_target="tpu_custom_call" | custom-call | flops 65536 | bytes 1048576 | tf_op jit(solution)/shard_map/pallas_call | solution.py:42
  28.5 0.6 %collective-permute-done.3.received = bf16[256,256]{1,0:T(8,128)(2,1)S(1)} collective-permute-done((bf16[256,256]{1,0:T(8,128)(2,1)S(1)}, bf16[256,256]{1,0:T(8,128)(2,1)S(1)}, u32[]{:S(2)}, u32[]{:S(2)}) %collective-permute-start.3) | collective-permute-done | bytes 131104 | tf_op jit(solution)/shard_map/ppermute | solution.py:15
  29.1 0.7 %shard_map.62 = f32[256,768]{1,0:T(8,128)} custom-call(f32[256,256]{1,0:T(8,128)S(1)} %get-tuple-element.29.kept, bf16[256,256]{1,0:T(8,128)(2,1)S(1)} %collective-permute-done.3.received, f32[256,768]{1,0:T(8,128)} %shard_map.61.rest_0_), custom_call_target="tpu_custom_call", output_to_operand_aliasing={{}: (2, {})} | custom-call | flops 65536 | bytes 1048576 | tf_op jit(solution)/shard_map/pallas_call | solution.py:42
Async XLA Ops:
  0.0 7.9 %copy-start = (s32[1,1,3,1]{2,3,1,0:T(1,128)S(1)}, s32[1,1,3,1]{2,3,1,0:T(1,128)}, u32[]{:S(2)}) copy-start(s32[1,1,3,1]{2,3,1,0:T(1,128)} %param.7) | copy-start | bytes 40
  0.0 7.9 %copy-start.1 = (s32[1,1,2]{2,1,0:T(1,128)S(1)}, s32[1,1,2]{2,1,0:T(1,128)}, u32[]{:S(2)}) copy-start(s32[1,1,2]{2,1,0:T(1,128)} %param.8) | copy-start | bytes 28
  1.9 6.0 %collective-permute-start.1 = (bf16[512,768]{1,0:T(8,128)(2,1)S(1)}, bf16[512,768]{1,0:T(8,128)(2,1)S(1)}, u32[]{:S(2)}, u32[]{:S(2)}) collective-permute-start(bf16[512,768]{1,0:T(8,128)(2,1)S(1)} %get-tuple-element.21.own), channel_id=1, source_target_pairs={{0,2},{2,0},{4,6},{6,4},{8,10},{10,8},{12,14},{14,12},{16,18},{18,... | collective-permute-start | bytes 2359304 | tf_op jit(solution)/shard_map/ppermute | solution.py:20
  3.1 18.2 %collective-permute-start.4 = (bf16[512,512]{1,0:T(8,128)(2,1)S(1)}, bf16[512,512]{1,0:T(8,128)(2,1)S(1)}, u32[]{:S(2)}, u32[]{:S(2)}) collective-permute-start(bf16[512,512]{1,0:T(8,128)(2,1)S(1)} %shard_map.59), channel_id=1, source_target_pairs={{0,30},{2,4},{4,2},{6,8},{8,6},{10,12},{12,10},{14,16},{16,14},{18... | collective-permute-start | bytes 1572872 | tf_op jit(solution)/shard_map/ppermute | solution.py:25
  5.7 5.5 %collective-permute-start.2 = (bf16[512,256]{1,0:T(8,128)(2,1)S(1)}, bf16[512,256]{1,0:T(8,128)(2,1)S(1)}, u32[]{:S(2)}, u32[]{:S(2)}) collective-permute-start(bf16[512,256]{1,0:T(8,128)(2,1)S(1)} %get-tuple-element.24), channel_id=1, source_target_pairs={{0,1},{1,0},{2,3},{3,2},{4,5},{5,4},{6,7},{7,6},{8,9},{9,8},{10,11... | collective-permute-start | bytes 786440 | tf_op jit(solution)/shard_map/ppermute | solution.py:15
  7.0 17.2 %collective-permute-start = (bf16[512,256]{1,0:T(8,128)(2,1)S(1)}, bf16[512,256]{1,0:T(8,128)(2,1)S(1)}, u32[]{:S(2)}, u32[]{:S(2)}) collective-permute-start(bf16[512,256]{1,0:T(8,128)(2,1)S(1)} %get-tuple-element.20), channel_id=1, source_target_pairs={{0,30},{2,4},{4,2},{6,8},{8,6},{10,12},{12,10},{14,16},{16,14},{18... | collective-permute-start | bytes 786440 | tf_op jit(solution)/shard_map/ppermute | solution.py:25
  22.0 5.7 %collective-permute-start.5 = (bf16[256,512]{1,0:T(8,128)(2,1)S(1)}, bf16[256,512]{1,0:T(8,128)(2,1)S(1)}, u32[]{:S(2)}, u32[]{:S(2)}) collective-permute-start(bf16[256,512]{1,0:T(8,128)(2,1)S(1)} %get-tuple-element.32), channel_id=1, source_target_pairs={{0,1},{1,0},{2,3},{3,2},{4,5},{5,4},{6,7},{7,6},{8,9},{9,8},{10,11... | collective-permute-start | bytes 786440 | tf_op jit(solution)/shard_map/ppermute | solution.py:15
  24.7 4.4 %collective-permute-start.3 = (bf16[256,256]{1,0:T(8,128)(2,1)S(1)}, bf16[256,256]{1,0:T(8,128)(2,1)S(1)}, u32[]{:S(2)}, u32[]{:S(2)}) collective-permute-start(bf16[256,256]{1,0:T(8,128)(2,1)S(1)} %get-tuple-element.30), channel_id=1, source_target_pairs={{0,1},{1,0},{2,3},{3,2},{4,5},{5,4},{6,7},{7,6},{8,9},{9,8},{10,11... | collective-permute-start | bytes 393224 | tf_op jit(solution)/shard_map/ppermute | solution.py:15

commit v7 on v6

--- a/solution.py
+++ b/solution.py
@@ -7,6 +7,7 @@
 from jax.experimental.pallas import tpu as pltpu
 from jax.sharding import PartitionSpec as P
 
+SHARES = (3, 2, 1)
 TRANSPOSED = (((0,), (0,)), ((), ()))
 
 
@@ -63,25 +64,25 @@
         copy.wait()
 
 
-def cut_kernel(sketch, first, sems):
-    copy_all([(sketch.at[:, pl.ds(0, first.shape[1])], first)], sems)
-
-
-def stage_kernel(sketch, tiles, basis, second, lent, own, staged, kept, sems):
-    half = lent.shape[0]
-    group = lax.axis_index("group")
-    ours, theirs = (
-        basis.at[0, 0, pl.ds(pl.multiple_of(g * half, half), half)] for g in (group, 1 - group)
-    )
-    width = second.shape[1]
-    pairs = [
-        (sketch.at[:, pl.ds(sketch.shape[1] - width, width)], second),
-        (theirs, lent),
-        (sketch, own),
-        (tiles.at[0, 0, :, 0], staged),
-        (ours, kept),
-    ]
-    copy_all(pairs, sems)
+def half_rows(basis, group, half):
+    return basis.at[0, 0, pl.ds(pl.multiple_of(group * half, half), half)]
+
+
+def cut_kernel(sketch, basis, first, lent, sems):
+    theirs = half_rows(basis, 1 - lax.axis_index("group"), lent.shape[0])
+    copy_all([(sketch.at[:, pl.ds(0, first.shape[1])], first), (theirs, lent)], sems)
+
+
+def stage_kernel(begun, sketch, tiles, basis, *outs):
+    del begun
+    *parts, own, staged, kept, sems = outs
+    ours = half_rows(basis, lax.axis_index("group"), kept.shape[0])
+    pairs = []
+    end = sketch.shape[1]
+    for part in reversed(parts):
+        end -= part.shape[1]
+        pairs.insert(0, (sketch.at[:, pl.ds(end, part.shape[1])], part))
+    copy_all([*pairs, (sketch, own), (tiles.at[0, 0, :, 0], staged), (ours, kept)], sems)
 
 
 def local_kernel(row_blocks, owner_route, tiles, own, near, hit, miss, stays):
@@ -131,30 +132,34 @@
     panels, columns = sketch.shape
     offsets, rows = far_tiles.shape[2], far_tiles.shape[4]
     half, rank = cluster_basis.shape[2] // 2, cluster_basis.shape[3]
-    early = 2 * columns // 3
+    widths = [columns * share // sum(SHARES) for share in SHARES]
+    starts = [sum(widths[:i]) for i in range(len(widths))]
     product = 2 * rows * panels * columns
     short, wide = sketch.dtype, jnp.float32
     copies = pltpu.SemaphoreType.DMA
-    first = call(
-        cut_kernel, on_chip((panels, early), short), (), 0, hbm=(sketch,), scratch=(copies((1,)),)
-    )
-    far_first = swap_far(first)
-    second, lent, own, tiles, kept = call(
+    first, lent = call(
+        cut_kernel,
+        (on_chip((panels, widths[0]), short), on_chip((half, rank), short)),
+        (),
+        0,
+        hbm=(sketch, cluster_basis),
+        scratch=(copies((2,)),),
+    )
+    *later, own, tiles, kept = call(
         stage_kernel,
         (
-            on_chip((panels, columns - early), short),
-            on_chip((half, rank), short),
+            *(on_chip((panels, width), short) for width in widths[1:]),
             on_chip((panels, columns), short),
             on_chip((offsets, rows, panels), short),
             on_chip((half, rank), short),
         ),
-        (),
+        (first,),
         0,
         hbm=(sketch, far_tiles, cluster_basis),
-        scratch=(copies((5,)),),
-    )
-    far_second = swap_far(second)
+        scratch=(copies((len(widths) + 2,)),),
+    )
     lent = from_behind(lent, "group", 1)
+    fars = [swap_far(part) for part in (first, *later)]
     near = swap_near(own)
     hit, miss, stays = call(
         local_kernel,
@@ -174,7 +179,7 @@
         product // 2,
     )
     out = None
-    for start, far in ((0, far_first), (early, far_second)):
+    for start, far in zip(starts, fars):
         width = far.shape[1]
         kept, sent = call(
             functools.partial(far_kernel, start),

time: 30 us -> 30.2 us (level)
  waiting for transfers between devices: 13.5 us -> 9.68 us
  starting transfers between devices: 8.47 us -> 11.3 us
  Pallas kernels: 7.74 us -> 8.87 us
    ppermute x2 -> x3, waiting for transfers between devices: 9.78 us -> 7.41 us  [swap_far(): lax.ppermute(array, 'blk', [(i, (i + 1 if i % 2 else i - 1) % devices) fo...]
    ppermute x3 -> x4, starting transfers between devices: 4.81 us -> 6.85 us  [from_behind(): lax.ppermute(array, axis, [(i, (i + by) % devices) for i in range(devices)])]
    ppermute x3 -> x4, waiting for transfers between devices: 3.72 us -> 2.26 us  [from_behind(): lax.ppermute(array, axis, [(i, (i + by) % devices) for i in range(devices)])]
    pallas_call x8 -> x10, Pallas kernels: 7.74 us -> 8.87 us  [call(): pl.pallas_call(kernel, out_shape=out_shape, in_specs=[scalar] * len(scala...]
    ppermute x2 -> x3, starting transfers between devices: 3.54 us -> 4.37 us  [swap_far(): lax.ppermute(array, 'blk', [(i, (i + 1 if i % 2 else i - 1) % devices) fo...]
  transfers between devices with their start and end apart: 6 -> 8, of which waited for: 5 -> 5; matrix products, arithmetic and copies ran while one was open for 0% -> 0% of each run, Pallas kernels for 17% -> 17%
where the time goes in v7:
time: 30.2 us; the launch traced here: 30 us
  starting transfers between devices  11.3 us (37%)
  waiting for transfers between devices  9.68 us (32%)
  Pallas kernels  8.87 us (29%)
    pallas_call x10, Pallas kernels, call(): pl.pallas_call(kernel, out_shape=out_shape, in_specs=[scalar] * len(scala...  8.87 us
    ppermute x3, waiting for transfers between devices, swap_far(): lax.ppermute(array, 'blk', [(i, (i + 1 if i % 2 else i - 1) % devices) fo...  7.41 us
    ppermute x4, starting transfers between devices, from_behind(): lax.ppermute(array, axis, [(i, (i + by) % devices) for i in range(devices)])  6.85 us
    ppermute x3, starting transfers between devices, swap_far(): lax.ppermute(array, 'blk', [(i, (i + 1 if i % 2 else i - 1) % devices) fo...  4.37 us
    ppermute x4, waiting for transfers between devices, from_behind(): lax.ppermute(array, axis, [(i, (i + by) % devices) for i in range(devices)])  2.26 us
  transfers between devices with their start and end apart: 8, of which 5 were waited for; matrix products, arithmetic and copies ran while one was open for 0% of the time, Pallas kernels for 17%

profile of v7, /device:TPU:1, one launch (start us, length us, event | category | flops | bytes accessed | tf_op | source)
XLA Modules:
  0.0 30.0 jit_solution(13741459597963449431)
XLA Ops:
  0.0 1.1 %shard_map.55 = (bf16[512,384]{1,0:T(8,128)(2,1)S(1)}, bf16[512,256]{1,0:T(8,128)(2,1)S(1)}) custom-call(bf16[512,768]{1,0:T(8,128)(2,1)} %sketch.3, bf16[1,1,1024,256]{3,2,1,0:T(8,128)(2,1)} %basis.3), custom_call_target="tpu_custom_call" | custom-call | bytes 1048576 | tf_op jit(solution)/shard_map/pallas_call | solution.py:43
  1.1 0.0 copy-start
  1.1 0.0 copy-start.1
  1.1 1.9 %shard_map.56 = (bf16[512,256]{1,0:T(8,128)(2,1)S(1)}, bf16[512,128]{1,0:T(8,128)(2,1)S(1)}, bf16[512,768]{1,0:T(8,128)(2,1)S(1)}, bf16[3,512,512]{2,1,0:T(8,128)(2,1)S(1)}, bf16[512,256]{1,0:T(8,128)(2,1)S(1)}) custom-call(bf16[512,384]{1,0:T(8,128)(2,1)S(1)} %get-tuple-element.23.begun, bf16[512,768]{1,0:T(8,128)(2,1)} %sketch.3, ...), custom_call_target="tpu_custom_call" | custom-call | bytes 1048576 | tf_op jit(solution)/shard_map/pallas_call | solution.py:43
  3.0 0.1 collective-permute-start.1
  3.1 2.6 %collective-permute-start.6 = (bf16[512,384]{1,0:T(8,128)(2,1)S(1)}, bf16[512,384]{1,0:T(8,128)(2,1)S(1)}, u32[]{:S(2)}, u32[]{:S(2)}) collective-permute-start(bf16[512,384]{1,0:T(8,128)(2,1)S(1)} %get-tuple-element.23.begun), channel_id=1, source_target_pairs={{0,30},{2,4},{4,2},{6,8},{8,6},{10,12},{12,10},{14,16},{16,14},{18... | collective-permute-start | bytes 1179656 | tf_op jit(solution)/shard_map/ppermute | solution.py:26
  5.7 1.2 %collective-permute-start.2 = (bf16[512,256]{1,0:T(8,128)(2,1)S(1)}, bf16[512,256]{1,0:T(8,128)(2,1)S(1)}, u32[]{:S(2)}, u32[]{:S(2)}) collective-permute-start(bf16[512,256]{1,0:T(8,128)(2,1)S(1)} %get-tuple-element.29), channel_id=1, source_target_pairs={{0,1},{1,0},{2,3},{3,2},{4,5},{5,4},{6,7},{7,6},{8,9},{9,8},{10,11... | collective-permute-start | bytes 786440 | tf_op jit(solution)/shard_map/ppermute | solution.py:16
  7.0 0.9 %collective-permute-start.4 = (bf16[512,256]{1,0:T(8,128)(2,1)S(1)}, bf16[512,256]{1,0:T(8,128)(2,1)S(1)}, u32[]{:S(2)}, u32[]{:S(2)}) collective-permute-start(bf16[512,256]{1,0:T(8,128)(2,1)S(1)} %get-tuple-element.36), channel_id=1, source_target_pairs={{0,30},{2,4},{4,2},{6,8},{8,6},{10,12},{12,10},{14,16},{16,14},{18... | collective-permute-start | bytes 786440 | tf_op jit(solution)/shard_map/ppermute | solution.py:26
  7.8 0.9 %collective-permute-start = (bf16[512,128]{1,0:T(8,128)(2,1)S(1)}, bf16[512,128]{1,0:T(8,128)(2,1)S(1)}, u32[]{:S(2)}, u32[]{:S(2)}) collective-permute-start(bf16[512,128]{1,0:T(8,128)(2,1)S(1)} %get-tuple-element.25), channel_id=1, source_target_pairs={{0,30},{2,4},{4,2},{6,8},{8,6},{10,12},{12,10},{14,16},{16,14},{18... | collective-permute-start | bytes 393224 | tf_op jit(solution)/shard_map/ppermute | solution.py:26
  8.7 0.0 collective-permute-done.1.near
  8.7 0.0 copy-done
  8.7 0.0 copy-done.1
  8.7 1.5 %shard_map.57 = (f32[512,768]{1,0:T(8,128)S(1)}, bf16[512,768]{1,0:T(8,128)(2,1)S(1)}, f32[1,768]{1,0:T(1,128)S(1)}) custom-call(s32[3]{0:T(128)S(1)} %bitcast.3, s32[2]{0:T(128)S(1)} %bitcast.4, bf16[3,512,512]{2,1,0:T(8,128)(2,1)S(1)} %get-tuple-element.24.tiles, bf16[512,768]{1,0:T(8,128)(2,1)S(1)} %get-tuple-element.26.own, ...), custom_call_target="tpu_custom_call" | custom-call | flops 805306368 | bytes 1048576 | tf_op jit(solution)/shard_map/pallas_call | solution.py:43
  10.3 1.0 %collective-permute-done.2.lent = bf16[512,256]{1,0:T(8,128)(2,1)S(1)} collective-permute-done((bf16[512,256]{1,0:T(8,128)(2,1)S(1)}, bf16[512,256]{1,0:T(8,128)(2,1)S(1)}, u32[]{:S(2)}, u32[]{:S(2)}) %collective-permute-start.2) | collective-permute-done | bytes 262176 | tf_op jit(solution)/shard_map/ppermute | solution.py:16
  11.3 0.5 %shard_map.58 = (bf16[256,512]{1,0:T(8,128)(2,1)S(1)}, f32[256,768]{1,0:T(8,128)S(1)}) custom-call(bf16[512,256]{1,0:T(8,128)(2,1)S(1)} %get-tuple-element.28.kept, bf16[512,256]{1,0:T(8,128)(2,1)S(1)} %collective-permute-done.2.lent, bf16[512,768]{1,0:T(8,128)(2,1)S(1)} %get-tuple-element.30.miss, f32[1,768]{1,0:T(1,128)S(1)} %get-tuple-element.31.stays), custom_call_target="tpu_custom_call" | custom-call | flops 201326592 | bytes 1048576 | tf_op jit(solution)/shard_map/pallas_call | solution.py:43
  11.8 7.1 %collective-permute-done.6.far = bf16[512,384]{1,0:T(8,128)(2,1)S(1)} collective-permute-done((bf16[512,384]{1,0:T(8,128)(2,1)S(1)}, bf16[512,384]{1,0:T(8,128)(2,1)S(1)}, u32[]{:S(2)}, u32[]{:S(2)}) %collective-permute-start.6) | collective-permute-done | bytes 393248 | tf_op jit(solution)/shard_map/ppermute | solution.py:26
  18.9 0.7 %shard_map.61 = (f32[256,384]{1,0:T(8,128)S(1)}, bf16[256,384]{1,0:T(8,128)(2,1)S(1)}) custom-call(bf16[3,512,512]{2,1,0:T(8,128)(2,1)S(1)} %get-tuple-element.24.tiles, bf16[512,384]{1,0:T(8,128)(2,1)S(1)} %collective-permute-done.6.far, f32[512,768]{1,0:T(8,128)S(1)} %get-tuple-element.27.hit, bf16[256,512]{1,0:T(8,128)(2,1)S(1)} %get-tuple-element.32.hit_turned, ...), custom_call_target="tpu_custom_call" | custom-call | flops 402653184 | bytes 1048576 | tf_op jit(solution)/shard_map/pallas_call | solution.py:43
  19.5 2.9 %collective-permute-start.7 = (bf16[256,384]{1,0:T(8,128)(2,1)S(1)}, bf16[256,384]{1,0:T(8,128)(2,1)S(1)}, u32[]{:S(2)}, u32[]{:S(2)}) collective-permute-start(bf16[256,384]{1,0:T(8,128)(2,1)S(1)} %get-tuple-element.40), channel_id=1, source_target_pairs={{0,1},{1,0},{2,3},{3,2},{4,5},{5,4},{6,7},{7,6},{8,9},{9,8},{10,11... | collective-permute-start | bytes 589832 | tf_op jit(solution)/shard_map/ppermute | solution.py:16
  22.5 0.3 collective-permute-done.4.far
  22.7 0.5 %shard_map.60 = (f32[256,256]{1,0:T(8,128)S(1)}, bf16[256,256]{1,0:T(8,128)(2,1)S(1)}) custom-call(bf16[3,512,512]{2,1,0:T(8,128)(2,1)S(1)} %get-tuple-element.24.tiles, bf16[512,256]{1,0:T(8,128)(2,1)S(1)} %collective-permute-done.4.far, f32[512,768]{1,0:T(8,128)S(1)} %get-tuple-element.27.hit, bf16[256,512]{1,0:T(8,128)(2,1)S(1)} %get-tuple-element.32.hit_turned, ...), custom_call_target="tpu_custom_call" | custom-call | flops 268435456 | bytes 1048576 | tf_op jit(solution)/shard_map/pallas_call | solution.py:43
  23.3 1.9 %collective-permute-start.5 = (bf16[256,256]{1,0:T(8,128)(2,1)S(1)}, bf16[256,256]{1,0:T(8,128)(2,1)S(1)}, u32[]{:S(2)}, u32[]{:S(2)}) collective-permute-start(bf16[256,256]{1,0:T(8,128)(2,1)S(1)} %get-tuple-element.38), channel_id=1, source_target_pairs={{0,1},{1,0},{2,3},{3,2},{4,5},{5,4},{6,7},{7,6},{8,9},{9,8},{10,11... | collective-permute-start | bytes 393224 | tf_op jit(solution)/shard_map/ppermute | solution.py:16
  25.2 0.0 collective-permute-done.far
  25.2 0.5 %shard_map.59 = (f32[256,128]{1,0:T(8,128)S(1)}, bf16[256,128]{1,0:T(8,128)(2,1)S(1)}) custom-call(bf16[3,512,512]{2,1,0:T(8,128)(2,1)S(1)} %get-tuple-element.24.tiles, bf16[512,128]{1,0:T(8,128)(2,1)S(1)} %collective-permute-done.far, f32[512,768]{1,0:T(8,128)S(1)} %get-tuple-element.27.hit, bf16[256,512]{1,0:T(8,128)(2,1)S(1)} %get-tuple-element.32.hit_turned, ...), custom_call_target="tpu_custom_call" | custom-call | flops 134217728 | bytes 1048576 | tf_op jit(solution)/shard_map/pallas_call | solution.py:43
  25.7 0.8 %collective-permute-start.3 = (bf16[256,128]{1,0:T(8,128)(2,1)S(1)}, bf16[256,128]{1,0:T(8,128)(2,1)S(1)}, u32[]{:S(2)}, u32[]{:S(2)}) collective-permute-start(bf16[256,128]{1,0:T(8,128)(2,1)S(1)} %get-tuple-element.35), channel_id=1, source_target_pairs={{0,1},{1,0},{2,3},{3,2},{4,5},{5,4},{6,7},{7,6},{8,9},{9,8},{10,11... | collective-permute-start | bytes 196616 | tf_op jit(solution)/shard_map/ppermute | solution.py:16
  26.5 0.7 %collective-permute-done.7.received = bf16[256,384]{1,0:T(8,128)(2,1)S(1)} collective-permute-done((bf16[256,384]{1,0:T(8,128)(2,1)S(1)}, bf16[256,384]{1,0:T(8,128)(2,1)S(1)}, u32[]{:S(2)}, u32[]{:S(2)}) %collective-permute-start.7) | collective-permute-done | bytes 196640 | tf_op jit(solution)/shard_map/ppermute | solution.py:16
  27.2 0.8 %shard_map.62.rest_0_ = f32[256,768]{1,0:T(8,128)} custom-call(f32[256,384]{1,0:T(8,128)S(1)} %get-tuple-element.39.kept, bf16[256,384]{1,0:T(8,128)(2,1)S(1)} %collective-permute-done.7.received), custom_call_target="tpu_custom_call" | custom-call | flops 65536 | bytes 1048576 | tf_op jit(solution)/shard_map/pallas_call | solution.py:43
  28.0 0.6 %collective-permute-done.5.received = bf16[256,256]{1,0:T(8,128)(2,1)S(1)} collective-permute-done((bf16[256,256]{1,0:T(8,128)(2,1)S(1)}, bf16[256,256]{1,0:T(8,128)(2,1)S(1)}, u32[]{:S(2)}, u32[]{:S(2)}) %collective-permute-start.5) | collective-permute-done | bytes 131104 | tf_op jit(solution)/shard_map/ppermute | solution.py:16
  28.6 0.7 %shard_map.63.rest_0_ = f32[256,768]{1,0:T(8,128)} custom-call(f32[256,256]{1,0:T(8,128)S(1)} %get-tuple-element.37.kept, bf16[256,256]{1,0:T(8,128)(2,1)S(1)} %collective-permute-done.5.received, f32[256,768]{1,0:T(8,128)} %shard_map.62.rest_0_), custom_call_target="tpu_custom_call", output_to_operand_aliasing={{}: (2, {})} | custom-call | flops 65536 | bytes 1048576 | tf_op jit(solution)/shard_map/pallas_call | solution.py:43
  29.3 0.0 collective-permute-done.3.received
  29.3 0.7 %shard_map.64 = f32[256,768]{1,0:T(8,128)} custom-call(f32[256,128]{1,0:T(8,128)S(1)} %get-tuple-element.34.kept, bf16[256,128]{1,0:T(8,128)(2,1)S(1)} %collective-permute-done.3.received, f32[256,768]{1,0:T(8,128)} %shard_map.63.rest_0_), custom_call_target="tpu_custom_call", output_to_operand_aliasing={{}: (2, {})} | custom-call | flops 65536 | bytes 1048576 | tf_op jit(solution)/shard_map/pallas_call | solution.py:43
Async XLA Ops:
  1.1 7.6 %copy-start = (s32[1,1,3,1]{2,3,1,0:T(1,128)S(1)}, s32[1,1,3,1]{2,3,1,0:T(1,128)}, u32[]{:S(2)}) copy-start(s32[1,1,3,1]{2,3,1,0:T(1,128)} %param.7) | copy-start | bytes 40
  1.1 7.6 %copy-start.1 = (s32[1,1,2]{2,1,0:T(1,128)S(1)}, s32[1,1,2]{2,1,0:T(1,128)}, u32[]{:S(2)}) copy-start(s32[1,1,2]{2,1,0:T(1,128)} %param.8) | copy-start | bytes 28
  3.0 5.7 %collective-permute-start.1 = (bf16[512,768]{1,0:T(8,128)(2,1)S(1)}, bf16[512,768]{1,0:T(8,128)(2,1)S(1)}, u32[]{:S(2)}, u32[]{:S(2)}) collective-permute-start(bf16[512,768]{1,0:T(8,128)(2,1)S(1)} %get-tuple-element.26.own), channel_id=1, source_target_pairs={{0,2},{2,0},{4,6},{6,4},{8,10},{10,8},{12,14},{14,12},{16,18},{18,... | collective-permute-start | bytes 2359304 | tf_op jit(solution)/shard_map/ppermute | solution.py:21
  3.1 15.8 %collective-permute-start.6 = (bf16[512,384]{1,0:T(8,128)(2,1)S(1)}, bf16[512,384]{1,0:T(8,128)(2,1)S(1)}, u32[]{:S(2)}, u32[]{:S(2)}) collective-permute-start(bf16[512,384]{1,0:T(8,128)(2,1)S(1)} %get-tuple-element.23.begun), channel_id=1, source_target_pairs={{0,30},{2,4},{4,2},{6,8},{8,6},{10,12},{12,10},{14,16},{16,14},{18... | collective-permute-start | bytes 1179656 | tf_op jit(solution)/shard_map/ppermute | solution.py:26
  5.7 5.5 %collective-permute-start.2 = (bf16[512,256]{1,0:T(8,128)(2,1)S(1)}, bf16[512,256]{1,0:T(8,128)(2,1)S(1)}, u32[]{:S(2)}, u32[]{:S(2)}) collective-permute-start(bf16[512,256]{1,0:T(8,128)(2,1)S(1)} %get-tuple-element.29), channel_id=1, source_target_pairs={{0,1},{1,0},{2,3},{3,2},{4,5},{5,4},{6,7},{7,6},{8,9},{9,8},{10,11... | collective-permute-start | bytes 786440 | tf_op jit(solution)/shard_map/ppermute | solution.py:16
  7.0 15.8 %collective-permute-start.4 = (bf16[512,256]{1,0:T(8,128)(2,1)S(1)}, bf16[512,256]{1,0:T(8,128)(2,1)S(1)}, u32[]{:S(2)}, u32[]{:S(2)}) collective-permute-start(bf16[512,256]{1,0:T(8,128)(2,1)S(1)} %get-tuple-element.36), channel_id=1, source_target_pairs={{0,30},{2,4},{4,2},{6,8},{8,6},{10,12},{12,10},{14,16},{16,14},{18... | collective-permute-start | bytes 786440 | tf_op jit(solution)/shard_map/ppermute | solution.py:26
  7.8 17.3 %collective-permute-start = (bf16[512,128]{1,0:T(8,128)(2,1)S(1)}, bf16[512,128]{1,0:T(8,128)(2,1)S(1)}, u32[]{:S(2)}, u32[]{:S(2)}) collective-permute-start(bf16[512,128]{1,0:T(8,128)(2,1)S(1)} %get-tuple-element.25), channel_id=1, source_target_pairs={{0,30},{2,4},{4,2},{6,8},{8,6},{10,12},{12,10},{14,16},{16,14},{18... | collective-permute-start | bytes 393224 | tf_op jit(solution)/shard_map/ppermute | solution.py:26
  19.5 7.6 %collective-permute-start.7 = (bf16[256,384]{1,0:T(8,128)(2,1)S(1)}, bf16[256,384]{1,0:T(8,128)(2,1)S(1)}, u32[]{:S(2)}, u32[]{:S(2)}) collective-permute-start(bf16[256,384]{1,0:T(8,128)(2,1)S(1)} %get-tuple-element.40), channel_id=1, source_target_pairs={{0,1},{1,0},{2,3},{3,2},{4,5},{5,4},{6,7},{7,6},{8,9},{9,8},{10,11... | collective-permute-start | bytes 589832 | tf_op jit(solution)/shard_map/ppermute | solution.py:16
  23.3 5.3 %collective-permute-start.5 = (bf16[256,256]{1,0:T(8,128)(2,1)S(1)}, bf16[256,256]{1,0:T(8,128)(2,1)S(1)}, u32[]{:S(2)}, u32[]{:S(2)}) collective-permute-start(bf16[256,256]{1,0:T(8,128)(2,1)S(1)} %get-tuple-element.38), channel_id=1, source_target_pairs={{0,1},{1,0},{2,3},{3,2},{4,5},{5,4},{6,7},{7,6},{8,9},{9,8},{10,11... | collective-permute-start | bytes 393224 | tf_op jit(solution)/shard_map/ppermute | solution.py:16
  25.7 3.7 %collective-permute-start.3 = (bf16[256,128]{1,0:T(8,128)(2,1)S(1)}, bf16[256,128]{1,0:T(8,128)(2,1)S(1)}, u32[]{:S(2)}, u32[]{:S(2)}) collective-permute-start(bf16[256,128]{1,0:T(8,128)(2,1)S(1)} %get-tuple-element.35), channel_id=1, source_target_pairs={{0,1},{1,0},{2,3},{3,2},{4,5},{5,4},{6,7},{7,6},{8,9},{9,8},{10,11... | collective-permute-start | bytes 196616 | tf_op jit(solution)/shard_map/ppermute | solution.py:16

commit v8 on v7

--- a/solution.py
+++ b/solution.py
@@ -160,7 +160,7 @@
     )
     lent = from_behind(lent, "group", 1)
     fars = [swap_far(part) for part in (first, *later)]
-    near = swap_near(own)
+    near = swap_near(sketch)
     hit, miss, stays = call(
         local_kernel,
         (

time: 30.2 us -> 29.9 us (0.990)
  starting transfers between devices: 11.3 us -> 10.1 us
  waiting for transfers between devices: 9.68 us -> 10.4 us
    ppermute x4, starting transfers between devices: 6.85 us -> 5.64 us  [from_behind(): lax.ppermute(array, axis, [(i, (i + by) % devices) for i in range(devices)])]
    ppermute x4, waiting for transfers between devices: 2.26 us -> 2.62 us  [from_behind(): lax.ppermute(array, axis, [(i, (i + by) % devices) for i in range(devices)])]
    ppermute x3, waiting for transfers between devices: 7.41 us -> 7.75 us  [swap_far(): lax.ppermute(array, 'blk', [(i, (i + 1 if i % 2 else i - 1) % devices) fo...]
  transfers between devices with their start and end apart: 8 -> 8, of which waited for: 5 -> 4; matrix products, arithmetic and copies ran while one was open for 0% -> 0% of each run, Pallas kernels for 17% -> 28%
where the time goes in v8:
time: 29.9 us; the launch traced here: 29.4 us
  waiting for transfers between devices  10.4 us (35%)
  starting transfers between devices  10.1 us (34%)
  Pallas kernels  8.85 us (30%)
    pallas_call x10, Pallas kernels, call(): pl.pallas_call(kernel, out_shape=out_shape, in_specs=[scalar] * len(scala...  8.85 us
    ppermute x3, waiting for transfers between devices, swap_far(): lax.ppermute(array, 'blk', [(i, (i + 1 if i % 2 else i - 1) % devices) fo...  7.75 us
    ppermute x4, starting transfers between devices, from_behind(): lax.ppermute(array, axis, [(i, (i + by) % devices) for i in range(devices)])  5.64 us
    ppermute x3, starting transfers between devices, swap_far(): lax.ppermute(array, 'blk', [(i, (i + 1 if i % 2 else i - 1) % devices) fo...  4.42 us
    ppermute x4, waiting for transfers between devices, from_behind(): lax.ppermute(array, axis, [(i, (i + by) % devices) for i in range(devices)])  2.62 us
  transfers between devices with their start and end apart: 8, of which 4 were waited for; matrix products, arithmetic and copies ran while one was open for 0% of the time, Pallas kernels for 28%

profile of v8, /device:TPU:1, one launch (start us, length us, event | category | flops | bytes accessed | tf_op | source)
XLA Modules:
  0.0 29.4 jit_solution(2850192260664864368)
XLA Ops:
  0.0 0.1 collective-permute-start.1
  0.1 1.1 %shard_map.55 = (bf16[512,384]{1,0:T(8,128)(2,1)S(1)}, bf16[512,256]{1,0:T(8,128)(2,1)S(1)}) custom-call(bf16[512,768]{1,0:T(8,128)(2,1)} %sketch.3, bf16[1,1,1024,256]{3,2,1,0:T(8,128)(2,1)} %basis.3), custom_call_target="tpu_custom_call" | custom-call | bytes 1048576 | tf_op jit(solution)/shard_map/pallas_call | solution.py:43
  1.2 2.6 %collective-permute-start.6 = (bf16[512,384]{1,0:T(8,128)(2,1)S(1)}, bf16[512,384]{1,0:T(8,128)(2,1)S(1)}, u32[]{:S(2)}, u32[]{:S(2)}) collective-permute-start(bf16[512,384]{1,0:T(8,128)(2,1)S(1)} %get-tuple-element.23.begun), channel_id=1, source_target_pairs={{0,30},{2,4},{4,2},{6,8},{8,6},{10,12},{12,10},{14,16},{16,14},{18... | collective-permute-start | bytes 1179656 | tf_op jit(solution)/shard_map/ppermute | solution.py:26
  3.8 0.0 copy-start
  3.8 0.0 copy-start.1
  3.8 1.2 %collective-permute-start.2 = (bf16[512,256]{1,0:T(8,128)(2,1)S(1)}, bf16[512,256]{1,0:T(8,128)(2,1)S(1)}, u32[]{:S(2)}, u32[]{:S(2)}) collective-permute-start(bf16[512,256]{1,0:T(8,128)(2,1)S(1)} %get-tuple-element.29), channel_id=1, source_target_pairs={{0,1},{1,0},{2,3},{3,2},{4,5},{5,4},{6,7},{7,6},{8,9},{9,8},{10,11... | collective-permute-start | bytes 786440 | tf_op jit(solution)/shard_map/ppermute | solution.py:16
  5.0 1.9 %shard_map.56 = (bf16[512,256]{1,0:T(8,128)(2,1)S(1)}, bf16[512,128]{1,0:T(8,128)(2,1)S(1)}, bf16[512,768]{1,0:T(8,128)(2,1)S(1)}, bf16[3,512,512]{2,1,0:T(8,128)(2,1)S(1)}, bf16[512,256]{1,0:T(8,128)(2,1)S(1)}) custom-call(bf16[512,384]{1,0:T(8,128)(2,1)S(1)} %get-tuple-element.23.begun, bf16[512,768]{1,0:T(8,128)(2,1)} %sketch.3, ...), custom_call_target="tpu_custom_call" | custom-call | bytes 1048576 | tf_op jit(solution)/shard_map/pallas_call | solution.py:43
  6.9 1.0 %collective-permute-start.4 = (bf16[512,256]{1,0:T(8,128)(2,1)S(1)}, bf16[512,256]{1,0:T(8,128)(2,1)S(1)}, u32[]{:S(2)}, u32[]{:S(2)}) collective-permute-start(bf16[512,256]{1,0:T(8,128)(2,1)S(1)} %get-tuple-element.36), channel_id=1, source_target_pairs={{0,30},{2,4},{4,2},{6,8},{8,6},{10,12},{12,10},{14,16},{16,14},{18... | collective-permute-start | bytes 786440 | tf_op jit(solution)/shard_map/ppermute | solution.py:26
  7.9 0.8 %collective-permute-start = (bf16[512,128]{1,0:T(8,128)(2,1)S(1)}, bf16[512,128]{1,0:T(8,128)(2,1)S(1)}, u32[]{:S(2)}, u32[]{:S(2)}) collective-permute-start(bf16[512,128]{1,0:T(8,128)(2,1)S(1)} %get-tuple-element.25), channel_id=1, source_target_pairs={{0,30},{2,4},{4,2},{6,8},{8,6},{10,12},{12,10},{14,16},{16,14},{18... | collective-permute-start | bytes 393224 | tf_op jit(solution)/shard_map/ppermute | solution.py:26
  8.7 0.0 collective-permute-done.1.near
  8.7 0.0 copy-done
  8.7 0.0 copy-done.1
  8.7 1.5 %shard_map.57 = (f32[512,768]{1,0:T(8,128)S(1)}, bf16[512,768]{1,0:T(8,128)(2,1)S(1)}, f32[1,768]{1,0:T(1,128)S(1)}) custom-call(s32[3]{0:T(128)S(1)} %bitcast.3, s32[2]{0:T(128)S(1)} %bitcast.4, bf16[3,512,512]{2,1,0:T(8,128)(2,1)S(1)} %get-tuple-element.24.tiles, bf16[512,768]{1,0:T(8,128)(2,1)S(1)} %get-tuple-element.26.own, ...), custom_call_target="tpu_custom_call" | custom-call | flops 805306368 | bytes 1048576 | tf_op jit(solution)/shard_map/pallas_call | solution.py:43
  10.2 0.0 collective-permute-done.2.lent
  10.2 0.5 %shard_map.58 = (bf16[256,512]{1,0:T(8,128)(2,1)S(1)}, f32[256,768]{1,0:T(8,128)S(1)}) custom-call(bf16[512,256]{1,0:T(8,128)(2,1)S(1)} %get-tuple-element.28.kept, bf16[512,256]{1,0:T(8,128)(2,1)S(1)} %collective-permute-done.2.lent, bf16[512,768]{1,0:T(8,128)(2,1)S(1)} %get-tuple-element.30.miss, f32[1,768]{1,0:T(1,128)S(1)} %get-tuple-element.31.stays), custom_call_target="tpu_custom_call" | custom-call | flops 201326592 | bytes 1048576 | tf_op jit(solution)/shard_map/pallas_call | solution.py:43
  10.7 6.2 %collective-permute-done.6.far = bf16[512,384]{1,0:T(8,128)(2,1)S(1)} collective-permute-done((bf16[512,384]{1,0:T(8,128)(2,1)S(1)}, bf16[512,384]{1,0:T(8,128)(2,1)S(1)}, u32[]{:S(2)}, u32[]{:S(2)}) %collective-permute-start.6) | collective-permute-done | bytes 393248 | tf_op jit(solution)/shard_map/ppermute | solution.py:26
  16.9 0.7 %shard_map.61 = (f32[256,384]{1,0:T(8,128)S(1)}, bf16[256,384]{1,0:T(8,128)(2,1)S(1)}) custom-call(bf16[3,512,512]{2,1,0:T(8,128)(2,1)S(1)} %get-tuple-element.24.tiles, bf16[512,384]{1,0:T(8,128)(2,1)S(1)} %collective-permute-done.6.far, f32[512,768]{1,0:T(8,128)S(1)} %get-tuple-element.27.hit, bf16[256,512]{1,0:T(8,128)(2,1)S(1)} %get-tuple-element.32.hit_turned, ...), custom_call_target="tpu_custom_call" | custom-call | flops 402653184 | bytes 1048576 | tf_op jit(solution)/shard_map/pallas_call | solution.py:43
  17.6 1.3 %collective-permute-start.7 = (bf16[256,384]{1,0:T(8,128)(2,1)S(1)}, bf16[256,384]{1,0:T(8,128)(2,1)S(1)}, u32[]{:S(2)}, u32[]{:S(2)}) collective-permute-start(bf16[256,384]{1,0:T(8,128)(2,1)S(1)} %get-tuple-element.40), channel_id=1, source_target_pairs={{0,1},{1,0},{2,3},{3,2},{4,5},{5,4},{6,7},{7,6},{8,9},{9,8},{10,11... | collective-permute-start | bytes 589832 | tf_op jit(solution)/shard_map/ppermute | solution.py:16
  18.9 1.6 %collective-permute-done.4.far = bf16[512,256]{1,0:T(8,128)(2,1)S(1)} collective-permute-done((bf16[512,256]{1,0:T(8,128)(2,1)S(1)}, bf16[512,256]{1,0:T(8,128)(2,1)S(1)}, u32[]{:S(2)}, u32[]{:S(2)}) %collective-permute-start.4) | collective-permute-done | bytes 262176 | tf_op jit(solution)/shard_map/ppermute | solution.py:26
  20.5 0.5 %shard_map.60 = (f32[256,256]{1,0:T(8,128)S(1)}, bf16[256,256]{1,0:T(8,128)(2,1)S(1)}) custom-call(bf16[3,512,512]{2,1,0:T(8,128)(2,1)S(1)} %get-tuple-element.24.tiles, bf16[512,256]{1,0:T(8,128)(2,1)S(1)} %collective-permute-done.4.far, f32[512,768]{1,0:T(8,128)S(1)} %get-tuple-element.27.hit, bf16[256,512]{1,0:T(8,128)(2,1)S(1)} %get-tuple-element.32.hit_turned, ...), custom_call_target="tpu_custom_call" | custom-call | flops 268435456 | bytes 1048576 | tf_op jit(solution)/shard_map/pallas_call | solution.py:43
  21.0 2.2 %collective-permute-start.5 = (bf16[256,256]{1,0:T(8,128)(2,1)S(1)}, bf16[256,256]{1,0:T(8,128)(2,1)S(1)}, u32[]{:S(2)}, u32[]{:S(2)}) collective-permute-start(bf16[256,256]{1,0:T(8,128)(2,1)S(1)} %get-tuple-element.38), channel_id=1, source_target_pairs={{0,1},{1,0},{2,3},{3,2},{4,5},{5,4},{6,7},{7,6},{8,9},{9,8},{10,11... | collective-permute-start | bytes 393224 | tf_op jit(solution)/shard_map/ppermute | solution.py:16
  23.3 0.0 collective-permute-done.far
  23.3 0.5 %shard_map.59 = (f32[256,128]{1,0:T(8,128)S(1)}, bf16[256,128]{1,0:T(8,128)(2,1)S(1)}) custom-call(bf16[3,512,512]{2,1,0:T(8,128)(2,1)S(1)} %get-tuple-element.24.tiles, bf16[512,128]{1,0:T(8,128)(2,1)S(1)} %collective-permute-done.far, f32[512,768]{1,0:T(8,128)S(1)} %get-tuple-element.27.hit, bf16[256,512]{1,0:T(8,128)(2,1)S(1)} %get-tuple-element.32.hit_turned, ...), custom_call_target="tpu_custom_call" | custom-call | flops 134217728 | bytes 1048576 | tf_op jit(solution)/shard_map/pallas_call | solution.py:43
  23.7 0.9 %collective-permute-start.3 = (bf16[256,128]{1,0:T(8,128)(2,1)S(1)}, bf16[256,128]{1,0:T(8,128)(2,1)S(1)}, u32[]{:S(2)}, u32[]{:S(2)}) collective-permute-start(bf16[256,128]{1,0:T(8,128)(2,1)S(1)} %get-tuple-element.35), channel_id=1, source_target_pairs={{0,1},{1,0},{2,3},{3,2},{4,5},{5,4},{6,7},{7,6},{8,9},{9,8},{10,11... | collective-permute-start | bytes 196616 | tf_op jit(solution)/shard_map/ppermute | solution.py:16
  24.6 0.0 collective-permute-done.7.received
  24.6 0.8 %shard_map.62.rest_0_ = f32[256,768]{1,0:T(8,128)} custom-call(f32[256,384]{1,0:T(8,128)S(1)} %get-tuple-element.39.kept, bf16[256,384]{1,0:T(8,128)(2,1)S(1)} %collective-permute-done.7.received), custom_call_target="tpu_custom_call" | custom-call | flops 65536 | bytes 1048576 | tf_op jit(solution)/shard_map/pallas_call | solution.py:43
  25.4 2.0 %collective-permute-done.5.received = bf16[256,256]{1,0:T(8,128)(2,1)S(1)} collective-permute-done((bf16[256,256]{1,0:T(8,128)(2,1)S(1)}, bf16[256,256]{1,0:T(8,128)(2,1)S(1)}, u32[]{:S(2)}, u32[]{:S(2)}) %collective-permute-start.5) | collective-permute-done | bytes 131104 | tf_op jit(solution)/shard_map/ppermute | solution.py:16
  27.4 0.7 %shard_map.63.rest_0_ = f32[256,768]{1,0:T(8,128)} custom-call(f32[256,256]{1,0:T(8,128)S(1)} %get-tuple-element.37.kept, bf16[256,256]{1,0:T(8,128)(2,1)S(1)} %collective-permute-done.5.received, f32[256,768]{1,0:T(8,128)} %shard_map.62.rest_0_), custom_call_target="tpu_custom_call", output_to_operand_aliasing={{}: (2, {})} | custom-call | flops 65536 | bytes 1048576 | tf_op jit(solution)/shard_map/pallas_call | solution.py:43
  28.1 0.6 %collective-permute-done.3.received = bf16[256,128]{1,0:T(8,128)(2,1)S(1)} collective-permute-done((bf16[256,128]{1,0:T(8,128)(2,1)S(1)}, bf16[256,128]{1,0:T(8,128)(2,1)S(1)}, u32[]{:S(2)}, u32[]{:S(2)}) %collective-permute-start.3) | collective-permute-done | bytes 65568 | tf_op jit(solution)/shard_map/ppermute | solution.py:16
  28.8 0.7 %shard_map.64 = f32[256,768]{1,0:T(8,128)} custom-call(f32[256,128]{1,0:T(8,128)S(1)} %get-tuple-element.34.kept, bf16[256,128]{1,0:T(8,128)(2,1)S(1)} %collective-permute-done.3.received, f32[256,768]{1,0:T(8,128)} %shard_map.63.rest_0_), custom_call_target="tpu_custom_call", output_to_operand_aliasing={{}: (2, {})} | custom-call | flops 65536 | bytes 1048576 | tf_op jit(solution)/shard_map/pallas_call | solution.py:43
Async XLA Ops:
  0.0 8.7 %collective-permute-start.1 = (bf16[512,768]{1,0:T(8,128)(2,1)}, bf16[512,768]{1,0:T(8,128)(2,1)S(1)}, u32[]{:S(2)}, u32[]{:S(2)}) collective-permute-start(bf16[512,768]{1,0:T(8,128)(2,1)} %sketch.3), channel_id=1, source_target_pairs={{0,2},{2,0},{4,6},{6,4},{8,10},{10,8},{12,14},{14,12},{16,18},{18,... | collective-permute-start | bytes 2359304 | tf_op jit(solution)/shard_map/ppermute | solution.py:21
  1.2 15.8 %collective-permute-start.6 = (bf16[512,384]{1,0:T(8,128)(2,1)S(1)}, bf16[512,384]{1,0:T(8,128)(2,1)S(1)}, u32[]{:S(2)}, u32[]{:S(2)}) collective-permute-start(bf16[512,384]{1,0:T(8,128)(2,1)S(1)} %get-tuple-element.23.begun), channel_id=1, source_target_pairs={{0,30},{2,4},{4,2},{6,8},{8,6},{10,12},{12,10},{14,16},{16,14},{18... | collective-permute-start | bytes 1179656 | tf_op jit(solution)/shard_map/ppermute | solution.py:26
  3.8 4.9 %copy-start = (s32[1,1,3,1]{2,3,1,0:T(1,128)S(1)}, s32[1,1,3,1]{2,3,1,0:T(1,128)}, u32[]{:S(2)}) copy-start(s32[1,1,3,1]{2,3,1,0:T(1,128)} %param.7) | copy-start | bytes 40
  3.8 4.9 %copy-start.1 = (s32[1,1,2]{2,1,0:T(1,128)S(1)}, s32[1,1,2]{2,1,0:T(1,128)}, u32[]{:S(2)}) copy-start(s32[1,1,2]{2,1,0:T(1,128)} %param.8) | copy-start | bytes 28
  3.8 6.5 %collective-permute-start.2 = (bf16[512,256]{1,0:T(8,128)(2,1)S(1)}, bf16[512,256]{1,0:T(8,128)(2,1)S(1)}, u32[]{:S(2)}, u32[]{:S(2)}) collective-permute-start(bf16[512,256]{1,0:T(8,128)(2,1)S(1)} %get-tuple-element.29), channel_id=1, source_target_pairs={{0,1},{1,0},{2,3},{3,2},{4,5},{5,4},{6,7},{7,6},{8,9},{9,8},{10,11... | collective-permute-start | bytes 786440 | tf_op jit(solution)/shard_map/ppermute | solution.py:16
  6.9 13.6 %collective-permute-start.4 = (bf16[512,256]{1,0:T(8,128)(2,1)S(1)}, bf16[512,256]{1,0:T(8,128)(2,1)S(1)}, u32[]{:S(2)}, u32[]{:S(2)}) collective-permute-start(bf16[512,256]{1,0:T(8,128)(2,1)S(1)} %get-tuple-element.36), channel_id=1, source_target_pairs={{0,30},{2,4},{4,2},{6,8},{8,6},{10,12},{12,10},{14,16},{16,14},{18... | collective-permute-start | bytes 786440 | tf_op jit(solution)/shard_map/ppermute | solution.py:26
  7.9 15.4 %collective-permute-start = (bf16[512,128]{1,0:T(8,128)(2,1)S(1)}, bf16[512,128]{1,0:T(8,128)(2,1)S(1)}, u32[]{:S(2)}, u32[]{:S(2)}) collective-permute-start(bf16[512,128]{1,0:T(8,128)(2,1)S(1)} %get-tuple-element.25), channel_id=1, source_target_pairs={{0,30},{2,4},{4,2},{6,8},{8,6},{10,12},{12,10},{14,16},{16,14},{18... | collective-permute-start | bytes 393224 | tf_op jit(solution)/shard_map/ppermute | solution.py:26
  17.6 7.0 %collective-permute-start.7 = (bf16[256,384]{1,0:T(8,128)(2,1)S(1)}, bf16[256,384]{1,0:T(8,128)(2,1)S(1)}, u32[]{:S(2)}, u32[]{:S(2)}) collective-permute-start(bf16[256,384]{1,0:T(8,128)(2,1)S(1)} %get-tuple-element.40), channel_id=1, source_target_pairs={{0,1},{1,0},{2,3},{3,2},{4,5},{5,4},{6,7},{7,6},{8,9},{9,8},{10,11... | collective-permute-start | bytes 589832 | tf_op jit(solution)/shard_map/ppermute | solution.py:16
  21.0 6.4 %collective-permute-start.5 = (bf16[256,256]{1,0:T(8,128)(2,1)S(1)}, bf16[256,256]{1,0:T(8,128)(2,1)S(1)}, u32[]{:S(2)}, u32[]{:S(2)}) collective-permute-start(bf16[256,256]{1,0:T(8,128)(2,1)S(1)} %get-tuple-element.38), channel_id=1, source_target_pairs={{0,1},{1,0},{2,3},{3,2},{4,5},{5,4},{6,7},{7,6},{8,9},{9,8},{10,11... | collective-permute-start | bytes 393224 | tf_op jit(solution)/shard_map/ppermute | solution.py:16
  23.7 5.0 %collective-permute-start.3 = (bf16[256,128]{1,0:T(8,128)(2,1)S(1)}, bf16[256,128]{1,0:T(8,128)(2,1)S(1)}, u32[]{:S(2)}, u32[]{:S(2)}) collective-permute-start(bf16[256,128]{1,0:T(8,128)(2,1)S(1)} %get-tuple-element.35), channel_id=1, source_target_pairs={{0,1},{1,0},{2,3},{3,2},{4,5},{5,4},{6,7},{7,6},{8,9},{9,8},{10,11... | collective-permute-start | bytes 196616 | tf_op jit(solution)/shard_map/ppermute | solution.py:16

commit v9 on v8

--- a/solution.py
+++ b/solution.py
@@ -68,28 +68,29 @@
     return basis.at[0, 0, pl.ds(pl.multiple_of(group * half, half), half)]
 
 
-def cut_kernel(sketch, basis, first, lent, sems):
+def cut_kernel(sketch, basis, lent, *rest):
+    *parts, sems = rest
     theirs = half_rows(basis, 1 - lax.axis_index("group"), lent.shape[0])
-    copy_all([(sketch.at[:, pl.ds(0, first.shape[1])], first), (theirs, lent)], sems)
-
-
-def stage_kernel(begun, sketch, tiles, basis, *outs):
+    pairs = []
+    start = 0
+    for part in parts:
+        pairs.append((sketch.at[:, pl.ds(start, part.shape[1])], part))
+        start += part.shape[1]
+    copy_all([*pairs, (theirs, lent)], sems)
+
+
+def stage_kernel(begun, sketch, tiles, basis, own, staged, kept, sems):
     del begun
-    *parts, own, staged, kept, sems = outs
     ours = half_rows(basis, lax.axis_index("group"), kept.shape[0])
-    pairs = []
-    end = sketch.shape[1]
-    for part in reversed(parts):
-        end -= part.shape[1]
-        pairs.insert(0, (sketch.at[:, pl.ds(end, part.shape[1])], part))
-    copy_all([*pairs, (sketch, own), (tiles.at[0, 0, :, 0], staged), (ours, kept)], sems)
-
-
-def local_kernel(row_blocks, owner_route, tiles, own, near, hit, miss, stays):
+    copy_all([(sketch, own), (tiles.at[0, 0, :, 0], staged), (ours, kept)], sems)
+
+
+def local_kernel(row_blocks, owner_route, tiles, own, near, hit, miss, stays, last):
     far = far_offset()
     owner = owner_route[row_blocks[far]]
     own_hits = owner_route[row_blocks[1]] == owner
     near_hits = owner_route[row_blocks[2 - far]] == owner
+    last[...] = own[:, pl.ds(own.shape[1] - last.shape[1], last.shape[1])]
     step = 256
     for start in range(0, own.shape[1], step):
         columns = pl.ds(start, step)
@@ -137,41 +138,45 @@
     product = 2 * rows * panels * columns
     short, wide = sketch.dtype, jnp.float32
     copies = pltpu.SemaphoreType.DMA
-    first, lent = call(
+    lent, *parts = call(
         cut_kernel,
-        (on_chip((panels, widths[0]), short), on_chip((half, rank), short)),
+        (
+            on_chip((half, rank), short),
+            *(on_chip((panels, width), short) for width in widths[:-1]),
+        ),
         (),
         0,
         hbm=(sketch, cluster_basis),
-        scratch=(copies((2,)),),
-    )
-    *later, own, tiles, kept = call(
+        scratch=(copies((len(widths),)),),
+    )
+    own, tiles, kept = call(
         stage_kernel,
         (
-            *(on_chip((panels, width), short) for width in widths[1:]),
             on_chip((panels, columns), short),
             on_chip((offsets, rows, panels), short),
             on_chip((half, rank), short),
         ),
-        (first,),
+        (parts[0],),
         0,
         hbm=(sketch, far_tiles, cluster_basis),
-        scratch=(copies((len(widths) + 2,)),),
+        scratch=(copies((3,)),),
     )
     lent = from_behind(lent, "group", 1)
-    fars = [swap_far(part) for part in (first, *later)]
+    fars = [swap_far(part) for part in parts]
     near = swap_near(sketch)
-    hit, miss, stays = call(
+    hit, miss, stays, last = call(
         local_kernel,
         (
             on_chip((rows, columns), wide),
             on_chip((rows, columns), short),
             on_chip((1, columns), wide),
+            on_chip((panels, widths[-1]), short),
         ),
         (tiles, own, near),
         2 * product,
         scalars=(row_blocks.reshape(-1), owner_route.reshape(-1)),
     )
+    fars.append(swap_far(last))
     hit_turned, missed = call(
         turn_kernel,
         (on_chip((rank, half), short), on_chip((rank, columns), wide)),

time: 29.9 us -> 30.3 us (1.013)
  starting transfers between devices: 10.1 us -> 11.5 us
  waiting for transfers between devices: 10.4 us -> 9.57 us
    ppermute x4, starting transfers between devices: 5.64 us -> 7.01 us  [from_behind(): lax.ppermute(array, axis, [(i, (i + by) % devices) for i in range(devices)])]
    ppermute x3, waiting for transfers between devices: 7.75 us -> 6.51 us  [swap_far(): lax.ppermute(array, 'blk', [(i, (i + 1 if i % 2 else i - 1) % devices) fo...]
    ppermute x4, waiting for transfers between devices: 2.62 us -> 3.06 us  [from_behind(): lax.ppermute(array, axis, [(i, (i + by) % devices) for i in range(devices)])]
  transfers between devices with their start and end apart: 8 -> 8, of which waited for: 4 -> 4; matrix products, arithmetic and copies ran while one was open for 0% -> 0% of each run, Pallas kernels for 28% -> 27%
where the time goes in v9:
time: 30.3 us; the launch traced here: 30 us
  starting transfers between devices  11.5 us (38%)
  waiting for transfers between devices  9.57 us (32%)
  Pallas kernels  8.8 us (29%)
    pallas_call x10, Pallas kernels, call(): pl.pallas_call(kernel, out_shape=out_shape, in_specs=[scalar] * len(scala...  8.8 us
    ppermute x4, starting transfers between devices, from_behind(): lax.ppermute(array, axis, [(i, (i + by) % devices) for i in range(devices)])  7.01 us
    ppermute x3, waiting for transfers between devices, swap_far(): lax.ppermute(array, 'blk', [(i, (i + 1 if i % 2 else i - 1) % devices) fo...  6.51 us
    ppermute x3, starting transfers between devices, swap_far(): lax.ppermute(array, 'blk', [(i, (i + 1 if i % 2 else i - 1) % devices) fo...  4.42 us
    ppermute x4, waiting for transfers between devices, from_behind(): lax.ppermute(array, axis, [(i, (i + by) % devices) for i in range(devices)])  3.06 us
  transfers between devices with their start and end apart: 8, of which 4 were waited for; matrix products, arithmetic and copies ran while one was open for 0% of the time, Pallas kernels for 27%

profile of v9, /device:TPU:1, one launch (start us, length us, event | category | flops | bytes accessed | tf_op | source)
XLA Modules:
  0.0 30.0 jit_solution(1103363803234593513)
XLA Ops:
  0.0 0.1 collective-permute-start
  0.1 1.2 %shard_map.55 = (bf16[512,256]{1,0:T(8,128)(2,1)S(1)}, bf16[512,384]{1,0:T(8,128)(2,1)S(1)}, bf16[512,256]{1,0:T(8,128)(2,1)S(1)}) custom-call(bf16[512,768]{1,0:T(8,128)(2,1)} %sketch.3, bf16[1,1,1024,256]{3,2,1,0:T(8,128)(2,1)} %basis.3), custom_call_target="tpu_custom_call" | custom-call | bytes 1048576 | tf_op jit(solution)/shard_map/pallas_call | solution.py:43
  1.2 2.6 %collective-permute-start.6 = (bf16[512,384]{1,0:T(8,128)(2,1)S(1)}, bf16[512,384]{1,0:T(8,128)(2,1)S(1)}, u32[]{:S(2)}, u32[]{:S(2)}) collective-permute-start(bf16[512,384]{1,0:T(8,128)(2,1)S(1)} %get-tuple-element.23.begun), channel_id=1, source_target_pairs={{0,30},{2,4},{4,2},{6,8},{8,6},{10,12},{12,10},{14,16},{16,14},{18... | collective-permute-start | bytes 1179656 | tf_op jit(solution)/shard_map/ppermute | solution.py:26
  3.9 1.2 %collective-permute-start.2 = (bf16[512,256]{1,0:T(8,128)(2,1)S(1)}, bf16[512,256]{1,0:T(8,128)(2,1)S(1)}, u32[]{:S(2)}, u32[]{:S(2)}) collective-permute-start(bf16[512,256]{1,0:T(8,128)(2,1)S(1)} %get-tuple-element.29), channel_id=1, source_target_pairs={{0,1},{1,0},{2,3},{3,2},{4,5},{5,4},{6,7},{7,6},{8,9},{9,8},{10,11... | collective-permute-start | bytes 786440 | tf_op jit(solution)/shard_map/ppermute | solution.py:16
  5.1 0.0 copy-start
  5.1 0.0 copy-start.1
  5.1 0.9 %collective-permute-start.4 = (bf16[512,256]{1,0:T(8,128)(2,1)S(1)}, bf16[512,256]{1,0:T(8,128)(2,1)S(1)}, u32[]{:S(2)}, u32[]{:S(2)}) collective-permute-start(bf16[512,256]{1,0:T(8,128)(2,1)S(1)} %get-tuple-element.36), channel_id=1, source_target_pairs={{0,30},{2,4},{4,2},{6,8},{8,6},{10,12},{12,10},{14,16},{16,14},{18... | collective-permute-start | bytes 786440 | tf_op jit(solution)/shard_map/ppermute | solution.py:26
  6.0 1.7 %shard_map.56 = (bf16[512,768]{1,0:T(8,128)(2,1)S(1)}, bf16[3,512,512]{2,1,0:T(8,128)(2,1)S(1)}, bf16[512,256]{1,0:T(8,128)(2,1)S(1)}) custom-call(bf16[512,384]{1,0:T(8,128)(2,1)S(1)} %get-tuple-element.23.begun, bf16[512,768]{1,0:T(8,128)(2,1)} %sketch.3, bf16[1,1,3,1,512,512]{5,4,3,2,1,0:T(8,128)(2,1)} %tiles.1, bf16[1,1,1024,256]{3,2,1,0:T(8,128)(2,1)} %basis.3), custom_call_target="tpu_custom_call" | custom-call | bytes 1048576 | tf_op jit(solution)/shard_map/pallas_call | solution.py:43
  7.7 0.0 collective-permute-done.near
  7.7 0.0 copy-done
  7.7 0.0 copy-done.1
  7.7 1.6 %shard_map.57 = (f32[512,768]{1,0:T(8,128)S(1)}, bf16[512,768]{1,0:T(8,128)(2,1)S(1)}, f32[1,768]{1,0:T(1,128)S(1)}, bf16[512,128]{1,0:T(8,128)(2,1)S(1)}) custom-call(s32[3]{0:T(128)S(1)} %bitcast.3, s32[2]{0:T(128)S(1)} %bitcast.4, bf16[3,512,512]{2,1,0:T(8,128)(2,1)S(1)} %get-tuple-element.24.tiles, bf16[512,768]{1,0:T(8,128)(2,1)S(1)} %get-tuple-element.25.own, ...), custom_call_target="tpu_custom_call" | custom-call | flops 805306368 | bytes 1048576 | tf_op jit(solution)/shard_map/pallas_call | solution.py:43
  9.3 0.9 %collective-permute-start.1 = (bf16[512,128]{1,0:T(8,128)(2,1)S(1)}, bf16[512,128]{1,0:T(8,128)(2,1)S(1)}, u32[]{:S(2)}, u32[]{:S(2)}) collective-permute-start(bf16[512,128]{1,0:T(8,128)(2,1)S(1)} %get-tuple-element.26), channel_id=1, source_target_pairs={{0,30},{2,4},{4,2},{6,8},{8,6},{10,12},{12,10},{14,16},{16,14},{18... | collective-permute-start | bytes 393224 | tf_op jit(solution)/shard_map/ppermute | solution.py:26
  10.2 0.0 collective-permute-done.2.lent
  10.2 0.5 %shard_map.58 = (bf16[256,512]{1,0:T(8,128)(2,1)S(1)}, f32[256,768]{1,0:T(8,128)S(1)}) custom-call(bf16[512,256]{1,0:T(8,128)(2,1)S(1)} %get-tuple-element.28.kept, bf16[512,256]{1,0:T(8,128)(2,1)S(1)} %collective-permute-done.2.lent, bf16[512,768]{1,0:T(8,128)(2,1)S(1)} %get-tuple-element.30.miss, f32[1,768]{1,0:T(1,128)S(1)} %get-tuple-element.31.stays), custom_call_target="tpu_custom_call" | custom-call | flops 201326592 | bytes 1048576 | tf_op jit(solution)/shard_map/pallas_call | solution.py:43
  10.7 6.3 %collective-permute-done.6.far = bf16[512,384]{1,0:T(8,128)(2,1)S(1)} collective-permute-done((bf16[512,384]{1,0:T(8,128)(2,1)S(1)}, bf16[512,384]{1,0:T(8,128)(2,1)S(1)}, u32[]{:S(2)}, u32[]{:S(2)}) %collective-permute-start.6) | collective-permute-done | bytes 393248 | tf_op jit(solution)/shard_map/ppermute | solution.py:26
  17.0 0.7 %shard_map.61 = (f32[256,384]{1,0:T(8,128)S(1)}, bf16[256,384]{1,0:T(8,128)(2,1)S(1)}) custom-call(bf16[3,512,512]{2,1,0:T(8,128)(2,1)S(1)} %get-tuple-element.24.tiles, bf16[512,384]{1,0:T(8,128)(2,1)S(1)} %collective-permute-done.6.far, f32[512,768]{1,0:T(8,128)S(1)} %get-tuple-element.27.hit, bf16[256,512]{1,0:T(8,128)(2,1)S(1)} %get-tuple-element.32.hit_turned, ...), custom_call_target="tpu_custom_call" | custom-call | flops 402653184 | bytes 1048576 | tf_op jit(solution)/shard_map/pallas_call | solution.py:43
  17.7 2.7 %collective-permute-start.7 = (bf16[256,384]{1,0:T(8,128)(2,1)S(1)}, bf16[256,384]{1,0:T(8,128)(2,1)S(1)}, u32[]{:S(2)}, u32[]{:S(2)}) collective-permute-start(bf16[256,384]{1,0:T(8,128)(2,1)S(1)} %get-tuple-element.40), channel_id=1, source_target_pairs={{0,1},{1,0},{2,3},{3,2},{4,5},{5,4},{6,7},{7,6},{8,9},{9,8},{10,11... | collective-permute-start | bytes 589832 | tf_op jit(solution)/shard_map/ppermute | solution.py:16
  20.3 0.2 collective-permute-done.4.far
  20.6 0.5 %shard_map.60 = (f32[256,256]{1,0:T(8,128)S(1)}, bf16[256,256]{1,0:T(8,128)(2,1)S(1)}) custom-call(bf16[3,512,512]{2,1,0:T(8,128)(2,1)S(1)} %get-tuple-element.24.tiles, bf16[512,256]{1,0:T(8,128)(2,1)S(1)} %collective-permute-done.4.far, f32[512,768]{1,0:T(8,128)S(1)} %get-tuple-element.27.hit, bf16[256,512]{1,0:T(8,128)(2,1)S(1)} %get-tuple-element.32.hit_turned, ...), custom_call_target="tpu_custom_call" | custom-call | flops 268435456 | bytes 1048576 | tf_op jit(solution)/shard_map/pallas_call | solution.py:43
  21.1 2.2 %collective-permute-start.5 = (bf16[256,256]{1,0:T(8,128)(2,1)S(1)}, bf16[256,256]{1,0:T(8,128)(2,1)S(1)}, u32[]{:S(2)}, u32[]{:S(2)}) collective-permute-start(bf16[256,256]{1,0:T(8,128)(2,1)S(1)} %get-tuple-element.38), channel_id=1, source_target_pairs={{0,1},{1,0},{2,3},{3,2},{4,5},{5,4},{6,7},{7,6},{8,9},{9,8},{10,11... | collective-permute-start | bytes 393224 | tf_op jit(solution)/shard_map/ppermute | solution.py:16
  23.3 0.0 collective-permute-done.1.far
  23.4 0.5 %shard_map.59 = (f32[256,128]{1,0:T(8,128)S(1)}, bf16[256,128]{1,0:T(8,128)(2,1)S(1)}) custom-call(bf16[3,512,512]{2,1,0:T(8,128)(2,1)S(1)} %get-tuple-element.24.tiles, bf16[512,128]{1,0:T(8,128)(2,1)S(1)} %collective-permute-done.1.far, f32[512,768]{1,0:T(8,128)S(1)} %get-tuple-element.27.hit, bf16[256,512]{1,0:T(8,128)(2,1)S(1)} %get-tuple-element.32.hit_turned, ...), custom_call_target="tpu_custom_call" | custom-call | flops 134217728 | bytes 1048576 | tf_op jit(solution)/shard_map/pallas_call | solution.py:43
  23.8 0.8 %collective-permute-start.3 = (bf16[256,128]{1,0:T(8,128)(2,1)S(1)}, bf16[256,128]{1,0:T(8,128)(2,1)S(1)}, u32[]{:S(2)}, u32[]{:S(2)}) collective-permute-start(bf16[256,128]{1,0:T(8,128)(2,1)S(1)} %get-tuple-element.35), channel_id=1, source_target_pairs={{0,1},{1,0},{2,3},{3,2},{4,5},{5,4},{6,7},{7,6},{8,9},{9,8},{10,11... | collective-permute-start | bytes 196616 | tf_op jit(solution)/shard_map/ppermute | solution.py:16
  24.7 1.0 %collective-permute-done.7.received = bf16[256,384]{1,0:T(8,128)(2,1)S(1)} collective-permute-done((bf16[256,384]{1,0:T(8,128)(2,1)S(1)}, bf16[256,384]{1,0:T(8,128)(2,1)S(1)}, u32[]{:S(2)}, u32[]{:S(2)}) %collective-permute-start.7) | collective-permute-done | bytes 196640 | tf_op jit(solution)/shard_map/ppermute | solution.py:16
  25.7 0.8 %shard_map.62.rest_0_ = f32[256,768]{1,0:T(8,128)} custom-call(f32[256,384]{1,0:T(8,128)S(1)} %get-tuple-element.39.kept, bf16[256,384]{1,0:T(8,128)(2,1)S(1)} %collective-permute-done.7.received), custom_call_target="tpu_custom_call" | custom-call | flops 65536 | bytes 1048576 | tf_op jit(solution)/shard_map/pallas_call | solution.py:43
  26.5 2.0 %collective-permute-done.5.received = bf16[256,256]{1,0:T(8,128)(2,1)S(1)} collective-permute-done((bf16[256,256]{1,0:T(8,128)(2,1)S(1)}, bf16[256,256]{1,0:T(8,128)(2,1)S(1)}, u32[]{:S(2)}, u32[]{:S(2)}) %collective-permute-start.5) | collective-permute-done | bytes 131104 | tf_op jit(solution)/shard_map/ppermute | solution.py:16
  28.5 0.7 %shard_map.63.rest_0_ = f32[256,768]{1,0:T(8,128)} custom-call(f32[256,256]{1,0:T(8,128)S(1)} %get-tuple-element.37.kept, bf16[256,256]{1,0:T(8,128)(2,1)S(1)} %collective-permute-done.5.received, f32[256,768]{1,0:T(8,128)} %shard_map.62.rest_0_), custom_call_target="tpu_custom_call", output_to_operand_aliasing={{}: (2, {})} | custom-call | flops 65536 | bytes 1048576 | tf_op jit(solution)/shard_map/pallas_call | solution.py:43
  29.3 0.0 collective-permute-done.3.received
  29.3 0.7 %shard_map.64 = f32[256,768]{1,0:T(8,128)} custom-call(f32[256,128]{1,0:T(8,128)S(1)} %get-tuple-element.34.kept, bf16[256,128]{1,0:T(8,128)(2,1)S(1)} %collective-permute-done.3.received, f32[256,768]{1,0:T(8,128)} %shard_map.63.rest_0_), custom_call_target="tpu_custom_call", output_to_operand_aliasing={{}: (2, {})} | custom-call | flops 65536 | bytes 1048576 | tf_op jit(solution)/shard_map/pallas_call | solution.py:43
Async XLA Ops:
  0.0 7.7 %collective-permute-start = (bf16[512,768]{1,0:T(8,128)(2,1)}, bf16[512,768]{1,0:T(8,128)(2,1)S(1)}, u32[]{:S(2)}, u32[]{:S(2)}) collective-permute-start(bf16[512,768]{1,0:T(8,128)(2,1)} %sketch.3), channel_id=1, source_target_pairs={{0,2},{2,0},{4,6},{6,4},{8,10},{10,8},{12,14},{14,12},{16,18},{18,... | collective-permute-start | bytes 2359304 | tf_op jit(solution)/shard_map/ppermute | solution.py:21
  1.2 15.8 %collective-permute-start.6 = (bf16[512,384]{1,0:T(8,128)(2,1)S(1)}, bf16[512,384]{1,0:T(8,128)(2,1)S(1)}, u32[]{:S(2)}, u32[]{:S(2)}) collective-permute-start(bf16[512,384]{1,0:T(8,128)(2,1)S(1)} %get-tuple-element.23.begun), channel_id=1, source_target_pairs={{0,30},{2,4},{4,2},{6,8},{8,6},{10,12},{12,10},{14,16},{16,14},{18... | collective-permute-start | bytes 1179656 | tf_op jit(solution)/shard_map/ppermute | solution.py:26
  3.9 6.3 %collective-permute-start.2 = (bf16[512,256]{1,0:T(8,128)(2,1)S(1)}, bf16[512,256]{1,0:T(8,128)(2,1)S(1)}, u32[]{:S(2)}, u32[]{:S(2)}) collective-permute-start(bf16[512,256]{1,0:T(8,128)(2,1)S(1)} %get-tuple-element.29), channel_id=1, source_target_pairs={{0,1},{1,0},{2,3},{3,2},{4,5},{5,4},{6,7},{7,6},{8,9},{9,8},{10,11... | collective-permute-start | bytes 786440 | tf_op jit(solution)/shard_map/ppermute | solution.py:16
  5.1 2.6 %copy-start = (s32[1,1,3,1]{2,3,1,0:T(1,128)S(1)}, s32[1,1,3,1]{2,3,1,0:T(1,128)}, u32[]{:S(2)}) copy-start(s32[1,1,3,1]{2,3,1,0:T(1,128)} %param.7) | copy-start | bytes 40
  5.1 2.6 %copy-start.1 = (s32[1,1,2]{2,1,0:T(1,128)S(1)}, s32[1,1,2]{2,1,0:T(1,128)}, u32[]{:S(2)}) copy-start(s32[1,1,2]{2,1,0:T(1,128)} %param.8) | copy-start | bytes 28
  5.1 15.5 %collective-permute-start.4 = (bf16[512,256]{1,0:T(8,128)(2,1)S(1)}, bf16[512,256]{1,0:T(8,128)(2,1)S(1)}, u32[]{:S(2)}, u32[]{:S(2)}) collective-permute-start(bf16[512,256]{1,0:T(8,128)(2,1)S(1)} %get-tuple-element.36), channel_id=1, source_target_pairs={{0,30},{2,4},{4,2},{6,8},{8,6},{10,12},{12,10},{14,16},{16,14},{18... | collective-permute-start | bytes 786440 | tf_op jit(solution)/shard_map/ppermute | solution.py:26
  9.3 14.0 %collective-permute-start.1 = (bf16[512,128]{1,0:T(8,128)(2,1)S(1)}, bf16[512,128]{1,0:T(8,128)(2,1)S(1)}, u32[]{:S(2)}, u32[]{:S(2)}) collective-permute-start(bf16[512,128]{1,0:T(8,128)(2,1)S(1)} %get-tuple-element.26), channel_id=1, source_target_pairs={{0,30},{2,4},{4,2},{6,8},{8,6},{10,12},{12,10},{14,16},{16,14},{18... | collective-permute-start | bytes 393224 | tf_op jit(solution)/shard_map/ppermute | solution.py:26
  17.7 8.1 %collective-permute-start.7 = (bf16[256,384]{1,0:T(8,128)(2,1)S(1)}, bf16[256,384]{1,0:T(8,128)(2,1)S(1)}, u32[]{:S(2)}, u32[]{:S(2)}) collective-permute-start(bf16[256,384]{1,0:T(8,128)(2,1)S(1)} %get-tuple-element.40), channel_id=1, source_target_pairs={{0,1},{1,0},{2,3},{3,2},{4,5},{5,4},{6,7},{7,6},{8,9},{9,8},{10,11... | collective-permute-start | bytes 589832 | tf_op jit(solution)/shard_map/ppermute | solution.py:16
  21.1 7.4 %collective-permute-start.5 = (bf16[256,256]{1,0:T(8,128)(2,1)S(1)}, bf16[256,256]{1,0:T(8,128)(2,1)S(1)}, u32[]{:S(2)}, u32[]{:S(2)}) collective-permute-start(bf16[256,256]{1,0:T(8,128)(2,1)S(1)} %get-tuple-element.38), channel_id=1, source_target_pairs={{0,1},{1,0},{2,3},{3,2},{4,5},{5,4},{6,7},{7,6},{8,9},{9,8},{10,11... | collective-permute-start | bytes 393224 | tf_op jit(solution)/shard_map/ppermute | solution.py:16
  23.8 5.4 %collective-permute-start.3 = (bf16[256,128]{1,0:T(8,128)(2,1)S(1)}, bf16[256,128]{1,0:T(8,128)(2,1)S(1)}, u32[]{:S(2)}, u32[]{:S(2)}) collective-permute-start(bf16[256,128]{1,0:T(8,128)(2,1)S(1)} %get-tuple-element.35), channel_id=1, source_target_pairs={{0,1},{1,0},{2,3},{3,2},{4,5},{5,4},{6,7},{7,6},{8,9},{9,8},{10,11... | collective-permute-start | bytes 196616 | tf_op jit(solution)/shard_map/ppermute | solution.py:16

commit v10 on v9

--- a/solution.py
+++ b/solution.py
@@ -68,15 +68,13 @@
     return basis.at[0, 0, pl.ds(pl.multiple_of(group * half, half), half)]
 
 
-def cut_kernel(sketch, basis, lent, *rest):
-    *parts, sems = rest
+def cut_kernel(sketch, basis, lent, part, sems):
     theirs = half_rows(basis, 1 - lax.axis_index("group"), lent.shape[0])
-    pairs = []
-    start = 0
-    for part in parts:
-        pairs.append((sketch.at[:, pl.ds(start, part.shape[1])], part))
-        start += part.shape[1]
-    copy_all([*pairs, (theirs, lent)], sems)
+    copy_all([(sketch.at[:, pl.ds(0, part.shape[1])], part), (theirs, lent)], sems)
+
+
+def hand_out(own, part, start):
+    part[...] = own[:, pl.ds(start, part.shape[1])]
 
 
 def stage_kernel(begun, sketch, tiles, basis, own, staged, kept, sems):
@@ -85,15 +83,15 @@
     copy_all([(sketch, own), (tiles.at[0, 0, :, 0], staged), (ours, kept)], sems)
 
 
-def local_kernel(row_blocks, owner_route, tiles, own, near, hit, miss, stays, last):
+def local_kernel(start, row_blocks, owner_route, tiles, own, near, hit, miss, stays, part):
     far = far_offset()
     owner = owner_route[row_blocks[far]]
     own_hits = owner_route[row_blocks[1]] == owner
     near_hits = owner_route[row_blocks[2 - far]] == owner
-    last[...] = own[:, pl.ds(own.shape[1] - last.shape[1], last.shape[1])]
+    hand_out(own, part, start)
     step = 256
-    for start in range(0, own.shape[1], step):
-        columns = pl.ds(start, step)
+    for place in range(0, own.shape[1], step):
+        columns = pl.ds(place, step)
         first = jnp.dot(tiles[1], own[:, columns], preferred_element_type=jnp.float32)
         second = jnp.dot(tiles[2 - far], near[:, columns], preferred_element_type=jnp.float32)
         hit[:, columns] = jnp.where(own_hits, first, 0.0) + jnp.where(near_hits, second, 0.0)
@@ -112,7 +110,10 @@
     )
 
 
-def far_kernel(start, tiles, far, hit, hit_turned, missed, stays, kept, sent):
+def far_kernel(start, next_start, tiles, far, hit, hit_turned, missed, stays, own, *outs):
+    kept, sent, *parts = outs
+    for part in parts:
+        hand_out(own, part, next_start)
     columns = pl.ds(start, far.shape[1])
     product = jnp.dot(tiles[far_offset()], far[...], preferred_element_type=jnp.float32)
     sampled = (hit[:, columns] + product).astype(jnp.bfloat16)
@@ -138,16 +139,13 @@
     product = 2 * rows * panels * columns
     short, wide = sketch.dtype, jnp.float32
     copies = pltpu.SemaphoreType.DMA
-    lent, *parts = call(
+    lent, part = call(
         cut_kernel,
-        (
-            on_chip((half, rank), short),
-            *(on_chip((panels, width), short) for width in widths[:-1]),
-        ),
+        (on_chip((half, rank), short), on_chip((panels, widths[0]), short)),
         (),
         0,
         hbm=(sketch, cluster_basis),
-        scratch=(copies((len(widths),)),),
+        scratch=(copies((2,)),),
     )
     own, tiles, kept = call(
         stage_kernel,
@@ -156,27 +154,27 @@
             on_chip((offsets, rows, panels), short),
             on_chip((half, rank), short),
         ),
-        (parts[0],),
+        (part,),
         0,
         hbm=(sketch, far_tiles, cluster_basis),
         scratch=(copies((3,)),),
     )
     lent = from_behind(lent, "group", 1)
-    fars = [swap_far(part) for part in parts]
+    fars = [swap_far(part)]
     near = swap_near(sketch)
-    hit, miss, stays, last = call(
-        local_kernel,
+    hit, miss, stays, part = call(
+        functools.partial(local_kernel, starts[1]),
         (
             on_chip((rows, columns), wide),
             on_chip((rows, columns), short),
             on_chip((1, columns), wide),
-            on_chip((panels, widths[-1]), short),
+            on_chip((panels, widths[1]), short),
         ),
         (tiles, own, near),
         2 * product,
         scalars=(row_blocks.reshape(-1), owner_route.reshape(-1)),
     )
-    fars.append(swap_far(last))
+    fars.append(swap_far(part))
     hit_turned, missed = call(
         turn_kernel,
         (on_chip((rank, half), short), on_chip((rank, columns), wide)),
@@ -184,14 +182,20 @@
         product // 2,
     )
     out = None
-    for start, far in zip(starts, fars):
-        width = far.shape[1]
-        kept, sent = call(
-            functools.partial(far_kernel, start),
-            (on_chip((rank, width), wide), on_chip((rank, width), short)),
-            (tiles, far, hit, hit_turned, missed, stays),
+    for i, (start, width) in enumerate(zip(starts, widths)):
+        ahead = i + 2
+        more = ahead < len(widths)
+        kept, sent, *parts = call(
+            functools.partial(far_kernel, start, starts[ahead] if more else None),
+            (
+                on_chip((rank, width), wide),
+                on_chip((rank, width), short),
+                *((on_chip((panels, widths[ahead]), short),) if more else ()),
+            ),
+            (tiles, fars[i], hit, hit_turned, missed, stays, own),
             2 * product * width // columns,
         )
+        fars += [swap_far(part) for part in parts]
         out = call(
             functools.partial(join_kernel, start),
             pltpu.HBM((rank, columns), wide),

time: 30.3 us -> 30.6 us (level)
  waiting for transfers between devices: 9.57 us -> 10.3 us
  starting transfers between devices: 11.5 us -> 11 us
    ppermute x4, starting transfers between devices: 7.01 us -> 4.77 us  [from_behind(): lax.ppermute(array, axis, [(i, (i + by) % devices) for i in range(devices)])]
    ppermute x3, starting transfers between devices: 4.42 us -> 6.15 us  [swap_far(): lax.ppermute(array, 'blk', [(i, (i + 1 if i % 2 else i - 1) % devices) fo...]
    ppermute x3, waiting for transfers between devices: 6.51 us -> 7.23 us  [swap_far(): lax.ppermute(array, 'blk', [(i, (i + 1 if i % 2 else i - 1) % devices) fo...]
  transfers between devices with their start and end apart: 8 -> 8, of which waited for: 4 -> 5; matrix products, arithmetic and copies ran while one was open for 0% -> 0% of each run, Pallas kernels for 27% -> 27%
where the time goes in v10:
time: 30.6 us; the launch traced here: 30.1 us
  starting transfers between devices  11 us (36%)
  waiting for transfers between devices  10.3 us (34%)
  Pallas kernels  8.73 us (29%)
    pallas_call x10, Pallas kernels, call(): pl.pallas_call(kernel, out_shape=out_shape, in_specs=[scalar] * len(scala...  8.73 us
    ppermute x3, waiting for transfers between devices, swap_far(): lax.ppermute(array, 'blk', [(i, (i + 1 if i % 2 else i - 1) % devices) fo...  7.23 us
    ppermute x3, starting transfers between devices, swap_far(): lax.ppermute(array, 'blk', [(i, (i + 1 if i % 2 else i - 1) % devices) fo...  6.15 us
    ppermute x4, starting transfers between devices, from_behind(): lax.ppermute(array, axis, [(i, (i + by) % devices) for i in range(devices)])  4.77 us
    ppermute x4, waiting for transfers between devices, from_behind(): lax.ppermute(array, axis, [(i, (i + by) % devices) for i in range(devices)])  3.07 us
  transfers between devices with their start and end apart: 8, of which 5 were waited for; matrix products, arithmetic and copies ran while one was open for 0% of the time, Pallas kernels for 27%

profile of v10, /device:TPU:1, one launch (start us, length us, event | category | flops | bytes accessed | tf_op | source)
XLA Modules:
  0.0 30.1 jit_solution(6524754110232866954)
XLA Ops:
  0.0 0.1 collective-permute-start.1
  0.1 1.1 %shard_map.55 = (bf16[512,256]{1,0:T(8,128)(2,1)S(1)}, bf16[512,384]{1,0:T(8,128)(2,1)S(1)}) custom-call(bf16[512,768]{1,0:T(8,128)(2,1)} %sketch.3, bf16[1,1,1024,256]{3,2,1,0:T(8,128)(2,1)} %basis.3), custom_call_target="tpu_custom_call" | custom-call | bytes 1048576 | tf_op jit(solution)/shard_map/pallas_call | solution.py:43
  1.2 2.6 %collective-permute-start = (bf16[512,384]{1,0:T(8,128)(2,1)S(1)}, bf16[512,384]{1,0:T(8,128)(2,1)S(1)}, u32[]{:S(2)}, u32[]{:S(2)}) collective-permute-start(bf16[512,384]{1,0:T(8,128)(2,1)S(1)} %get-tuple-element.23.begun), channel_id=1, source_target_pairs={{0,30},{2,4},{4,2},{6,8},{8,6},{10,12},{12,10},{14,16},{16,14},{18... | collective-permute-start | bytes 1179656 | tf_op jit(solution)/shard_map/ppermute | solution.py:26
  3.8 0.0 copy-start
  3.8 0.0 copy-start.1
  3.8 1.2 %collective-permute-start.2 = (bf16[512,256]{1,0:T(8,128)(2,1)S(1)}, bf16[512,256]{1,0:T(8,128)(2,1)S(1)}, u32[]{:S(2)}, u32[]{:S(2)}) collective-permute-start(bf16[512,256]{1,0:T(8,128)(2,1)S(1)} %get-tuple-element.28), channel_id=1, source_target_pairs={{0,1},{1,0},{2,3},{3,2},{4,5},{5,4},{6,7},{7,6},{8,9},{9,8},{10,11... | collective-permute-start | bytes 786440 | tf_op jit(solution)/shard_map/ppermute | solution.py:16
  5.0 1.7 %shard_map.56 = (bf16[512,768]{1,0:T(8,128)(2,1)S(1)}, bf16[3,512,512]{2,1,0:T(8,128)(2,1)S(1)}, bf16[512,256]{1,0:T(8,128)(2,1)S(1)}) custom-call(bf16[512,384]{1,0:T(8,128)(2,1)S(1)} %get-tuple-element.23.begun, bf16[512,768]{1,0:T(8,128)(2,1)} %sketch.3, bf16[1,1,3,1,512,512]{5,4,3,2,1,0:T(8,128)(2,1)} %tiles.1, bf16[1,1,1024,256]{3,2,1,0:T(8,128)(2,1)} %basis.3), custom_call_target="tpu_custom_call" | custom-call | bytes 1048576 | tf_op jit(solution)/shard_map/pallas_call | solution.py:43
  6.7 0.0 collective-permute-done.1.near
  6.7 0.0 copy-done
  6.7 0.0 copy-done.1
  6.7 1.6 %shard_map.57 = (f32[512,768]{1,0:T(8,128)S(1)}, bf16[512,768]{1,0:T(8,128)(2,1)S(1)}, f32[1,768]{1,0:T(1,128)S(1)}, bf16[512,256]{1,0:T(8,128)(2,1)S(1)}) custom-call(s32[3]{0:T(128)S(1)} %bitcast.3, s32[2]{0:T(128)S(1)} %bitcast.4, bf16[3,512,512]{2,1,0:T(8,128)(2,1)S(1)} %get-tuple-element.24.tiles, bf16[512,768]{1,0:T(8,128)(2,1)S(1)} %get-tuple-element.25.own, ...), custom_call_target="tpu_custom_call" | custom-call | flops 805306368 | bytes 1048576 | tf_op jit(solution)/shard_map/pallas_call | solution.py:43
  8.3 1.0 %collective-permute-start.5 = (bf16[512,256]{1,0:T(8,128)(2,1)S(1)}, bf16[512,256]{1,0:T(8,128)(2,1)S(1)}, u32[]{:S(2)}, u32[]{:S(2)}) collective-permute-start(bf16[512,256]{1,0:T(8,128)(2,1)S(1)} %get-tuple-element.36), channel_id=1, source_target_pairs={{0,30},{2,4},{4,2},{6,8},{8,6},{10,12},{12,10},{14,16},{16,14},{18... | collective-permute-start | bytes 786440 | tf_op jit(solution)/shard_map/ppermute | solution.py:26
  9.3 0.0 collective-permute-done.2.lent
  9.3 0.5 %shard_map.58 = (bf16[256,512]{1,0:T(8,128)(2,1)S(1)}, f32[256,768]{1,0:T(8,128)S(1)}) custom-call(bf16[512,256]{1,0:T(8,128)(2,1)S(1)} %get-tuple-element.27.kept, bf16[512,256]{1,0:T(8,128)(2,1)S(1)} %collective-permute-done.2.lent, bf16[512,768]{1,0:T(8,128)(2,1)S(1)} %get-tuple-element.29.miss, f32[1,768]{1,0:T(1,128)S(1)} %get-tuple-element.30.stays), custom_call_target="tpu_custom_call" | custom-call | flops 201326592 | bytes 1048576 | tf_op jit(solution)/shard_map/pallas_call | solution.py:43
  9.8 5.7 %collective-permute-done.far = bf16[512,384]{1,0:T(8,128)(2,1)S(1)} collective-permute-done((bf16[512,384]{1,0:T(8,128)(2,1)S(1)}, bf16[512,384]{1,0:T(8,128)(2,1)S(1)}, u32[]{:S(2)}, u32[]{:S(2)}) %collective-permute-start) | collective-permute-done | bytes 393248 | tf_op jit(solution)/shard_map/ppermute | solution.py:26
  15.5 0.7 %shard_map.59 = (f32[256,384]{1,0:T(8,128)S(1)}, bf16[256,384]{1,0:T(8,128)(2,1)S(1)}, bf16[512,128]{1,0:T(8,128)(2,1)S(1)}) custom-call(bf16[3,512,512]{2,1,0:T(8,128)(2,1)S(1)} %get-tuple-element.24.tiles, bf16[512,384]{1,0:T(8,128)(2,1)S(1)} %collective-permute-done.far, f32[512,768]{1,0:T(8,128)S(1)} %get-tuple-element.26.hit, ...), custom_call_target="tpu_custom_call" | custom-call | flops 402653184 | bytes 1048576 | tf_op jit(solution)/shard_map/pallas_call | solution.py:43
  16.2 2.5 %collective-permute-start.3 = (bf16[512,128]{1,0:T(8,128)(2,1)S(1)}, bf16[512,128]{1,0:T(8,128)(2,1)S(1)}, u32[]{:S(2)}, u32[]{:S(2)}) collective-permute-start(bf16[512,128]{1,0:T(8,128)(2,1)S(1)} %get-tuple-element.33), channel_id=1, source_target_pairs={{0,30},{2,4},{4,2},{6,8},{8,6},{10,12},{12,10},{14,16},{16,14},{18... | collective-permute-start | bytes 393224 | tf_op jit(solution)/shard_map/ppermute | solution.py:26
  18.7 1.2 %collective-permute-start.7 = (bf16[256,384]{1,0:T(8,128)(2,1)S(1)}, bf16[256,384]{1,0:T(8,128)(2,1)S(1)}, u32[]{:S(2)}, u32[]{:S(2)}) collective-permute-start(bf16[256,384]{1,0:T(8,128)(2,1)S(1)} %get-tuple-element.40), channel_id=1, source_target_pairs={{0,1},{1,0},{2,3},{3,2},{4,5},{5,4},{6,7},{7,6},{8,9},{9,8},{10,11... | collective-permute-start | bytes 589832 | tf_op jit(solution)/shard_map/ppermute | solution.py:16
  20.0 0.0 collective-permute-done.5.far
  20.0 0.6 %shard_map.61 = (f32[256,256]{1,0:T(8,128)S(1)}, bf16[256,256]{1,0:T(8,128)(2,1)S(1)}) custom-call(bf16[3,512,512]{2,1,0:T(8,128)(2,1)S(1)} %get-tuple-element.24.tiles, bf16[512,256]{1,0:T(8,128)(2,1)S(1)} %collective-permute-done.5.far, f32[512,768]{1,0:T(8,128)S(1)} %get-tuple-element.26.hit, bf16[256,512]{1,0:T(8,128)(2,1)S(1)} %get-tuple-element.31.hit_turned, ...), custom_call_target="tpu_custom_call" | custom-call | flops 268435456 | bytes 1048576 | tf_op jit(solution)/shard_map/pallas_call | solution.py:43
  20.5 1.0 %collective-permute-start.6 = (bf16[256,256]{1,0:T(8,128)(2,1)S(1)}, bf16[256,256]{1,0:T(8,128)(2,1)S(1)}, u32[]{:S(2)}, u32[]{:S(2)}) collective-permute-start(bf16[256,256]{1,0:T(8,128)(2,1)S(1)} %get-tuple-element.38), channel_id=1, source_target_pairs={{0,1},{1,0},{2,3},{3,2},{4,5},{5,4},{6,7},{7,6},{8,9},{9,8},{10,11... | collective-permute-start | bytes 393224 | tf_op jit(solution)/shard_map/ppermute | solution.py:16
  21.6 1.5 %collective-permute-done.3.far = bf16[512,128]{1,0:T(8,128)(2,1)S(1)} collective-permute-done((bf16[512,128]{1,0:T(8,128)(2,1)S(1)}, bf16[512,128]{1,0:T(8,128)(2,1)S(1)}, u32[]{:S(2)}, u32[]{:S(2)}) %collective-permute-start.3) | collective-permute-done | bytes 131104 | tf_op jit(solution)/shard_map/ppermute | solution.py:26
  23.1 0.5 %shard_map.60 = (f32[256,128]{1,0:T(8,128)S(1)}, bf16[256,128]{1,0:T(8,128)(2,1)S(1)}) custom-call(bf16[3,512,512]{2,1,0:T(8,128)(2,1)S(1)} %get-tuple-element.24.tiles, bf16[512,128]{1,0:T(8,128)(2,1)S(1)} %collective-permute-done.3.far, f32[512,768]{1,0:T(8,128)S(1)} %get-tuple-element.26.hit, bf16[256,512]{1,0:T(8,128)(2,1)S(1)} %get-tuple-element.31.hit_turned, ...), custom_call_target="tpu_custom_call" | custom-call | flops 134217728 | bytes 1048576 | tf_op jit(solution)/shard_map/pallas_call | solution.py:43
  23.6 1.2 %collective-permute-start.4 = (bf16[256,128]{1,0:T(8,128)(2,1)S(1)}, bf16[256,128]{1,0:T(8,128)(2,1)S(1)}, u32[]{:S(2)}, u32[]{:S(2)}) collective-permute-start(bf16[256,128]{1,0:T(8,128)(2,1)S(1)} %get-tuple-element.35), channel_id=1, source_target_pairs={{0,1},{1,0},{2,3},{3,2},{4,5},{5,4},{6,7},{7,6},{8,9},{9,8},{10,11... | collective-permute-start | bytes 196616 | tf_op jit(solution)/shard_map/ppermute | solution.py:16
  24.8 0.8 %collective-permute-done.7.received = bf16[256,384]{1,0:T(8,128)(2,1)S(1)} collective-permute-done((bf16[256,384]{1,0:T(8,128)(2,1)S(1)}, bf16[256,384]{1,0:T(8,128)(2,1)S(1)}, u32[]{:S(2)}, u32[]{:S(2)}) %collective-permute-start.7) | collective-permute-done | bytes 196640 | tf_op jit(solution)/shard_map/ppermute | solution.py:16
  25.7 0.8 %shard_map.62.rest_0_ = f32[256,768]{1,0:T(8,128)} custom-call(f32[256,384]{1,0:T(8,128)S(1)} %get-tuple-element.39.kept, bf16[256,384]{1,0:T(8,128)(2,1)S(1)} %collective-permute-done.7.received), custom_call_target="tpu_custom_call" | custom-call | flops 65536 | bytes 1048576 | tf_op jit(solution)/shard_map/pallas_call | solution.py:43
  26.5 2.0 %collective-permute-done.6.received = bf16[256,256]{1,0:T(8,128)(2,1)S(1)} collective-permute-done((bf16[256,256]{1,0:T(8,128)(2,1)S(1)}, bf16[256,256]{1,0:T(8,128)(2,1)S(1)}, u32[]{:S(2)}, u32[]{:S(2)}) %collective-permute-start.6) | collective-permute-done | bytes 131104 | tf_op jit(solution)/shard_map/ppermute | solution.py:16
  28.5 0.7 %shard_map.63.rest_0_ = f32[256,768]{1,0:T(8,128)} custom-call(f32[256,256]{1,0:T(8,128)S(1)} %get-tuple-element.37.kept, bf16[256,256]{1,0:T(8,128)(2,1)S(1)} %collective-permute-done.6.received, f32[256,768]{1,0:T(8,128)} %shard_map.62.rest_0_), custom_call_target="tpu_custom_call", output_to_operand_aliasing={{}: (2, {})} | custom-call | flops 65536 | bytes 1048576 | tf_op jit(solution)/shard_map/pallas_call | solution.py:43
  29.2 0.2 collective-permute-done.4.received
  29.4 0.7 %shard_map.64 = f32[256,768]{1,0:T(8,128)} custom-call(f32[256,128]{1,0:T(8,128)S(1)} %get-tuple-element.34.kept, bf16[256,128]{1,0:T(8,128)(2,1)S(1)} %collective-permute-done.4.received, f32[256,768]{1,0:T(8,128)} %shard_map.63.rest_0_), custom_call_target="tpu_custom_call", output_to_operand_aliasing={{}: (2, {})} | custom-call | flops 65536 | bytes 1048576 | tf_op jit(solution)/shard_map/pallas_call | solution.py:43
Async XLA Ops:
  0.0 6.7 %collective-permute-start.1 = (bf16[512,768]{1,0:T(8,128)(2,1)}, bf16[512,768]{1,0:T(8,128)(2,1)S(1)}, u32[]{:S(2)}, u32[]{:S(2)}) collective-permute-start(bf16[512,768]{1,0:T(8,128)(2,1)} %sketch.3), channel_id=1, source_target_pairs={{0,2},{2,0},{4,6},{6,4},{8,10},{10,8},{12,14},{14,12},{16,18},{18,... | collective-permute-start | bytes 2359304 | tf_op jit(solution)/shard_map/ppermute | solution.py:21
  1.2 14.4 %collective-permute-start = (bf16[512,384]{1,0:T(8,128)(2,1)S(1)}, bf16[512,384]{1,0:T(8,128)(2,1)S(1)}, u32[]{:S(2)}, u32[]{:S(2)}) collective-permute-start(bf16[512,384]{1,0:T(8,128)(2,1)S(1)} %get-tuple-element.23.begun), channel_id=1, source_target_pairs={{0,30},{2,4},{4,2},{6,8},{8,6},{10,12},{12,10},{14,16},{16,14},{18... | collective-permute-start | bytes 1179656 | tf_op jit(solution)/shard_map/ppermute | solution.py:26
  3.8 2.9 %copy-start = (s32[1,1,3,1]{2,3,1,0:T(1,128)S(1)}, s32[1,1,3,1]{2,3,1,0:T(1,128)}, u32[]{:S(2)}) copy-start(s32[1,1,3,1]{2,3,1,0:T(1,128)} %param.7) | copy-start | bytes 40
  3.8 3.0 %copy-start.1 = (s32[1,1,2]{2,1,0:T(1,128)S(1)}, s32[1,1,2]{2,1,0:T(1,128)}, u32[]{:S(2)}) copy-start(s32[1,1,2]{2,1,0:T(1,128)} %param.8) | copy-start | bytes 28
  3.8 5.5 %collective-permute-start.2 = (bf16[512,256]{1,0:T(8,128)(2,1)S(1)}, bf16[512,256]{1,0:T(8,128)(2,1)S(1)}, u32[]{:S(2)}, u32[]{:S(2)}) collective-permute-start(bf16[512,256]{1,0:T(8,128)(2,1)S(1)} %get-tuple-element.28), channel_id=1, source_target_pairs={{0,1},{1,0},{2,3},{3,2},{4,5},{5,4},{6,7},{7,6},{8,9},{9,8},{10,11... | collective-permute-start | bytes 786440 | tf_op jit(solution)/shard_map/ppermute | solution.py:16
  8.3 11.7 %collective-permute-start.5 = (bf16[512,256]{1,0:T(8,128)(2,1)S(1)}, bf16[512,256]{1,0:T(8,128)(2,1)S(1)}, u32[]{:S(2)}, u32[]{:S(2)}) collective-permute-start(bf16[512,256]{1,0:T(8,128)(2,1)S(1)} %get-tuple-element.36), channel_id=1, source_target_pairs={{0,30},{2,4},{4,2},{6,8},{8,6},{10,12},{12,10},{14,16},{16,14},{18... | collective-permute-start | bytes 786440 | tf_op jit(solution)/shard_map/ppermute | solution.py:26
  16.2 6.9 %collective-permute-start.3 = (bf16[512,128]{1,0:T(8,128)(2,1)S(1)}, bf16[512,128]{1,0:T(8,128)(2,1)S(1)}, u32[]{:S(2)}, u32[]{:S(2)}) collective-permute-start(bf16[512,128]{1,0:T(8,128)(2,1)S(1)} %get-tuple-element.33), channel_id=1, source_target_pairs={{0,30},{2,4},{4,2},{6,8},{8,6},{10,12},{12,10},{14,16},{16,14},{18... | collective-permute-start | bytes 393224 | tf_op jit(solution)/shard_map/ppermute | solution.py:26
  18.7 6.9 %collective-permute-start.7 = (bf16[256,384]{1,0:T(8,128)(2,1)S(1)}, bf16[256,384]{1,0:T(8,128)(2,1)S(1)}, u32[]{:S(2)}, u32[]{:S(2)}) collective-permute-start(bf16[256,384]{1,0:T(8,128)(2,1)S(1)} %get-tuple-element.40), channel_id=1, source_target_pairs={{0,1},{1,0},{2,3},{3,2},{4,5},{5,4},{6,7},{7,6},{8,9},{9,8},{10,11... | collective-permute-start | bytes 589832 | tf_op jit(solution)/shard_map/ppermute | solution.py:16
  20.5 7.9 %collective-permute-start.6 = (bf16[256,256]{1,0:T(8,128)(2,1)S(1)}, bf16[256,256]{1,0:T(8,128)(2,1)S(1)}, u32[]{:S(2)}, u32[]{:S(2)}) collective-permute-start(bf16[256,256]{1,0:T(8,128)(2,1)S(1)} %get-tuple-element.38), channel_id=1, source_target_pairs={{0,1},{1,0},{2,3},{3,2},{4,5},{5,4},{6,7},{7,6},{8,9},{9,8},{10,11... | collective-permute-start | bytes 393224 | tf_op jit(solution)/shard_map/ppermute | solution.py:16
  23.6 5.9 %collective-permute-start.4 = (bf16[256,128]{1,0:T(8,128)(2,1)S(1)}, bf16[256,128]{1,0:T(8,128)(2,1)S(1)}, u32[]{:S(2)}, u32[]{:S(2)}) collective-permute-start(bf16[256,128]{1,0:T(8,128)(2,1)S(1)} %get-tuple-element.35), channel_id=1, source_target_pairs={{0,1},{1,0},{2,3},{3,2},{4,5},{5,4},{6,7},{7,6},{8,9},{9,8},{10,11... | collective-permute-start | bytes 196616 | tf_op jit(solution)/shard_map/ppermute | solution.py:16

commit v11 on v10

--- a/solution.py
+++ b/solution.py
@@ -7,7 +7,7 @@
 from jax.experimental.pallas import tpu as pltpu
 from jax.sharding import PartitionSpec as P
 
-SHARES = (3, 2, 1)
+SHARES = (2, 1)
 TRANSPOSED = (((0,), (0,)), ((), ()))
 
 
@@ -73,10 +73,6 @@
     copy_all([(sketch.at[:, pl.ds(0, part.shape[1])], part), (theirs, lent)], sems)
 
 
-def hand_out(own, part, start):
-    part[...] = own[:, pl.ds(start, part.shape[1])]
-
-
 def stage_kernel(begun, sketch, tiles, basis, own, staged, kept, sems):
     del begun
     ours = half_rows(basis, lax.axis_index("group"), kept.shape[0])
@@ -88,7 +84,7 @@
     owner = owner_route[row_blocks[far]]
     own_hits = owner_route[row_blocks[1]] == owner
     near_hits = owner_route[row_blocks[2 - far]] == owner
-    hand_out(own, part, start)
+    part[...] = own[:, pl.ds(start, part.shape[1])]
     step = 256
     for place in range(0, own.shape[1], step):
         columns = pl.ds(place, step)
@@ -110,10 +106,7 @@
     )
 
 
-def far_kernel(start, next_start, tiles, far, hit, hit_turned, missed, stays, own, *outs):
-    kept, sent, *parts = outs
-    for part in parts:
-        hand_out(own, part, next_start)
+def far_kernel(start, tiles, far, hit, hit_turned, missed, stays, kept, sent):
     columns = pl.ds(start, far.shape[1])
     product = jnp.dot(tiles[far_offset()], far[...], preferred_element_type=jnp.float32)
     sampled = (hit[:, columns] + product).astype(jnp.bfloat16)
@@ -183,19 +176,12 @@
     )
     out = None
     for i, (start, width) in enumerate(zip(starts, widths)):
-        ahead = i + 2
-        more = ahead < len(widths)
-        kept, sent, *parts = call(
-            functools.partial(far_kernel, start, starts[ahead] if more else None),
-            (
-                on_chip((rank, width), wide),
-                on_chip((rank, width), short),
-                *((on_chip((panels, widths[ahead]), short),) if more else ()),
-            ),
-            (tiles, fars[i], hit, hit_turned, missed, stays, own),
+        kept, sent = call(
+            functools.partial(far_kernel, start),
+            (on_chip((rank, width), wide), on_chip((rank, width), short)),
+            (tiles, fars[i], hit, hit_turned, missed, stays),
             2 * product * width // columns,
         )
-        fars += [swap_far(part) for part in parts]
         out = call(
             functools.partial(join_kernel, start),
             pltpu.HBM((rank, columns), wide),

time: 30.6 us -> 29.5 us (0.964)
  waiting for transfers between devices: 10.3 us -> 11.8 us
  starting transfers between devices: 11 us -> 9.74 us
  Pallas kernels: 8.73 us -> 7.62 us
    ppermute x3 -> x2, starting transfers between devices: 6.15 us -> 3.6 us  [swap_far(): lax.ppermute(array, 'blk', [(i, (i + 1 if i % 2 else i - 1) % devices) fo...]
    ppermute x4 -> x3, starting transfers between devices: 4.77 us -> 6.08 us  [from_behind(): lax.ppermute(array, axis, [(i, (i + by) % devices) for i in range(devices)])]
    ppermute x3 -> x2, waiting for transfers between devices: 7.23 us -> 8.53 us  [swap_far(): lax.ppermute(array, 'blk', [(i, (i + 1 if i % 2 else i - 1) % devices) fo...]
    pallas_call x10 -> x8, Pallas kernels: 8.73 us -> 7.62 us  [call(): pl.pallas_call(kernel, out_shape=out_shape, in_specs=[scalar] * len(scala...]
    ppermute x4 -> x3, waiting for transfers between devices: 3.07 us -> 3.31 us  [from_behind(): lax.ppermute(array, axis, [(i, (i + by) % devices) for i in range(devices)])]
  transfers between devices with their start and end apart: 8 -> 6, of which waited for: 5 -> 3; matrix products, arithmetic and copies ran while one was open for 0% -> 0% of each run, Pallas kernels for 27% -> 24%
where the time goes in v11:
time: 29.5 us; the launch traced here: 29.3 us
  waiting for transfers between devices  11.8 us (40%)
  starting transfers between devices  9.74 us (33%)
  Pallas kernels  7.62 us (26%)
    ppermute x2, waiting for transfers between devices, swap_far(): lax.ppermute(array, 'blk', [(i, (i + 1 if i % 2 else i - 1) % devices) fo...  8.53 us
    pallas_call x8, Pallas kernels, call(): pl.pallas_call(kernel, out_shape=out_shape, in_specs=[scalar] * len(scala...  7.62 us
    ppermute x3, starting transfers between devices, from_behind(): lax.ppermute(array, axis, [(i, (i + by) % devices) for i in range(devices)])  6.08 us
    ppermute x2, starting transfers between devices, swap_far(): lax.ppermute(array, 'blk', [(i, (i + 1 if i % 2 else i - 1) % devices) fo...  3.6 us
    ppermute x3, waiting for transfers between devices, from_behind(): lax.ppermute(array, axis, [(i, (i + by) % devices) for i in range(devices)])  3.31 us
  transfers between devices with their start and end apart: 6, of which 3 were waited for; matrix products, arithmetic and copies ran while one was open for 0% of the time, Pallas kernels for 24%

profile of v11, /device:TPU:1, one launch (start us, length us, event | category | flops | bytes accessed | tf_op | source)
XLA Modules:
  0.0 29.3 jit_solution(8793588420670214084)
XLA Ops:
  0.0 0.1 collective-permute-start
  0.1 1.1 %shard_map.55 = (bf16[512,256]{1,0:T(8,128)(2,1)S(1)}, bf16[512,512]{1,0:T(8,128)(2,1)S(1)}) custom-call(bf16[512,768]{1,0:T(8,128)(2,1)} %sketch.3, bf16[1,1,1024,256]{3,2,1,0:T(8,128)(2,1)} %basis.3), custom_call_target="tpu_custom_call" | custom-call | bytes 1048576 | tf_op jit(solution)/shard_map/pallas_call | solution.py:43
  1.2 2.6 %collective-permute-start.4 = (bf16[512,512]{1,0:T(8,128)(2,1)S(1)}, bf16[512,512]{1,0:T(8,128)(2,1)S(1)}, u32[]{:S(2)}, u32[]{:S(2)}) collective-permute-start(bf16[512,512]{1,0:T(8,128)(2,1)S(1)} %get-tuple-element.20.begun), channel_id=1, source_target_pairs={{0,30},{2,4},{4,2},{6,8},{8,6},{10,12},{12,10},{14,16},{16,14},{18... | collective-permute-start | bytes 1572872 | tf_op jit(solution)/shard_map/ppermute | solution.py:26
  3.8 0.0 copy-start
  3.8 0.0 copy-start.1
  3.8 1.2 %collective-permute-start.2 = (bf16[512,256]{1,0:T(8,128)(2,1)S(1)}, bf16[512,256]{1,0:T(8,128)(2,1)S(1)}, u32[]{:S(2)}, u32[]{:S(2)}) collective-permute-start(bf16[512,256]{1,0:T(8,128)(2,1)S(1)} %get-tuple-element.26), channel_id=1, source_target_pairs={{0,1},{1,0},{2,3},{3,2},{4,5},{5,4},{6,7},{7,6},{8,9},{9,8},{10,11... | collective-permute-start | bytes 786440 | tf_op jit(solution)/shard_map/ppermute | solution.py:16
  5.0 1.7 %shard_map.56 = (bf16[512,768]{1,0:T(8,128)(2,1)S(1)}, bf16[3,512,512]{2,1,0:T(8,128)(2,1)S(1)}, bf16[512,256]{1,0:T(8,128)(2,1)S(1)}) custom-call(bf16[512,512]{1,0:T(8,128)(2,1)S(1)} %get-tuple-element.20.begun, bf16[512,768]{1,0:T(8,128)(2,1)} %sketch.3, bf16[1,1,3,1,512,512]{5,4,3,2,1,0:T(8,128)(2,1)} %tiles.1, bf16[1,1,1024,256]{3,2,1,0:T(8,128)(2,1)} %basis.3), custom_call_target="tpu_custom_call" | custom-call | bytes 1048576 | tf_op jit(solution)/shard_map/pallas_call | solution.py:43
  6.7 0.0 collective-permute-done.near
  6.7 0.0 copy-done
  6.8 0.0 copy-done.1
  6.8 1.5 %shard_map.57 = (f32[512,768]{1,0:T(8,128)S(1)}, bf16[512,768]{1,0:T(8,128)(2,1)S(1)}, f32[1,768]{1,0:T(1,128)S(1)}, bf16[512,256]{1,0:T(8,128)(2,1)S(1)}) custom-call(s32[3]{0:T(128)S(1)} %bitcast.3, s32[2]{0:T(128)S(1)} %bitcast.4, bf16[3,512,512]{2,1,0:T(8,128)(2,1)S(1)} %get-tuple-element.21.tiles, bf16[512,768]{1,0:T(8,128)(2,1)S(1)} %get-tuple-element.22.own, ...), custom_call_target="tpu_custom_call" | custom-call | flops 805306368 | bytes 1048576 | tf_op jit(solution)/shard_map/pallas_call | solution.py:43
  8.3 1.0 %collective-permute-start.1 = (bf16[512,256]{1,0:T(8,128)(2,1)S(1)}, bf16[512,256]{1,0:T(8,128)(2,1)S(1)}, u32[]{:S(2)}, u32[]{:S(2)}) collective-permute-start(bf16[512,256]{1,0:T(8,128)(2,1)S(1)} %get-tuple-element.23), channel_id=1, source_target_pairs={{0,30},{2,4},{4,2},{6,8},{8,6},{10,12},{12,10},{14,16},{16,14},{18... | collective-permute-start | bytes 786440 | tf_op jit(solution)/shard_map/ppermute | solution.py:26
  9.3 0.0 collective-permute-done.2.lent
  9.3 0.5 %shard_map.58 = (bf16[256,512]{1,0:T(8,128)(2,1)S(1)}, f32[256,768]{1,0:T(8,128)S(1)}) custom-call(bf16[512,256]{1,0:T(8,128)(2,1)S(1)} %get-tuple-element.25.kept, bf16[512,256]{1,0:T(8,128)(2,1)S(1)} %collective-permute-done.2.lent, bf16[512,768]{1,0:T(8,128)(2,1)S(1)} %get-tuple-element.27.miss, f32[1,768]{1,0:T(1,128)S(1)} %get-tuple-element.28.stays), custom_call_target="tpu_custom_call" | custom-call | flops 201326592 | bytes 1048576 | tf_op jit(solution)/shard_map/pallas_call | solution.py:43
  9.8 8.5 %collective-permute-done.4.far = bf16[512,512]{1,0:T(8,128)(2,1)S(1)} collective-permute-done((bf16[512,512]{1,0:T(8,128)(2,1)S(1)}, bf16[512,512]{1,0:T(8,128)(2,1)S(1)}, u32[]{:S(2)}, u32[]{:S(2)}) %collective-permute-start.4) | collective-permute-done | bytes 524320 | tf_op jit(solution)/shard_map/ppermute | solution.py:26
  18.4 0.6 %shard_map.60 = (f32[256,512]{1,0:T(8,128)S(1)}, bf16[256,512]{1,0:T(8,128)(2,1)S(1)}) custom-call(bf16[3,512,512]{2,1,0:T(8,128)(2,1)S(1)} %get-tuple-element.21.tiles, bf16[512,512]{1,0:T(8,128)(2,1)S(1)} %collective-permute-done.4.far, f32[512,768]{1,0:T(8,128)S(1)} %get-tuple-element.24.hit, bf16[256,512]{1,0:T(8,128)(2,1)S(1)} %get-tuple-element.29.hit_turned, ...), custom_call_target="tpu_custom_call" | custom-call | flops 536870912 | bytes 1048576 | tf_op jit(solution)/shard_map/pallas_call | solution.py:43
  19.0 3.0 %collective-permute-start.5 = (bf16[256,512]{1,0:T(8,128)(2,1)S(1)}, bf16[256,512]{1,0:T(8,128)(2,1)S(1)}, u32[]{:S(2)}, u32[]{:S(2)}) collective-permute-start(bf16[256,512]{1,0:T(8,128)(2,1)S(1)} %get-tuple-element.34), channel_id=1, source_target_pairs={{0,1},{1,0},{2,3},{3,2},{4,5},{5,4},{6,7},{7,6},{8,9},{9,8},{10,11... | collective-permute-start | bytes 786440 | tf_op jit(solution)/shard_map/ppermute | solution.py:16
  22.0 0.0 collective-permute-done.1.far
  22.0 0.6 %shard_map.59 = (f32[256,256]{1,0:T(8,128)S(1)}, bf16[256,256]{1,0:T(8,128)(2,1)S(1)}) custom-call(bf16[3,512,512]{2,1,0:T(8,128)(2,1)S(1)} %get-tuple-element.21.tiles, bf16[512,256]{1,0:T(8,128)(2,1)S(1)} %collective-permute-done.1.far, f32[512,768]{1,0:T(8,128)S(1)} %get-tuple-element.24.hit, bf16[256,512]{1,0:T(8,128)(2,1)S(1)} %get-tuple-element.29.hit_turned, ...), custom_call_target="tpu_custom_call" | custom-call | flops 268435456 | bytes 1048576 | tf_op jit(solution)/shard_map/pallas_call | solution.py:43
  22.6 1.9 %collective-permute-start.3 = (bf16[256,256]{1,0:T(8,128)(2,1)S(1)}, bf16[256,256]{1,0:T(8,128)(2,1)S(1)}, u32[]{:S(2)}, u32[]{:S(2)}) collective-permute-start(bf16[256,256]{1,0:T(8,128)(2,1)S(1)} %get-tuple-element.32), channel_id=1, source_target_pairs={{0,1},{1,0},{2,3},{3,2},{4,5},{5,4},{6,7},{7,6},{8,9},{9,8},{10,11... | collective-permute-start | bytes 393224 | tf_op jit(solution)/shard_map/ppermute | solution.py:16
  24.4 3.0 %collective-permute-done.5.received = bf16[256,512]{1,0:T(8,128)(2,1)S(1)} collective-permute-done((bf16[256,512]{1,0:T(8,128)(2,1)S(1)}, bf16[256,512]{1,0:T(8,128)(2,1)S(1)}, u32[]{:S(2)}, u32[]{:S(2)}) %collective-permute-start.5) | collective-permute-done | bytes 262176 | tf_op jit(solution)/shard_map/ppermute | solution.py:16
  27.4 0.8 %shard_map.61.rest_0_ = f32[256,768]{1,0:T(8,128)} custom-call(f32[256,512]{1,0:T(8,128)S(1)} %get-tuple-element.33.kept, bf16[256,512]{1,0:T(8,128)(2,1)S(1)} %collective-permute-done.5.received), custom_call_target="tpu_custom_call" | custom-call | flops 65536 | bytes 1048576 | tf_op jit(solution)/shard_map/pallas_call | solution.py:43
  28.3 0.3 collective-permute-done.3.received
  28.6 0.7 %shard_map.62 = f32[256,768]{1,0:T(8,128)} custom-call(f32[256,256]{1,0:T(8,128)S(1)} %get-tuple-element.31.kept, bf16[256,256]{1,0:T(8,128)(2,1)S(1)} %collective-permute-done.3.received, f32[256,768]{1,0:T(8,128)} %shard_map.61.rest_0_), custom_call_target="tpu_custom_call", output_to_operand_aliasing={{}: (2, {})} | custom-call | flops 65536 | bytes 1048576 | tf_op jit(solution)/shard_map/pallas_call | solution.py:43
Async XLA Ops:
  0.0 6.7 %collective-permute-start = (bf16[512,768]{1,0:T(8,128)(2,1)}, bf16[512,768]{1,0:T(8,128)(2,1)S(1)}, u32[]{:S(2)}, u32[]{:S(2)}) collective-permute-start(bf16[512,768]{1,0:T(8,128)(2,1)} %sketch.3), channel_id=1, source_target_pairs={{0,2},{2,0},{4,6},{6,4},{8,10},{10,8},{12,14},{14,12},{16,18},{18,... | collective-permute-start | bytes 2359304 | tf_op jit(solution)/shard_map/ppermute | solution.py:21
  1.2 17.2 %collective-permute-start.4 = (bf16[512,512]{1,0:T(8,128)(2,1)S(1)}, bf16[512,512]{1,0:T(8,128)(2,1)S(1)}, u32[]{:S(2)}, u32[]{:S(2)}) collective-permute-start(bf16[512,512]{1,0:T(8,128)(2,1)S(1)} %get-tuple-element.20.begun), channel_id=1, source_target_pairs={{0,30},{2,4},{4,2},{6,8},{8,6},{10,12},{12,10},{14,16},{16,14},{18... | collective-permute-start | bytes 1572872 | tf_op jit(solution)/shard_map/ppermute | solution.py:26
  3.8 2.9 %copy-start = (s32[1,1,3,1]{2,3,1,0:T(1,128)S(1)}, s32[1,1,3,1]{2,3,1,0:T(1,128)}, u32[]{:S(2)}) copy-start(s32[1,1,3,1]{2,3,1,0:T(1,128)} %param.7) | copy-start | bytes 40
  3.8 3.0 %copy-start.1 = (s32[1,1,2]{2,1,0:T(1,128)S(1)}, s32[1,1,2]{2,1,0:T(1,128)}, u32[]{:S(2)}) copy-start(s32[1,1,2]{2,1,0:T(1,128)} %param.8) | copy-start | bytes 28
  3.8 5.5 %collective-permute-start.2 = (bf16[512,256]{1,0:T(8,128)(2,1)S(1)}, bf16[512,256]{1,0:T(8,128)(2,1)S(1)}, u32[]{:S(2)}, u32[]{:S(2)}) collective-permute-start(bf16[512,256]{1,0:T(8,128)(2,1)S(1)} %get-tuple-element.26), channel_id=1, source_target_pairs={{0,1},{1,0},{2,3},{3,2},{4,5},{5,4},{6,7},{7,6},{8,9},{9,8},{10,11... | collective-permute-start | bytes 786440 | tf_op jit(solution)/shard_map/ppermute | solution.py:16
  8.3 13.7 %collective-permute-start.1 = (bf16[512,256]{1,0:T(8,128)(2,1)S(1)}, bf16[512,256]{1,0:T(8,128)(2,1)S(1)}, u32[]{:S(2)}, u32[]{:S(2)}) collective-permute-start(bf16[512,256]{1,0:T(8,128)(2,1)S(1)} %get-tuple-element.23), channel_id=1, source_target_pairs={{0,30},{2,4},{4,2},{6,8},{8,6},{10,12},{12,10},{14,16},{16,14},{18... | collective-permute-start | bytes 786440 | tf_op jit(solution)/shard_map/ppermute | solution.py:26
  19.0 8.4 %collective-permute-start.5 = (bf16[256,512]{1,0:T(8,128)(2,1)S(1)}, bf16[256,512]{1,0:T(8,128)(2,1)S(1)}, u32[]{:S(2)}, u32[]{:S(2)}) collective-permute-start(bf16[256,512]{1,0:T(8,128)(2,1)S(1)} %get-tuple-element.34), channel_id=1, source_target_pairs={{0,1},{1,0},{2,3},{3,2},{4,5},{5,4},{6,7},{7,6},{8,9},{9,8},{10,11... | collective-permute-start | bytes 786440 | tf_op jit(solution)/shard_map/ppermute | solution.py:16
  22.6 6.0 %collective-permute-start.3 = (bf16[256,256]{1,0:T(8,128)(2,1)S(1)}, bf16[256,256]{1,0:T(8,128)(2,1)S(1)}, u32[]{:S(2)}, u32[]{:S(2)}) collective-permute-start(bf16[256,256]{1,0:T(8,128)(2,1)S(1)} %get-tuple-element.32), channel_id=1, source_target_pairs={{0,1},{1,0},{2,3},{3,2},{4,5},{5,4},{6,7},{7,6},{8,9},{9,8},{10,11... | collective-permute-start | bytes 393224 | tf_op jit(solution)/shard_map/ppermute | solution.py:16

commit v12 on v11

--- a/solution.py
+++ b/solution.py
@@ -7,7 +7,7 @@
 from jax.experimental.pallas import tpu as pltpu
 from jax.sharding import PartitionSpec as P
 
-SHARES = (2, 1)
+SHARES = (3, 2, 1)
 TRANSPOSED = (((0,), (0,)), ((), ()))
 
 
@@ -97,7 +97,8 @@
     stays[...] = jnp.full(stays.shape, jnp.where(owner == lax.axis_index("group"), 1.0, 0.0))
 
 
-def turn_kernel(kept, lent, miss, stays, hit_turned, missed):
+def turn_kernel(start, kept, lent, miss, stays, own, hit_turned, missed, part):
+    part[...] = own[:, pl.ds(start, part.shape[1])]
     stay = stays[:, pl.ds(0, kept.shape[0])] > 0.0
     ours, theirs = kept[...].T, lent[...].T
     hit_turned[...] = jnp.where(stay, ours, theirs)
@@ -168,12 +169,17 @@
         scalars=(row_blocks.reshape(-1), owner_route.reshape(-1)),
     )
     fars.append(swap_far(part))
-    hit_turned, missed = call(
-        turn_kernel,
-        (on_chip((rank, half), short), on_chip((rank, columns), wide)),
-        (kept, lent, miss, stays),
+    hit_turned, missed, part = call(
+        functools.partial(turn_kernel, starts[2]),
+        (
+            on_chip((rank, half), short),
+            on_chip((rank, columns), wide),
+            on_chip((panels, widths[2]), short),
+        ),
+        (kept, lent, miss, stays, own),
         product // 2,
     )
+    fars.append(swap_far(part))
     out = None
     for i, (start, width) in enumerate(zip(starts, widths)):
         kept, sent = call(

time: 29.5 us -> 29.9 us (1.014); the launches traced: 29.3 us -> 29.3 us
  waiting for transfers between devices: 11.8 us -> 7.12 us
  starting transfers between devices: 9.74 us -> 13.4 us
  Pallas kernels: 7.62 us -> 8.69 us
    ppermute x2 -> x3, waiting for transfers between devices: 8.53 us -> 4.59 us  [swap_far(): lax.ppermute(array, 'blk', [(i, (i + 1 if i % 2 else i - 1) % devices) fo...]
    ppermute x2 -> x3, starting transfers between devices: 3.6 us -> 6.99 us  [swap_far(): lax.ppermute(array, 'blk', [(i, (i + 1 if i % 2 else i - 1) % devices) fo...]
    pallas_call x8 -> x10, Pallas kernels: 7.62 us -> 8.69 us  [call(): pl.pallas_call(kernel, out_shape=out_shape, in_specs=[scalar] * len(scala...]
    ppermute x3 -> x4, waiting for transfers between devices: 3.31 us -> 2.53 us  [from_behind(): lax.ppermute(array, axis, [(i, (i + by) % devices) for i in range(devices)])]
    ppermute x3 -> x4, starting transfers between devices: 6.08 us -> 6.37 us  [from_behind(): lax.ppermute(array, axis, [(i, (i + by) % devices) for i in range(devices)])]
  transfers between devices with their start and end apart: 6 -> 8, of which waited for: 3 -> 4; matrix products, arithmetic and copies ran while one was open for 0% -> 0% of each run, Pallas kernels for 24% -> 27%
where the time goes in v12:
time: 29.9 us; the launch traced here: 29.3 us
  starting transfers between devices  13.4 us (45%)
  Pallas kernels  8.69 us (29%)
  waiting for transfers between devices  7.12 us (24%)
    pallas_call x10, Pallas kernels, call(): pl.pallas_call(kernel, out_shape=out_shape, in_specs=[scalar] * len(scala...  8.69 us
    ppermute x3, starting transfers between devices, swap_far(): lax.ppermute(array, 'blk', [(i, (i + 1 if i % 2 else i - 1) % devices) fo...  6.99 us
    ppermute x4, starting transfers between devices, from_behind(): lax.ppermute(array, axis, [(i, (i + by) % devices) for i in range(devices)])  6.37 us
    ppermute x3, waiting for transfers between devices, swap_far(): lax.ppermute(array, 'blk', [(i, (i + 1 if i % 2 else i - 1) % devices) fo...  4.59 us
    ppermute x4, waiting for transfers between devices, from_behind(): lax.ppermute(array, axis, [(i, (i + by) % devices) for i in range(devices)])  2.53 us
  transfers between devices with their start and end apart: 8, of which 4 were waited for; matrix products, arithmetic and copies ran while one was open for 0% of the time, Pallas kernels for 27%

profile of v12, /device:TPU:1, one launch (start us, length us, event | category | flops | bytes accessed | tf_op | source)
XLA Modules:
  0.0 29.3 jit_solution(2869518475134317732)
XLA Ops:
  0.0 0.1 collective-permute-start.1
  0.1 1.1 %shard_map.55 = (bf16[512,256]{1,0:T(8,128)(2,1)S(1)}, bf16[512,384]{1,0:T(8,128)(2,1)S(1)}) custom-call(bf16[512,768]{1,0:T(8,128)(2,1)} %sketch.3, bf16[1,1,1024,256]{3,2,1,0:T(8,128)(2,1)} %basis.3), custom_call_target="tpu_custom_call" | custom-call | bytes 1048576 | tf_op jit(solution)/shard_map/pallas_call | solution.py:43
  1.2 2.6 %collective-permute-start.6 = (bf16[512,384]{1,0:T(8,128)(2,1)S(1)}, bf16[512,384]{1,0:T(8,128)(2,1)S(1)}, u32[]{:S(2)}, u32[]{:S(2)}) collective-permute-start(bf16[512,384]{1,0:T(8,128)(2,1)S(1)} %get-tuple-element.23.begun), channel_id=1, source_target_pairs={{0,30},{2,4},{4,2},{6,8},{8,6},{10,12},{12,10},{14,16},{16,14},{18... | collective-permute-start | bytes 1179656 | tf_op jit(solution)/shard_map/ppermute | solution.py:26
  3.8 0.0 copy-start
  3.8 0.0 copy-start.1
  3.8 1.2 %collective-permute-start = (bf16[512,256]{1,0:T(8,128)(2,1)S(1)}, bf16[512,256]{1,0:T(8,128)(2,1)S(1)}, u32[]{:S(2)}, u32[]{:S(2)}) collective-permute-start(bf16[512,256]{1,0:T(8,128)(2,1)S(1)} %get-tuple-element.26), channel_id=1, source_target_pairs={{0,1},{1,0},{2,3},{3,2},{4,5},{5,4},{6,7},{7,6},{8,9},{9,8},{10,11... | collective-permute-start | bytes 786440 | tf_op jit(solution)/shard_map/ppermute | solution.py:16
  5.0 1.7 %shard_map.56 = (bf16[512,768]{1,0:T(8,128)(2,1)S(1)}, bf16[3,512,512]{2,1,0:T(8,128)(2,1)S(1)}, bf16[512,256]{1,0:T(8,128)(2,1)S(1)}) custom-call(bf16[512,384]{1,0:T(8,128)(2,1)S(1)} %get-tuple-element.23.begun, bf16[512,768]{1,0:T(8,128)(2,1)} %sketch.3, bf16[1,1,3,1,512,512]{5,4,3,2,1,0:T(8,128)(2,1)} %tiles.1, bf16[1,1,1024,256]{3,2,1,0:T(8,128)(2,1)} %basis.3), custom_call_target="tpu_custom_call" | custom-call | bytes 1048576 | tf_op jit(solution)/shard_map/pallas_call | solution.py:43
  6.7 0.0 collective-permute-done.1.near
  6.7 0.0 copy-done
  6.7 0.0 copy-done.1
  6.7 1.5 %shard_map.57 = (f32[512,768]{1,0:T(8,128)S(1)}, bf16[512,768]{1,0:T(8,128)(2,1)S(1)}, f32[1,768]{1,0:T(1,128)S(1)}, bf16[512,256]{1,0:T(8,128)(2,1)S(1)}) custom-call(s32[3]{0:T(128)S(1)} %bitcast.3, s32[2]{0:T(128)S(1)} %bitcast.4, bf16[3,512,512]{2,1,0:T(8,128)(2,1)S(1)} %get-tuple-element.24.tiles, bf16[512,768]{1,0:T(8,128)(2,1)S(1)} %get-tuple-element.27.own, ...), custom_call_target="tpu_custom_call" | custom-call | flops 805306368 | bytes 1048576 | tf_op jit(solution)/shard_map/pallas_call | solution.py:43
  8.3 1.0 %collective-permute-start.4 = (bf16[512,256]{1,0:T(8,128)(2,1)S(1)}, bf16[512,256]{1,0:T(8,128)(2,1)S(1)}, u32[]{:S(2)}, u32[]{:S(2)}) collective-permute-start(bf16[512,256]{1,0:T(8,128)(2,1)S(1)} %get-tuple-element.36), channel_id=1, source_target_pairs={{0,30},{2,4},{4,2},{6,8},{8,6},{10,12},{12,10},{14,16},{16,14},{18... | collective-permute-start | bytes 786440 | tf_op jit(solution)/shard_map/ppermute | solution.py:26
  9.3 0.0 collective-permute-done.lent
  9.3 0.5 %shard_map.58 = (bf16[256,512]{1,0:T(8,128)(2,1)S(1)}, f32[256,768]{1,0:T(8,128)S(1)}, bf16[512,128]{1,0:T(8,128)(2,1)S(1)}) custom-call(bf16[512,256]{1,0:T(8,128)(2,1)S(1)} %get-tuple-element.25.kept, bf16[512,256]{1,0:T(8,128)(2,1)S(1)} %collective-permute-done.lent, bf16[512,768]{1,0:T(8,128)(2,1)S(1)} %get-tuple-element.28.miss, ...), custom_call_target="tpu_custom_call" | custom-call | flops 201326592 | bytes 1048576 | tf_op jit(solution)/shard_map/pallas_call | solution.py:43
  9.8 3.4 %collective-permute-start.2 = (bf16[512,128]{1,0:T(8,128)(2,1)S(1)}, bf16[512,128]{1,0:T(8,128)(2,1)S(1)}, u32[]{:S(2)}, u32[]{:S(2)}) collective-permute-start(bf16[512,128]{1,0:T(8,128)(2,1)S(1)} %get-tuple-element.30), channel_id=1, source_target_pairs={{0,30},{2,4},{4,2},{6,8},{8,6},{10,12},{12,10},{14,16},{16,14},{18... | collective-permute-start | bytes 393224 | tf_op jit(solution)/shard_map/ppermute | solution.py:26
  13.2 2.3 %collective-permute-done.6.far = bf16[512,384]{1,0:T(8,128)(2,1)S(1)} collective-permute-done((bf16[512,384]{1,0:T(8,128)(2,1)S(1)}, bf16[512,384]{1,0:T(8,128)(2,1)S(1)}, u32[]{:S(2)}, u32[]{:S(2)}) %collective-permute-start.6) | collective-permute-done | bytes 393248 | tf_op jit(solution)/shard_map/ppermute | solution.py:26
  15.5 0.7 %shard_map.61 = (f32[256,384]{1,0:T(8,128)S(1)}, bf16[256,384]{1,0:T(8,128)(2,1)S(1)}) custom-call(bf16[3,512,512]{2,1,0:T(8,128)(2,1)S(1)} %get-tuple-element.24.tiles, bf16[512,384]{1,0:T(8,128)(2,1)S(1)} %collective-permute-done.6.far, f32[512,768]{1,0:T(8,128)S(1)} %get-tuple-element.31.hit, bf16[256,512]{1,0:T(8,128)(2,1)S(1)} %get-tuple-element.32.hit_turned, ...), custom_call_target="tpu_custom_call" | custom-call | flops 402653184 | bytes 1048576 | tf_op jit(solution)/shard_map/pallas_call | solution.py:43
  16.2 1.3 %collective-permute-start.7 = (bf16[256,384]{1,0:T(8,128)(2,1)S(1)}, bf16[256,384]{1,0:T(8,128)(2,1)S(1)}, u32[]{:S(2)}, u32[]{:S(2)}) collective-permute-start(bf16[256,384]{1,0:T(8,128)(2,1)S(1)} %get-tuple-element.40), channel_id=1, source_target_pairs={{0,1},{1,0},{2,3},{3,2},{4,5},{5,4},{6,7},{7,6},{8,9},{9,8},{10,11... | collective-permute-start | bytes 589832 | tf_op jit(solution)/shard_map/ppermute | solution.py:16
  17.5 2.2 %collective-permute-done.4.far = bf16[512,256]{1,0:T(8,128)(2,1)S(1)} collective-permute-done((bf16[512,256]{1,0:T(8,128)(2,1)S(1)}, bf16[512,256]{1,0:T(8,128)(2,1)S(1)}, u32[]{:S(2)}, u32[]{:S(2)}) %collective-permute-start.4) | collective-permute-done | bytes 262176 | tf_op jit(solution)/shard_map/ppermute | solution.py:26
  19.7 0.5 %shard_map.60 = (f32[256,256]{1,0:T(8,128)S(1)}, bf16[256,256]{1,0:T(8,128)(2,1)S(1)}) custom-call(bf16[3,512,512]{2,1,0:T(8,128)(2,1)S(1)} %get-tuple-element.24.tiles, bf16[512,256]{1,0:T(8,128)(2,1)S(1)} %collective-permute-done.4.far, f32[512,768]{1,0:T(8,128)S(1)} %get-tuple-element.31.hit, bf16[256,512]{1,0:T(8,128)(2,1)S(1)} %get-tuple-element.32.hit_turned, ...), custom_call_target="tpu_custom_call" | custom-call | flops 268435456 | bytes 1048576 | tf_op jit(solution)/shard_map/pallas_call | solution.py:43
  20.3 3.0 %collective-permute-start.5 = (bf16[256,256]{1,0:T(8,128)(2,1)S(1)}, bf16[256,256]{1,0:T(8,128)(2,1)S(1)}, u32[]{:S(2)}, u32[]{:S(2)}) collective-permute-start(bf16[256,256]{1,0:T(8,128)(2,1)S(1)} %get-tuple-element.38), channel_id=1, source_target_pairs={{0,1},{1,0},{2,3},{3,2},{4,5},{5,4},{6,7},{7,6},{8,9},{9,8},{10,11... | collective-permute-start | bytes 393224 | tf_op jit(solution)/shard_map/ppermute | solution.py:16
  23.3 0.0 collective-permute-done.2.far
  23.3 0.5 %shard_map.59 = (f32[256,128]{1,0:T(8,128)S(1)}, bf16[256,128]{1,0:T(8,128)(2,1)S(1)}) custom-call(bf16[3,512,512]{2,1,0:T(8,128)(2,1)S(1)} %get-tuple-element.24.tiles, bf16[512,128]{1,0:T(8,128)(2,1)S(1)} %collective-permute-done.2.far, f32[512,768]{1,0:T(8,128)S(1)} %get-tuple-element.31.hit, bf16[256,512]{1,0:T(8,128)(2,1)S(1)} %get-tuple-element.32.hit_turned, ...), custom_call_target="tpu_custom_call" | custom-call | flops 134217728 | bytes 1048576 | tf_op jit(solution)/shard_map/pallas_call | solution.py:43
  23.7 0.8 %collective-permute-start.3 = (bf16[256,128]{1,0:T(8,128)(2,1)S(1)}, bf16[256,128]{1,0:T(8,128)(2,1)S(1)}, u32[]{:S(2)}, u32[]{:S(2)}) collective-permute-start(bf16[256,128]{1,0:T(8,128)(2,1)S(1)} %get-tuple-element.35), channel_id=1, source_target_pairs={{0,1},{1,0},{2,3},{3,2},{4,5},{5,4},{6,7},{7,6},{8,9},{9,8},{10,11... | collective-permute-start | bytes 196616 | tf_op jit(solution)/shard_map/ppermute | solution.py:16
  24.6 0.0 collective-permute-done.7.received
  24.6 0.8 %shard_map.62.rest_0_ = f32[256,768]{1,0:T(8,128)} custom-call(f32[256,384]{1,0:T(8,128)S(1)} %get-tuple-element.39.kept, bf16[256,384]{1,0:T(8,128)(2,1)S(1)} %collective-permute-done.7.received), custom_call_target="tpu_custom_call" | custom-call | flops 65536 | bytes 1048576 | tf_op jit(solution)/shard_map/pallas_call | solution.py:43
  25.4 1.9 %collective-permute-done.5.received = bf16[256,256]{1,0:T(8,128)(2,1)S(1)} collective-permute-done((bf16[256,256]{1,0:T(8,128)(2,1)S(1)}, bf16[256,256]{1,0:T(8,128)(2,1)S(1)}, u32[]{:S(2)}, u32[]{:S(2)}) %collective-permute-start.5) | collective-permute-done | bytes 131104 | tf_op jit(solution)/shard_map/ppermute | solution.py:16
  27.3 0.7 %shard_map.63.rest_0_ = f32[256,768]{1,0:T(8,128)} custom-call(f32[256,256]{1,0:T(8,128)S(1)} %get-tuple-element.37.kept, bf16[256,256]{1,0:T(8,128)(2,1)S(1)} %collective-permute-done.5.received, f32[256,768]{1,0:T(8,128)} %shard_map.62.rest_0_), custom_call_target="tpu_custom_call", output_to_operand_aliasing={{}: (2, {})} | custom-call | flops 65536 | bytes 1048576 | tf_op jit(solution)/shard_map/pallas_call | solution.py:43
  28.0 0.7 %collective-permute-done.3.received = bf16[256,128]{1,0:T(8,128)(2,1)S(1)} collective-permute-done((bf16[256,128]{1,0:T(8,128)(2,1)S(1)}, bf16[256,128]{1,0:T(8,128)(2,1)S(1)}, u32[]{:S(2)}, u32[]{:S(2)}) %collective-permute-start.3) | collective-permute-done | bytes 65568 | tf_op jit(solution)/shard_map/ppermute | solution.py:16
  28.7 0.7 %shard_map.64 = f32[256,768]{1,0:T(8,128)} custom-call(f32[256,128]{1,0:T(8,128)S(1)} %get-tuple-element.34.kept, bf16[256,128]{1,0:T(8,128)(2,1)S(1)} %collective-permute-done.3.received, f32[256,768]{1,0:T(8,128)} %shard_map.63.rest_0_), custom_call_target="tpu_custom_call", output_to_operand_aliasing={{}: (2, {})} | custom-call | flops 65536 | bytes 1048576 | tf_op jit(solution)/shard_map/pallas_call | solution.py:43
Async XLA Ops:
  0.0 6.7 %collective-permute-start.1 = (bf16[512,768]{1,0:T(8,128)(2,1)}, bf16[512,768]{1,0:T(8,128)(2,1)S(1)}, u32[]{:S(2)}, u32[]{:S(2)}) collective-permute-start(bf16[512,768]{1,0:T(8,128)(2,1)} %sketch.3), channel_id=1, source_target_pairs={{0,2},{2,0},{4,6},{6,4},{8,10},{10,8},{12,14},{14,12},{16,18},{18,... | collective-permute-start | bytes 2359304 | tf_op jit(solution)/shard_map/ppermute | solution.py:21
  1.2 14.4 %collective-permute-start.6 = (bf16[512,384]{1,0:T(8,128)(2,1)S(1)}, bf16[512,384]{1,0:T(8,128)(2,1)S(1)}, u32[]{:S(2)}, u32[]{:S(2)}) collective-permute-start(bf16[512,384]{1,0:T(8,128)(2,1)S(1)} %get-tuple-element.23.begun), channel_id=1, source_target_pairs={{0,30},{2,4},{4,2},{6,8},{8,6},{10,12},{12,10},{14,16},{16,14},{18... | collective-permute-start | bytes 1179656 | tf_op jit(solution)/shard_map/ppermute | solution.py:26
  3.8 2.9 %copy-start = (s32[1,1,3,1]{2,3,1,0:T(1,128)S(1)}, s32[1,1,3,1]{2,3,1,0:T(1,128)}, u32[]{:S(2)}) copy-start(s32[1,1,3,1]{2,3,1,0:T(1,128)} %param.7) | copy-start | bytes 40
  3.8 3.0 %copy-start.1 = (s32[1,1,2]{2,1,0:T(1,128)S(1)}, s32[1,1,2]{2,1,0:T(1,128)}, u32[]{:S(2)}) copy-start(s32[1,1,2]{2,1,0:T(1,128)} %param.8) | copy-start | bytes 28
  3.8 5.5 %collective-permute-start = (bf16[512,256]{1,0:T(8,128)(2,1)S(1)}, bf16[512,256]{1,0:T(8,128)(2,1)S(1)}, u32[]{:S(2)}, u32[]{:S(2)}) collective-permute-start(bf16[512,256]{1,0:T(8,128)(2,1)S(1)} %get-tuple-element.26), channel_id=1, source_target_pairs={{0,1},{1,0},{2,3},{3,2},{4,5},{5,4},{6,7},{7,6},{8,9},{9,8},{10,11... | collective-permute-start | bytes 786440 | tf_op jit(solution)/shard_map/ppermute | solution.py:16
  8.3 11.4 %collective-permute-start.4 = (bf16[512,256]{1,0:T(8,128)(2,1)S(1)}, bf16[512,256]{1,0:T(8,128)(2,1)S(1)}, u32[]{:S(2)}, u32[]{:S(2)}) collective-permute-start(bf16[512,256]{1,0:T(8,128)(2,1)S(1)} %get-tuple-element.36), channel_id=1, source_target_pairs={{0,30},{2,4},{4,2},{6,8},{8,6},{10,12},{12,10},{14,16},{16,14},{18... | collective-permute-start | bytes 786440 | tf_op jit(solution)/shard_map/ppermute | solution.py:26
  9.8 13.5 %collective-permute-start.2 = (bf16[512,128]{1,0:T(8,128)(2,1)S(1)}, bf16[512,128]{1,0:T(8,128)(2,1)S(1)}, u32[]{:S(2)}, u32[]{:S(2)}) collective-permute-start(bf16[512,128]{1,0:T(8,128)(2,1)S(1)} %get-tuple-element.30), channel_id=1, source_target_pairs={{0,30},{2,4},{4,2},{6,8},{8,6},{10,12},{12,10},{14,16},{16,14},{18... | collective-permute-start | bytes 393224 | tf_op jit(solution)/shard_map/ppermute | solution.py:26
  16.2 8.4 %collective-permute-start.7 = (bf16[256,384]{1,0:T(8,128)(2,1)S(1)}, bf16[256,384]{1,0:T(8,128)(2,1)S(1)}, u32[]{:S(2)}, u32[]{:S(2)}) collective-permute-start(bf16[256,384]{1,0:T(8,128)(2,1)S(1)} %get-tuple-element.40), channel_id=1, source_target_pairs={{0,1},{1,0},{2,3},{3,2},{4,5},{5,4},{6,7},{7,6},{8,9},{9,8},{10,11... | collective-permute-start | bytes 589832 | tf_op jit(solution)/shard_map/ppermute | solution.py:16
  20.3 7.0 %collective-permute-start.5 = (bf16[256,256]{1,0:T(8,128)(2,1)S(1)}, bf16[256,256]{1,0:T(8,128)(2,1)S(1)}, u32[]{:S(2)}, u32[]{:S(2)}) collective-permute-start(bf16[256,256]{1,0:T(8,128)(2,1)S(1)} %get-tuple-element.38), channel_id=1, source_target_pairs={{0,1},{1,0},{2,3},{3,2},{4,5},{5,4},{6,7},{7,6},{8,9},{9,8},{10,11... | collective-permute-start | bytes 393224 | tf_op jit(solution)/shard_map/ppermute | solution.py:16
  23.7 4.9 %collective-permute-start.3 = (bf16[256,128]{1,0:T(8,128)(2,1)S(1)}, bf16[256,128]{1,0:T(8,128)(2,1)S(1)}, u32[]{:S(2)}, u32[]{:S(2)}) collective-permute-start(bf16[256,128]{1,0:T(8,128)(2,1)S(1)} %get-tuple-element.35), channel_id=1, source_target_pairs={{0,1},{1,0},{2,3},{3,2},{4,5},{5,4},{6,7},{7,6},{8,9},{9,8},{10,11... | collective-permute-start | bytes 196616 | tf_op jit(solution)/shard_map/ppermute | solution.py:16

commit v13 on v11

--- a/solution.py
+++ b/solution.py
@@ -68,9 +68,15 @@
     return basis.at[0, 0, pl.ds(pl.multiple_of(group * half, half), half)]
 
 
-def cut_kernel(sketch, basis, lent, part, sems):
+def cut_kernel(sketch, basis, lent, first, second, sems):
     theirs = half_rows(basis, 1 - lax.axis_index("group"), lent.shape[0])
-    copy_all([(sketch.at[:, pl.ds(0, part.shape[1])], part), (theirs, lent)], sems)
+    early, late = first.shape[1], second.shape[1]
+    pairs = [
+        (sketch.at[:, pl.ds(0, early)], first),
+        (theirs, lent),
+        (sketch.at[:, pl.ds(early, late)], second),
+    ]
+    copy_all(pairs, sems)
 
 
 def stage_kernel(begun, sketch, tiles, basis, own, staged, kept, sems):
@@ -79,12 +85,11 @@
     copy_all([(sketch, own), (tiles.at[0, 0, :, 0], staged), (ours, kept)], sems)
 
 
-def local_kernel(start, row_blocks, owner_route, tiles, own, near, hit, miss, stays, part):
+def local_kernel(row_blocks, owner_route, tiles, own, near, hit, miss, stays):
     far = far_offset()
     owner = owner_route[row_blocks[far]]
     own_hits = owner_route[row_blocks[1]] == owner
     near_hits = owner_route[row_blocks[2 - far]] == owner
-    part[...] = own[:, pl.ds(start, part.shape[1])]
     step = 256
     for place in range(0, own.shape[1], step):
         columns = pl.ds(place, step)
@@ -132,13 +137,13 @@
     product = 2 * rows * panels * columns
     short, wide = sketch.dtype, jnp.float32
     copies = pltpu.SemaphoreType.DMA
-    lent, part = call(
+    lent, *parts = call(
         cut_kernel,
-        (on_chip((half, rank), short), on_chip((panels, widths[0]), short)),
+        (on_chip((half, rank), short), *(on_chip((panels, width), short) for width in widths)),
         (),
         0,
         hbm=(sketch, cluster_basis),
-        scratch=(copies((2,)),),
+        scratch=(copies((3,)),),
     )
     own, tiles, kept = call(
         stage_kernel,
@@ -147,27 +152,25 @@
             on_chip((offsets, rows, panels), short),
             on_chip((half, rank), short),
         ),
-        (part,),
+        (parts[0],),
         0,
         hbm=(sketch, far_tiles, cluster_basis),
         scratch=(copies((3,)),),
     )
     lent = from_behind(lent, "group", 1)
-    fars = [swap_far(part)]
+    fars = [swap_far(part) for part in parts]
     near = swap_near(sketch)
-    hit, miss, stays, part = call(
-        functools.partial(local_kernel, starts[1]),
+    hit, miss, stays = call(
+        local_kernel,
         (
             on_chip((rows, columns), wide),
             on_chip((rows, columns), short),
             on_chip((1, columns), wide),
-            on_chip((panels, widths[1]), short),
         ),
         (tiles, own, near),
         2 * product,
         scalars=(row_blocks.reshape(-1), owner_route.reshape(-1)),
     )
-    fars.append(swap_far(part))
     hit_turned, missed = call(
         turn_kernel,
         (on_chip((rank, half), short), on_chip((rank, columns), wide)),

time: 29.5 us -> 28.2 us (0.956)
  starting transfers between devices: 9.74 us -> 8.43 us
    ppermute x3, waiting for transfers between devices: 3.31 us -> 1.98 us  [from_behind(): lax.ppermute(array, axis, [(i, (i + by) % devices) for i in range(devices)])]
    ppermute x2, waiting for transfers between devices: 8.53 us -> 9.78 us  [swap_far(): lax.ppermute(array, 'blk', [(i, (i + 1 if i % 2 else i - 1) % devices) fo...]
    ppermute x3, starting transfers between devices: 6.08 us -> 4.83 us  [from_behind(): lax.ppermute(array, axis, [(i, (i + by) % devices) for i in range(devices)])]
  transfers between devices with their start and end apart: 6 -> 6, of which waited for: 3 -> 5; matrix products, arithmetic and copies ran while one was open for 0% -> 0% of each run, Pallas kernels for 24% -> 25%
where the time goes in v13:
time: 28.2 us; the launch traced here: 28 us
  waiting for transfers between devices  11.8 us (42%)
  starting transfers between devices  8.43 us (30%)
  Pallas kernels  7.7 us (27%)
    ppermute x2, waiting for transfers between devices, swap_far(): lax.ppermute(array, 'blk', [(i, (i + 1 if i % 2 else i - 1) % devices) fo...  9.78 us
    pallas_call x8, Pallas kernels, call(): pl.pallas_call(kernel, out_shape=out_shape, in_specs=[scalar] * len(scala...  7.7 us
    ppermute x3, starting transfers between devices, from_behind(): lax.ppermute(array, axis, [(i, (i + by) % devices) for i in range(devices)])  4.83 us
    ppermute x2, starting transfers between devices, swap_far(): lax.ppermute(array, 'blk', [(i, (i + 1 if i % 2 else i - 1) % devices) fo...  3.54 us
    ppermute x3, waiting for transfers between devices, from_behind(): lax.ppermute(array, axis, [(i, (i + by) % devices) for i in range(devices)])  1.98 us
  transfers between devices with their start and end apart: 6, of which 5 were waited for; matrix products, arithmetic and copies ran while one was open for 0% of the time, Pallas kernels for 25%

profile of v13, /device:TPU:1, one launch (start us, length us, event | category | flops | bytes accessed | tf_op | source)
XLA Modules:
  0.0 28.0 jit_solution(9796950237749291713)
XLA Ops:
  0.0 0.1 collective-permute-start.1
  0.1 1.2 %shard_map.55 = (bf16[512,256]{1,0:T(8,128)(2,1)S(1)}, bf16[512,512]{1,0:T(8,128)(2,1)S(1)}, bf16[512,256]{1,0:T(8,128)(2,1)S(1)}) custom-call(bf16[512,768]{1,0:T(8,128)(2,1)} %sketch.3, bf16[1,1,1024,256]{3,2,1,0:T(8,128)(2,1)} %basis.3), custom_call_target="tpu_custom_call" | custom-call | bytes 1048576 | tf_op jit(solution)/shard_map/pallas_call | solution.py:43
  1.3 2.6 %collective-permute-start.4 = (bf16[512,512]{1,0:T(8,128)(2,1)S(1)}, bf16[512,512]{1,0:T(8,128)(2,1)S(1)}, u32[]{:S(2)}, u32[]{:S(2)}) collective-permute-start(bf16[512,512]{1,0:T(8,128)(2,1)S(1)} %get-tuple-element.20.begun), channel_id=1, source_target_pairs={{0,30},{2,4},{4,2},{6,8},{8,6},{10,12},{12,10},{14,16},{16,14},{18... | collective-permute-start | bytes 1572872 | tf_op jit(solution)/shard_map/ppermute | solution.py:26
  3.9 1.2 %collective-permute-start.2 = (bf16[512,256]{1,0:T(8,128)(2,1)S(1)}, bf16[512,256]{1,0:T(8,128)(2,1)S(1)}, u32[]{:S(2)}, u32[]{:S(2)}) collective-permute-start(bf16[512,256]{1,0:T(8,128)(2,1)S(1)} %get-tuple-element.26), channel_id=1, source_target_pairs={{0,1},{1,0},{2,3},{3,2},{4,5},{5,4},{6,7},{7,6},{8,9},{9,8},{10,11... | collective-permute-start | bytes 786440 | tf_op jit(solution)/shard_map/ppermute | solution.py:16
  5.1 0.0 copy-start
  5.1 0.0 copy-start.1
  5.1 0.9 %collective-permute-start = (bf16[512,256]{1,0:T(8,128)(2,1)S(1)}, bf16[512,256]{1,0:T(8,128)(2,1)S(1)}, u32[]{:S(2)}, u32[]{:S(2)}) collective-permute-start(bf16[512,256]{1,0:T(8,128)(2,1)S(1)} %get-tuple-element.22), channel_id=1, source_target_pairs={{0,30},{2,4},{4,2},{6,8},{8,6},{10,12},{12,10},{14,16},{16,14},{18... | collective-permute-start | bytes 786440 | tf_op jit(solution)/shard_map/ppermute | solution.py:26
  6.1 1.7 %shard_map.56 = (bf16[512,768]{1,0:T(8,128)(2,1)S(1)}, bf16[3,512,512]{2,1,0:T(8,128)(2,1)S(1)}, bf16[512,256]{1,0:T(8,128)(2,1)S(1)}) custom-call(bf16[512,512]{1,0:T(8,128)(2,1)S(1)} %get-tuple-element.20.begun, bf16[512,768]{1,0:T(8,128)(2,1)} %sketch.3, bf16[1,1,3,1,512,512]{5,4,3,2,1,0:T(8,128)(2,1)} %tiles.1, bf16[1,1,1024,256]{3,2,1,0:T(8,128)(2,1)} %basis.3), custom_call_target="tpu_custom_call" | custom-call | bytes 1048576 | tf_op jit(solution)/shard_map/pallas_call | solution.py:43
  7.8 0.0 collective-permute-done.1.near
  7.8 0.0 copy-done
  7.8 0.0 copy-done.1
  7.8 1.5 %shard_map.57 = (f32[512,768]{1,0:T(8,128)S(1)}, bf16[512,768]{1,0:T(8,128)(2,1)S(1)}, f32[1,768]{1,0:T(1,128)S(1)}) custom-call(s32[3]{0:T(128)S(1)} %bitcast.3, s32[2]{0:T(128)S(1)} %bitcast.4, bf16[3,512,512]{2,1,0:T(8,128)(2,1)S(1)} %get-tuple-element.21.tiles, bf16[512,768]{1,0:T(8,128)(2,1)S(1)} %get-tuple-element.23.own, ...), custom_call_target="tpu_custom_call" | custom-call | flops 805306368 | bytes 1048576 | tf_op jit(solution)/shard_map/pallas_call | solution.py:43
  9.3 0.1 collective-permute-done.2.lent
  9.4 0.5 %shard_map.58 = (bf16[256,512]{1,0:T(8,128)(2,1)S(1)}, f32[256,768]{1,0:T(8,128)S(1)}) custom-call(bf16[512,256]{1,0:T(8,128)(2,1)S(1)} %get-tuple-element.25.kept, bf16[512,256]{1,0:T(8,128)(2,1)S(1)} %collective-permute-done.2.lent, bf16[512,768]{1,0:T(8,128)(2,1)S(1)} %get-tuple-element.27.miss, f32[1,768]{1,0:T(1,128)S(1)} %get-tuple-element.28.stays), custom_call_target="tpu_custom_call" | custom-call | flops 201326592 | bytes 1048576 | tf_op jit(solution)/shard_map/pallas_call | solution.py:43
  9.9 9.6 %collective-permute-done.4.far = bf16[512,512]{1,0:T(8,128)(2,1)S(1)} collective-permute-done((bf16[512,512]{1,0:T(8,128)(2,1)S(1)}, bf16[512,512]{1,0:T(8,128)(2,1)S(1)}, u32[]{:S(2)}, u32[]{:S(2)}) %collective-permute-start.4) | collective-permute-done | bytes 524320 | tf_op jit(solution)/shard_map/ppermute | solution.py:26
  19.5 0.6 %shard_map.60 = (f32[256,512]{1,0:T(8,128)S(1)}, bf16[256,512]{1,0:T(8,128)(2,1)S(1)}) custom-call(bf16[3,512,512]{2,1,0:T(8,128)(2,1)S(1)} %get-tuple-element.21.tiles, bf16[512,512]{1,0:T(8,128)(2,1)S(1)} %collective-permute-done.4.far, f32[512,768]{1,0:T(8,128)S(1)} %get-tuple-element.24.hit, bf16[256,512]{1,0:T(8,128)(2,1)S(1)} %get-tuple-element.29.hit_turned, ...), custom_call_target="tpu_custom_call" | custom-call | flops 536870912 | bytes 1048576 | tf_op jit(solution)/shard_map/pallas_call | solution.py:43
  20.1 1.9 %collective-permute-start.5 = (bf16[256,512]{1,0:T(8,128)(2,1)S(1)}, bf16[256,512]{1,0:T(8,128)(2,1)S(1)}, u32[]{:S(2)}, u32[]{:S(2)}) collective-permute-start(bf16[256,512]{1,0:T(8,128)(2,1)S(1)} %get-tuple-element.34), channel_id=1, source_target_pairs={{0,1},{1,0},{2,3},{3,2},{4,5},{5,4},{6,7},{7,6},{8,9},{9,8},{10,11... | collective-permute-start | bytes 786440 | tf_op jit(solution)/shard_map/ppermute | solution.py:16
  22.1 0.2 collective-permute-done.far
  22.3 0.6 %shard_map.59 = (f32[256,256]{1,0:T(8,128)S(1)}, bf16[256,256]{1,0:T(8,128)(2,1)S(1)}) custom-call(bf16[3,512,512]{2,1,0:T(8,128)(2,1)S(1)} %get-tuple-element.21.tiles, bf16[512,256]{1,0:T(8,128)(2,1)S(1)} %collective-permute-done.far, f32[512,768]{1,0:T(8,128)S(1)} %get-tuple-element.24.hit, bf16[256,512]{1,0:T(8,128)(2,1)S(1)} %get-tuple-element.29.hit_turned, ...), custom_call_target="tpu_custom_call" | custom-call | flops 268435456 | bytes 1048576 | tf_op jit(solution)/shard_map/pallas_call | solution.py:43
  22.8 1.6 %collective-permute-start.3 = (bf16[256,256]{1,0:T(8,128)(2,1)S(1)}, bf16[256,256]{1,0:T(8,128)(2,1)S(1)}, u32[]{:S(2)}, u32[]{:S(2)}) collective-permute-start(bf16[256,256]{1,0:T(8,128)(2,1)S(1)} %get-tuple-element.32), channel_id=1, source_target_pairs={{0,1},{1,0},{2,3},{3,2},{4,5},{5,4},{6,7},{7,6},{8,9},{9,8},{10,11... | collective-permute-start | bytes 393224 | tf_op jit(solution)/shard_map/ppermute | solution.py:16
  24.5 1.3 %collective-permute-done.5.received = bf16[256,512]{1,0:T(8,128)(2,1)S(1)} collective-permute-done((bf16[256,512]{1,0:T(8,128)(2,1)S(1)}, bf16[256,512]{1,0:T(8,128)(2,1)S(1)}, u32[]{:S(2)}, u32[]{:S(2)}) %collective-permute-start.5) | collective-permute-done | bytes 262176 | tf_op jit(solution)/shard_map/ppermute | solution.py:16
  25.8 0.8 %shard_map.61.rest_0_ = f32[256,768]{1,0:T(8,128)} custom-call(f32[256,512]{1,0:T(8,128)S(1)} %get-tuple-element.33.kept, bf16[256,512]{1,0:T(8,128)(2,1)S(1)} %collective-permute-done.5.received), custom_call_target="tpu_custom_call" | custom-call | flops 65536 | bytes 1048576 | tf_op jit(solution)/shard_map/pallas_call | solution.py:43
  26.7 0.6 %collective-permute-done.3.received = bf16[256,256]{1,0:T(8,128)(2,1)S(1)} collective-permute-done((bf16[256,256]{1,0:T(8,128)(2,1)S(1)}, bf16[256,256]{1,0:T(8,128)(2,1)S(1)}, u32[]{:S(2)}, u32[]{:S(2)}) %collective-permute-start.3) | collective-permute-done | bytes 131104 | tf_op jit(solution)/shard_map/ppermute | solution.py:16
  27.2 0.7 %shard_map.62 = f32[256,768]{1,0:T(8,128)} custom-call(f32[256,256]{1,0:T(8,128)S(1)} %get-tuple-element.31.kept, bf16[256,256]{1,0:T(8,128)(2,1)S(1)} %collective-permute-done.3.received, f32[256,768]{1,0:T(8,128)} %shard_map.61.rest_0_), custom_call_target="tpu_custom_call", output_to_operand_aliasing={{}: (2, {})} | custom-call | flops 65536 | bytes 1048576 | tf_op jit(solution)/shard_map/pallas_call | solution.py:43
Async XLA Ops:
  0.0 7.8 %collective-permute-start.1 = (bf16[512,768]{1,0:T(8,128)(2,1)}, bf16[512,768]{1,0:T(8,128)(2,1)S(1)}, u32[]{:S(2)}, u32[]{:S(2)}) collective-permute-start(bf16[512,768]{1,0:T(8,128)(2,1)} %sketch.3), channel_id=1, source_target_pairs={{0,2},{2,0},{4,6},{6,4},{8,10},{10,8},{12,14},{14,12},{16,18},{18,... | collective-permute-start | bytes 2359304 | tf_op jit(solution)/shard_map/ppermute | solution.py:21
  1.3 18.2 %collective-permute-start.4 = (bf16[512,512]{1,0:T(8,128)(2,1)S(1)}, bf16[512,512]{1,0:T(8,128)(2,1)S(1)}, u32[]{:S(2)}, u32[]{:S(2)}) collective-permute-start(bf16[512,512]{1,0:T(8,128)(2,1)S(1)} %get-tuple-element.20.begun), channel_id=1, source_target_pairs={{0,30},{2,4},{4,2},{6,8},{8,6},{10,12},{12,10},{14,16},{16,14},{18... | collective-permute-start | bytes 1572872 | tf_op jit(solution)/shard_map/ppermute | solution.py:26
  3.9 5.5 %collective-permute-start.2 = (bf16[512,256]{1,0:T(8,128)(2,1)S(1)}, bf16[512,256]{1,0:T(8,128)(2,1)S(1)}, u32[]{:S(2)}, u32[]{:S(2)}) collective-permute-start(bf16[512,256]{1,0:T(8,128)(2,1)S(1)} %get-tuple-element.26), channel_id=1, source_target_pairs={{0,1},{1,0},{2,3},{3,2},{4,5},{5,4},{6,7},{7,6},{8,9},{9,8},{10,11... | collective-permute-start | bytes 786440 | tf_op jit(solution)/shard_map/ppermute | solution.py:16
  5.1 2.6 %copy-start = (s32[1,1,3,1]{2,3,1,0:T(1,128)S(1)}, s32[1,1,3,1]{2,3,1,0:T(1,128)}, u32[]{:S(2)}) copy-start(s32[1,1,3,1]{2,3,1,0:T(1,128)} %param.7) | copy-start | bytes 40
  5.1 2.6 %copy-start.1 = (s32[1,1,2]{2,1,0:T(1,128)S(1)}, s32[1,1,2]{2,1,0:T(1,128)}, u32[]{:S(2)}) copy-start(s32[1,1,2]{2,1,0:T(1,128)} %param.8) | copy-start | bytes 28
  5.1 17.2 %collective-permute-start = (bf16[512,256]{1,0:T(8,128)(2,1)S(1)}, bf16[512,256]{1,0:T(8,128)(2,1)S(1)}, u32[]{:S(2)}, u32[]{:S(2)}) collective-permute-start(bf16[512,256]{1,0:T(8,128)(2,1)S(1)} %get-tuple-element.22), channel_id=1, source_target_pairs={{0,30},{2,4},{4,2},{6,8},{8,6},{10,12},{12,10},{14,16},{16,14},{18... | collective-permute-start | bytes 786440 | tf_op jit(solution)/shard_map/ppermute | solution.py:26
  20.1 5.7 %collective-permute-start.5 = (bf16[256,512]{1,0:T(8,128)(2,1)S(1)}, bf16[256,512]{1,0:T(8,128)(2,1)S(1)}, u32[]{:S(2)}, u32[]{:S(2)}) collective-permute-start(bf16[256,512]{1,0:T(8,128)(2,1)S(1)} %get-tuple-element.34), channel_id=1, source_target_pairs={{0,1},{1,0},{2,3},{3,2},{4,5},{5,4},{6,7},{7,6},{8,9},{9,8},{10,11... | collective-permute-start | bytes 786440 | tf_op jit(solution)/shard_map/ppermute | solution.py:16
  22.8 4.4 %collective-permute-start.3 = (bf16[256,256]{1,0:T(8,128)(2,1)S(1)}, bf16[256,256]{1,0:T(8,128)(2,1)S(1)}, u32[]{:S(2)}, u32[]{:S(2)}) collective-permute-start(bf16[256,256]{1,0:T(8,128)(2,1)S(1)} %get-tuple-element.32), channel_id=1, source_target_pairs={{0,1},{1,0},{2,3},{3,2},{4,5},{5,4},{6,7},{7,6},{8,9},{9,8},{10,11... | collective-permute-start | bytes 393224 | tf_op jit(solution)/shard_map/ppermute | solution.py:16

commit v14 on v13

--- a/solution.py
+++ b/solution.py
@@ -7,7 +7,6 @@
 from jax.experimental.pallas import tpu as pltpu
 from jax.sharding import PartitionSpec as P
 
-SHARES = (2, 1)
 TRANSPOSED = (((0,), (0,)), ((), ()))
 
 
@@ -16,16 +15,38 @@
     return lax.ppermute(array, axis, [(i, (i + by) % devices) for i in range(devices)])
 
 
+def permuted(array, target):
+    blocks, groups = lax.axis_size("blk"), lax.axis_size("group")
+    pairs = []
+    for b in range(blocks):
+        for g in range(groups):
+            to_b, to_g = target(b, g)
+            pairs.append((b * groups + g, to_b % blocks * groups + to_g))
+    return lax.ppermute(array, ("blk", "group"), pairs)
+
+
+def shares_rows(b):
+    return (b + 1) // 2 % 2 == 0
+
+
+def far_of(b, g):
+    return (b + 1 if b % 2 else b - 1), g
+
+
+def far_if_alone(b, g):
+    return (b, g) if shares_rows(b) else far_of(b, g)
+
+
+def other_group(b, g):
+    return b, 1 - g
+
+
+def other_group_if_shared(b, g):
+    return other_group(b, g) if shares_rows(b) else (b, g)
+
+
 def swap_near(array):
-    devices = lax.axis_size("blk")
-    return lax.ppermute(array, "blk", [(i, i ^ 1) for i in range(devices)])
-
-
-def swap_far(array):
-    devices = lax.axis_size("blk")
-    return lax.ppermute(
-        array, "blk", [(i, (i + 1 if i % 2 else i - 1) % devices) for i in range(devices)]
-    )
+    return permuted(array, lambda b, g: (b ^ 1, g))
 
 
 def on_chip(shape, dtype):
@@ -48,7 +69,7 @@
         scratch_shapes=list(scratch),
         input_output_aliases={len(placed) - 1: 0} if alias else {},
         compiler_params=pltpu.CompilerParams(vmem_limit_bytes=16 << 20),
-        cost_estimate=pl.CostEstimate(flops=flops, bytes_accessed=1 << 20, transcendentals=0),
+        cost_estimate=pl.CostEstimate(flops=flops, bytes_accessed=1 << 10, transcendentals=0),
     )(*placed)
 
 
@@ -68,15 +89,38 @@
     return basis.at[0, 0, pl.ds(pl.multiple_of(group * half, half), half)]
 
 
-def cut_kernel(sketch, basis, lent, first, second, sems):
-    theirs = half_rows(basis, 1 - lax.axis_index("group"), lent.shape[0])
-    early, late = first.shape[1], second.shape[1]
-    pairs = [
-        (sketch.at[:, pl.ds(0, early)], first),
-        (theirs, lent),
-        (sketch.at[:, pl.ds(early, late)], second),
+def shared_here():
+    return lax.rem((lax.axis_index("blk") + 1) // 2, 2) == 0
+
+
+def half_start(group, half):
+    return pl.multiple_of(group * half, half)
+
+
+def cut_kernel(sketch, basis, lent, first, last, sems):
+    group = lax.axis_index("group")
+    width = last.shape[1]
+    half = first.shape[0] // 2
+    part = [pl.ds(i * width, width) for i in range(3)]
+    shared = shared_here()
+    copies = [
+        (sketch.at[:, part[0]], first.at[:, part[0]]),
+        (half_rows(basis, 1 - group, lent.shape[0]), lent),
+        (sketch.at[:, part[2]], last),
     ]
-    copy_all(pairs, sems)
+    whole = [(sketch.at[:, part[1]], first.at[:, part[1]])]
+    rows = pl.ds(half_start(group, half), half)
+    halves = [
+        (sketch.at[rows, part[i + 1]], first.at[pl.ds(i * half, half), part[1]]) for i in range(2)
+    ]
+
+    @pl.when(shared)
+    def _():
+        copy_all(copies + halves, sems)
+
+    @pl.when(jnp.logical_not(shared))
+    def _():
+        copy_all(copies + whole, sems)
 
 
 def stage_kernel(begun, sketch, tiles, basis, own, staged, kept, sems):
@@ -111,9 +155,9 @@
     )
 
 
-def far_kernel(start, tiles, far, hit, hit_turned, missed, stays, kept, sent):
-    columns = pl.ds(start, far.shape[1])
-    product = jnp.dot(tiles[far_offset()], far[...], preferred_element_type=jnp.float32)
+def finish(start, tiles, far, hit, hit_turned, missed, stays, kept, sent):
+    columns = pl.ds(start, kept.shape[1])
+    product = jnp.dot(tiles[far_offset()], far, preferred_element_type=jnp.float32)
     sampled = (hit[:, columns] + product).astype(jnp.bfloat16)
     made = jnp.dot(hit_turned[...], sampled, preferred_element_type=jnp.float32)
     stay = stays[:, columns] > 0.0
@@ -122,6 +166,32 @@
     kept[...] = jnp.where(stay, made, other)
 
 
+def first_kernel(first, tiles, hit, hit_turned, missed, stays, kept, sent, *halves):
+    width = kept.shape[1]
+    for i, ours in enumerate(halves):
+        rows = ours.shape[0]
+        ours[...] = first[pl.ds(i * rows, rows), pl.ds(width, width)]
+    finish(0, tiles, first[:, pl.ds(0, width)], hit, hit_turned, missed, stays, kept, sent)
+
+
+def later_kernel(i, before, alone, ours, theirs, tiles, hit, hit_turned, missed, stays, kept, sent, far):
+    del before
+    half, width = ours.shape
+    group = lax.axis_index("group")
+    shared = shared_here()
+
+    @pl.when(shared)
+    def _():
+        far[pl.ds(half_start(group, half), half), :] = ours[...]
+        far[pl.ds(half_start(1 - group, half), half), :] = theirs[...]
+
+    @pl.when(jnp.logical_not(shared))
+    def _():
+        far[...] = alone[:, pl.ds(alone.shape[1] - width, width)]
+
+    finish(i * width, tiles, far[...], hit, hit_turned, missed, stays, kept, sent)
+
+
 def join_kernel(start, kept, received, *rest):
     out, total, sems = rest[-3:]
     total[...] = kept[...] + received[...].astype(jnp.float32)
@@ -132,18 +202,21 @@
     panels, columns = sketch.shape
     offsets, rows = far_tiles.shape[2], far_tiles.shape[4]
     half, rank = cluster_basis.shape[2] // 2, cluster_basis.shape[3]
-    widths = [columns * share // sum(SHARES) for share in SHARES]
-    starts = [sum(widths[:i]) for i in range(len(widths))]
+    width = columns // 3
     product = 2 * rows * panels * columns
     short, wide = sketch.dtype, jnp.float32
     copies = pltpu.SemaphoreType.DMA
-    lent, *parts = call(
+    lent, first, last = call(
         cut_kernel,
-        (on_chip((half, rank), short), *(on_chip((panels, width), short) for width in widths)),
+        (
+            on_chip((half, rank), short),
+            on_chip((panels, 2 * width), short),
+            on_chip((panels, width), short),
+        ),
         (),
         0,
         hbm=(sketch, cluster_basis),
-        scratch=(copies((3,)),),
+        scratch=(copies((5,)),),
     )
     own, tiles, kept = call(
         stage_kernel,
@@ -152,13 +225,14 @@
             on_chip((offsets, rows, panels), short),
             on_chip((half, rank), short),
         ),
-        (parts[0],),
+        (lent,),
         0,
         hbm=(sketch, far_tiles, cluster_basis),
         scratch=(copies((3,)),),
     )
-    lent = from_behind(lent, "group", 1)
-    fars = [swap_far(part) for part in parts]
+    first = permuted(first, far_of)
+    lent = permuted(lent, other_group)
+    last = permuted(last, far_if_alone)
     near = swap_near(sketch)
     hit, miss, stays = call(
         local_kernel,
@@ -177,18 +251,31 @@
         (kept, lent, miss, stays),
         product // 2,
     )
+    results = on_chip((rank, width), wide), on_chip((rank, width), short)
+    common = tiles, hit, hit_turned, missed, stays
+    kept, sent, *ours = call(
+        first_kernel,
+        (*results, *(on_chip((panels // 2, width), short),) * 2),
+        (first, *common),
+        0,
+    )
+    theirs = [permuted(part, other_group_if_shared) for part in ours]
+    done = [(kept, permuted(sent, other_group))]
+    for i, alone in ((1, first), (2, last)):
+        kept, sent = call(
+            functools.partial(later_kernel, i),
+            results,
+            (sent, alone, ours[i - 1], theirs[i - 1], *common),
+            0,
+            scratch=(on_chip((panels, width), short),),
+        )
+        done.append((kept, permuted(sent, other_group)))
     out = None
-    for i, (start, width) in enumerate(zip(starts, widths)):
-        kept, sent = call(
-            functools.partial(far_kernel, start),
-            (on_chip((rank, width), wide), on_chip((rank, width), short)),
-            (tiles, fars[i], hit, hit_turned, missed, stays),
-            2 * product * width // columns,
-        )
+    for i, pair in enumerate(done):
         out = call(
-            functools.partial(join_kernel, start),
+            functools.partial(join_kernel, i * width),
             pltpu.HBM((rank, columns), wide),
-            (kept, from_behind(sent, "group", 1)),
+            pair,
             1 << 16,
             hbm=() if out is None else (out,),
             scratch=(on_chip((rank, width), wide), copies((1,))),
@@ -227,7 +314,7 @@
 
 def body(sketch, far_tiles, row_blocks, owner_route, cluster_basis):
     small = cluster_basis.shape[3] < far_tiles.shape[4]
-    paired = lax.axis_size("group") == 2 and lax.axis_size("blk") % 2 == 0
+    paired = lax.axis_size("group") == 2 and lax.axis_size("blk") % 4 == 0
     if small and paired and far_tiles.shape[2:4] == (3, 1):
         return paired_body(sketch, far_tiles, row_blocks, owner_route, cluster_basis)
     return ring_body(sketch, far_tiles, row_blocks, owner_route, cluster_basis)

time: 28.2 us -> 33.2 us (1.18)
  the two profiles are of different devices: /device:TPU:1 before, /device:TPU:0 now
where the time goes in v14:
time: 33.2 us; the launch traced here: 33 us
  starting transfers between devices  17.6 us (53%)
  Pallas kernels  8.87 us (27%)
  waiting for transfers between devices  6.44 us (19%)
    ppermute x9, starting transfers between devices, permuted(): return lax.ppermute(array, ('blk', 'group'), pairs)  17.6 us
    pallas_call x10, Pallas kernels, call(): pl.pallas_call(kernel, out_shape=out_shape, in_specs=[scalar] * len(scala...  8.87 us
    ppermute x9, waiting for transfers between devices, permuted(): return lax.ppermute(array, ('blk', 'group'), pairs)  6.44 us
  transfers between devices with their start and end apart: 9, of which 6 were waited for; matrix products, arithmetic and copies ran while one was open for 0% of the time, Pallas kernels for 25%

profile of v14, /device:TPU:0, one launch (start us, length us, event | category | flops | bytes accessed | tf_op | source)
XLA Modules:
  0.0 33.0 jit_solution(6081416879387063306)
XLA Ops:
  0.0 0.5 %collective-permute-start.1 = (bf16[512,768]{1,0:T(8,128)(2,1)}, bf16[512,768]{1,0:T(8,128)(2,1)S(1)}, u32[]{:S(2)}, u32[]{:S(2)}) collective-permute-start(bf16[512,768]{1,0:T(8,128)(2,1)} %sketch.3), channel_id=1, source_target_pairs={{0,2},{1,3},{2,0},{3,1},{4,6},{5,7},{6,4},{7,5},{8,10},{9,11},{10,... | collective-permute-start | bytes 2359304 | tf_op jit(solution)/shard_map/ppermute | solution.py:25
  0.5 1.2 %shard_map.55 = (bf16[512,256]{1,0:T(8,128)(2,1)S(1)}, bf16[512,512]{1,0:T(8,128)(2,1)S(1)}, bf16[512,256]{1,0:T(8,128)(2,1)S(1)}) custom-call(bf16[512,768]{1,0:T(8,128)(2,1)} %sketch.3, bf16[1,1,1024,256]{3,2,1,0:T(8,128)(2,1)} %basis.3), custom_call_target="tpu_custom_call" | custom-call | bytes 1024 | tf_op jit(solution)/shard_map/pallas_call | solution.py:64
  1.7 5.7 %collective-permute-start = (bf16[512,512]{1,0:T(8,128)(2,1)S(1)}, bf16[512,512]{1,0:T(8,128)(2,1)S(1)}, u32[]{:S(2)}, u32[]{:S(2)}) collective-permute-start(bf16[512,512]{1,0:T(8,128)(2,1)S(1)} %get-tuple-element.24), channel_id=1, source_target_pairs={{0,30},{1,31},{2,4},{3,5},{4,2},{5,3},{6,8},{7,9},{8,6},{9,7},{10,... | collective-permute-start | bytes 1572872 | tf_op jit(solution)/shard_map/ppermute | solution.py:25
  7.4 1.5 %collective-permute-start.2 = (bf16[512,256]{1,0:T(8,128)(2,1)S(1)}, bf16[512,256]{1,0:T(8,128)(2,1)S(1)}, u32[]{:S(2)}, u32[]{:S(2)}) collective-permute-start(bf16[512,256]{1,0:T(8,128)(2,1)S(1)} %get-tuple-element.25.begun), channel_id=1, source_target_pairs={{0,1},{1,0},{2,3},{3,2},{4,5},{5,4},{6,7},{7,6},{8,9},{9,8},{10,11... | collective-permute-start | bytes 786440 | tf_op jit(solution)/shard_map/ppermute | solution.py:25
  8.9 0.0 copy-start
  8.9 0.0 copy-start.1
  8.9 0.8 %collective-permute-start.4 = (bf16[512,256]{1,0:T(8,128)(2,1)S(1)}, bf16[512,256]{1,0:T(8,128)(2,1)S(1)}, u32[]{:S(2)}, u32[]{:S(2)}) collective-permute-start(bf16[512,256]{1,0:T(8,128)(2,1)S(1)} %get-tuple-element.37), channel_id=1, source_target_pairs={{0,0},{1,1},{2,4},{3,5},{4,2},{5,3},{6,6},{7,7},{8,8},{9,9},{10,12... | collective-permute-start | bytes 786440 | tf_op jit(solution)/shard_map/ppermute | solution.py:25
  9.7 1.7 %shard_map.56 = (bf16[512,768]{1,0:T(8,128)(2,1)S(1)}, bf16[3,512,512]{2,1,0:T(8,128)(2,1)S(1)}, bf16[512,256]{1,0:T(8,128)(2,1)S(1)}) custom-call(bf16[512,256]{1,0:T(8,128)(2,1)S(1)} %get-tuple-element.25.begun, bf16[512,768]{1,0:T(8,128)(2,1)} %sketch.3, bf16[1,1,3,1,512,512]{5,4,3,2,1,0:T(8,128)(2,1)} %tiles.1, bf16[1,1,1024,256]{3,2,1,0:T(8,128)(2,1)} %basis.3), custom_call_target="tpu_custom_call" | custom-call | bytes 1024 | tf_op jit(solution)/shard_map/pallas_call | solution.py:64
  11.4 0.0 collective-permute-done.1.near
  11.4 0.0 copy-done
  11.4 0.0 copy-done.1
  11.5 1.5 %shard_map.57 = (f32[512,768]{1,0:T(8,128)S(1)}, bf16[512,768]{1,0:T(8,128)(2,1)S(1)}, f32[1,768]{1,0:T(1,128)S(1)}) custom-call(s32[3]{0:T(128)S(1)} %bitcast.3, s32[2]{0:T(128)S(1)} %bitcast.4, bf16[3,512,512]{2,1,0:T(8,128)(2,1)S(1)} %get-tuple-element.26.tiles, bf16[512,768]{1,0:T(8,128)(2,1)S(1)} %get-tuple-element.27.own, ...), custom_call_target="tpu_custom_call" | custom-call | flops 805306368 | bytes 1024 | tf_op jit(solution)/shard_map/pallas_call | solution.py:64
  13.0 0.8 %collective-permute-done.2.lent = bf16[512,256]{1,0:T(8,128)(2,1)S(1)} collective-permute-done((bf16[512,256]{1,0:T(8,128)(2,1)S(1)}, bf16[512,256]{1,0:T(8,128)(2,1)S(1)}, u32[]{:S(2)}, u32[]{:S(2)}) %collective-permute-start.2) | collective-permute-done | bytes 262176 | tf_op jit(solution)/shard_map/ppermute | solution.py:25
  13.8 0.5 %shard_map.58 = (bf16[256,512]{1,0:T(8,128)(2,1)S(1)}, f32[256,768]{1,0:T(8,128)S(1)}) custom-call(bf16[512,256]{1,0:T(8,128)(2,1)S(1)} %get-tuple-element.29.kept, bf16[512,256]{1,0:T(8,128)(2,1)S(1)} %collective-permute-done.2.lent, bf16[512,768]{1,0:T(8,128)(2,1)S(1)} %get-tuple-element.30.miss, f32[1,768]{1,0:T(1,128)S(1)} %get-tuple-element.31.stays), custom_call_target="tpu_custom_call" | custom-call | flops 201326592 | bytes 1024 | tf_op jit(solution)/shard_map/pallas_call | solution.py:64
  14.3 0.1 collective-permute-done.first.alone
  14.4 0.6 %shard_map.59 = (f32[256,256]{1,0:T(8,128)S(1)}, bf16[256,256]{1,0:T(8,128)(2,1)S(1)}, bf16[256,256]{1,0:T(8,128)(2,1)S(1)}, bf16[256,256]{1,0:T(8,128)(2,1)S(1)}) custom-call(bf16[512,512]{1,0:T(8,128)(2,1)S(1)} %collective-permute-done.first.alone, bf16[3,512,512]{2,1,0:T(8,128)(2,1)S(1)} %get-tuple-element.26.tiles, ...), custom_call_target="tpu_custom_call" | custom-call | bytes 1024 | tf_op jit(solution)/shard_map/pallas_call | solution.py:64
  14.9 3.4 %collective-permute-start.3 = (bf16[256,256]{1,0:T(8,128)(2,1)S(1)}, bf16[256,256]{1,0:T(8,128)(2,1)S(1)}, u32[]{:S(2)}, u32[]{:S(2)}) collective-permute-start(bf16[256,256]{1,0:T(8,128)(2,1)S(1)} %get-tuple-element.35.ours), channel_id=1, source_target_pairs={{0,1},{1,0},{2,2},{3,3},{4,4},{5,5},{6,7},{7,6},{8,9},{9,8},{10,10... | collective-permute-start | bytes 393224 | tf_op jit(solution)/shard_map/ppermute | solution.py:25
  18.4 2.4 %collective-permute-start.5 = (bf16[256,256]{1,0:T(8,128)(2,1)S(1)}, bf16[256,256]{1,0:T(8,128)(2,1)S(1)}, u32[]{:S(2)}, u32[]{:S(2)}) collective-permute-start(bf16[256,256]{1,0:T(8,128)(2,1)S(1)} %get-tuple-element.38.ours), channel_id=1, source_target_pairs={{0,1},{1,0},{2,2},{3,3},{4,4},{5,5},{6,7},{7,6},{8,9},{9,8},{10,10... | collective-permute-start | bytes 393224 | tf_op jit(solution)/shard_map/ppermute | solution.py:25
  20.8 1.6 %collective-permute-start.8 = (bf16[256,256]{1,0:T(8,128)(2,1)S(1)}, bf16[256,256]{1,0:T(8,128)(2,1)S(1)}, u32[]{:S(2)}, u32[]{:S(2)}) collective-permute-start(bf16[256,256]{1,0:T(8,128)(2,1)S(1)} %get-tuple-element.34.before), channel_id=1, source_target_pairs={{0,1},{1,0},{2,3},{3,2},{4,5},{5,4},{6,7},{7,6},{8,9},{9,8},{10,11... | collective-permute-start | bytes 393224 | tf_op jit(solution)/shard_map/ppermute | solution.py:25
  22.4 0.0 collective-permute-done.3.theirs
  22.4 0.6 %shard_map.60 = (f32[256,256]{1,0:T(8,128)S(1)}, bf16[256,256]{1,0:T(8,128)(2,1)S(1)}) custom-call(bf16[256,256]{1,0:T(8,128)(2,1)S(1)} %get-tuple-element.34.before, bf16[512,512]{1,0:T(8,128)(2,1)S(1)} %collective-permute-done.first.alone, bf16[256,256]{1,0:T(8,128)(2,1)S(1)} %get-tuple-element.35.ours, ...), custom_call_target="tpu_custom_call" | custom-call | bytes 1024 | tf_op jit(solution)/shard_map/pallas_call | solution.py:64
  23.0 1.0 %collective-permute-start.7 = (bf16[256,256]{1,0:T(8,128)(2,1)S(1)}, bf16[256,256]{1,0:T(8,128)(2,1)S(1)}, u32[]{:S(2)}, u32[]{:S(2)}) collective-permute-start(bf16[256,256]{1,0:T(8,128)(2,1)S(1)} %get-tuple-element.36.before), channel_id=1, source_target_pairs={{0,1},{1,0},{2,3},{3,2},{4,5},{5,4},{6,7},{7,6},{8,9},{9,8},{10,11... | collective-permute-start | bytes 393224 | tf_op jit(solution)/shard_map/ppermute | solution.py:25
  24.0 0.0 collective-permute-done.4.alone
  24.0 2.6 %collective-permute-done.5.theirs = bf16[256,256]{1,0:T(8,128)(2,1)S(1)} collective-permute-done((bf16[256,256]{1,0:T(8,128)(2,1)S(1)}, bf16[256,256]{1,0:T(8,128)(2,1)S(1)}, u32[]{:S(2)}, u32[]{:S(2)}) %collective-permute-start.5) | collective-permute-done | bytes 131104 | tf_op jit(solution)/shard_map/ppermute | solution.py:25
  26.5 0.6 %shard_map.61 = (f32[256,256]{1,0:T(8,128)S(1)}, bf16[256,256]{1,0:T(8,128)(2,1)S(1)}) custom-call(bf16[256,256]{1,0:T(8,128)(2,1)S(1)} %get-tuple-element.36.before, bf16[512,256]{1,0:T(8,128)(2,1)S(1)} %collective-permute-done.4.alone, bf16[256,256]{1,0:T(8,128)(2,1)S(1)} %get-tuple-element.38.ours, bf16[256,256]{1,0:T(8,128)(2,1)S(1)} %collective-permute-done.5.theirs, ...), custom_call_target="tpu_custom_call" | custom-call | bytes 1024 | tf_op jit(solution)/shard_map/pallas_call | solution.py:64
  27.1 0.7 %collective-permute-start.6 = (bf16[256,256]{1,0:T(8,128)(2,1)S(1)}, bf16[256,256]{1,0:T(8,128)(2,1)S(1)}, u32[]{:S(2)}, u32[]{:S(2)}) collective-permute-start(bf16[256,256]{1,0:T(8,128)(2,1)S(1)} %get-tuple-element.40), channel_id=1, source_target_pairs={{0,1},{1,0},{2,3},{3,2},{4,5},{5,4},{6,7},{7,6},{8,9},{9,8},{10,11... | collective-permute-start | bytes 393224 | tf_op jit(solution)/shard_map/ppermute | solution.py:25
  27.8 1.6 %collective-permute-done.8.received = bf16[256,256]{1,0:T(8,128)(2,1)S(1)} collective-permute-done((bf16[256,256]{1,0:T(8,128)(2,1)S(1)}, bf16[256,256]{1,0:T(8,128)(2,1)S(1)}, u32[]{:S(2)}, u32[]{:S(2)}) %collective-permute-start.8) | collective-permute-done | bytes 131104 | tf_op jit(solution)/shard_map/ppermute | solution.py:25
  29.3 0.7 %shard_map.62.rest_0_ = f32[256,768]{1,0:T(8,128)} custom-call(f32[256,256]{1,0:T(8,128)S(1)} %get-tuple-element.42.kept, bf16[256,256]{1,0:T(8,128)(2,1)S(1)} %collective-permute-done.8.received), custom_call_target="tpu_custom_call" | custom-call | flops 65536 | bytes 1024 | tf_op jit(solution)/shard_map/pallas_call | solution.py:64
  30.1 0.8 %collective-permute-done.7.received = bf16[256,256]{1,0:T(8,128)(2,1)S(1)} collective-permute-done((bf16[256,256]{1,0:T(8,128)(2,1)S(1)}, bf16[256,256]{1,0:T(8,128)(2,1)S(1)}, u32[]{:S(2)}, u32[]{:S(2)}) %collective-permute-start.7) | collective-permute-done | bytes 131104 | tf_op jit(solution)/shard_map/ppermute | solution.py:25
  30.9 0.7 %shard_map.63.rest_0_ = f32[256,768]{1,0:T(8,128)} custom-call(f32[256,256]{1,0:T(8,128)S(1)} %get-tuple-element.41.kept, bf16[256,256]{1,0:T(8,128)(2,1)S(1)} %collective-permute-done.7.received, f32[256,768]{1,0:T(8,128)} %shard_map.62.rest_0_), custom_call_target="tpu_custom_call", output_to_operand_aliasing={{}: (2, {})} | custom-call | flops 65536 | bytes 1024 | tf_op jit(solution)/shard_map/pallas_call | solution.py:64
  31.6 0.7 %collective-permute-done.6.received = bf16[256,256]{1,0:T(8,128)(2,1)S(1)} collective-permute-done((bf16[256,256]{1,0:T(8,128)(2,1)S(1)}, bf16[256,256]{1,0:T(8,128)(2,1)S(1)}, u32[]{:S(2)}, u32[]{:S(2)}) %collective-permute-start.6) | collective-permute-done | bytes 131104 | tf_op jit(solution)/shard_map/ppermute | solution.py:25
  32.3 0.7 %shard_map.64 = f32[256,768]{1,0:T(8,128)} custom-call(f32[256,256]{1,0:T(8,128)S(1)} %get-tuple-element.39.kept, bf16[256,256]{1,0:T(8,128)(2,1)S(1)} %collective-permute-done.6.received, f32[256,768]{1,0:T(8,128)} %shard_map.63.rest_0_), custom_call_target="tpu_custom_call", output_to_operand_aliasing={{}: (2, {})} | custom-call | flops 65536 | bytes 1024 | tf_op jit(solution)/shard_map/pallas_call | solution.py:64
Async XLA Ops:
  0.0 11.4 %collective-permute-start.1 = (bf16[512,768]{1,0:T(8,128)(2,1)}, bf16[512,768]{1,0:T(8,128)(2,1)S(1)}, u32[]{:S(2)}, u32[]{:S(2)}) collective-permute-start(bf16[512,768]{1,0:T(8,128)(2,1)} %sketch.3), channel_id=1, source_target_pairs={{0,2},{1,3},{2,0},{3,1},{4,6},{5,7},{6,4},{7,5},{8,10},{9,11},{10,... | collective-permute-start | bytes 2359304 | tf_op jit(solution)/shard_map/ppermute | solution.py:25
  1.7 12.7 %collective-permute-start = (bf16[512,512]{1,0:T(8,128)(2,1)S(1)}, bf16[512,512]{1,0:T(8,128)(2,1)S(1)}, u32[]{:S(2)}, u32[]{:S(2)}) collective-permute-start(bf16[512,512]{1,0:T(8,128)(2,1)S(1)} %get-tuple-element.24), channel_id=1, source_target_pairs={{0,30},{1,31},{2,4},{3,5},{4,2},{5,3},{6,8},{7,9},{8,6},{9,7},{10,... | collective-permute-start | bytes 1572872 | tf_op jit(solution)/shard_map/ppermute | solution.py:25
  7.4 6.4 %collective-permute-start.2 = (bf16[512,256]{1,0:T(8,128)(2,1)S(1)}, bf16[512,256]{1,0:T(8,128)(2,1)S(1)}, u32[]{:S(2)}, u32[]{:S(2)}) collective-permute-start(bf16[512,256]{1,0:T(8,128)(2,1)S(1)} %get-tuple-element.25.begun), channel_id=1, source_target_pairs={{0,1},{1,0},{2,3},{3,2},{4,5},{5,4},{6,7},{7,6},{8,9},{9,8},{10,11... | collective-permute-start | bytes 786440 | tf_op jit(solution)/shard_map/ppermute | solution.py:25
  8.9 2.5 %copy-start = (s32[1,1,3,1]{2,3,1,0:T(1,128)S(1)}, s32[1,1,3,1]{2,3,1,0:T(1,128)}, u32[]{:S(2)}) copy-start(s32[1,1,3,1]{2,3,1,0:T(1,128)} %param.7) | copy-start | bytes 40
  8.9 2.5 %copy-start.1 = (s32[1,1,2]{2,1,0:T(1,128)S(1)}, s32[1,1,2]{2,1,0:T(1,128)}, u32[]{:S(2)}) copy-start(s32[1,1,2]{2,1,0:T(1,128)} %param.8) | copy-start | bytes 28
  8.9 15.1 %collective-permute-start.4 = (bf16[512,256]{1,0:T(8,128)(2,1)S(1)}, bf16[512,256]{1,0:T(8,128)(2,1)S(1)}, u32[]{:S(2)}, u32[]{:S(2)}) collective-permute-start(bf16[512,256]{1,0:T(8,128)(2,1)S(1)} %get-tuple-element.37), channel_id=1, source_target_pairs={{0,0},{1,1},{2,4},{3,5},{4,2},{5,3},{6,6},{7,7},{8,8},{9,9},{10,12... | collective-permute-start | bytes 786440 | tf_op jit(solution)/shard_map/ppermute | solution.py:25
  14.9 7.4 %collective-permute-start.3 = (bf16[256,256]{1,0:T(8,128)(2,1)S(1)}, bf16[256,256]{1,0:T(8,128)(2,1)S(1)}, u32[]{:S(2)}, u32[]{:S(2)}) collective-permute-start(bf16[256,256]{1,0:T(8,128)(2,1)S(1)} %get-tuple-element.35.ours), channel_id=1, source_target_pairs={{0,1},{1,0},{2,2},{3,3},{4,4},{5,5},{6,7},{7,6},{8,9},{9,8},{10,10... | collective-permute-start | bytes 393224 | tf_op jit(solution)/shard_map/ppermute | solution.py:25
  18.4 8.1 %collective-permute-start.5 = (bf16[256,256]{1,0:T(8,128)(2,1)S(1)}, bf16[256,256]{1,0:T(8,128)(2,1)S(1)}, u32[]{:S(2)}, u32[]{:S(2)}) collective-permute-start(bf16[256,256]{1,0:T(8,128)(2,1)S(1)} %get-tuple-element.38.ours), channel_id=1, source_target_pairs={{0,1},{1,0},{2,2},{3,3},{4,4},{5,5},{6,7},{7,6},{8,9},{9,8},{10,10... | collective-permute-start | bytes 393224 | tf_op jit(solution)/shard_map/ppermute | solution.py:25
  20.8 8.5 %collective-permute-start.8 = (bf16[256,256]{1,0:T(8,128)(2,1)S(1)}, bf16[256,256]{1,0:T(8,128)(2,1)S(1)}, u32[]{:S(2)}, u32[]{:S(2)}) collective-permute-start(bf16[256,256]{1,0:T(8,128)(2,1)S(1)} %get-tuple-element.34.before), channel_id=1, source_target_pairs={{0,1},{1,0},{2,3},{3,2},{4,5},{5,4},{6,7},{7,6},{8,9},{9,8},{10,11... | collective-permute-start | bytes 393224 | tf_op jit(solution)/shard_map/ppermute | solution.py:25
  23.0 7.9 %collective-permute-start.7 = (bf16[256,256]{1,0:T(8,128)(2,1)S(1)}, bf16[256,256]{1,0:T(8,128)(2,1)S(1)}, u32[]{:S(2)}, u32[]{:S(2)}) collective-permute-start(bf16[256,256]{1,0:T(8,128)(2,1)S(1)} %get-tuple-element.36.before), channel_id=1, source_target_pairs={{0,1},{1,0},{2,3},{3,2},{4,5},{5,4},{6,7},{7,6},{8,9},{9,8},{10,11... | collective-permute-start | bytes 393224 | tf_op jit(solution)/shard_map/ppermute | solution.py:25
  27.1 5.2 %collective-permute-start.6 = (bf16[256,256]{1,0:T(8,128)(2,1)S(1)}, bf16[256,256]{1,0:T(8,128)(2,1)S(1)}, u32[]{:S(2)}, u32[]{:S(2)}) collective-permute-start(bf16[256,256]{1,0:T(8,128)(2,1)S(1)} %get-tuple-element.40), channel_id=1, source_target_pairs={{0,1},{1,0},{2,3},{3,2},{4,5},{5,4},{6,7},{7,6},{8,9},{9,8},{10,11... | collective-permute-start | bytes 393224 | tf_op jit(solution)/shard_map/ppermute | solution.py:25

commit v15 on v13

--- a/solution.py
+++ b/solution.py
@@ -7,7 +7,6 @@
 from jax.experimental.pallas import tpu as pltpu
 from jax.sharding import PartitionSpec as P
 
-SHARES = (2, 1)
 TRANSPOSED = (((0,), (0,)), ((), ()))
 
 
@@ -48,7 +47,7 @@
         scratch_shapes=list(scratch),
         input_output_aliases={len(placed) - 1: 0} if alias else {},
         compiler_params=pltpu.CompilerParams(vmem_limit_bytes=16 << 20),
-        cost_estimate=pl.CostEstimate(flops=flops, bytes_accessed=1 << 20, transcendentals=0),
+        cost_estimate=pl.CostEstimate(flops=flops, bytes_accessed=1 << 10, transcendentals=0),
     )(*placed)
 
 
@@ -68,13 +67,21 @@
     return basis.at[0, 0, pl.ds(pl.multiple_of(group * half, half), half)]
 
 
-def cut_kernel(sketch, basis, lent, first, second, sems):
-    theirs = half_rows(basis, 1 - lax.axis_index("group"), lent.shape[0])
-    early, late = first.shape[1], second.shape[1]
+def half_start(group, half):
+    return pl.multiple_of(group * half, half)
+
+
+def cut_kernel(sketch, basis, lent, first, last, sems):
+    group = lax.axis_index("group")
+    panels, width = last.shape
+    half = panels // 2
+    part = [pl.ds(i * width, width) for i in range(3)]
+    ours = pl.ds(half_start(group, half), half)
     pairs = [
-        (sketch.at[:, pl.ds(0, early)], first),
-        (theirs, lent),
-        (sketch.at[:, pl.ds(early, late)], second),
+        (sketch.at[ours, part[0]], first.at[pl.ds(0, half)]),
+        (sketch.at[:, part[1]], first.at[pl.ds(half, panels)]),
+        (half_rows(basis, 1 - group, lent.shape[0]), lent),
+        (sketch.at[:, part[2]], last),
     ]
     copy_all(pairs, sems)
 
@@ -111,9 +118,14 @@
     )
 
 
-def far_kernel(start, tiles, far, hit, hit_turned, missed, stays, kept, sent):
-    columns = pl.ds(start, far.shape[1])
-    product = jnp.dot(tiles[far_offset()], far[...], preferred_element_type=jnp.float32)
+def hand_kernel(before, first, ours):
+    del before
+    ours[...] = first[pl.ds(0, ours.shape[0]), :]
+
+
+def finish(start, tiles, far, hit, hit_turned, missed, stays, kept, sent):
+    columns = pl.ds(start, kept.shape[1])
+    product = jnp.dot(tiles[far_offset()], far, preferred_element_type=jnp.float32)
     sampled = (hit[:, columns] + product).astype(jnp.bfloat16)
     made = jnp.dot(hit_turned[...], sampled, preferred_element_type=jnp.float32)
     stay = stays[:, columns] > 0.0
@@ -122,6 +134,21 @@
     kept[...] = jnp.where(stay, made, other)
 
 
+def whole_kernel(start, before, far, tiles, *refs):
+    del before
+    panels = tiles.shape[2]
+    finish(start, tiles, far[pl.ds(far.shape[0] - panels, panels), :], *refs)
+
+
+def shared_kernel(start, before, ours, theirs, tiles, hit, hit_turned, missed, stays, kept, sent, far):
+    del before
+    half = ours.shape[0]
+    group = lax.axis_index("group")
+    far[pl.ds(half_start(group, half), half), :] = ours[...]
+    far[pl.ds(half_start(1 - group, half), half), :] = theirs[...]
+    finish(start, tiles, far[...], hit, hit_turned, missed, stays, kept, sent)
+
+
 def join_kernel(start, kept, received, *rest):
     out, total, sems = rest[-3:]
     total[...] = kept[...] + received[...].astype(jnp.float32)
@@ -132,18 +159,21 @@
     panels, columns = sketch.shape
     offsets, rows = far_tiles.shape[2], far_tiles.shape[4]
     half, rank = cluster_basis.shape[2] // 2, cluster_basis.shape[3]
-    widths = [columns * share // sum(SHARES) for share in SHARES]
-    starts = [sum(widths[:i]) for i in range(len(widths))]
+    width = columns // 3
     product = 2 * rows * panels * columns
     short, wide = sketch.dtype, jnp.float32
     copies = pltpu.SemaphoreType.DMA
-    lent, *parts = call(
+    lent, first, last = call(
         cut_kernel,
-        (on_chip((half, rank), short), *(on_chip((panels, width), short) for width in widths)),
+        (
+            on_chip((half, rank), short),
+            on_chip((panels + panels // 2, width), short),
+            on_chip((panels, width), short),
+        ),
         (),
         0,
         hbm=(sketch, cluster_basis),
-        scratch=(copies((3,)),),
+        scratch=(copies((4,)),),
     )
     own, tiles, kept = call(
         stage_kernel,
@@ -152,13 +182,14 @@
             on_chip((offsets, rows, panels), short),
             on_chip((half, rank), short),
         ),
-        (parts[0],),
+        (lent,),
         0,
         hbm=(sketch, far_tiles, cluster_basis),
         scratch=(copies((3,)),),
     )
+    first = swap_far(first)
     lent = from_behind(lent, "group", 1)
-    fars = [swap_far(part) for part in parts]
+    last = swap_far(last)
     near = swap_near(sketch)
     hit, miss, stays = call(
         local_kernel,
@@ -177,19 +208,28 @@
         (kept, lent, miss, stays),
         product // 2,
     )
-    out = None
-    for i, (start, width) in enumerate(zip(starts, widths)):
-        kept, sent = call(
-            functools.partial(far_kernel, start),
+    ours = call(hand_kernel, on_chip((panels // 2, width), short), (hit_turned, first), 0)
+    theirs = from_behind(ours, "group", 1)
+    far = on_chip((panels, width), short)
+    work = (
+        (width, whole_kernel, (first,), ()),
+        (2 * width, whole_kernel, (last,), ()),
+        (0, shared_kernel, (ours, theirs), (far,)),
+    )
+    out, before = None, ours
+    for start, kernel, panel, scratch in work:
+        kept, before = call(
+            functools.partial(kernel, start),
             (on_chip((rank, width), wide), on_chip((rank, width), short)),
-            (tiles, fars[i], hit, hit_turned, missed, stays),
-            2 * product * width // columns,
+            (before, *panel, tiles, hit, hit_turned, missed, stays),
+            0,
+            scratch=scratch,
         )
         out = call(
             functools.partial(join_kernel, start),
             pltpu.HBM((rank, columns), wide),
-            (kept, from_behind(sent, "group", 1)),
-            1 << 16,
+            (kept, from_behind(before, "group", 1)),
+            0,
             hbm=() if out is None else (out,),
             scratch=(on_chip((rank, width), wide), copies((1,))),
             to_hbm=True,

time: 28.2 us -> 30 us (1.064)
  starting transfers between devices: 8.43 us -> 11.6 us
  waiting for transfers between devices: 11.8 us -> 9.35 us
  Pallas kernels: 7.7 us -> 8.83 us
    ppermute x2, waiting for transfers between devices: 9.78 us -> 5.93 us  [swap_far(): lax.ppermute(array, 'blk', [(i, (i + 1 if i % 2 else i - 1) % devices) fo...]
    ppermute x3 -> x5, starting transfers between devices: 4.83 us -> 7.97 us  [from_behind(): lax.ppermute(array, axis, [(i, (i + by) % devices) for i in range(devices)])]
    ppermute x3 -> x5, waiting for transfers between devices: 1.98 us -> 3.41 us  [from_behind(): lax.ppermute(array, axis, [(i, (i + by) % devices) for i in range(devices)])]
    pallas_call x8 -> x11, Pallas kernels: 7.7 us -> 8.83 us  [call(): pl.pallas_call(kernel, out_shape=out_shape, in_specs=[scalar] * len(scala...]
  transfers between devices with their start and end apart: 6 -> 8, of which waited for: 5 -> 7; matrix products, arithmetic and copies ran while one was open for 0% -> 0% of each run, Pallas kernels for 25% -> 27%
where the time goes in v15:
time: 30 us; the launch traced here: 29.9 us
  starting transfers between devices  11.6 us (39%)
  waiting for transfers between devices  9.35 us (31%)
  Pallas kernels  8.83 us (29%)
    pallas_call x11, Pallas kernels, call(): pl.pallas_call(kernel, out_shape=out_shape, in_specs=[scalar] * len(scala...  8.83 us
    ppermute x5, starting transfers between devices, from_behind(): lax.ppermute(array, axis, [(i, (i + by) % devices) for i in range(devices)])  7.97 us
    ppermute x2, waiting for transfers between devices, swap_far(): lax.ppermute(array, 'blk', [(i, (i + 1 if i % 2 else i - 1) % devices) fo...  5.93 us
    ppermute x2, starting transfers between devices, swap_far(): lax.ppermute(array, 'blk', [(i, (i + 1 if i % 2 else i - 1) % devices) fo...  3.54 us
    ppermute x5, waiting for transfers between devices, from_behind(): lax.ppermute(array, axis, [(i, (i + by) % devices) for i in range(devices)])  3.41 us
  transfers between devices with their start and end apart: 8, of which 7 were waited for; matrix products, arithmetic and copies ran while one was open for 0% of the time, Pallas kernels for 27%

profile of v15, /device:TPU:1, one launch (start us, length us, event | category | flops | bytes accessed | tf_op | source)
XLA Modules:
  0.0 29.9 jit_solution(17043311395996683598)
XLA Ops:
  0.0 0.1 collective-permute-start.1
  0.1 1.2 %shard_map.55 = (bf16[512,256]{1,0:T(8,128)(2,1)S(1)}, bf16[768,256]{1,0:T(8,128)(2,1)S(1)}, bf16[512,256]{1,0:T(8,128)(2,1)S(1)}) custom-call(bf16[512,768]{1,0:T(8,128)(2,1)} %sketch.3, bf16[1,1,1024,256]{3,2,1,0:T(8,128)(2,1)} %basis.3), custom_call_target="tpu_custom_call" | custom-call | bytes 1024 | tf_op jit(solution)/shard_map/pallas_call | solution.py:42
  1.3 2.6 %collective-permute-start.2 = (bf16[768,256]{1,0:T(8,128)(2,1)S(1)}, bf16[768,256]{1,0:T(8,128)(2,1)S(1)}, u32[]{:S(2)}, u32[]{:S(2)}) collective-permute-start(bf16[768,256]{1,0:T(8,128)(2,1)S(1)} %get-tuple-element.29), channel_id=1, source_target_pairs={{0,30},{2,4},{4,2},{6,8},{8,6},{10,12},{12,10},{14,16},{16,14},{18... | collective-permute-start | bytes 1179656 | tf_op jit(solution)/shard_map/ppermute | solution.py:25
  3.9 1.2 %collective-permute-start = (bf16[512,256]{1,0:T(8,128)(2,1)S(1)}, bf16[512,256]{1,0:T(8,128)(2,1)S(1)}, u32[]{:S(2)}, u32[]{:S(2)}) collective-permute-start(bf16[512,256]{1,0:T(8,128)(2,1)S(1)} %get-tuple-element.22.begun), channel_id=1, source_target_pairs={{0,1},{1,0},{2,3},{3,2},{4,5},{5,4},{6,7},{7,6},{8,9},{9,8},{10,11... | collective-permute-start | bytes 786440 | tf_op jit(solution)/shard_map/ppermute | solution.py:15
  5.1 0.0 copy-start
  5.1 0.0 copy-start.1
  5.1 0.9 %collective-permute-start.3 = (bf16[512,256]{1,0:T(8,128)(2,1)S(1)}, bf16[512,256]{1,0:T(8,128)(2,1)S(1)}, u32[]{:S(2)}, u32[]{:S(2)}) collective-permute-start(bf16[512,256]{1,0:T(8,128)(2,1)S(1)} %get-tuple-element.33), channel_id=1, source_target_pairs={{0,30},{2,4},{4,2},{6,8},{8,6},{10,12},{12,10},{14,16},{16,14},{18... | collective-permute-start | bytes 786440 | tf_op jit(solution)/shard_map/ppermute | solution.py:25
  6.1 1.7 %shard_map.56 = (bf16[512,768]{1,0:T(8,128)(2,1)S(1)}, bf16[3,512,512]{2,1,0:T(8,128)(2,1)S(1)}, bf16[512,256]{1,0:T(8,128)(2,1)S(1)}) custom-call(bf16[512,256]{1,0:T(8,128)(2,1)S(1)} %get-tuple-element.22.begun, bf16[512,768]{1,0:T(8,128)(2,1)} %sketch.3, bf16[1,1,3,1,512,512]{5,4,3,2,1,0:T(8,128)(2,1)} %tiles.1, bf16[1,1,1024,256]{3,2,1,0:T(8,128)(2,1)} %basis.3), custom_call_target="tpu_custom_call" | custom-call | bytes 1024 | tf_op jit(solution)/shard_map/pallas_call | solution.py:42
  7.8 0.0 collective-permute-done.1.near
  7.8 0.0 copy-done
  7.8 0.0 copy-done.1
  7.8 1.5 %shard_map.57 = (f32[512,768]{1,0:T(8,128)S(1)}, bf16[512,768]{1,0:T(8,128)(2,1)S(1)}, f32[1,768]{1,0:T(1,128)S(1)}) custom-call(s32[3]{0:T(128)S(1)} %bitcast.3, s32[2]{0:T(128)S(1)} %bitcast.4, bf16[3,512,512]{2,1,0:T(8,128)(2,1)S(1)} %get-tuple-element.24.tiles, bf16[512,768]{1,0:T(8,128)(2,1)S(1)} %get-tuple-element.25.own, ...), custom_call_target="tpu_custom_call" | custom-call | flops 805306368 | bytes 1024 | tf_op jit(solution)/shard_map/pallas_call | solution.py:42
  9.3 0.1 collective-permute-done.lent
  9.4 0.5 %shard_map.58 = (bf16[256,512]{1,0:T(8,128)(2,1)S(1)}, f32[256,768]{1,0:T(8,128)S(1)}) custom-call(bf16[512,256]{1,0:T(8,128)(2,1)S(1)} %get-tuple-element.23.kept, bf16[512,256]{1,0:T(8,128)(2,1)S(1)} %collective-permute-done.lent, bf16[512,768]{1,0:T(8,128)(2,1)S(1)} %get-tuple-element.26.miss, f32[1,768]{1,0:T(1,128)S(1)} %get-tuple-element.27.stays.refs_3_), custom_call_target="tpu_custom_call" | custom-call | flops 201326592 | bytes 1024 | tf_op jit(solution)/shard_map/pallas_call | solution.py:42
  9.9 5.7 %collective-permute-done.2.first.far = bf16[768,256]{1,0:T(8,128)(2,1)S(1)} collective-permute-done((bf16[768,256]{1,0:T(8,128)(2,1)S(1)}, bf16[768,256]{1,0:T(8,128)(2,1)S(1)}, u32[]{:S(2)}, u32[]{:S(2)}) %collective-permute-start.2) | collective-permute-done | bytes 393248 | tf_op jit(solution)/shard_map/ppermute | solution.py:25
  15.7 2.7 %collective-permute-start.4 = (bf16[256,256]{1,0:T(8,128)(2,1)S(1)}, bf16[256,256]{1,0:T(8,128)(2,1)S(1)}, u32[]{:S(2)}, u32[]{:S(2)}) collective-permute-start(bf16[256,256]{1,0:T(8,128)(2,1)S(1)} %shard_map.59.before.ours), channel_id=1, source_target_pairs={{0,1},{1,0},{2,3},{3,2},{4,5},{5,4},{6,7},{7,6},{8,9},{9,8},{10,11... | collective-permute-start | bytes 393224 | tf_op jit(solution)/shard_map/ppermute | solution.py:15
  18.3 0.5 %shard_map.60 = (f32[256,256]{1,0:T(8,128)S(1)}, bf16[256,256]{1,0:T(8,128)(2,1)S(1)}) custom-call(bf16[256,256]{1,0:T(8,128)(2,1)S(1)} %shard_map.59.before.ours, bf16[768,256]{1,0:T(8,128)(2,1)S(1)} %collective-permute-done.2.first.far, bf16[3,512,512]{2,1,0:T(8,128)(2,1)S(1)} %get-tuple-element.24.tiles, f32[512,768]{1,0:T(8,128)S(1)} %get-tuple-element.30.refs_0_.hit, ...), custom_call_target="tpu_custom_call" | custom-call | bytes 1024 | tf_op jit(solution)/shard_map/pallas_call | solution.py:42
  18.9 0.1 collective-permute-start.7
  19.0 0.2 collective-permute-done.3.far
  19.2 0.6 %shard_map.61 = (f32[256,256]{1,0:T(8,128)S(1)}, bf16[256,256]{1,0:T(8,128)(2,1)S(1)}) custom-call(bf16[256,256]{1,0:T(8,128)(2,1)S(1)} %get-tuple-element.32.before, bf16[512,256]{1,0:T(8,128)(2,1)S(1)} %collective-permute-done.3.far, bf16[3,512,512]{2,1,0:T(8,128)(2,1)S(1)} %get-tuple-element.24.tiles, f32[512,768]{1,0:T(8,128)S(1)} %get-tuple-element.30.refs_0_.hit, ...), custom_call_target="tpu_custom_call" | custom-call | bytes 1024 | tf_op jit(solution)/shard_map/pallas_call | solution.py:42
  19.7 2.2 %collective-permute-start.6 = (bf16[256,256]{1,0:T(8,128)(2,1)S(1)}, bf16[256,256]{1,0:T(8,128)(2,1)S(1)}, u32[]{:S(2)}, u32[]{:S(2)}) collective-permute-start(bf16[256,256]{1,0:T(8,128)(2,1)S(1)} %get-tuple-element.34.before), channel_id=1, source_target_pairs={{0,1},{1,0},{2,3},{3,2},{4,5},{5,4},{6,7},{7,6},{8,9},{9,8},{10,11... | collective-permute-start | bytes 393224 | tf_op jit(solution)/shard_map/ppermute | solution.py:15
  22.0 0.3 collective-permute-done.4.theirs
  22.3 0.6 %shard_map.62 = (f32[256,256]{1,0:T(8,128)S(1)}, bf16[256,256]{1,0:T(8,128)(2,1)S(1)}) custom-call(bf16[256,256]{1,0:T(8,128)(2,1)S(1)} %get-tuple-element.34.before, bf16[256,256]{1,0:T(8,128)(2,1)S(1)} %shard_map.59.before.ours, bf16[256,256]{1,0:T(8,128)(2,1)S(1)} %collective-permute-done.4.theirs, bf16[3,512,512]{2,1,0:T(8,128)(2,1)S(1)} %get-tuple-element.24.tiles, ...), custom_call_target="tpu_custom_call" | custom-call | bytes 1024 | tf_op jit(solution)/shard_map/pallas_call | solution.py:42
  22.8 1.7 %collective-permute-start.5 = (bf16[256,256]{1,0:T(8,128)(2,1)S(1)}, bf16[256,256]{1,0:T(8,128)(2,1)S(1)}, u32[]{:S(2)}, u32[]{:S(2)}) collective-permute-start(bf16[256,256]{1,0:T(8,128)(2,1)S(1)} %get-tuple-element.36), channel_id=1, source_target_pairs={{0,1},{1,0},{2,3},{3,2},{4,5},{5,4},{6,7},{7,6},{8,9},{9,8},{10,11... | collective-permute-start | bytes 393224 | tf_op jit(solution)/shard_map/ppermute | solution.py:15
  24.6 0.5 %collective-permute-done.7.received = bf16[256,256]{1,0:T(8,128)(2,1)S(1)} collective-permute-done((bf16[256,256]{1,0:T(8,128)(2,1)S(1)}, bf16[256,256]{1,0:T(8,128)(2,1)S(1)}, u32[]{:S(2)}, u32[]{:S(2)}) %collective-permute-start.7) | collective-permute-done | bytes 131104 | tf_op jit(solution)/shard_map/ppermute | solution.py:15
  25.1 0.7 %shard_map.63.rest_0_ = f32[256,768]{1,0:T(8,128)} custom-call(f32[256,256]{1,0:T(8,128)S(1)} %get-tuple-element.38.kept, bf16[256,256]{1,0:T(8,128)(2,1)S(1)} %collective-permute-done.7.received), custom_call_target="tpu_custom_call" | custom-call | bytes 1024 | tf_op jit(solution)/shard_map/pallas_call | solution.py:42
  25.8 2.1 %collective-permute-done.6.received = bf16[256,256]{1,0:T(8,128)(2,1)S(1)} collective-permute-done((bf16[256,256]{1,0:T(8,128)(2,1)S(1)}, bf16[256,256]{1,0:T(8,128)(2,1)S(1)}, u32[]{:S(2)}, u32[]{:S(2)}) %collective-permute-start.6) | collective-permute-done | bytes 131104 | tf_op jit(solution)/shard_map/ppermute | solution.py:15
  27.9 0.7 %shard_map.64.rest_0_ = f32[256,768]{1,0:T(8,128)} custom-call(f32[256,256]{1,0:T(8,128)S(1)} %get-tuple-element.37.kept, bf16[256,256]{1,0:T(8,128)(2,1)S(1)} %collective-permute-done.6.received, f32[256,768]{1,0:T(8,128)} %shard_map.63.rest_0_), custom_call_target="tpu_custom_call", output_to_operand_aliasing={{}: (2, {})} | custom-call | bytes 1024 | tf_op jit(solution)/shard_map/pallas_call | solution.py:42
  28.6 0.5 %collective-permute-done.5.received = bf16[256,256]{1,0:T(8,128)(2,1)S(1)} collective-permute-done((bf16[256,256]{1,0:T(8,128)(2,1)S(1)}, bf16[256,256]{1,0:T(8,128)(2,1)S(1)}, u32[]{:S(2)}, u32[]{:S(2)}) %collective-permute-start.5) | collective-permute-done | bytes 131104 | tf_op jit(solution)/shard_map/ppermute | solution.py:15
  29.1 0.7 %shard_map.65 = f32[256,768]{1,0:T(8,128)} custom-call(f32[256,256]{1,0:T(8,128)S(1)} %get-tuple-element.35.kept, bf16[256,256]{1,0:T(8,128)(2,1)S(1)} %collective-permute-done.5.received, f32[256,768]{1,0:T(8,128)} %shard_map.64.rest_0_), custom_call_target="tpu_custom_call", output_to_operand_aliasing={{}: (2, {})} | custom-call | bytes 1024 | tf_op jit(solution)/shard_map/pallas_call | solution.py:42
  (1 shorter events, 0.0 us)
Async XLA Ops:
  0.0 7.8 %collective-permute-start.1 = (bf16[512,768]{1,0:T(8,128)(2,1)}, bf16[512,768]{1,0:T(8,128)(2,1)S(1)}, u32[]{:S(2)}, u32[]{:S(2)}) collective-permute-start(bf16[512,768]{1,0:T(8,128)(2,1)} %sketch.3), channel_id=1, source_target_pairs={{0,2},{2,0},{4,6},{6,4},{8,10},{10,8},{12,14},{14,12},{16,18},{18,... | collective-permute-start | bytes 2359304 | tf_op jit(solution)/shard_map/ppermute | solution.py:20
  1.3 14.4 %collective-permute-start.2 = (bf16[768,256]{1,0:T(8,128)(2,1)S(1)}, bf16[768,256]{1,0:T(8,128)(2,1)S(1)}, u32[]{:S(2)}, u32[]{:S(2)}) collective-permute-start(bf16[768,256]{1,0:T(8,128)(2,1)S(1)} %get-tuple-element.29), channel_id=1, source_target_pairs={{0,30},{2,4},{4,2},{6,8},{8,6},{10,12},{12,10},{14,16},{16,14},{18... | collective-permute-start | bytes 1179656 | tf_op jit(solution)/shard_map/ppermute | solution.py:25
  3.9 5.5 %collective-permute-start = (bf16[512,256]{1,0:T(8,128)(2,1)S(1)}, bf16[512,256]{1,0:T(8,128)(2,1)S(1)}, u32[]{:S(2)}, u32[]{:S(2)}) collective-permute-start(bf16[512,256]{1,0:T(8,128)(2,1)S(1)} %get-tuple-element.22.begun), channel_id=1, source_target_pairs={{0,1},{1,0},{2,3},{3,2},{4,5},{5,4},{6,7},{7,6},{8,9},{9,8},{10,11... | collective-permute-start | bytes 786440 | tf_op jit(solution)/shard_map/ppermute | solution.py:15
  5.1 2.6 %copy-start = (s32[1,1,3,1]{2,3,1,0:T(1,128)S(1)}, s32[1,1,3,1]{2,3,1,0:T(1,128)}, u32[]{:S(2)}) copy-start(s32[1,1,3,1]{2,3,1,0:T(1,128)} %param.7) | copy-start | bytes 40
  5.1 2.6 %copy-start.1 = (s32[1,1,2]{2,1,0:T(1,128)S(1)}, s32[1,1,2]{2,1,0:T(1,128)}, u32[]{:S(2)}) copy-start(s32[1,1,2]{2,1,0:T(1,128)} %param.8) | copy-start | bytes 28
  5.1 14.0 %collective-permute-start.3 = (bf16[512,256]{1,0:T(8,128)(2,1)S(1)}, bf16[512,256]{1,0:T(8,128)(2,1)S(1)}, u32[]{:S(2)}, u32[]{:S(2)}) collective-permute-start(bf16[512,256]{1,0:T(8,128)(2,1)S(1)} %get-tuple-element.33), channel_id=1, source_target_pairs={{0,30},{2,4},{4,2},{6,8},{8,6},{10,12},{12,10},{14,16},{16,14},{18... | collective-permute-start | bytes 786440 | tf_op jit(solution)/shard_map/ppermute | solution.py:25
  15.7 6.6 %collective-permute-start.4 = (bf16[256,256]{1,0:T(8,128)(2,1)S(1)}, bf16[256,256]{1,0:T(8,128)(2,1)S(1)}, u32[]{:S(2)}, u32[]{:S(2)}) collective-permute-start(bf16[256,256]{1,0:T(8,128)(2,1)S(1)} %shard_map.59.before.ours), channel_id=1, source_target_pairs={{0,1},{1,0},{2,3},{3,2},{4,5},{5,4},{6,7},{7,6},{8,9},{9,8},{10,11... | collective-permute-start | bytes 393224 | tf_op jit(solution)/shard_map/ppermute | solution.py:15
  18.9 6.2 %collective-permute-start.7 = (bf16[256,256]{1,0:T(8,128)(2,1)S(1)}, bf16[256,256]{1,0:T(8,128)(2,1)S(1)}, u32[]{:S(2)}, u32[]{:S(2)}) collective-permute-start(bf16[256,256]{1,0:T(8,128)(2,1)S(1)} %get-tuple-element.32.before), channel_id=1, source_target_pairs={{0,1},{1,0},{2,3},{3,2},{4,5},{5,4},{6,7},{7,6},{8,9},{9,8},{10,11... | collective-permute-start | bytes 393224 | tf_op jit(solution)/shard_map/ppermute | solution.py:15
  19.7 8.1 %collective-permute-start.6 = (bf16[256,256]{1,0:T(8,128)(2,1)S(1)}, bf16[256,256]{1,0:T(8,128)(2,1)S(1)}, u32[]{:S(2)}, u32[]{:S(2)}) collective-permute-start(bf16[256,256]{1,0:T(8,128)(2,1)S(1)} %get-tuple-element.34.before), channel_id=1, source_target_pairs={{0,1},{1,0},{2,3},{3,2},{4,5},{5,4},{6,7},{7,6},{8,9},{9,8},{10,11... | collective-permute-start | bytes 393224 | tf_op jit(solution)/shard_map/ppermute | solution.py:15
  22.8 6.3 %collective-permute-start.5 = (bf16[256,256]{1,0:T(8,128)(2,1)S(1)}, bf16[256,256]{1,0:T(8,128)(2,1)S(1)}, u32[]{:S(2)}, u32[]{:S(2)}) collective-permute-start(bf16[256,256]{1,0:T(8,128)(2,1)S(1)} %get-tuple-element.36), channel_id=1, source_target_pairs={{0,1},{1,0},{2,3},{3,2},{4,5},{5,4},{6,7},{7,6},{8,9},{9,8},{10,11... | collective-permute-start | bytes 393224 | tf_op jit(solution)/shard_map/ppermute | solution.py:15

commit v16 on v13

--- a/solution.py
+++ b/solution.py
@@ -68,14 +68,16 @@
     return basis.at[0, 0, pl.ds(pl.multiple_of(group * half, half), half)]
 
 
+def row_blocks_of(array, count=4):
+    rows = array.shape[0] // count
+    return [pl.ds(i * rows, rows) for i in range(count)]
+
+
 def cut_kernel(sketch, basis, lent, first, second, sems):
     theirs = half_rows(basis, 1 - lax.axis_index("group"), lent.shape[0])
-    early, late = first.shape[1], second.shape[1]
-    pairs = [
-        (sketch.at[:, pl.ds(0, early)], first),
-        (theirs, lent),
-        (sketch.at[:, pl.ds(early, late)], second),
-    ]
+    early, late = pl.ds(0, first.shape[1]), pl.ds(first.shape[1], second.shape[1])
+    pairs = [(sketch.at[rows, early], first.at[rows]) for rows in row_blocks_of(first)]
+    pairs += [(theirs, lent), (sketch.at[:, late], second)]
     copy_all(pairs, sems)
 
 
@@ -113,9 +115,14 @@
 
 def far_kernel(start, tiles, far, hit, hit_turned, missed, stays, kept, sent):
     columns = pl.ds(start, far.shape[1])
-    product = jnp.dot(tiles[far_offset()], far[...], preferred_element_type=jnp.float32)
-    sampled = (hit[:, columns] + product).astype(jnp.bfloat16)
-    made = jnp.dot(hit_turned[...], sampled, preferred_element_type=jnp.float32)
+    offset = far_offset()
+    sampled = []
+    for rows in row_blocks_of(hit, 2):
+        product = jnp.dot(tiles[offset, rows], far[...], preferred_element_type=jnp.float32)
+        sampled.append((hit[rows, columns] + product).astype(jnp.bfloat16))
+    made = jnp.dot(
+        hit_turned[...], jnp.concatenate(sampled), preferred_element_type=jnp.float32
+    )
     stay = stays[:, columns] > 0.0
     other = missed[:, columns]
     sent[...] = jnp.where(stay, other, made).astype(jnp.bfloat16)
@@ -124,8 +131,15 @@
 
 def join_kernel(start, kept, received, *rest):
     out, total, sems = rest[-3:]
-    total[...] = kept[...] + received[...].astype(jnp.float32)
-    copy_all([(total, out.at[:, pl.ds(start, total.shape[1])])], sems)
+    columns = pl.ds(start, total.shape[1])
+    under_way = []
+    for i, rows in enumerate(row_blocks_of(total, 2)):
+        total[rows] = kept[rows] + received[rows].astype(jnp.float32)
+        copy = pltpu.make_async_copy(total.at[rows], out.at[rows, columns], sems.at[i])
+        copy.start()
+        under_way.append(copy)
+    for copy in under_way:
+        copy.wait()
 
 
 def paired_body(sketch, far_tiles, row_blocks, owner_route, cluster_basis):
@@ -143,7 +157,7 @@
         (),
         0,
         hbm=(sketch, cluster_basis),
-        scratch=(copies((3,)),),
+        scratch=(copies((6,)),),
     )
     own, tiles, kept = call(
         stage_kernel,
@@ -191,7 +205,7 @@
             (kept, from_behind(sent, "group", 1)),
             1 << 16,
             hbm=() if out is None else (out,),
-            scratch=(on_chip((rank, width), wide), copies((1,))),
+            scratch=(on_chip((rank, width), wide), copies((2,))),
             to_hbm=True,
             alias=out is not None,
         )

time: 28.2 us -> 28.3 us (level)
  no operation moved by 1% of the time
where the time goes in v16:
time: 28.3 us; the launch traced here: 28.1 us
  waiting for transfers between devices  11.8 us (42%)
  starting transfers between devices  8.43 us (30%)
  Pallas kernels  7.79 us (28%)
    ppermute x2, waiting for transfers between devices, swap_far(): lax.ppermute(array, 'blk', [(i, (i + 1 if i % 2 else i - 1) % devices) fo...  9.8 us
    pallas_call x8, Pallas kernels, call(): pl.pallas_call(kernel, out_shape=out_shape, in_specs=[scalar] * len(scala...  7.79 us
    ppermute x3, starting transfers between devices, from_behind(): lax.ppermute(array, axis, [(i, (i + by) % devices) for i in range(devices)])  4.83 us
    ppermute x2, starting transfers between devices, swap_far(): lax.ppermute(array, 'blk', [(i, (i + 1 if i % 2 else i - 1) % devices) fo...  3.54 us
    ppermute x3, waiting for transfers between devices, from_behind(): lax.ppermute(array, axis, [(i, (i + by) % devices) for i in range(devices)])  1.98 us
  transfers between devices with their start and end apart: 6, of which 5 were waited for; matrix products, arithmetic and copies ran while one was open for 0% of the time, Pallas kernels for 25%

profile of v16, /device:TPU:1, one launch (start us, length us, event | category | flops | bytes accessed | tf_op | source)
XLA Modules:
  0.0 28.1 jit_solution(487920470458650517)
XLA Ops:
  0.0 0.1 collective-permute-start.1
  0.1 1.3 %shard_map.55 = (bf16[512,256]{1,0:T(8,128)(2,1)S(1)}, bf16[512,512]{1,0:T(8,128)(2,1)S(1)}, bf16[512,256]{1,0:T(8,128)(2,1)S(1)}) custom-call(bf16[512,768]{1,0:T(8,128)(2,1)} %sketch.3, bf16[1,1,1024,256]{3,2,1,0:T(8,128)(2,1)} %basis.3), custom_call_target="tpu_custom_call" | custom-call | bytes 1048576 | tf_op jit(solution)/shard_map/pallas_call | solution.py:43
  1.4 2.6 %collective-permute-start.4 = (bf16[512,512]{1,0:T(8,128)(2,1)S(1)}, bf16[512,512]{1,0:T(8,128)(2,1)S(1)}, u32[]{:S(2)}, u32[]{:S(2)}) collective-permute-start(bf16[512,512]{1,0:T(8,128)(2,1)S(1)} %get-tuple-element.20.begun), channel_id=1, source_target_pairs={{0,30},{2,4},{4,2},{6,8},{8,6},{10,12},{12,10},{14,16},{16,14},{18... | collective-permute-start | bytes 1572872 | tf_op jit(solution)/shard_map/ppermute | solution.py:26
  4.0 1.2 %collective-permute-start.2 = (bf16[512,256]{1,0:T(8,128)(2,1)S(1)}, bf16[512,256]{1,0:T(8,128)(2,1)S(1)}, u32[]{:S(2)}, u32[]{:S(2)}) collective-permute-start(bf16[512,256]{1,0:T(8,128)(2,1)S(1)} %get-tuple-element.26), channel_id=1, source_target_pairs={{0,1},{1,0},{2,3},{3,2},{4,5},{5,4},{6,7},{7,6},{8,9},{9,8},{10,11... | collective-permute-start | bytes 786440 | tf_op jit(solution)/shard_map/ppermute | solution.py:16
  5.3 0.0 copy-start
  5.3 0.0 copy-start.1
  5.3 0.9 %collective-permute-start = (bf16[512,256]{1,0:T(8,128)(2,1)S(1)}, bf16[512,256]{1,0:T(8,128)(2,1)S(1)}, u32[]{:S(2)}, u32[]{:S(2)}) collective-permute-start(bf16[512,256]{1,0:T(8,128)(2,1)S(1)} %get-tuple-element.22), channel_id=1, source_target_pairs={{0,30},{2,4},{4,2},{6,8},{8,6},{10,12},{12,10},{14,16},{16,14},{18... | collective-permute-start | bytes 786440 | tf_op jit(solution)/shard_map/ppermute | solution.py:26
  6.2 1.7 %shard_map.56 = (bf16[512,768]{1,0:T(8,128)(2,1)S(1)}, bf16[3,512,512]{2,1,0:T(8,128)(2,1)S(1)}, bf16[512,256]{1,0:T(8,128)(2,1)S(1)}) custom-call(bf16[512,512]{1,0:T(8,128)(2,1)S(1)} %get-tuple-element.20.begun, bf16[512,768]{1,0:T(8,128)(2,1)} %sketch.3, bf16[1,1,3,1,512,512]{5,4,3,2,1,0:T(8,128)(2,1)} %tiles.1, bf16[1,1,1024,256]{3,2,1,0:T(8,128)(2,1)} %basis.3), custom_call_target="tpu_custom_call" | custom-call | bytes 1048576 | tf_op jit(solution)/shard_map/pallas_call | solution.py:43
  7.9 0.0 collective-permute-done.1.near
  7.9 0.0 copy-done
  7.9 0.0 copy-done.1
  7.9 1.5 %shard_map.57 = (f32[512,768]{1,0:T(8,128)S(1)}, bf16[512,768]{1,0:T(8,128)(2,1)S(1)}, f32[1,768]{1,0:T(1,128)S(1)}) custom-call(s32[3]{0:T(128)S(1)} %bitcast.3, s32[2]{0:T(128)S(1)} %bitcast.4, bf16[3,512,512]{2,1,0:T(8,128)(2,1)S(1)} %get-tuple-element.21.tiles, bf16[512,768]{1,0:T(8,128)(2,1)S(1)} %get-tuple-element.23.own, ...), custom_call_target="tpu_custom_call" | custom-call | flops 805306368 | bytes 1048576 | tf_op jit(solution)/shard_map/pallas_call | solution.py:43
  9.4 0.1 collective-permute-done.2.lent
  9.5 0.5 %shard_map.58 = (bf16[256,512]{1,0:T(8,128)(2,1)S(1)}, f32[256,768]{1,0:T(8,128)S(1)}) custom-call(bf16[512,256]{1,0:T(8,128)(2,1)S(1)} %get-tuple-element.25.kept, bf16[512,256]{1,0:T(8,128)(2,1)S(1)} %collective-permute-done.2.lent, bf16[512,768]{1,0:T(8,128)(2,1)S(1)} %get-tuple-element.27.miss, f32[1,768]{1,0:T(1,128)S(1)} %get-tuple-element.28.stays), custom_call_target="tpu_custom_call" | custom-call | flops 201326592 | bytes 1048576 | tf_op jit(solution)/shard_map/pallas_call | solution.py:43
  10.0 9.6 %collective-permute-done.4.far = bf16[512,512]{1,0:T(8,128)(2,1)S(1)} collective-permute-done((bf16[512,512]{1,0:T(8,128)(2,1)S(1)}, bf16[512,512]{1,0:T(8,128)(2,1)S(1)}, u32[]{:S(2)}, u32[]{:S(2)}) %collective-permute-start.4) | collective-permute-done | bytes 524320 | tf_op jit(solution)/shard_map/ppermute | solution.py:26
  19.6 0.6 %shard_map.60 = (f32[256,512]{1,0:T(8,128)S(1)}, bf16[256,512]{1,0:T(8,128)(2,1)S(1)}) custom-call(bf16[3,512,512]{2,1,0:T(8,128)(2,1)S(1)} %get-tuple-element.21.tiles, bf16[512,512]{1,0:T(8,128)(2,1)S(1)} %collective-permute-done.4.far, f32[512,768]{1,0:T(8,128)S(1)} %get-tuple-element.24.hit, bf16[256,512]{1,0:T(8,128)(2,1)S(1)} %get-tuple-element.29.hit_turned, ...), custom_call_target="tpu_custom_call" | custom-call | flops 536870912 | bytes 1048576 | tf_op jit(solution)/shard_map/pallas_call | solution.py:43
  20.2 1.9 %collective-permute-start.5 = (bf16[256,512]{1,0:T(8,128)(2,1)S(1)}, bf16[256,512]{1,0:T(8,128)(2,1)S(1)}, u32[]{:S(2)}, u32[]{:S(2)}) collective-permute-start(bf16[256,512]{1,0:T(8,128)(2,1)S(1)} %get-tuple-element.34), channel_id=1, source_target_pairs={{0,1},{1,0},{2,3},{3,2},{4,5},{5,4},{6,7},{7,6},{8,9},{9,8},{10,11... | collective-permute-start | bytes 786440 | tf_op jit(solution)/shard_map/ppermute | solution.py:16
  22.2 0.2 collective-permute-done.far
  22.4 0.6 %shard_map.59 = (f32[256,256]{1,0:T(8,128)S(1)}, bf16[256,256]{1,0:T(8,128)(2,1)S(1)}) custom-call(bf16[3,512,512]{2,1,0:T(8,128)(2,1)S(1)} %get-tuple-element.21.tiles, bf16[512,256]{1,0:T(8,128)(2,1)S(1)} %collective-permute-done.far, f32[512,768]{1,0:T(8,128)S(1)} %get-tuple-element.24.hit, bf16[256,512]{1,0:T(8,128)(2,1)S(1)} %get-tuple-element.29.hit_turned, ...), custom_call_target="tpu_custom_call" | custom-call | flops 268435456 | bytes 1048576 | tf_op jit(solution)/shard_map/pallas_call | solution.py:43
  23.0 1.6 %collective-permute-start.3 = (bf16[256,256]{1,0:T(8,128)(2,1)S(1)}, bf16[256,256]{1,0:T(8,128)(2,1)S(1)}, u32[]{:S(2)}, u32[]{:S(2)}) collective-permute-start(bf16[256,256]{1,0:T(8,128)(2,1)S(1)} %get-tuple-element.32), channel_id=1, source_target_pairs={{0,1},{1,0},{2,3},{3,2},{4,5},{5,4},{6,7},{7,6},{8,9},{9,8},{10,11... | collective-permute-start | bytes 393224 | tf_op jit(solution)/shard_map/ppermute | solution.py:16
  24.6 1.3 %collective-permute-done.5.received = bf16[256,512]{1,0:T(8,128)(2,1)S(1)} collective-permute-done((bf16[256,512]{1,0:T(8,128)(2,1)S(1)}, bf16[256,512]{1,0:T(8,128)(2,1)S(1)}, u32[]{:S(2)}, u32[]{:S(2)}) %collective-permute-start.5) | collective-permute-done | bytes 262176 | tf_op jit(solution)/shard_map/ppermute | solution.py:16
  25.9 0.8 %shard_map.61.rest_0_ = f32[256,768]{1,0:T(8,128)} custom-call(f32[256,512]{1,0:T(8,128)S(1)} %get-tuple-element.33.kept, bf16[256,512]{1,0:T(8,128)(2,1)S(1)} %collective-permute-done.5.received), custom_call_target="tpu_custom_call" | custom-call | flops 65536 | bytes 1048576 | tf_op jit(solution)/shard_map/pallas_call | solution.py:43
  26.8 0.6 %collective-permute-done.3.received = bf16[256,256]{1,0:T(8,128)(2,1)S(1)} collective-permute-done((bf16[256,256]{1,0:T(8,128)(2,1)S(1)}, bf16[256,256]{1,0:T(8,128)(2,1)S(1)}, u32[]{:S(2)}, u32[]{:S(2)}) %collective-permute-start.3) | collective-permute-done | bytes 131104 | tf_op jit(solution)/shard_map/ppermute | solution.py:16
  27.4 0.7 %shard_map.62 = f32[256,768]{1,0:T(8,128)} custom-call(f32[256,256]{1,0:T(8,128)S(1)} %get-tuple-element.31.kept, bf16[256,256]{1,0:T(8,128)(2,1)S(1)} %collective-permute-done.3.received, f32[256,768]{1,0:T(8,128)} %shard_map.61.rest_0_), custom_call_target="tpu_custom_call", output_to_operand_aliasing={{}: (2, {})} | custom-call | flops 65536 | bytes 1048576 | tf_op jit(solution)/shard_map/pallas_call | solution.py:43
Async XLA Ops:
  0.0 7.9 %collective-permute-start.1 = (bf16[512,768]{1,0:T(8,128)(2,1)}, bf16[512,768]{1,0:T(8,128)(2,1)S(1)}, u32[]{:S(2)}, u32[]{:S(2)}) collective-permute-start(bf16[512,768]{1,0:T(8,128)(2,1)} %sketch.3), channel_id=1, source_target_pairs={{0,2},{2,0},{4,6},{6,4},{8,10},{10,8},{12,14},{14,12},{16,18},{18,... | collective-permute-start | bytes 2359304 | tf_op jit(solution)/shard_map/ppermute | solution.py:21
  1.4 18.2 %collective-permute-start.4 = (bf16[512,512]{1,0:T(8,128)(2,1)S(1)}, bf16[512,512]{1,0:T(8,128)(2,1)S(1)}, u32[]{:S(2)}, u32[]{:S(2)}) collective-permute-start(bf16[512,512]{1,0:T(8,128)(2,1)S(1)} %get-tuple-element.20.begun), channel_id=1, source_target_pairs={{0,30},{2,4},{4,2},{6,8},{8,6},{10,12},{12,10},{14,16},{16,14},{18... | collective-permute-start | bytes 1572872 | tf_op jit(solution)/shard_map/ppermute | solution.py:26
  4.0 5.5 %collective-permute-start.2 = (bf16[512,256]{1,0:T(8,128)(2,1)S(1)}, bf16[512,256]{1,0:T(8,128)(2,1)S(1)}, u32[]{:S(2)}, u32[]{:S(2)}) collective-permute-start(bf16[512,256]{1,0:T(8,128)(2,1)S(1)} %get-tuple-element.26), channel_id=1, source_target_pairs={{0,1},{1,0},{2,3},{3,2},{4,5},{5,4},{6,7},{7,6},{8,9},{9,8},{10,11... | collective-permute-start | bytes 786440 | tf_op jit(solution)/shard_map/ppermute | solution.py:16
  5.3 2.6 %copy-start = (s32[1,1,3,1]{2,3,1,0:T(1,128)S(1)}, s32[1,1,3,1]{2,3,1,0:T(1,128)}, u32[]{:S(2)}) copy-start(s32[1,1,3,1]{2,3,1,0:T(1,128)} %param.7) | copy-start | bytes 40
  5.3 2.6 %copy-start.1 = (s32[1,1,2]{2,1,0:T(1,128)S(1)}, s32[1,1,2]{2,1,0:T(1,128)}, u32[]{:S(2)}) copy-start(s32[1,1,2]{2,1,0:T(1,128)} %param.8) | copy-start | bytes 28
  5.3 17.2 %collective-permute-start = (bf16[512,256]{1,0:T(8,128)(2,1)S(1)}, bf16[512,256]{1,0:T(8,128)(2,1)S(1)}, u32[]{:S(2)}, u32[]{:S(2)}) collective-permute-start(bf16[512,256]{1,0:T(8,128)(2,1)S(1)} %get-tuple-element.22), channel_id=1, source_target_pairs={{0,30},{2,4},{4,2},{6,8},{8,6},{10,12},{12,10},{14,16},{16,14},{18... | collective-permute-start | bytes 786440 | tf_op jit(solution)/shard_map/ppermute | solution.py:26
  20.2 5.7 %collective-permute-start.5 = (bf16[256,512]{1,0:T(8,128)(2,1)S(1)}, bf16[256,512]{1,0:T(8,128)(2,1)S(1)}, u32[]{:S(2)}, u32[]{:S(2)}) collective-permute-start(bf16[256,512]{1,0:T(8,128)(2,1)S(1)} %get-tuple-element.34), channel_id=1, source_target_pairs={{0,1},{1,0},{2,3},{3,2},{4,5},{5,4},{6,7},{7,6},{8,9},{9,8},{10,11... | collective-permute-start | bytes 786440 | tf_op jit(solution)/shard_map/ppermute | solution.py:16
  23.0 4.4 %collective-permute-start.3 = (bf16[256,256]{1,0:T(8,128)(2,1)S(1)}, bf16[256,256]{1,0:T(8,128)(2,1)S(1)}, u32[]{:S(2)}, u32[]{:S(2)}) collective-permute-start(bf16[256,256]{1,0:T(8,128)(2,1)S(1)} %get-tuple-element.32), channel_id=1, source_target_pairs={{0,1},{1,0},{2,3},{3,2},{4,5},{5,4},{6,7},{7,6},{8,9},{9,8},{10,11... | collective-permute-start | bytes 393224 | tf_op jit(solution)/shard_map/ppermute | solution.py:16

commit v17 on v13

--- a/solution.py
+++ b/solution.py
@@ -7,7 +7,7 @@
 from jax.experimental.pallas import tpu as pltpu
 from jax.sharding import PartitionSpec as P
 
-SHARES = (2, 1)
+SHARES = (1, 2)
 TRANSPOSED = (((0,), (0,)), ((), ()))
 
 
@@ -48,7 +48,7 @@
         scratch_shapes=list(scratch),
         input_output_aliases={len(placed) - 1: 0} if alias else {},
         compiler_params=pltpu.CompilerParams(vmem_limit_bytes=16 << 20),
-        cost_estimate=pl.CostEstimate(flops=flops, bytes_accessed=1 << 20, transcendentals=0),
+        cost_estimate=pl.CostEstimate(flops=flops, bytes_accessed=1 << 10, transcendentals=0),
     )(*placed)
 
 
@@ -68,15 +68,22 @@
     return basis.at[0, 0, pl.ds(pl.multiple_of(group * half, half), half)]
 
 
-def cut_kernel(sketch, basis, lent, first, second, sems):
+def half_start(group, half):
+    return pl.multiple_of(group * half, half)
+
+
+def share_kernel(sketch, shared, sems):
+    half, width = shared.shape
+    rows = pl.ds(half_start(lax.axis_index("group"), half), half)
+    copy_all([(sketch.at[rows, pl.ds(0, width)], shared)], sems)
+
+
+def cut_kernel(begun, sketch, basis, lent, whole, sems):
+    del begun
     theirs = half_rows(basis, 1 - lax.axis_index("group"), lent.shape[0])
-    early, late = first.shape[1], second.shape[1]
-    pairs = [
-        (sketch.at[:, pl.ds(0, early)], first),
-        (theirs, lent),
-        (sketch.at[:, pl.ds(early, late)], second),
-    ]
-    copy_all(pairs, sems)
+    width = whole.shape[1]
+    columns = pl.ds(sketch.shape[1] - width, width)
+    copy_all([(sketch.at[:, columns], whole), (theirs, lent)], sems)
 
 
 def stage_kernel(begun, sketch, tiles, basis, own, staged, kept, sems):
@@ -111,6 +118,19 @@
     )
 
 
+def shared_kernel(start, tiles, ours, theirs, hit, hit_turned, missed, stays, kept, sent, far):
+    half = ours.shape[0]
+    group = lax.axis_index("group")
+    far[pl.ds(half_start(group, half), half), :] = ours[...]
+    far[pl.ds(half_start(1 - group, half), half), :] = theirs[...]
+    far_kernel(start, tiles, far, hit, hit_turned, missed, stays, kept, sent)
+
+
+def whole_kernel(start, before, *refs):
+    del before
+    far_kernel(start, *refs)
+
+
 def far_kernel(start, tiles, far, hit, hit_turned, missed, stays, kept, sent):
     columns = pl.ds(start, far.shape[1])
     product = jnp.dot(tiles[far_offset()], far[...], preferred_element_type=jnp.float32)
@@ -137,13 +157,21 @@
     product = 2 * rows * panels * columns
     short, wide = sketch.dtype, jnp.float32
     copies = pltpu.SemaphoreType.DMA
-    lent, *parts = call(
-        cut_kernel,
-        (on_chip((half, rank), short), *(on_chip((panels, width), short) for width in widths)),
+    shared = call(
+        share_kernel,
+        on_chip((panels // 2, widths[0]), short),
         (),
         0,
+        hbm=(sketch,),
+        scratch=(copies((1,)),),
+    )
+    lent, whole = call(
+        cut_kernel,
+        (on_chip((half, rank), short), on_chip((panels, widths[1]), short)),
+        (shared,),
+        0,
         hbm=(sketch, cluster_basis),
-        scratch=(copies((3,)),),
+        scratch=(copies((2,)),),
     )
     own, tiles, kept = call(
         stage_kernel,
@@ -152,13 +180,15 @@
             on_chip((offsets, rows, panels), short),
             on_chip((half, rank), short),
         ),
-        (parts[0],),
-        0,
+        (lent,),
+        10**10,
         hbm=(sketch, far_tiles, cluster_basis),
         scratch=(copies((3,)),),
     )
     lent = from_behind(lent, "group", 1)
-    fars = [swap_far(part) for part in parts]
+    ours = swap_far(shared)
+    whole = swap_far(whole)
+    theirs = from_behind(ours, "group", 1)
     near = swap_near(sketch)
     hit, miss, stays = call(
         local_kernel,
@@ -168,28 +198,34 @@
             on_chip((1, columns), wide),
         ),
         (tiles, own, near),
-        2 * product,
+        3 * 10**9,
         scalars=(row_blocks.reshape(-1), owner_route.reshape(-1)),
     )
     hit_turned, missed = call(
         turn_kernel,
         (on_chip((rank, half), short), on_chip((rank, columns), wide)),
         (kept, lent, miss, stays),
-        product // 2,
-    )
-    out = None
-    for i, (start, width) in enumerate(zip(starts, widths)):
+        0,
+    )
+    far = pltpu.VMEM((panels, widths[0]), short)
+    work = (
+        (0, widths[0], shared_kernel, (tiles, ours, theirs), 0, (far,)),
+        (starts[1], widths[1], whole_kernel, (tiles, whole), 0, ()),
+    )
+    out = sent = None
+    for start, width, kernel, inputs, flops, scratch in work:
         kept, sent = call(
-            functools.partial(far_kernel, start),
+            functools.partial(kernel, start),
             (on_chip((rank, width), wide), on_chip((rank, width), short)),
-            (tiles, fars[i], hit, hit_turned, missed, stays),
-            2 * product * width // columns,
+            (*(() if sent is None else (sent,)), *inputs, hit, hit_turned, missed, stays),
+            flops,
+            scratch=scratch,
         )
         out = call(
             functools.partial(join_kernel, start),
             pltpu.HBM((rank, columns), wide),
             (kept, from_behind(sent, "group", 1)),
-            1 << 16,
+            10**10 if out is None else 0,
             hbm=() if out is None else (out,),
             scratch=(on_chip((rank, width), wide), copies((1,))),
             to_hbm=True,

time: 28.2 us -> 30.8 us (1.092)
  the two profiles are of different devices: /device:TPU:1 before, /device:TPU:0 now
where the time goes in v17:
time: 30.8 us; the launch traced here: 30.6 us
  waiting for transfers between devices  12.5 us (41%)
  starting transfers between devices  9.45 us (31%)
  Pallas kernels  8.57 us (28%)
    ppermute x4, waiting for transfers between devices, from_behind(): lax.ppermute(array, axis, [(i, (i + by) % devices) for i in range(devices)])  9.84 us
    pallas_call x9, Pallas kernels, call(): pl.pallas_call(kernel, out_shape=out_shape, in_specs=[scalar] * len(scala...  8.57 us
    ppermute x2, starting transfers between devices, swap_far(): lax.ppermute(array, 'blk', [(i, (i + 1 if i % 2 else i - 1) % devices) fo...  5.71 us
    ppermute x4, starting transfers between devices, from_behind(): lax.ppermute(array, axis, [(i, (i + by) % devices) for i in range(devices)])  3.29 us
    ppermute x2, waiting for transfers between devices, swap_far(): lax.ppermute(array, 'blk', [(i, (i + 1 if i % 2 else i - 1) % devices) fo...  2.68 us
  transfers between devices with their start and end apart: 7, of which 5 were waited for; matrix products, arithmetic and copies ran while one was open for 0% of the time, Pallas kernels for 25%

profile of v17, /device:TPU:0, one launch (start us, length us, event | category | flops | bytes accessed | tf_op | source)
XLA Modules:
  0.0 30.6 jit_solution(8120627368906663312)
XLA Ops:
  0.0 0.5 %collective-permute-start.2 = (bf16[512,768]{1,0:T(8,128)(2,1)}, bf16[512,768]{1,0:T(8,128)(2,1)S(1)}, u32[]{:S(2)}, u32[]{:S(2)}) collective-permute-start(bf16[512,768]{1,0:T(8,128)(2,1)} %sketch.5), channel_id=1, source_target_pairs={{0,2},{2,0},{4,6},{6,4},{8,10},{10,8},{12,14},{14,12},{16,18},{18,... | collective-permute-start | bytes 2359304 | tf_op jit(solution)/shard_map/ppermute | solution.py:21
  0.5 0.9 %shard_map.55.begun = bf16[256,256]{1,0:T(8,128)(2,1)S(1)} custom-call(bf16[512,768]{1,0:T(8,128)(2,1)} %sketch.5), custom_call_target="tpu_custom_call" | custom-call | bytes 1024 | tf_op jit(solution)/shard_map/pallas_call | solution.py:43
  1.4 5.7 %collective-permute-start = (bf16[256,256]{1,0:T(8,128)(2,1)S(1)}, bf16[256,256]{1,0:T(8,128)(2,1)S(1)}, u32[]{:S(2)}, u32[]{:S(2)}) collective-permute-start(bf16[256,256]{1,0:T(8,128)(2,1)S(1)} %shard_map.55.begun), channel_id=1, source_target_pairs={{0,30},{2,4},{4,2},{6,8},{8,6},{10,12},{12,10},{14,16},{16,14},{18... | collective-permute-start | bytes 393224 | tf_op jit(solution)/shard_map/ppermute | solution.py:26
  7.1 1.1 %shard_map.56 = (bf16[512,256]{1,0:T(8,128)(2,1)S(1)}, bf16[512,512]{1,0:T(8,128)(2,1)S(1)}) custom-call(bf16[256,256]{1,0:T(8,128)(2,1)S(1)} %shard_map.55.begun, bf16[512,768]{1,0:T(8,128)(2,1)} %sketch.5, bf16[1,1,1024,256]{3,2,1,0:T(8,128)(2,1)} %basis.3), custom_call_target="tpu_custom_call" | custom-call | bytes 1024 | tf_op jit(solution)/shard_map/pallas_call | solution.py:43
  8.2 1.6 %collective-permute-start.3 = (bf16[512,256]{1,0:T(8,128)(2,1)S(1)}, bf16[512,256]{1,0:T(8,128)(2,1)S(1)}, u32[]{:S(2)}, u32[]{:S(2)}) collective-permute-start(bf16[512,256]{1,0:T(8,128)(2,1)S(1)} %get-tuple-element.19.begun), channel_id=1, source_target_pairs={{0,1},{1,0},{2,3},{3,2},{4,5},{5,4},{6,7},{7,6},{8,9},{9,8},{10,11... | collective-permute-start | bytes 786440 | tf_op jit(solution)/shard_map/ppermute | solution.py:16
  9.8 0.0 copy-start
  9.8 0.0 copy-start.1
  9.8 0.0 collective-permute-start.4
  9.8 1.7 %shard_map.57 = (bf16[512,768]{1,0:T(8,128)(2,1)S(1)}, bf16[3,512,512]{2,1,0:T(8,128)(2,1)S(1)}, bf16[512,256]{1,0:T(8,128)(2,1)S(1)}) custom-call(bf16[512,256]{1,0:T(8,128)(2,1)S(1)} %get-tuple-element.19.begun, bf16[512,768]{1,0:T(8,128)(2,1)} %sketch.5, bf16[1,1,3,1,512,512]{5,4,3,2,1,0:T(8,128)(2,1)} %tiles.1, bf16[1,1,1024,256]{3,2,1,0:T(8,128)(2,1)} %basis.3), custom_call_target="tpu_custom_call" | custom-call | flops 10000000000 | bytes 1024 | tf_op jit(solution)/shard_map/pallas_call | solution.py:43
  11.5 0.0 collective-permute-done.ours
  11.5 0.6 %collective-permute-start.1 = (bf16[256,256]{1,0:T(8,128)(2,1)S(1)}, bf16[256,256]{1,0:T(8,128)(2,1)S(1)}, u32[]{:S(2)}, u32[]{:S(2)}) collective-permute-start(bf16[256,256]{1,0:T(8,128)(2,1)S(1)} %collective-permute-done.ours), channel_id=1, source_target_pairs={{0,1},{1,0},{2,3},{3,2},{4,5},{5,4},{6,7},{7,6},{8,9},{9,8},{10,11... | collective-permute-start | bytes 393224 | tf_op jit(solution)/shard_map/ppermute | solution.py:16
  12.1 0.0 collective-permute-done.2.near
  12.1 0.0 copy-done
  12.1 0.0 copy-done.1
  12.1 1.5 %shard_map.58 = (f32[512,768]{1,0:T(8,128)S(1)}, bf16[512,768]{1,0:T(8,128)(2,1)S(1)}, f32[1,768]{1,0:T(1,128)S(1)}) custom-call(s32[3]{0:T(128)S(1)} %bitcast.3, s32[2]{0:T(128)S(1)} %bitcast.4, bf16[3,512,512]{2,1,0:T(8,128)(2,1)S(1)} %get-tuple-element.20.tiles.refs_0_, bf16[512,768]{1,0:T(8,128)(2,1)S(1)} %get-tuple-element.21.own, ...), custom_call_target="tpu_custom_call" | custom-call | flops 3000000000 | bytes 1024 | tf_op jit(solution)/shard_map/pallas_call | solution.py:43
  13.7 2.3 %collective-permute-done.3.lent = bf16[512,256]{1,0:T(8,128)(2,1)S(1)} collective-permute-done((bf16[512,256]{1,0:T(8,128)(2,1)S(1)}, bf16[512,256]{1,0:T(8,128)(2,1)S(1)}, u32[]{:S(2)}, u32[]{:S(2)}) %collective-permute-start.3) | collective-permute-done | bytes 262176 | tf_op jit(solution)/shard_map/ppermute | solution.py:16
  16.0 0.5 %shard_map.59 = (bf16[256,512]{1,0:T(8,128)(2,1)S(1)}, f32[256,768]{1,0:T(8,128)S(1)}) custom-call(bf16[512,256]{1,0:T(8,128)(2,1)S(1)} %get-tuple-element.23.kept, bf16[512,256]{1,0:T(8,128)(2,1)S(1)} %collective-permute-done.3.lent, bf16[512,768]{1,0:T(8,128)(2,1)S(1)} %get-tuple-element.24.miss, f32[1,768]{1,0:T(1,128)S(1)} %get-tuple-element.25.stays.refs_5_), custom_call_target="tpu_custom_call" | custom-call | bytes 1024 | tf_op jit(solution)/shard_map/pallas_call | solution.py:43
  16.5 0.9 %collective-permute-done.1.theirs = bf16[256,256]{1,0:T(8,128)(2,1)S(1)} collective-permute-done((bf16[256,256]{1,0:T(8,128)(2,1)S(1)}, bf16[256,256]{1,0:T(8,128)(2,1)S(1)}, u32[]{:S(2)}, u32[]{:S(2)}) %collective-permute-start.1) | collective-permute-done | bytes 131104 | tf_op jit(solution)/shard_map/ppermute | solution.py:16
  17.4 0.6 %shard_map.60 = (f32[256,256]{1,0:T(8,128)S(1)}, bf16[256,256]{1,0:T(8,128)(2,1)S(1)}) custom-call(bf16[3,512,512]{2,1,0:T(8,128)(2,1)S(1)} %get-tuple-element.20.tiles.refs_0_, bf16[256,256]{1,0:T(8,128)(2,1)S(1)} %collective-permute-done.ours, bf16[256,256]{1,0:T(8,128)(2,1)S(1)} %collective-permute-done.1.theirs, ...), custom_call_target="tpu_custom_call" | custom-call | bytes 1024 | tf_op jit(solution)/shard_map/pallas_call | solution.py:43
  18.0 0.5 %collective-permute-start.6 = (bf16[256,256]{1,0:T(8,128)(2,1)S(1)}, bf16[256,256]{1,0:T(8,128)(2,1)S(1)}, u32[]{:S(2)}, u32[]{:S(2)}) collective-permute-start(bf16[256,256]{1,0:T(8,128)(2,1)S(1)} %get-tuple-element.28.before), channel_id=1, source_target_pairs={{0,1},{1,0},{2,3},{3,2},{4,5},{5,4},{6,7},{7,6},{8,9},{9,8},{10,11... | collective-permute-start | bytes 393224 | tf_op jit(solution)/shard_map/ppermute | solution.py:16
  18.4 2.7 %collective-permute-done.4.refs_1_ = bf16[512,512]{1,0:T(8,128)(2,1)S(1)} collective-permute-done((bf16[512,512]{1,0:T(8,128)(2,1)S(1)}, bf16[512,512]{1,0:T(8,128)(2,1)S(1)}, u32[]{:S(2)}, u32[]{:S(2)}) %collective-permute-start.4) | collective-permute-done | bytes 524320 | tf_op jit(solution)/shard_map/ppermute | solution.py:26
  21.1 0.6 %shard_map.61 = (f32[256,512]{1,0:T(8,128)S(1)}, bf16[256,512]{1,0:T(8,128)(2,1)S(1)}) custom-call(bf16[256,256]{1,0:T(8,128)(2,1)S(1)} %get-tuple-element.28.before, bf16[3,512,512]{2,1,0:T(8,128)(2,1)S(1)} %get-tuple-element.20.tiles.refs_0_, bf16[512,512]{1,0:T(8,128)(2,1)S(1)} %collective-permute-done.4.refs_1_, ...), custom_call_target="tpu_custom_call" | custom-call | bytes 1024 | tf_op jit(solution)/shard_map/pallas_call | solution.py:43
  21.8 0.7 %collective-permute-start.5 = (bf16[256,512]{1,0:T(8,128)(2,1)S(1)}, bf16[256,512]{1,0:T(8,128)(2,1)S(1)}, u32[]{:S(2)}, u32[]{:S(2)}) collective-permute-start(bf16[256,512]{1,0:T(8,128)(2,1)S(1)} %get-tuple-element.31), channel_id=1, source_target_pairs={{0,1},{1,0},{2,3},{3,2},{4,5},{5,4},{6,7},{7,6},{8,9},{9,8},{10,11... | collective-permute-start | bytes 786440 | tf_op jit(solution)/shard_map/ppermute | solution.py:16
  22.4 0.6 %collective-permute-done.6.received = bf16[256,256]{1,0:T(8,128)(2,1)S(1)} collective-permute-done((bf16[256,256]{1,0:T(8,128)(2,1)S(1)}, bf16[256,256]{1,0:T(8,128)(2,1)S(1)}, u32[]{:S(2)}, u32[]{:S(2)}) %collective-permute-start.6) | collective-permute-done | bytes 131104 | tf_op jit(solution)/shard_map/ppermute | solution.py:16
  23.0 0.7 %shard_map.62.rest_0_ = f32[256,768]{1,0:T(8,128)} custom-call(f32[256,256]{1,0:T(8,128)S(1)} %get-tuple-element.32.kept, bf16[256,256]{1,0:T(8,128)(2,1)S(1)} %collective-permute-done.6.received), custom_call_target="tpu_custom_call" | custom-call | flops 10000000000 | bytes 1024 | tf_op jit(solution)/shard_map/pallas_call | solution.py:43
  23.7 6.0 %collective-permute-done.5.received = bf16[256,512]{1,0:T(8,128)(2,1)S(1)} collective-permute-done((bf16[256,512]{1,0:T(8,128)(2,1)S(1)}, bf16[256,512]{1,0:T(8,128)(2,1)S(1)}, u32[]{:S(2)}, u32[]{:S(2)}) %collective-permute-start.5) | collective-permute-done | bytes 262176 | tf_op jit(solution)/shard_map/ppermute | solution.py:16
  29.8 0.8 %shard_map.63 = f32[256,768]{1,0:T(8,128)} custom-call(f32[256,512]{1,0:T(8,128)S(1)} %get-tuple-element.30.kept, bf16[256,512]{1,0:T(8,128)(2,1)S(1)} %collective-permute-done.5.received, f32[256,768]{1,0:T(8,128)} %shard_map.62.rest_0_), custom_call_target="tpu_custom_call", output_to_operand_aliasing={{}: (2, {})} | custom-call | bytes 1024 | tf_op jit(solution)/shard_map/pallas_call | solution.py:43
Async XLA Ops:
  0.0 12.1 %collective-permute-start.2 = (bf16[512,768]{1,0:T(8,128)(2,1)}, bf16[512,768]{1,0:T(8,128)(2,1)S(1)}, u32[]{:S(2)}, u32[]{:S(2)}) collective-permute-start(bf16[512,768]{1,0:T(8,128)(2,1)} %sketch.5), channel_id=1, source_target_pairs={{0,2},{2,0},{4,6},{6,4},{8,10},{10,8},{12,14},{14,12},{16,18},{18,... | collective-permute-start | bytes 2359304 | tf_op jit(solution)/shard_map/ppermute | solution.py:21
  1.4 10.1 %collective-permute-start = (bf16[256,256]{1,0:T(8,128)(2,1)S(1)}, bf16[256,256]{1,0:T(8,128)(2,1)S(1)}, u32[]{:S(2)}, u32[]{:S(2)}) collective-permute-start(bf16[256,256]{1,0:T(8,128)(2,1)S(1)} %shard_map.55.begun), channel_id=1, source_target_pairs={{0,30},{2,4},{4,2},{6,8},{8,6},{10,12},{12,10},{14,16},{16,14},{18... | collective-permute-start | bytes 393224 | tf_op jit(solution)/shard_map/ppermute | solution.py:26
  8.2 7.8 %collective-permute-start.3 = (bf16[512,256]{1,0:T(8,128)(2,1)S(1)}, bf16[512,256]{1,0:T(8,128)(2,1)S(1)}, u32[]{:S(2)}, u32[]{:S(2)}) collective-permute-start(bf16[512,256]{1,0:T(8,128)(2,1)S(1)} %get-tuple-element.19.begun), channel_id=1, source_target_pairs={{0,1},{1,0},{2,3},{3,2},{4,5},{5,4},{6,7},{7,6},{8,9},{9,8},{10,11... | collective-permute-start | bytes 786440 | tf_op jit(solution)/shard_map/ppermute | solution.py:16
  9.8 2.3 %copy-start = (s32[1,1,3,1]{2,3,1,0:T(1,128)S(1)}, s32[1,1,3,1]{2,3,1,0:T(1,128)}, u32[]{:S(2)}) copy-start(s32[1,1,3,1]{2,3,1,0:T(1,128)} %param.7) | copy-start | bytes 40
  9.8 2.3 %copy-start.1 = (s32[1,1,2]{2,1,0:T(1,128)S(1)}, s32[1,1,2]{2,1,0:T(1,128)}, u32[]{:S(2)}) copy-start(s32[1,1,2]{2,1,0:T(1,128)} %param.8) | copy-start | bytes 28
  9.8 11.3 %collective-permute-start.4 = (bf16[512,512]{1,0:T(8,128)(2,1)S(1)}, bf16[512,512]{1,0:T(8,128)(2,1)S(1)}, u32[]{:S(2)}, u32[]{:S(2)}) collective-permute-start(bf16[512,512]{1,0:T(8,128)(2,1)S(1)} %get-tuple-element.29), channel_id=1, source_target_pairs={{0,30},{2,4},{4,2},{6,8},{8,6},{10,12},{12,10},{14,16},{16,14},{18... | collective-permute-start | bytes 1572872 | tf_op jit(solution)/shard_map/ppermute | solution.py:26
  11.5 5.9 %collective-permute-start.1 = (bf16[256,256]{1,0:T(8,128)(2,1)S(1)}, bf16[256,256]{1,0:T(8,128)(2,1)S(1)}, u32[]{:S(2)}, u32[]{:S(2)}) collective-permute-start(bf16[256,256]{1,0:T(8,128)(2,1)S(1)} %collective-permute-done.ours), channel_id=1, source_target_pairs={{0,1},{1,0},{2,3},{3,2},{4,5},{5,4},{6,7},{7,6},{8,9},{9,8},{10,11... | collective-permute-start | bytes 393224 | tf_op jit(solution)/shard_map/ppermute | solution.py:16
  18.0 5.0 %collective-permute-start.6 = (bf16[256,256]{1,0:T(8,128)(2,1)S(1)}, bf16[256,256]{1,0:T(8,128)(2,1)S(1)}, u32[]{:S(2)}, u32[]{:S(2)}) collective-permute-start(bf16[256,256]{1,0:T(8,128)(2,1)S(1)} %get-tuple-element.28.before), channel_id=1, source_target_pairs={{0,1},{1,0},{2,3},{3,2},{4,5},{5,4},{6,7},{7,6},{8,9},{9,8},{10,11... | collective-permute-start | bytes 393224 | tf_op jit(solution)/shard_map/ppermute | solution.py:16
  21.8 8.0 %collective-permute-start.5 = (bf16[256,512]{1,0:T(8,128)(2,1)S(1)}, bf16[256,512]{1,0:T(8,128)(2,1)S(1)}, u32[]{:S(2)}, u32[]{:S(2)}) collective-permute-start(bf16[256,512]{1,0:T(8,128)(2,1)S(1)} %get-tuple-element.31), channel_id=1, source_target_pairs={{0,1},{1,0},{2,3},{3,2},{4,5},{5,4},{6,7},{7,6},{8,9},{9,8},{10,11... | collective-permute-start | bytes 786440 | tf_op jit(solution)/shard_map/ppermute | solution.py:16

commit v18 on v13

--- a/solution.py
+++ b/solution.py
@@ -7,7 +7,7 @@
 from jax.experimental.pallas import tpu as pltpu
 from jax.sharding import PartitionSpec as P
 
-SHARES = (2, 1)
+SHARES = (3, 2, 1)
 TRANSPOSED = (((0,), (0,)), ((), ()))
 
 
@@ -102,7 +102,8 @@
     stays[...] = jnp.full(stays.shape, jnp.where(owner == lax.axis_index("group"), 1.0, 0.0))
 
 
-def turn_kernel(kept, lent, miss, stays, hit_turned, missed):
+def turn_kernel(start, kept, lent, miss, stays, own, hit_turned, missed, part):
+    part[...] = own[:, pl.ds(start, part.shape[1])]
     stay = stays[:, pl.ds(0, kept.shape[0])] > 0.0
     ours, theirs = kept[...].T, lent[...].T
     hit_turned[...] = jnp.where(stay, ours, theirs)
@@ -139,7 +140,7 @@
     copies = pltpu.SemaphoreType.DMA
     lent, *parts = call(
         cut_kernel,
-        (on_chip((half, rank), short), *(on_chip((panels, width), short) for width in widths)),
+        (on_chip((half, rank), short), *(on_chip((panels, width), short) for width in widths[:2])),
         (),
         0,
         hbm=(sketch, cluster_basis),
@@ -171,12 +172,17 @@
         2 * product,
         scalars=(row_blocks.reshape(-1), owner_route.reshape(-1)),
     )
-    hit_turned, missed = call(
-        turn_kernel,
-        (on_chip((rank, half), short), on_chip((rank, columns), wide)),
-        (kept, lent, miss, stays),
+    hit_turned, missed, part = call(
+        functools.partial(turn_kernel, starts[2]),
+        (
+            on_chip((rank, half), short),
+            on_chip((rank, columns), wide),
+            on_chip((panels, widths[2]), short),
+        ),
+        (kept, lent, miss, stays, own),
         product // 2,
     )
+    fars.append(swap_far(part))
     out = None
     for i, (start, width) in enumerate(zip(starts, widths)):
         kept, sent = call(

time: 28.2 us -> 29.5 us (1.046)
  waiting for transfers between devices: 11.8 us -> 5.41 us
  starting transfers between devices: 8.43 us -> 14.7 us
  Pallas kernels: 7.7 us -> 8.78 us
    ppermute x2 -> x3, waiting for transfers between devices: 9.78 us -> 3.21 us  [swap_far(): lax.ppermute(array, 'blk', [(i, (i + 1 if i % 2 else i - 1) % devices) fo...]
    ppermute x2 -> x3, starting transfers between devices: 3.54 us -> 6.92 us  [swap_far(): lax.ppermute(array, 'blk', [(i, (i + 1 if i % 2 else i - 1) % devices) fo...]
    ppermute x3 -> x4, starting transfers between devices: 4.83 us -> 7.75 us  [from_behind(): lax.ppermute(array, axis, [(i, (i + by) % devices) for i in range(devices)])]
    pallas_call x8 -> x10, Pallas kernels: 7.7 us -> 8.78 us  [call(): pl.pallas_call(kernel, out_shape=out_shape, in_specs=[scalar] * len(scala...]
    ppermute x3 -> x4, waiting for transfers between devices: 1.98 us -> 2.2 us  [from_behind(): lax.ppermute(array, axis, [(i, (i + by) % devices) for i in range(devices)])]
  transfers between devices with their start and end apart: 6 -> 8, of which waited for: 5 -> 5; matrix products, arithmetic and copies ran while one was open for 0% -> 0% of each run, Pallas kernels for 25% -> 28%
where the time goes in v18:
time: 29.5 us; the launch traced here: 29 us
  starting transfers between devices  14.7 us (50%)
  Pallas kernels  8.78 us (30%)
  waiting for transfers between devices  5.41 us (18%)
    pallas_call x10, Pallas kernels, call(): pl.pallas_call(kernel, out_shape=out_shape, in_specs=[scalar] * len(scala...  8.78 us
    ppermute x4, starting transfers between devices, from_behind(): lax.ppermute(array, axis, [(i, (i + by) % devices) for i in range(devices)])  7.75 us
    ppermute x3, starting transfers between devices, swap_far(): lax.ppermute(array, 'blk', [(i, (i + 1 if i % 2 else i - 1) % devices) fo...  6.92 us
    ppermute x3, waiting for transfers between devices, swap_far(): lax.ppermute(array, 'blk', [(i, (i + 1 if i % 2 else i - 1) % devices) fo...  3.21 us
    ppermute x4, waiting for transfers between devices, from_behind(): lax.ppermute(array, axis, [(i, (i + by) % devices) for i in range(devices)])  2.2 us
  transfers between devices with their start and end apart: 8, of which 5 were waited for; matrix products, arithmetic and copies ran while one was open for 0% of the time, Pallas kernels for 28%

profile of v18, /device:TPU:1, one launch (start us, length us, event | category | flops | bytes accessed | tf_op | source)
XLA Modules:
  0.0 29.0 jit_solution(10747398580678845279)
XLA Ops:
  0.0 0.1 collective-permute-start.1
  0.1 1.2 %shard_map.55 = (bf16[512,256]{1,0:T(8,128)(2,1)S(1)}, bf16[512,384]{1,0:T(8,128)(2,1)S(1)}, bf16[512,256]{1,0:T(8,128)(2,1)S(1)}) custom-call(bf16[512,768]{1,0:T(8,128)(2,1)} %sketch.3, bf16[1,1,1024,256]{3,2,1,0:T(8,128)(2,1)} %basis.3), custom_call_target="tpu_custom_call" | custom-call | bytes 1048576 | tf_op jit(solution)/shard_map/pallas_call | solution.py:43
  1.2 2.6 %collective-permute-start.6 = (bf16[512,384]{1,0:T(8,128)(2,1)S(1)}, bf16[512,384]{1,0:T(8,128)(2,1)S(1)}, u32[]{:S(2)}, u32[]{:S(2)}) collective-permute-start(bf16[512,384]{1,0:T(8,128)(2,1)S(1)} %get-tuple-element.23.begun), channel_id=1, source_target_pairs={{0,30},{2,4},{4,2},{6,8},{8,6},{10,12},{12,10},{14,16},{16,14},{18... | collective-permute-start | bytes 1179656 | tf_op jit(solution)/shard_map/ppermute | solution.py:26
  3.9 1.2 %collective-permute-start = (bf16[512,256]{1,0:T(8,128)(2,1)S(1)}, bf16[512,256]{1,0:T(8,128)(2,1)S(1)}, u32[]{:S(2)}, u32[]{:S(2)}) collective-permute-start(bf16[512,256]{1,0:T(8,128)(2,1)S(1)} %get-tuple-element.26), channel_id=1, source_target_pairs={{0,1},{1,0},{2,3},{3,2},{4,5},{5,4},{6,7},{7,6},{8,9},{9,8},{10,11... | collective-permute-start | bytes 786440 | tf_op jit(solution)/shard_map/ppermute | solution.py:16
  5.1 0.0 copy-start
  5.1 0.0 copy-start.1
  5.1 0.9 %collective-permute-start.4 = (bf16[512,256]{1,0:T(8,128)(2,1)S(1)}, bf16[512,256]{1,0:T(8,128)(2,1)S(1)}, u32[]{:S(2)}, u32[]{:S(2)}) collective-permute-start(bf16[512,256]{1,0:T(8,128)(2,1)S(1)} %get-tuple-element.36), channel_id=1, source_target_pairs={{0,30},{2,4},{4,2},{6,8},{8,6},{10,12},{12,10},{14,16},{16,14},{18... | collective-permute-start | bytes 786440 | tf_op jit(solution)/shard_map/ppermute | solution.py:26
  6.0 1.7 %shard_map.56 = (bf16[512,768]{1,0:T(8,128)(2,1)S(1)}, bf16[3,512,512]{2,1,0:T(8,128)(2,1)S(1)}, bf16[512,256]{1,0:T(8,128)(2,1)S(1)}) custom-call(bf16[512,384]{1,0:T(8,128)(2,1)S(1)} %get-tuple-element.23.begun, bf16[512,768]{1,0:T(8,128)(2,1)} %sketch.3, bf16[1,1,3,1,512,512]{5,4,3,2,1,0:T(8,128)(2,1)} %tiles.1, bf16[1,1,1024,256]{3,2,1,0:T(8,128)(2,1)} %basis.3), custom_call_target="tpu_custom_call" | custom-call | bytes 1048576 | tf_op jit(solution)/shard_map/pallas_call | solution.py:43
  7.7 0.0 collective-permute-done.1.near
  7.7 0.0 copy-done
  7.7 0.0 copy-done.1
  7.7 1.5 %shard_map.57 = (f32[512,768]{1,0:T(8,128)S(1)}, bf16[512,768]{1,0:T(8,128)(2,1)S(1)}, f32[1,768]{1,0:T(1,128)S(1)}) custom-call(s32[3]{0:T(128)S(1)} %bitcast.3, s32[2]{0:T(128)S(1)} %bitcast.4, bf16[3,512,512]{2,1,0:T(8,128)(2,1)S(1)} %get-tuple-element.24.tiles, bf16[512,768]{1,0:T(8,128)(2,1)S(1)} %get-tuple-element.27.own, ...), custom_call_target="tpu_custom_call" | custom-call | flops 805306368 | bytes 1048576 | tf_op jit(solution)/shard_map/pallas_call | solution.py:43
  9.3 0.1 collective-permute-done.lent
  9.4 0.5 %shard_map.58 = (bf16[256,512]{1,0:T(8,128)(2,1)S(1)}, f32[256,768]{1,0:T(8,128)S(1)}, bf16[512,128]{1,0:T(8,128)(2,1)S(1)}) custom-call(bf16[512,256]{1,0:T(8,128)(2,1)S(1)} %get-tuple-element.25.kept, bf16[512,256]{1,0:T(8,128)(2,1)S(1)} %collective-permute-done.lent, bf16[512,768]{1,0:T(8,128)(2,1)S(1)} %get-tuple-element.28.miss, ...), custom_call_target="tpu_custom_call" | custom-call | flops 201326592 | bytes 1048576 | tf_op jit(solution)/shard_map/pallas_call | solution.py:43
  9.9 3.4 %collective-permute-start.2 = (bf16[512,128]{1,0:T(8,128)(2,1)S(1)}, bf16[512,128]{1,0:T(8,128)(2,1)S(1)}, u32[]{:S(2)}, u32[]{:S(2)}) collective-permute-start(bf16[512,128]{1,0:T(8,128)(2,1)S(1)} %get-tuple-element.30), channel_id=1, source_target_pairs={{0,30},{2,4},{4,2},{6,8},{8,6},{10,12},{12,10},{14,16},{16,14},{18... | collective-permute-start | bytes 393224 | tf_op jit(solution)/shard_map/ppermute | solution.py:26
  13.3 2.3 %collective-permute-done.6.far = bf16[512,384]{1,0:T(8,128)(2,1)S(1)} collective-permute-done((bf16[512,384]{1,0:T(8,128)(2,1)S(1)}, bf16[512,384]{1,0:T(8,128)(2,1)S(1)}, u32[]{:S(2)}, u32[]{:S(2)}) %collective-permute-start.6) | collective-permute-done | bytes 393248 | tf_op jit(solution)/shard_map/ppermute | solution.py:26
  15.6 0.7 %shard_map.61 = (f32[256,384]{1,0:T(8,128)S(1)}, bf16[256,384]{1,0:T(8,128)(2,1)S(1)}) custom-call(bf16[3,512,512]{2,1,0:T(8,128)(2,1)S(1)} %get-tuple-element.24.tiles, bf16[512,384]{1,0:T(8,128)(2,1)S(1)} %collective-permute-done.6.far, f32[512,768]{1,0:T(8,128)S(1)} %get-tuple-element.31.hit, bf16[256,512]{1,0:T(8,128)(2,1)S(1)} %get-tuple-element.32.hit_turned, ...), custom_call_target="tpu_custom_call" | custom-call | flops 402653184 | bytes 1048576 | tf_op jit(solution)/shard_map/pallas_call | solution.py:43
  16.3 2.7 %collective-permute-start.7 = (bf16[256,384]{1,0:T(8,128)(2,1)S(1)}, bf16[256,384]{1,0:T(8,128)(2,1)S(1)}, u32[]{:S(2)}, u32[]{:S(2)}) collective-permute-start(bf16[256,384]{1,0:T(8,128)(2,1)S(1)} %get-tuple-element.40), channel_id=1, source_target_pairs={{0,1},{1,0},{2,3},{3,2},{4,5},{5,4},{6,7},{7,6},{8,9},{9,8},{10,11... | collective-permute-start | bytes 589832 | tf_op jit(solution)/shard_map/ppermute | solution.py:16
  18.9 0.9 %collective-permute-done.4.far = bf16[512,256]{1,0:T(8,128)(2,1)S(1)} collective-permute-done((bf16[512,256]{1,0:T(8,128)(2,1)S(1)}, bf16[512,256]{1,0:T(8,128)(2,1)S(1)}, u32[]{:S(2)}, u32[]{:S(2)}) %collective-permute-start.4) | collective-permute-done | bytes 262176 | tf_op jit(solution)/shard_map/ppermute | solution.py:26
  19.8 0.5 %shard_map.60 = (f32[256,256]{1,0:T(8,128)S(1)}, bf16[256,256]{1,0:T(8,128)(2,1)S(1)}) custom-call(bf16[3,512,512]{2,1,0:T(8,128)(2,1)S(1)} %get-tuple-element.24.tiles, bf16[512,256]{1,0:T(8,128)(2,1)S(1)} %collective-permute-done.4.far, f32[512,768]{1,0:T(8,128)S(1)} %get-tuple-element.31.hit, bf16[256,512]{1,0:T(8,128)(2,1)S(1)} %get-tuple-element.32.hit_turned, ...), custom_call_target="tpu_custom_call" | custom-call | flops 268435456 | bytes 1048576 | tf_op jit(solution)/shard_map/pallas_call | solution.py:43
  20.4 3.0 %collective-permute-start.5 = (bf16[256,256]{1,0:T(8,128)(2,1)S(1)}, bf16[256,256]{1,0:T(8,128)(2,1)S(1)}, u32[]{:S(2)}, u32[]{:S(2)}) collective-permute-start(bf16[256,256]{1,0:T(8,128)(2,1)S(1)} %get-tuple-element.38), channel_id=1, source_target_pairs={{0,1},{1,0},{2,3},{3,2},{4,5},{5,4},{6,7},{7,6},{8,9},{9,8},{10,11... | collective-permute-start | bytes 393224 | tf_op jit(solution)/shard_map/ppermute | solution.py:16
  23.3 0.0 collective-permute-done.2.far
  23.3 0.5 %shard_map.59 = (f32[256,128]{1,0:T(8,128)S(1)}, bf16[256,128]{1,0:T(8,128)(2,1)S(1)}) custom-call(bf16[3,512,512]{2,1,0:T(8,128)(2,1)S(1)} %get-tuple-element.24.tiles, bf16[512,128]{1,0:T(8,128)(2,1)S(1)} %collective-permute-done.2.far, f32[512,768]{1,0:T(8,128)S(1)} %get-tuple-element.31.hit, bf16[256,512]{1,0:T(8,128)(2,1)S(1)} %get-tuple-element.32.hit_turned, ...), custom_call_target="tpu_custom_call" | custom-call | flops 134217728 | bytes 1048576 | tf_op jit(solution)/shard_map/pallas_call | solution.py:43
  23.8 0.8 %collective-permute-start.3 = (bf16[256,128]{1,0:T(8,128)(2,1)S(1)}, bf16[256,128]{1,0:T(8,128)(2,1)S(1)}, u32[]{:S(2)}, u32[]{:S(2)}) collective-permute-start(bf16[256,128]{1,0:T(8,128)(2,1)S(1)} %get-tuple-element.35), channel_id=1, source_target_pairs={{0,1},{1,0},{2,3},{3,2},{4,5},{5,4},{6,7},{7,6},{8,9},{9,8},{10,11... | collective-permute-start | bytes 196616 | tf_op jit(solution)/shard_map/ppermute | solution.py:16
  24.7 0.0 collective-permute-done.7.received
  24.7 0.8 %shard_map.62.rest_0_ = f32[256,768]{1,0:T(8,128)} custom-call(f32[256,384]{1,0:T(8,128)S(1)} %get-tuple-element.39.kept, bf16[256,384]{1,0:T(8,128)(2,1)S(1)} %collective-permute-done.7.received), custom_call_target="tpu_custom_call" | custom-call | flops 65536 | bytes 1048576 | tf_op jit(solution)/shard_map/pallas_call | solution.py:43
  25.5 2.0 %collective-permute-done.5.received = bf16[256,256]{1,0:T(8,128)(2,1)S(1)} collective-permute-done((bf16[256,256]{1,0:T(8,128)(2,1)S(1)}, bf16[256,256]{1,0:T(8,128)(2,1)S(1)}, u32[]{:S(2)}, u32[]{:S(2)}) %collective-permute-start.5) | collective-permute-done | bytes 131104 | tf_op jit(solution)/shard_map/ppermute | solution.py:16
  27.5 0.7 %shard_map.63.rest_0_ = f32[256,768]{1,0:T(8,128)} custom-call(f32[256,256]{1,0:T(8,128)S(1)} %get-tuple-element.37.kept, bf16[256,256]{1,0:T(8,128)(2,1)S(1)} %collective-permute-done.5.received, f32[256,768]{1,0:T(8,128)} %shard_map.62.rest_0_), custom_call_target="tpu_custom_call", output_to_operand_aliasing={{}: (2, {})} | custom-call | flops 65536 | bytes 1048576 | tf_op jit(solution)/shard_map/pallas_call | solution.py:43
  28.2 0.1 collective-permute-done.3.received
  28.4 0.7 %shard_map.64 = f32[256,768]{1,0:T(8,128)} custom-call(f32[256,128]{1,0:T(8,128)S(1)} %get-tuple-element.34.kept, bf16[256,128]{1,0:T(8,128)(2,1)S(1)} %collective-permute-done.3.received, f32[256,768]{1,0:T(8,128)} %shard_map.63.rest_0_), custom_call_target="tpu_custom_call", output_to_operand_aliasing={{}: (2, {})} | custom-call | flops 65536 | bytes 1048576 | tf_op jit(solution)/shard_map/pallas_call | solution.py:43
Async XLA Ops:
  0.0 7.7 %collective-permute-start.1 = (bf16[512,768]{1,0:T(8,128)(2,1)}, bf16[512,768]{1,0:T(8,128)(2,1)S(1)}, u32[]{:S(2)}, u32[]{:S(2)}) collective-permute-start(bf16[512,768]{1,0:T(8,128)(2,1)} %sketch.3), channel_id=1, source_target_pairs={{0,2},{2,0},{4,6},{6,4},{8,10},{10,8},{12,14},{14,12},{16,18},{18,... | collective-permute-start | bytes 2359304 | tf_op jit(solution)/shard_map/ppermute | solution.py:21
  1.2 14.4 %collective-permute-start.6 = (bf16[512,384]{1,0:T(8,128)(2,1)S(1)}, bf16[512,384]{1,0:T(8,128)(2,1)S(1)}, u32[]{:S(2)}, u32[]{:S(2)}) collective-permute-start(bf16[512,384]{1,0:T(8,128)(2,1)S(1)} %get-tuple-element.23.begun), channel_id=1, source_target_pairs={{0,30},{2,4},{4,2},{6,8},{8,6},{10,12},{12,10},{14,16},{16,14},{18... | collective-permute-start | bytes 1179656 | tf_op jit(solution)/shard_map/ppermute | solution.py:26
  3.9 5.5 %collective-permute-start = (bf16[512,256]{1,0:T(8,128)(2,1)S(1)}, bf16[512,256]{1,0:T(8,128)(2,1)S(1)}, u32[]{:S(2)}, u32[]{:S(2)}) collective-permute-start(bf16[512,256]{1,0:T(8,128)(2,1)S(1)} %get-tuple-element.26), channel_id=1, source_target_pairs={{0,1},{1,0},{2,3},{3,2},{4,5},{5,4},{6,7},{7,6},{8,9},{9,8},{10,11... | collective-permute-start | bytes 786440 | tf_op jit(solution)/shard_map/ppermute | solution.py:16
  5.1 2.6 %copy-start = (s32[1,1,3,1]{2,3,1,0:T(1,128)S(1)}, s32[1,1,3,1]{2,3,1,0:T(1,128)}, u32[]{:S(2)}) copy-start(s32[1,1,3,1]{2,3,1,0:T(1,128)} %param.7) | copy-start | bytes 40
  5.1 2.6 %copy-start.1 = (s32[1,1,2]{2,1,0:T(1,128)S(1)}, s32[1,1,2]{2,1,0:T(1,128)}, u32[]{:S(2)}) copy-start(s32[1,1,2]{2,1,0:T(1,128)} %param.8) | copy-start | bytes 28
  5.1 14.7 %collective-permute-start.4 = (bf16[512,256]{1,0:T(8,128)(2,1)S(1)}, bf16[512,256]{1,0:T(8,128)(2,1)S(1)}, u32[]{:S(2)}, u32[]{:S(2)}) collective-permute-start(bf16[512,256]{1,0:T(8,128)(2,1)S(1)} %get-tuple-element.36), channel_id=1, source_target_pairs={{0,30},{2,4},{4,2},{6,8},{8,6},{10,12},{12,10},{14,16},{16,14},{18... | collective-permute-start | bytes 786440 | tf_op jit(solution)/shard_map/ppermute | solution.py:26
  9.9 13.5 %collective-permute-start.2 = (bf16[512,128]{1,0:T(8,128)(2,1)S(1)}, bf16[512,128]{1,0:T(8,128)(2,1)S(1)}, u32[]{:S(2)}, u32[]{:S(2)}) collective-permute-start(bf16[512,128]{1,0:T(8,128)(2,1)S(1)} %get-tuple-element.30), channel_id=1, source_target_pairs={{0,30},{2,4},{4,2},{6,8},{8,6},{10,12},{12,10},{14,16},{16,14},{18... | collective-permute-start | bytes 393224 | tf_op jit(solution)/shard_map/ppermute | solution.py:26
  16.3 8.4 %collective-permute-start.7 = (bf16[256,384]{1,0:T(8,128)(2,1)S(1)}, bf16[256,384]{1,0:T(8,128)(2,1)S(1)}, u32[]{:S(2)}, u32[]{:S(2)}) collective-permute-start(bf16[256,384]{1,0:T(8,128)(2,1)S(1)} %get-tuple-element.40), channel_id=1, source_target_pairs={{0,1},{1,0},{2,3},{3,2},{4,5},{5,4},{6,7},{7,6},{8,9},{9,8},{10,11... | collective-permute-start | bytes 589832 | tf_op jit(solution)/shard_map/ppermute | solution.py:16
  20.4 7.1 %collective-permute-start.5 = (bf16[256,256]{1,0:T(8,128)(2,1)S(1)}, bf16[256,256]{1,0:T(8,128)(2,1)S(1)}, u32[]{:S(2)}, u32[]{:S(2)}) collective-permute-start(bf16[256,256]{1,0:T(8,128)(2,1)S(1)} %get-tuple-element.38), channel_id=1, source_target_pairs={{0,1},{1,0},{2,3},{3,2},{4,5},{5,4},{6,7},{7,6},{8,9},{9,8},{10,11... | collective-permute-start | bytes 393224 | tf_op jit(solution)/shard_map/ppermute | solution.py:16
  23.8 4.5 %collective-permute-start.3 = (bf16[256,128]{1,0:T(8,128)(2,1)S(1)}, bf16[256,128]{1,0:T(8,128)(2,1)S(1)}, u32[]{:S(2)}, u32[]{:S(2)}) collective-permute-start(bf16[256,128]{1,0:T(8,128)(2,1)S(1)} %get-tuple-element.35), channel_id=1, source_target_pairs={{0,1},{1,0},{2,3},{3,2},{4,5},{5,4},{6,7},{7,6},{8,9},{9,8},{10,11... | collective-permute-start | bytes 196616 | tf_op jit(solution)/shard_map/ppermute | solution.py:16

commit v19 on v13

--- a/solution.py
+++ b/solution.py
@@ -68,15 +68,16 @@
     return basis.at[0, 0, pl.ds(pl.multiple_of(group * half, half), half)]
 
 
-def cut_kernel(sketch, basis, lent, first, second, sems):
+def first_kernel(sketch, first, sems):
+    copy_all([(sketch.at[:, pl.ds(0, first.shape[1])], first)], sems)
+
+
+def cut_kernel(begun, sketch, basis, lent, second, sems):
+    del begun
     theirs = half_rows(basis, 1 - lax.axis_index("group"), lent.shape[0])
-    early, late = first.shape[1], second.shape[1]
-    pairs = [
-        (sketch.at[:, pl.ds(0, early)], first),
-        (theirs, lent),
-        (sketch.at[:, pl.ds(early, late)], second),
-    ]
-    copy_all(pairs, sems)
+    width = second.shape[1]
+    columns = pl.ds(sketch.shape[1] - width, width)
+    copy_all([(theirs, lent), (sketch.at[:, columns], second)], sems)
 
 
 def stage_kernel(begun, sketch, tiles, basis, own, staged, kept, sems):
@@ -137,13 +138,21 @@
     product = 2 * rows * panels * columns
     short, wide = sketch.dtype, jnp.float32
     copies = pltpu.SemaphoreType.DMA
-    lent, *parts = call(
-        cut_kernel,
-        (on_chip((half, rank), short), *(on_chip((panels, width), short) for width in widths)),
+    first = call(
+        first_kernel,
+        on_chip((panels, widths[0]), short),
         (),
         0,
+        hbm=(sketch,),
+        scratch=(copies((1,)),),
+    )
+    lent, second = call(
+        cut_kernel,
+        (on_chip((half, rank), short), on_chip((panels, widths[1]), short)),
+        (first,),
+        0,
         hbm=(sketch, cluster_basis),
-        scratch=(copies((3,)),),
+        scratch=(copies((2,)),),
     )
     own, tiles, kept = call(
         stage_kernel,
@@ -152,13 +161,13 @@
             on_chip((offsets, rows, panels), short),
             on_chip((half, rank), short),
         ),
-        (parts[0],),
+        (lent,),
         0,
         hbm=(sketch, far_tiles, cluster_basis),
         scratch=(copies((3,)),),
     )
     lent = from_behind(lent, "group", 1)
-    fars = [swap_far(part) for part in parts]
+    fars = [swap_far(part) for part in (first, second)]
     near = swap_near(sketch)
     hit, miss, stays = call(
         local_kernel,

time: 28.2 us -> 28.6 us (1.014)
  waiting for transfers between devices: 11.8 us -> 10.7 us
  Pallas kernels: 7.7 us -> 8.6 us
  starting transfers between devices: 8.43 us -> 8.94 us
    ppermute x2, waiting for transfers between devices: 9.78 us -> 8.51 us  [swap_far(): lax.ppermute(array, 'blk', [(i, (i + 1 if i % 2 else i - 1) % devices) fo...]
    pallas_call x8 -> x9, Pallas kernels: 7.7 us -> 8.6 us  [call(): pl.pallas_call(kernel, out_shape=out_shape, in_specs=[scalar] * len(scala...]
    ppermute x3, starting transfers between devices: 4.83 us -> 5.35 us  [from_behind(): lax.ppermute(array, axis, [(i, (i + by) % devices) for i in range(devices)])]
  transfers between devices with their start and end apart: 6 -> 6, of which waited for: 5 -> 5; matrix products, arithmetic and copies ran while one was open for 0% -> 0% of each run, Pallas kernels for 25% -> 28%
where the time goes in v19:
time: 28.6 us; the launch traced here: 28.4 us
  waiting for transfers between devices  10.7 us (37%)
  starting transfers between devices  8.94 us (31%)
  Pallas kernels  8.6 us (30%)
    pallas_call x9, Pallas kernels, call(): pl.pallas_call(kernel, out_shape=out_shape, in_specs=[scalar] * len(scala...  8.6 us
    ppermute x2, waiting for transfers between devices, swap_far(): lax.ppermute(array, 'blk', [(i, (i + 1 if i % 2 else i - 1) % devices) fo...  8.51 us
    ppermute x3, starting transfers between devices, from_behind(): lax.ppermute(array, axis, [(i, (i + by) % devices) for i in range(devices)])  5.35 us
    ppermute x2, starting transfers between devices, swap_far(): lax.ppermute(array, 'blk', [(i, (i + 1 if i % 2 else i - 1) % devices) fo...  3.54 us
    ppermute x3, waiting for transfers between devices, from_behind(): lax.ppermute(array, axis, [(i, (i + by) % devices) for i in range(devices)])  2.22 us
  transfers between devices with their start and end apart: 6, of which 5 were waited for; matrix products, arithmetic and copies ran while one was open for 0% of the time, Pallas kernels for 28%

profile of v19, /device:TPU:1, one launch (start us, length us, event | category | flops | bytes accessed | tf_op | source)
XLA Modules:
  0.0 28.4 jit_solution(15952191690489262706)
XLA Ops:
  0.0 0.1 collective-permute-start.1
  0.1 1.0 %shard_map.55.begun = bf16[512,512]{1,0:T(8,128)(2,1)S(1)} custom-call(bf16[512,768]{1,0:T(8,128)(2,1)} %sketch.5), custom_call_target="tpu_custom_call" | custom-call | bytes 1048576 | tf_op jit(solution)/shard_map/pallas_call | solution.py:43
  1.1 2.6 %collective-permute-start.4 = (bf16[512,512]{1,0:T(8,128)(2,1)S(1)}, bf16[512,512]{1,0:T(8,128)(2,1)S(1)}, u32[]{:S(2)}, u32[]{:S(2)}) collective-permute-start(bf16[512,512]{1,0:T(8,128)(2,1)S(1)} %shard_map.55.begun), channel_id=1, source_target_pairs={{0,30},{2,4},{4,2},{6,8},{8,6},{10,12},{12,10},{14,16},{16,14},{18... | collective-permute-start | bytes 1572872 | tf_op jit(solution)/shard_map/ppermute | solution.py:26
  3.7 1.0 %shard_map.56 = (bf16[512,256]{1,0:T(8,128)(2,1)S(1)}, bf16[512,256]{1,0:T(8,128)(2,1)S(1)}) custom-call(bf16[512,512]{1,0:T(8,128)(2,1)S(1)} %shard_map.55.begun, bf16[512,768]{1,0:T(8,128)(2,1)} %sketch.5, bf16[1,1,1024,256]{3,2,1,0:T(8,128)(2,1)} %basis.3), custom_call_target="tpu_custom_call" | custom-call | bytes 1048576 | tf_op jit(solution)/shard_map/pallas_call | solution.py:43
  4.8 1.3 %collective-permute-start.2 = (bf16[512,256]{1,0:T(8,128)(2,1)S(1)}, bf16[512,256]{1,0:T(8,128)(2,1)S(1)}, u32[]{:S(2)}, u32[]{:S(2)}) collective-permute-start(bf16[512,256]{1,0:T(8,128)(2,1)S(1)} %get-tuple-element.19.begun), channel_id=1, source_target_pairs={{0,1},{1,0},{2,3},{3,2},{4,5},{5,4},{6,7},{7,6},{8,9},{9,8},{10,11... | collective-permute-start | bytes 786440 | tf_op jit(solution)/shard_map/ppermute | solution.py:16
  6.1 0.0 copy-start
  6.1 0.0 copy-start.1
  6.1 0.9 %collective-permute-start = (bf16[512,256]{1,0:T(8,128)(2,1)S(1)}, bf16[512,256]{1,0:T(8,128)(2,1)S(1)}, u32[]{:S(2)}, u32[]{:S(2)}) collective-permute-start(bf16[512,256]{1,0:T(8,128)(2,1)S(1)} %get-tuple-element.21), channel_id=1, source_target_pairs={{0,30},{2,4},{4,2},{6,8},{8,6},{10,12},{12,10},{14,16},{16,14},{18... | collective-permute-start | bytes 786440 | tf_op jit(solution)/shard_map/ppermute | solution.py:26
  7.0 1.7 %shard_map.57 = (bf16[512,768]{1,0:T(8,128)(2,1)S(1)}, bf16[3,512,512]{2,1,0:T(8,128)(2,1)S(1)}, bf16[512,256]{1,0:T(8,128)(2,1)S(1)}) custom-call(bf16[512,256]{1,0:T(8,128)(2,1)S(1)} %get-tuple-element.19.begun, bf16[512,768]{1,0:T(8,128)(2,1)} %sketch.5, bf16[1,1,3,1,512,512]{5,4,3,2,1,0:T(8,128)(2,1)} %tiles.1, bf16[1,1,1024,256]{3,2,1,0:T(8,128)(2,1)} %basis.3), custom_call_target="tpu_custom_call" | custom-call | bytes 1048576 | tf_op jit(solution)/shard_map/pallas_call | solution.py:43
  8.7 0.0 collective-permute-done.1.near
  8.7 0.0 copy-done
  8.7 0.0 copy-done.1
  8.7 1.5 %shard_map.58 = (f32[512,768]{1,0:T(8,128)S(1)}, bf16[512,768]{1,0:T(8,128)(2,1)S(1)}, f32[1,768]{1,0:T(1,128)S(1)}) custom-call(s32[3]{0:T(128)S(1)} %bitcast.3, s32[2]{0:T(128)S(1)} %bitcast.4, bf16[3,512,512]{2,1,0:T(8,128)(2,1)S(1)} %get-tuple-element.20.tiles, bf16[512,768]{1,0:T(8,128)(2,1)S(1)} %get-tuple-element.22.own, ...), custom_call_target="tpu_custom_call" | custom-call | flops 805306368 | bytes 1048576 | tf_op jit(solution)/shard_map/pallas_call | solution.py:43
  10.3 0.1 collective-permute-done.2.lent
  10.4 0.5 %shard_map.59 = (bf16[256,512]{1,0:T(8,128)(2,1)S(1)}, f32[256,768]{1,0:T(8,128)S(1)}) custom-call(bf16[512,256]{1,0:T(8,128)(2,1)S(1)} %get-tuple-element.24.kept, bf16[512,256]{1,0:T(8,128)(2,1)S(1)} %collective-permute-done.2.lent, bf16[512,768]{1,0:T(8,128)(2,1)S(1)} %get-tuple-element.25.miss, f32[1,768]{1,0:T(1,128)S(1)} %get-tuple-element.26.stays), custom_call_target="tpu_custom_call" | custom-call | flops 201326592 | bytes 1048576 | tf_op jit(solution)/shard_map/pallas_call | solution.py:43
  10.9 8.4 %collective-permute-done.4.far = bf16[512,512]{1,0:T(8,128)(2,1)S(1)} collective-permute-done((bf16[512,512]{1,0:T(8,128)(2,1)S(1)}, bf16[512,512]{1,0:T(8,128)(2,1)S(1)}, u32[]{:S(2)}, u32[]{:S(2)}) %collective-permute-start.4) | collective-permute-done | bytes 524320 | tf_op jit(solution)/shard_map/ppermute | solution.py:26
  19.3 0.6 %shard_map.61 = (f32[256,512]{1,0:T(8,128)S(1)}, bf16[256,512]{1,0:T(8,128)(2,1)S(1)}) custom-call(bf16[3,512,512]{2,1,0:T(8,128)(2,1)S(1)} %get-tuple-element.20.tiles, bf16[512,512]{1,0:T(8,128)(2,1)S(1)} %collective-permute-done.4.far, f32[512,768]{1,0:T(8,128)S(1)} %get-tuple-element.23.hit, bf16[256,512]{1,0:T(8,128)(2,1)S(1)} %get-tuple-element.27.hit_turned, ...), custom_call_target="tpu_custom_call" | custom-call | flops 536870912 | bytes 1048576 | tf_op jit(solution)/shard_map/pallas_call | solution.py:43
  20.0 1.9 %collective-permute-start.5 = (bf16[256,512]{1,0:T(8,128)(2,1)S(1)}, bf16[256,512]{1,0:T(8,128)(2,1)S(1)}, u32[]{:S(2)}, u32[]{:S(2)}) collective-permute-start(bf16[256,512]{1,0:T(8,128)(2,1)S(1)} %get-tuple-element.32), channel_id=1, source_target_pairs={{0,1},{1,0},{2,3},{3,2},{4,5},{5,4},{6,7},{7,6},{8,9},{9,8},{10,11... | collective-permute-start | bytes 786440 | tf_op jit(solution)/shard_map/ppermute | solution.py:16
  21.9 0.1 collective-permute-done.far
  22.0 0.6 %shard_map.60 = (f32[256,256]{1,0:T(8,128)S(1)}, bf16[256,256]{1,0:T(8,128)(2,1)S(1)}) custom-call(bf16[3,512,512]{2,1,0:T(8,128)(2,1)S(1)} %get-tuple-element.20.tiles, bf16[512,256]{1,0:T(8,128)(2,1)S(1)} %collective-permute-done.far, f32[512,768]{1,0:T(8,128)S(1)} %get-tuple-element.23.hit, bf16[256,512]{1,0:T(8,128)(2,1)S(1)} %get-tuple-element.27.hit_turned, ...), custom_call_target="tpu_custom_call" | custom-call | flops 268435456 | bytes 1048576 | tf_op jit(solution)/shard_map/pallas_call | solution.py:43
  22.5 2.1 %collective-permute-start.3 = (bf16[256,256]{1,0:T(8,128)(2,1)S(1)}, bf16[256,256]{1,0:T(8,128)(2,1)S(1)}, u32[]{:S(2)}, u32[]{:S(2)}) collective-permute-start(bf16[256,256]{1,0:T(8,128)(2,1)S(1)} %get-tuple-element.30), channel_id=1, source_target_pairs={{0,1},{1,0},{2,3},{3,2},{4,5},{5,4},{6,7},{7,6},{8,9},{9,8},{10,11... | collective-permute-start | bytes 393224 | tf_op jit(solution)/shard_map/ppermute | solution.py:16
  24.6 1.6 %collective-permute-done.5.received = bf16[256,512]{1,0:T(8,128)(2,1)S(1)} collective-permute-done((bf16[256,512]{1,0:T(8,128)(2,1)S(1)}, bf16[256,512]{1,0:T(8,128)(2,1)S(1)}, u32[]{:S(2)}, u32[]{:S(2)}) %collective-permute-start.5) | collective-permute-done | bytes 262176 | tf_op jit(solution)/shard_map/ppermute | solution.py:16
  26.2 0.8 %shard_map.62.rest_0_ = f32[256,768]{1,0:T(8,128)} custom-call(f32[256,512]{1,0:T(8,128)S(1)} %get-tuple-element.31.kept, bf16[256,512]{1,0:T(8,128)(2,1)S(1)} %collective-permute-done.5.received), custom_call_target="tpu_custom_call" | custom-call | flops 65536 | bytes 1048576 | tf_op jit(solution)/shard_map/pallas_call | solution.py:43
  27.1 0.6 %collective-permute-done.3.received = bf16[256,256]{1,0:T(8,128)(2,1)S(1)} collective-permute-done((bf16[256,256]{1,0:T(8,128)(2,1)S(1)}, bf16[256,256]{1,0:T(8,128)(2,1)S(1)}, u32[]{:S(2)}, u32[]{:S(2)}) %collective-permute-start.3) | collective-permute-done | bytes 131104 | tf_op jit(solution)/shard_map/ppermute | solution.py:16
  27.6 0.7 %shard_map.63 = f32[256,768]{1,0:T(8,128)} custom-call(f32[256,256]{1,0:T(8,128)S(1)} %get-tuple-element.29.kept, bf16[256,256]{1,0:T(8,128)(2,1)S(1)} %collective-permute-done.3.received, f32[256,768]{1,0:T(8,128)} %shard_map.62.rest_0_), custom_call_target="tpu_custom_call", output_to_operand_aliasing={{}: (2, {})} | custom-call | flops 65536 | bytes 1048576 | tf_op jit(solution)/shard_map/pallas_call | solution.py:43
Async XLA Ops:
  0.0 8.7 %collective-permute-start.1 = (bf16[512,768]{1,0:T(8,128)(2,1)}, bf16[512,768]{1,0:T(8,128)(2,1)S(1)}, u32[]{:S(2)}, u32[]{:S(2)}) collective-permute-start(bf16[512,768]{1,0:T(8,128)(2,1)} %sketch.5), channel_id=1, source_target_pairs={{0,2},{2,0},{4,6},{6,4},{8,10},{10,8},{12,14},{14,12},{16,18},{18,... | collective-permute-start | bytes 2359304 | tf_op jit(solution)/shard_map/ppermute | solution.py:21
  1.1 18.2 %collective-permute-start.4 = (bf16[512,512]{1,0:T(8,128)(2,1)S(1)}, bf16[512,512]{1,0:T(8,128)(2,1)S(1)}, u32[]{:S(2)}, u32[]{:S(2)}) collective-permute-start(bf16[512,512]{1,0:T(8,128)(2,1)S(1)} %shard_map.55.begun), channel_id=1, source_target_pairs={{0,30},{2,4},{4,2},{6,8},{8,6},{10,12},{12,10},{14,16},{16,14},{18... | collective-permute-start | bytes 1572872 | tf_op jit(solution)/shard_map/ppermute | solution.py:26
  4.8 5.6 %collective-permute-start.2 = (bf16[512,256]{1,0:T(8,128)(2,1)S(1)}, bf16[512,256]{1,0:T(8,128)(2,1)S(1)}, u32[]{:S(2)}, u32[]{:S(2)}) collective-permute-start(bf16[512,256]{1,0:T(8,128)(2,1)S(1)} %get-tuple-element.19.begun), channel_id=1, source_target_pairs={{0,1},{1,0},{2,3},{3,2},{4,5},{5,4},{6,7},{7,6},{8,9},{9,8},{10,11... | collective-permute-start | bytes 786440 | tf_op jit(solution)/shard_map/ppermute | solution.py:16
  6.1 2.6 %copy-start = (s32[1,1,3,1]{2,3,1,0:T(1,128)S(1)}, s32[1,1,3,1]{2,3,1,0:T(1,128)}, u32[]{:S(2)}) copy-start(s32[1,1,3,1]{2,3,1,0:T(1,128)} %param.7) | copy-start | bytes 40
  6.1 2.6 %copy-start.1 = (s32[1,1,2]{2,1,0:T(1,128)S(1)}, s32[1,1,2]{2,1,0:T(1,128)}, u32[]{:S(2)}) copy-start(s32[1,1,2]{2,1,0:T(1,128)} %param.8) | copy-start | bytes 28
  6.1 15.9 %collective-permute-start = (bf16[512,256]{1,0:T(8,128)(2,1)S(1)}, bf16[512,256]{1,0:T(8,128)(2,1)S(1)}, u32[]{:S(2)}, u32[]{:S(2)}) collective-permute-start(bf16[512,256]{1,0:T(8,128)(2,1)S(1)} %get-tuple-element.21), channel_id=1, source_target_pairs={{0,30},{2,4},{4,2},{6,8},{8,6},{10,12},{12,10},{14,16},{16,14},{18... | collective-permute-start | bytes 786440 | tf_op jit(solution)/shard_map/ppermute | solution.py:26
  20.0 6.3 %collective-permute-start.5 = (bf16[256,512]{1,0:T(8,128)(2,1)S(1)}, bf16[256,512]{1,0:T(8,128)(2,1)S(1)}, u32[]{:S(2)}, u32[]{:S(2)}) collective-permute-start(bf16[256,512]{1,0:T(8,128)(2,1)S(1)} %get-tuple-element.32), channel_id=1, source_target_pairs={{0,1},{1,0},{2,3},{3,2},{4,5},{5,4},{6,7},{7,6},{8,9},{9,8},{10,11... | collective-permute-start | bytes 786440 | tf_op jit(solution)/shard_map/ppermute | solution.py:16
  22.5 5.1 %collective-permute-start.3 = (bf16[256,256]{1,0:T(8,128)(2,1)S(1)}, bf16[256,256]{1,0:T(8,128)(2,1)S(1)}, u32[]{:S(2)}, u32[]{:S(2)}) collective-permute-start(bf16[256,256]{1,0:T(8,128)(2,1)S(1)} %get-tuple-element.30), channel_id=1, source_target_pairs={{0,1},{1,0},{2,3},{3,2},{4,5},{5,4},{6,7},{7,6},{8,9},{9,8},{10,11... | collective-permute-start | bytes 393224 | tf_op jit(solution)/shard_map/ppermute | solution.py:16

commit v20 on v19

--- a/solution.py
+++ b/solution.py
@@ -68,16 +68,15 @@
     return basis.at[0, 0, pl.ds(pl.multiple_of(group * half, half), half)]
 
 
-def first_kernel(sketch, first, sems):
-    copy_all([(sketch.at[:, pl.ds(0, first.shape[1])], first)], sems)
-
-
-def cut_kernel(begun, sketch, basis, lent, second, sems):
+def first_kernel(sketch, basis, lent, first, sems):
+    theirs = half_rows(basis, 1 - lax.axis_index("group"), lent.shape[0])
+    copy_all([(sketch.at[:, pl.ds(0, first.shape[1])], first), (theirs, lent)], sems)
+
+
+def second_kernel(begun, sketch, second, sems):
     del begun
-    theirs = half_rows(basis, 1 - lax.axis_index("group"), lent.shape[0])
     width = second.shape[1]
-    columns = pl.ds(sketch.shape[1] - width, width)
-    copy_all([(theirs, lent), (sketch.at[:, columns], second)], sems)
+    copy_all([(sketch.at[:, pl.ds(sketch.shape[1] - width, width)], second)], sems)
 
 
 def stage_kernel(begun, sketch, tiles, basis, own, staged, kept, sems):
@@ -138,21 +137,21 @@
     product = 2 * rows * panels * columns
     short, wide = sketch.dtype, jnp.float32
     copies = pltpu.SemaphoreType.DMA
-    first = call(
+    lent, first = call(
         first_kernel,
-        on_chip((panels, widths[0]), short),
+        (on_chip((half, rank), short), on_chip((panels, widths[0]), short)),
         (),
+        0,
+        hbm=(sketch, cluster_basis),
+        scratch=(copies((2,)),),
+    )
+    second = call(
+        second_kernel,
+        on_chip((panels, widths[1]), short),
+        (first,),
         0,
         hbm=(sketch,),
         scratch=(copies((1,)),),
-    )
-    lent, second = call(
-        cut_kernel,
-        (on_chip((half, rank), short), on_chip((panels, widths[1]), short)),
-        (first,),
-        0,
-        hbm=(sketch, cluster_basis),
-        scratch=(copies((2,)),),
     )
     own, tiles, kept = call(
         stage_kernel,
@@ -161,7 +160,7 @@
             on_chip((offsets, rows, panels), short),
             on_chip((half, rank), short),
         ),
-        (lent,),
+        (second,),
         0,
         hbm=(sketch, far_tiles, cluster_basis),
         scratch=(copies((3,)),),

time: 28.6 us -> 28.6 us (level)
  transfers between devices with their start and end apart: 6 -> 6, of which waited for: 5 -> 3; matrix products, arithmetic and copies ran while one was open for 0% -> 0% of each run, Pallas kernels for 28% -> 28%
where the time goes in v20:
time: 28.6 us; the launch traced here: 28.4 us
  waiting for transfers between devices  10.9 us (38%)
  starting transfers between devices  8.82 us (31%)
  Pallas kernels  8.57 us (30%)
    ppermute x2, waiting for transfers between devices, swap_far(): lax.ppermute(array, 'blk', [(i, (i + 1 if i % 2 else i - 1) % devices) fo...  8.6 us
    pallas_call x9, Pallas kernels, call(): pl.pallas_call(kernel, out_shape=out_shape, in_specs=[scalar] * len(scala...  8.57 us
    ppermute x3, starting transfers between devices, from_behind(): lax.ppermute(array, axis, [(i, (i + by) % devices) for i in range(devices)])  5.16 us
    ppermute x2, starting transfers between devices, swap_far(): lax.ppermute(array, 'blk', [(i, (i + 1 if i % 2 else i - 1) % devices) fo...  3.6 us
    ppermute x3, waiting for transfers between devices, from_behind(): lax.ppermute(array, axis, [(i, (i + by) % devices) for i in range(devices)])  2.26 us
  transfers between devices with their start and end apart: 6, of which 3 were waited for; matrix products, arithmetic and copies ran while one was open for 0% of the time, Pallas kernels for 28%

profile of v20, /device:TPU:1, one launch (start us, length us, event | category | flops | bytes accessed | tf_op | source)
XLA Modules:
  0.0 28.4 jit_solution(4887196618311148343)
XLA Ops:
  0.0 0.1 collective-permute-start.1
  0.1 1.1 %shard_map.55 = (bf16[512,256]{1,0:T(8,128)(2,1)S(1)}, bf16[512,512]{1,0:T(8,128)(2,1)S(1)}) custom-call(bf16[512,768]{1,0:T(8,128)(2,1)} %sketch.5, bf16[1,1,1024,256]{3,2,1,0:T(8,128)(2,1)} %basis.3), custom_call_target="tpu_custom_call" | custom-call | bytes 1048576 | tf_op jit(solution)/shard_map/pallas_call | solution.py:43
  1.2 2.6 %collective-permute-start.4 = (bf16[512,512]{1,0:T(8,128)(2,1)S(1)}, bf16[512,512]{1,0:T(8,128)(2,1)S(1)}, u32[]{:S(2)}, u32[]{:S(2)}) collective-permute-start(bf16[512,512]{1,0:T(8,128)(2,1)S(1)} %get-tuple-element.19.begun), channel_id=1, source_target_pairs={{0,30},{2,4},{4,2},{6,8},{8,6},{10,12},{12,10},{14,16},{16,14},{18... | collective-permute-start | bytes 1572872 | tf_op jit(solution)/shard_map/ppermute | solution.py:26
  3.8 1.2 %collective-permute-start.2 = (bf16[512,256]{1,0:T(8,128)(2,1)S(1)}, bf16[512,256]{1,0:T(8,128)(2,1)S(1)}, u32[]{:S(2)}, u32[]{:S(2)}) collective-permute-start(bf16[512,256]{1,0:T(8,128)(2,1)S(1)} %get-tuple-element.24), channel_id=1, source_target_pairs={{0,1},{1,0},{2,3},{3,2},{4,5},{5,4},{6,7},{7,6},{8,9},{9,8},{10,11... | collective-permute-start | bytes 786440 | tf_op jit(solution)/shard_map/ppermute | solution.py:16
  5.0 1.0 %shard_map.56.begun = bf16[512,256]{1,0:T(8,128)(2,1)S(1)} custom-call(bf16[512,512]{1,0:T(8,128)(2,1)S(1)} %get-tuple-element.19.begun, bf16[512,768]{1,0:T(8,128)(2,1)} %sketch.5), custom_call_target="tpu_custom_call" | custom-call | bytes 1048576 | tf_op jit(solution)/shard_map/pallas_call | solution.py:43
  6.0 0.0 copy-start
  6.0 0.0 copy-start.1
  6.0 1.0 %collective-permute-start = (bf16[512,256]{1,0:T(8,128)(2,1)S(1)}, bf16[512,256]{1,0:T(8,128)(2,1)S(1)}, u32[]{:S(2)}, u32[]{:S(2)}) collective-permute-start(bf16[512,256]{1,0:T(8,128)(2,1)S(1)} %shard_map.56.begun), channel_id=1, source_target_pairs={{0,30},{2,4},{4,2},{6,8},{8,6},{10,12},{12,10},{14,16},{16,14},{18... | collective-permute-start | bytes 786440 | tf_op jit(solution)/shard_map/ppermute | solution.py:26
  7.0 1.7 %shard_map.57 = (bf16[512,768]{1,0:T(8,128)(2,1)S(1)}, bf16[3,512,512]{2,1,0:T(8,128)(2,1)S(1)}, bf16[512,256]{1,0:T(8,128)(2,1)S(1)}) custom-call(bf16[512,256]{1,0:T(8,128)(2,1)S(1)} %shard_map.56.begun, bf16[512,768]{1,0:T(8,128)(2,1)} %sketch.5, bf16[1,1,3,1,512,512]{5,4,3,2,1,0:T(8,128)(2,1)} %tiles.1, bf16[1,1,1024,256]{3,2,1,0:T(8,128)(2,1)} %basis.3), custom_call_target="tpu_custom_call" | custom-call | bytes 1048576 | tf_op jit(solution)/shard_map/pallas_call | solution.py:43
  8.7 0.0 collective-permute-done.1.near
  8.7 0.0 copy-done
  8.7 0.0 copy-done.1
  8.7 1.5 %shard_map.58 = (f32[512,768]{1,0:T(8,128)S(1)}, bf16[512,768]{1,0:T(8,128)(2,1)S(1)}, f32[1,768]{1,0:T(1,128)S(1)}) custom-call(s32[3]{0:T(128)S(1)} %bitcast.3, s32[2]{0:T(128)S(1)} %bitcast.4, bf16[3,512,512]{2,1,0:T(8,128)(2,1)S(1)} %get-tuple-element.20.tiles, bf16[512,768]{1,0:T(8,128)(2,1)S(1)} %get-tuple-element.21.own, ...), custom_call_target="tpu_custom_call" | custom-call | flops 805306368 | bytes 1048576 | tf_op jit(solution)/shard_map/pallas_call | solution.py:43
  10.3 0.0 collective-permute-done.2.lent
  10.3 0.5 %shard_map.59 = (bf16[256,512]{1,0:T(8,128)(2,1)S(1)}, f32[256,768]{1,0:T(8,128)S(1)}) custom-call(bf16[512,256]{1,0:T(8,128)(2,1)S(1)} %get-tuple-element.23.kept, bf16[512,256]{1,0:T(8,128)(2,1)S(1)} %collective-permute-done.2.lent, bf16[512,768]{1,0:T(8,128)(2,1)S(1)} %get-tuple-element.25.miss, f32[1,768]{1,0:T(1,128)S(1)} %get-tuple-element.26.stays), custom_call_target="tpu_custom_call" | custom-call | flops 201326592 | bytes 1048576 | tf_op jit(solution)/shard_map/pallas_call | solution.py:43
  10.8 8.6 %collective-permute-done.4.far = bf16[512,512]{1,0:T(8,128)(2,1)S(1)} collective-permute-done((bf16[512,512]{1,0:T(8,128)(2,1)S(1)}, bf16[512,512]{1,0:T(8,128)(2,1)S(1)}, u32[]{:S(2)}, u32[]{:S(2)}) %collective-permute-start.4) | collective-permute-done | bytes 524320 | tf_op jit(solution)/shard_map/ppermute | solution.py:26
  19.4 0.6 %shard_map.61 = (f32[256,512]{1,0:T(8,128)S(1)}, bf16[256,512]{1,0:T(8,128)(2,1)S(1)}) custom-call(bf16[3,512,512]{2,1,0:T(8,128)(2,1)S(1)} %get-tuple-element.20.tiles, bf16[512,512]{1,0:T(8,128)(2,1)S(1)} %collective-permute-done.4.far, f32[512,768]{1,0:T(8,128)S(1)} %get-tuple-element.22.hit, bf16[256,512]{1,0:T(8,128)(2,1)S(1)} %get-tuple-element.27.hit_turned, ...), custom_call_target="tpu_custom_call" | custom-call | flops 536870912 | bytes 1048576 | tf_op jit(solution)/shard_map/pallas_call | solution.py:43
  20.0 1.9 %collective-permute-start.5 = (bf16[256,512]{1,0:T(8,128)(2,1)S(1)}, bf16[256,512]{1,0:T(8,128)(2,1)S(1)}, u32[]{:S(2)}, u32[]{:S(2)}) collective-permute-start(bf16[256,512]{1,0:T(8,128)(2,1)S(1)} %get-tuple-element.32), channel_id=1, source_target_pairs={{0,1},{1,0},{2,3},{3,2},{4,5},{5,4},{6,7},{7,6},{8,9},{9,8},{10,11... | collective-permute-start | bytes 786440 | tf_op jit(solution)/shard_map/ppermute | solution.py:16
  22.0 0.0 collective-permute-done.far
  22.0 0.6 %shard_map.60 = (f32[256,256]{1,0:T(8,128)S(1)}, bf16[256,256]{1,0:T(8,128)(2,1)S(1)}) custom-call(bf16[3,512,512]{2,1,0:T(8,128)(2,1)S(1)} %get-tuple-element.20.tiles, bf16[512,256]{1,0:T(8,128)(2,1)S(1)} %collective-permute-done.far, f32[512,768]{1,0:T(8,128)S(1)} %get-tuple-element.22.hit, bf16[256,512]{1,0:T(8,128)(2,1)S(1)} %get-tuple-element.27.hit_turned, ...), custom_call_target="tpu_custom_call" | custom-call | flops 268435456 | bytes 1048576 | tf_op jit(solution)/shard_map/pallas_call | solution.py:43
  22.6 2.0 %collective-permute-start.3 = (bf16[256,256]{1,0:T(8,128)(2,1)S(1)}, bf16[256,256]{1,0:T(8,128)(2,1)S(1)}, u32[]{:S(2)}, u32[]{:S(2)}) collective-permute-start(bf16[256,256]{1,0:T(8,128)(2,1)S(1)} %get-tuple-element.30), channel_id=1, source_target_pairs={{0,1},{1,0},{2,3},{3,2},{4,5},{5,4},{6,7},{7,6},{8,9},{9,8},{10,11... | collective-permute-start | bytes 393224 | tf_op jit(solution)/shard_map/ppermute | solution.py:16
  24.5 1.7 %collective-permute-done.5.received = bf16[256,512]{1,0:T(8,128)(2,1)S(1)} collective-permute-done((bf16[256,512]{1,0:T(8,128)(2,1)S(1)}, bf16[256,512]{1,0:T(8,128)(2,1)S(1)}, u32[]{:S(2)}, u32[]{:S(2)}) %collective-permute-start.5) | collective-permute-done | bytes 262176 | tf_op jit(solution)/shard_map/ppermute | solution.py:16
  26.2 0.8 %shard_map.62.rest_0_ = f32[256,768]{1,0:T(8,128)} custom-call(f32[256,512]{1,0:T(8,128)S(1)} %get-tuple-element.31.kept, bf16[256,512]{1,0:T(8,128)(2,1)S(1)} %collective-permute-done.5.received), custom_call_target="tpu_custom_call" | custom-call | flops 65536 | bytes 1048576 | tf_op jit(solution)/shard_map/pallas_call | solution.py:43
  27.1 0.5 %collective-permute-done.3.received = bf16[256,256]{1,0:T(8,128)(2,1)S(1)} collective-permute-done((bf16[256,256]{1,0:T(8,128)(2,1)S(1)}, bf16[256,256]{1,0:T(8,128)(2,1)S(1)}, u32[]{:S(2)}, u32[]{:S(2)}) %collective-permute-start.3) | collective-permute-done | bytes 131104 | tf_op jit(solution)/shard_map/ppermute | solution.py:16
  27.6 0.7 %shard_map.63 = f32[256,768]{1,0:T(8,128)} custom-call(f32[256,256]{1,0:T(8,128)S(1)} %get-tuple-element.29.kept, bf16[256,256]{1,0:T(8,128)(2,1)S(1)} %collective-permute-done.3.received, f32[256,768]{1,0:T(8,128)} %shard_map.62.rest_0_), custom_call_target="tpu_custom_call", output_to_operand_aliasing={{}: (2, {})} | custom-call | flops 65536 | bytes 1048576 | tf_op jit(solution)/shard_map/pallas_call | solution.py:43
Async XLA Ops:
  0.0 8.7 %collective-permute-start.1 = (bf16[512,768]{1,0:T(8,128)(2,1)}, bf16[512,768]{1,0:T(8,128)(2,1)S(1)}, u32[]{:S(2)}, u32[]{:S(2)}) collective-permute-start(bf16[512,768]{1,0:T(8,128)(2,1)} %sketch.5), channel_id=1, source_target_pairs={{0,2},{2,0},{4,6},{6,4},{8,10},{10,8},{12,14},{14,12},{16,18},{18,... | collective-permute-start | bytes 2359304 | tf_op jit(solution)/shard_map/ppermute | solution.py:21
  1.2 18.2 %collective-permute-start.4 = (bf16[512,512]{1,0:T(8,128)(2,1)S(1)}, bf16[512,512]{1,0:T(8,128)(2,1)S(1)}, u32[]{:S(2)}, u32[]{:S(2)}) collective-permute-start(bf16[512,512]{1,0:T(8,128)(2,1)S(1)} %get-tuple-element.19.begun), channel_id=1, source_target_pairs={{0,30},{2,4},{4,2},{6,8},{8,6},{10,12},{12,10},{14,16},{16,14},{18... | collective-permute-start | bytes 1572872 | tf_op jit(solution)/shard_map/ppermute | solution.py:26
  3.8 6.5 %collective-permute-start.2 = (bf16[512,256]{1,0:T(8,128)(2,1)S(1)}, bf16[512,256]{1,0:T(8,128)(2,1)S(1)}, u32[]{:S(2)}, u32[]{:S(2)}) collective-permute-start(bf16[512,256]{1,0:T(8,128)(2,1)S(1)} %get-tuple-element.24), channel_id=1, source_target_pairs={{0,1},{1,0},{2,3},{3,2},{4,5},{5,4},{6,7},{7,6},{8,9},{9,8},{10,11... | collective-permute-start | bytes 786440 | tf_op jit(solution)/shard_map/ppermute | solution.py:16
  6.0 2.7 %copy-start = (s32[1,1,3,1]{2,3,1,0:T(1,128)S(1)}, s32[1,1,3,1]{2,3,1,0:T(1,128)}, u32[]{:S(2)}) copy-start(s32[1,1,3,1]{2,3,1,0:T(1,128)} %param.7) | copy-start | bytes 40
  6.0 2.7 %copy-start.1 = (s32[1,1,2]{2,1,0:T(1,128)S(1)}, s32[1,1,2]{2,1,0:T(1,128)}, u32[]{:S(2)}) copy-start(s32[1,1,2]{2,1,0:T(1,128)} %param.8) | copy-start | bytes 28
  6.0 16.0 %collective-permute-start = (bf16[512,256]{1,0:T(8,128)(2,1)S(1)}, bf16[512,256]{1,0:T(8,128)(2,1)S(1)}, u32[]{:S(2)}, u32[]{:S(2)}) collective-permute-start(bf16[512,256]{1,0:T(8,128)(2,1)S(1)} %shard_map.56.begun), channel_id=1, source_target_pairs={{0,30},{2,4},{4,2},{6,8},{8,6},{10,12},{12,10},{14,16},{16,14},{18... | collective-permute-start | bytes 786440 | tf_op jit(solution)/shard_map/ppermute | solution.py:26
  20.0 6.2 %collective-permute-start.5 = (bf16[256,512]{1,0:T(8,128)(2,1)S(1)}, bf16[256,512]{1,0:T(8,128)(2,1)S(1)}, u32[]{:S(2)}, u32[]{:S(2)}) collective-permute-start(bf16[256,512]{1,0:T(8,128)(2,1)S(1)} %get-tuple-element.32), channel_id=1, source_target_pairs={{0,1},{1,0},{2,3},{3,2},{4,5},{5,4},{6,7},{7,6},{8,9},{9,8},{10,11... | collective-permute-start | bytes 786440 | tf_op jit(solution)/shard_map/ppermute | solution.py:16
  22.6 5.1 %collective-permute-start.3 = (bf16[256,256]{1,0:T(8,128)(2,1)S(1)}, bf16[256,256]{1,0:T(8,128)(2,1)S(1)}, u32[]{:S(2)}, u32[]{:S(2)}) collective-permute-start(bf16[256,256]{1,0:T(8,128)(2,1)S(1)} %get-tuple-element.30), channel_id=1, source_target_pairs={{0,1},{1,0},{2,3},{3,2},{4,5},{5,4},{6,7},{7,6},{8,9},{9,8},{10,11... | collective-permute-start | bytes 393224 | tf_op jit(solution)/shard_map/ppermute | solution.py:16

commit v21 on v16

--- a/solution.py
+++ b/solution.py
@@ -68,7 +68,7 @@
     return basis.at[0, 0, pl.ds(pl.multiple_of(group * half, half), half)]
 
 
-def row_blocks_of(array, count=4):
+def row_blocks_of(array, count):
     rows = array.shape[0] // count
     return [pl.ds(i * rows, rows) for i in range(count)]
 
@@ -76,7 +76,7 @@
 def cut_kernel(sketch, basis, lent, first, second, sems):
     theirs = half_rows(basis, 1 - lax.axis_index("group"), lent.shape[0])
     early, late = pl.ds(0, first.shape[1]), pl.ds(first.shape[1], second.shape[1])
-    pairs = [(sketch.at[rows, early], first.at[rows]) for rows in row_blocks_of(first)]
+    pairs = [(sketch.at[:, early], first)]
     pairs += [(theirs, lent), (sketch.at[:, late], second)]
     copy_all(pairs, sems)
 
@@ -157,7 +157,7 @@
         (),
         0,
         hbm=(sketch, cluster_basis),
-        scratch=(copies((6,)),),
+        scratch=(copies((3,)),),
     )
     own, tiles, kept = call(
         stage_kernel,

time: 28.3 us -> 28.1 us (level)
  no operation moved by 1% of the time
where the time goes in v21:
time: 28.1 us; the launch traced here: 28 us
  waiting for transfers between devices  11.8 us (42%)
  starting transfers between devices  8.42 us (30%)
  Pallas kernels  7.67 us (27%)
    ppermute x2, waiting for transfers between devices, swap_far(): lax.ppermute(array, 'blk', [(i, (i + 1 if i % 2 else i - 1) % devices) fo...  9.79 us
    pallas_call x8, Pallas kernels, call(): pl.pallas_call(kernel, out_shape=out_shape, in_specs=[scalar] * len(scala...  7.67 us
    ppermute x3, starting transfers between devices, from_behind(): lax.ppermute(array, axis, [(i, (i + by) % devices) for i in range(devices)])  4.83 us
    ppermute x2, starting transfers between devices, swap_far(): lax.ppermute(array, 'blk', [(i, (i + 1 if i % 2 else i - 1) % devices) fo...  3.54 us
    ppermute x3, waiting for transfers between devices, from_behind(): lax.ppermute(array, axis, [(i, (i + by) % devices) for i in range(devices)])  1.98 us
  transfers between devices with their start and end apart: 6, of which 5 were waited for; matrix products, arithmetic and copies ran while one was open for 0% of the time, Pallas kernels for 25%

profile of v21, /device:TPU:1, one launch (start us, length us, event | category | flops | bytes accessed | tf_op | source)
XLA Modules:
  0.0 28.0 jit_solution(3843240324763739249)
XLA Ops:
  0.0 0.1 collective-permute-start.1
  0.1 1.2 %shard_map.55 = (bf16[512,256]{1,0:T(8,128)(2,1)S(1)}, bf16[512,512]{1,0:T(8,128)(2,1)S(1)}, bf16[512,256]{1,0:T(8,128)(2,1)S(1)}) custom-call(bf16[512,768]{1,0:T(8,128)(2,1)} %sketch.3, bf16[1,1,1024,256]{3,2,1,0:T(8,128)(2,1)} %basis.3), custom_call_target="tpu_custom_call" | custom-call | bytes 1048576 | tf_op jit(solution)/shard_map/pallas_call | solution.py:43
  1.3 2.6 %collective-permute-start.4 = (bf16[512,512]{1,0:T(8,128)(2,1)S(1)}, bf16[512,512]{1,0:T(8,128)(2,1)S(1)}, u32[]{:S(2)}, u32[]{:S(2)}) collective-permute-start(bf16[512,512]{1,0:T(8,128)(2,1)S(1)} %get-tuple-element.20.begun), channel_id=1, source_target_pairs={{0,30},{2,4},{4,2},{6,8},{8,6},{10,12},{12,10},{14,16},{16,14},{18... | collective-permute-start | bytes 1572872 | tf_op jit(solution)/shard_map/ppermute | solution.py:26
  3.9 1.2 %collective-permute-start.2 = (bf16[512,256]{1,0:T(8,128)(2,1)S(1)}, bf16[512,256]{1,0:T(8,128)(2,1)S(1)}, u32[]{:S(2)}, u32[]{:S(2)}) collective-permute-start(bf16[512,256]{1,0:T(8,128)(2,1)S(1)} %get-tuple-element.26), channel_id=1, source_target_pairs={{0,1},{1,0},{2,3},{3,2},{4,5},{5,4},{6,7},{7,6},{8,9},{9,8},{10,11... | collective-permute-start | bytes 786440 | tf_op jit(solution)/shard_map/ppermute | solution.py:16
  5.1 0.0 copy-start
  5.1 0.0 copy-start.1
  5.1 0.9 %collective-permute-start = (bf16[512,256]{1,0:T(8,128)(2,1)S(1)}, bf16[512,256]{1,0:T(8,128)(2,1)S(1)}, u32[]{:S(2)}, u32[]{:S(2)}) collective-permute-start(bf16[512,256]{1,0:T(8,128)(2,1)S(1)} %get-tuple-element.22), channel_id=1, source_target_pairs={{0,30},{2,4},{4,2},{6,8},{8,6},{10,12},{12,10},{14,16},{16,14},{18... | collective-permute-start | bytes 786440 | tf_op jit(solution)/shard_map/ppermute | solution.py:26
  6.1 1.7 %shard_map.56 = (bf16[512,768]{1,0:T(8,128)(2,1)S(1)}, bf16[3,512,512]{2,1,0:T(8,128)(2,1)S(1)}, bf16[512,256]{1,0:T(8,128)(2,1)S(1)}) custom-call(bf16[512,512]{1,0:T(8,128)(2,1)S(1)} %get-tuple-element.20.begun, bf16[512,768]{1,0:T(8,128)(2,1)} %sketch.3, bf16[1,1,3,1,512,512]{5,4,3,2,1,0:T(8,128)(2,1)} %tiles.1, bf16[1,1,1024,256]{3,2,1,0:T(8,128)(2,1)} %basis.3), custom_call_target="tpu_custom_call" | custom-call | bytes 1048576 | tf_op jit(solution)/shard_map/pallas_call | solution.py:43
  7.8 0.0 collective-permute-done.1.near
  7.8 0.0 copy-done
  7.8 0.0 copy-done.1
  7.8 1.5 %shard_map.57 = (f32[512,768]{1,0:T(8,128)S(1)}, bf16[512,768]{1,0:T(8,128)(2,1)S(1)}, f32[1,768]{1,0:T(1,128)S(1)}) custom-call(s32[3]{0:T(128)S(1)} %bitcast.3, s32[2]{0:T(128)S(1)} %bitcast.4, bf16[3,512,512]{2,1,0:T(8,128)(2,1)S(1)} %get-tuple-element.21.tiles, bf16[512,768]{1,0:T(8,128)(2,1)S(1)} %get-tuple-element.23.own, ...), custom_call_target="tpu_custom_call" | custom-call | flops 805306368 | bytes 1048576 | tf_op jit(solution)/shard_map/pallas_call | solution.py:43
  9.3 0.1 collective-permute-done.2.lent
  9.4 0.5 %shard_map.58 = (bf16[256,512]{1,0:T(8,128)(2,1)S(1)}, f32[256,768]{1,0:T(8,128)S(1)}) custom-call(bf16[512,256]{1,0:T(8,128)(2,1)S(1)} %get-tuple-element.25.kept, bf16[512,256]{1,0:T(8,128)(2,1)S(1)} %collective-permute-done.2.lent, bf16[512,768]{1,0:T(8,128)(2,1)S(1)} %get-tuple-element.27.miss, f32[1,768]{1,0:T(1,128)S(1)} %get-tuple-element.28.stays), custom_call_target="tpu_custom_call" | custom-call | flops 201326592 | bytes 1048576 | tf_op jit(solution)/shard_map/pallas_call | solution.py:43
  9.9 9.6 %collective-permute-done.4.far = bf16[512,512]{1,0:T(8,128)(2,1)S(1)} collective-permute-done((bf16[512,512]{1,0:T(8,128)(2,1)S(1)}, bf16[512,512]{1,0:T(8,128)(2,1)S(1)}, u32[]{:S(2)}, u32[]{:S(2)}) %collective-permute-start.4) | collective-permute-done | bytes 524320 | tf_op jit(solution)/shard_map/ppermute | solution.py:26
  19.5 0.6 %shard_map.60 = (f32[256,512]{1,0:T(8,128)S(1)}, bf16[256,512]{1,0:T(8,128)(2,1)S(1)}) custom-call(bf16[3,512,512]{2,1,0:T(8,128)(2,1)S(1)} %get-tuple-element.21.tiles, bf16[512,512]{1,0:T(8,128)(2,1)S(1)} %collective-permute-done.4.far, f32[512,768]{1,0:T(8,128)S(1)} %get-tuple-element.24.hit, bf16[256,512]{1,0:T(8,128)(2,1)S(1)} %get-tuple-element.29.hit_turned, ...), custom_call_target="tpu_custom_call" | custom-call | flops 536870912 | bytes 1048576 | tf_op jit(solution)/shard_map/pallas_call | solution.py:43
  20.1 1.9 %collective-permute-start.5 = (bf16[256,512]{1,0:T(8,128)(2,1)S(1)}, bf16[256,512]{1,0:T(8,128)(2,1)S(1)}, u32[]{:S(2)}, u32[]{:S(2)}) collective-permute-start(bf16[256,512]{1,0:T(8,128)(2,1)S(1)} %get-tuple-element.34), channel_id=1, source_target_pairs={{0,1},{1,0},{2,3},{3,2},{4,5},{5,4},{6,7},{7,6},{8,9},{9,8},{10,11... | collective-permute-start | bytes 786440 | tf_op jit(solution)/shard_map/ppermute | solution.py:16
  22.1 0.2 collective-permute-done.far
  22.3 0.6 %shard_map.59 = (f32[256,256]{1,0:T(8,128)S(1)}, bf16[256,256]{1,0:T(8,128)(2,1)S(1)}) custom-call(bf16[3,512,512]{2,1,0:T(8,128)(2,1)S(1)} %get-tuple-element.21.tiles, bf16[512,256]{1,0:T(8,128)(2,1)S(1)} %collective-permute-done.far, f32[512,768]{1,0:T(8,128)S(1)} %get-tuple-element.24.hit, bf16[256,512]{1,0:T(8,128)(2,1)S(1)} %get-tuple-element.29.hit_turned, ...), custom_call_target="tpu_custom_call" | custom-call | flops 268435456 | bytes 1048576 | tf_op jit(solution)/shard_map/pallas_call | solution.py:43
  22.8 1.6 %collective-permute-start.3 = (bf16[256,256]{1,0:T(8,128)(2,1)S(1)}, bf16[256,256]{1,0:T(8,128)(2,1)S(1)}, u32[]{:S(2)}, u32[]{:S(2)}) collective-permute-start(bf16[256,256]{1,0:T(8,128)(2,1)S(1)} %get-tuple-element.32), channel_id=1, source_target_pairs={{0,1},{1,0},{2,3},{3,2},{4,5},{5,4},{6,7},{7,6},{8,9},{9,8},{10,11... | collective-permute-start | bytes 393224 | tf_op jit(solution)/shard_map/ppermute | solution.py:16
  24.5 1.3 %collective-permute-done.5.received = bf16[256,512]{1,0:T(8,128)(2,1)S(1)} collective-permute-done((bf16[256,512]{1,0:T(8,128)(2,1)S(1)}, bf16[256,512]{1,0:T(8,128)(2,1)S(1)}, u32[]{:S(2)}, u32[]{:S(2)}) %collective-permute-start.5) | collective-permute-done | bytes 262176 | tf_op jit(solution)/shard_map/ppermute | solution.py:16
  25.8 0.8 %shard_map.61.rest_0_ = f32[256,768]{1,0:T(8,128)} custom-call(f32[256,512]{1,0:T(8,128)S(1)} %get-tuple-element.33.kept, bf16[256,512]{1,0:T(8,128)(2,1)S(1)} %collective-permute-done.5.received), custom_call_target="tpu_custom_call" | custom-call | flops 65536 | bytes 1048576 | tf_op jit(solution)/shard_map/pallas_call | solution.py:43
  26.7 0.6 %collective-permute-done.3.received = bf16[256,256]{1,0:T(8,128)(2,1)S(1)} collective-permute-done((bf16[256,256]{1,0:T(8,128)(2,1)S(1)}, bf16[256,256]{1,0:T(8,128)(2,1)S(1)}, u32[]{:S(2)}, u32[]{:S(2)}) %collective-permute-start.3) | collective-permute-done | bytes 131104 | tf_op jit(solution)/shard_map/ppermute | solution.py:16
  27.2 0.7 %shard_map.62 = f32[256,768]{1,0:T(8,128)} custom-call(f32[256,256]{1,0:T(8,128)S(1)} %get-tuple-element.31.kept, bf16[256,256]{1,0:T(8,128)(2,1)S(1)} %collective-permute-done.3.received, f32[256,768]{1,0:T(8,128)} %shard_map.61.rest_0_), custom_call_target="tpu_custom_call", output_to_operand_aliasing={{}: (2, {})} | custom-call | flops 65536 | bytes 1048576 | tf_op jit(solution)/shard_map/pallas_call | solution.py:43
Async XLA Ops:
  0.0 7.8 %collective-permute-start.1 = (bf16[512,768]{1,0:T(8,128)(2,1)}, bf16[512,768]{1,0:T(8,128)(2,1)S(1)}, u32[]{:S(2)}, u32[]{:S(2)}) collective-permute-start(bf16[512,768]{1,0:T(8,128)(2,1)} %sketch.3), channel_id=1, source_target_pairs={{0,2},{2,0},{4,6},{6,4},{8,10},{10,8},{12,14},{14,12},{16,18},{18,... | collective-permute-start | bytes 2359304 | tf_op jit(solution)/shard_map/ppermute | solution.py:21
  1.3 18.2 %collective-permute-start.4 = (bf16[512,512]{1,0:T(8,128)(2,1)S(1)}, bf16[512,512]{1,0:T(8,128)(2,1)S(1)}, u32[]{:S(2)}, u32[]{:S(2)}) collective-permute-start(bf16[512,512]{1,0:T(8,128)(2,1)S(1)} %get-tuple-element.20.begun), channel_id=1, source_target_pairs={{0,30},{2,4},{4,2},{6,8},{8,6},{10,12},{12,10},{14,16},{16,14},{18... | collective-permute-start | bytes 1572872 | tf_op jit(solution)/shard_map/ppermute | solution.py:26
  3.9 5.5 %collective-permute-start.2 = (bf16[512,256]{1,0:T(8,128)(2,1)S(1)}, bf16[512,256]{1,0:T(8,128)(2,1)S(1)}, u32[]{:S(2)}, u32[]{:S(2)}) collective-permute-start(bf16[512,256]{1,0:T(8,128)(2,1)S(1)} %get-tuple-element.26), channel_id=1, source_target_pairs={{0,1},{1,0},{2,3},{3,2},{4,5},{5,4},{6,7},{7,6},{8,9},{9,8},{10,11... | collective-permute-start | bytes 786440 | tf_op jit(solution)/shard_map/ppermute | solution.py:16
  5.1 2.6 %copy-start = (s32[1,1,3,1]{2,3,1,0:T(1,128)S(1)}, s32[1,1,3,1]{2,3,1,0:T(1,128)}, u32[]{:S(2)}) copy-start(s32[1,1,3,1]{2,3,1,0:T(1,128)} %param.7) | copy-start | bytes 40
  5.1 2.6 %copy-start.1 = (s32[1,1,2]{2,1,0:T(1,128)S(1)}, s32[1,1,2]{2,1,0:T(1,128)}, u32[]{:S(2)}) copy-start(s32[1,1,2]{2,1,0:T(1,128)} %param.8) | copy-start | bytes 28
  5.1 17.2 %collective-permute-start = (bf16[512,256]{1,0:T(8,128)(2,1)S(1)}, bf16[512,256]{1,0:T(8,128)(2,1)S(1)}, u32[]{:S(2)}, u32[]{:S(2)}) collective-permute-start(bf16[512,256]{1,0:T(8,128)(2,1)S(1)} %get-tuple-element.22), channel_id=1, source_target_pairs={{0,30},{2,4},{4,2},{6,8},{8,6},{10,12},{12,10},{14,16},{16,14},{18... | collective-permute-start | bytes 786440 | tf_op jit(solution)/shard_map/ppermute | solution.py:26
  20.1 5.7 %collective-permute-start.5 = (bf16[256,512]{1,0:T(8,128)(2,1)S(1)}, bf16[256,512]{1,0:T(8,128)(2,1)S(1)}, u32[]{:S(2)}, u32[]{:S(2)}) collective-permute-start(bf16[256,512]{1,0:T(8,128)(2,1)S(1)} %get-tuple-element.34), channel_id=1, source_target_pairs={{0,1},{1,0},{2,3},{3,2},{4,5},{5,4},{6,7},{7,6},{8,9},{9,8},{10,11... | collective-permute-start | bytes 786440 | tf_op jit(solution)/shard_map/ppermute | solution.py:16
  22.8 4.4 %collective-permute-start.3 = (bf16[256,256]{1,0:T(8,128)(2,1)S(1)}, bf16[256,256]{1,0:T(8,128)(2,1)S(1)}, u32[]{:S(2)}, u32[]{:S(2)}) collective-permute-start(bf16[256,256]{1,0:T(8,128)(2,1)S(1)} %get-tuple-element.32), channel_id=1, source_target_pairs={{0,1},{1,0},{2,3},{3,2},{4,5},{5,4},{6,7},{7,6},{8,9},{9,8},{10,11... | collective-permute-start | bytes 393224 | tf_op jit(solution)/shard_map/ppermute | solution.py:16
